TPU v7x, 32 devices: a whole 2x2x4 slice. The times are simulated.
32 devices in a mesh: group: 4 (over y, x), dev: 8 (over z, core).
Axes of the slice: x: 2, y: 2, z: 4, core: 2. Of those that a mesh axis runs over, the one named last changes fastest.
Arguments:
- queries: bfloat16 [16384, 1024], P(('group', 'dev')), may hold values from -2.5 to 2.5
- passages: bfloat16 [512, 32, 1024], P(('group', 'dev')), may hold values from -2.5 to 2.5
- block_ids: int32 [32, 4], replicated, may hold values from 0 to 31, as said below
- positives: int32 [16384], P(('group', 'dev')), may hold values from 0 to 511
Outputs:
- query_loss: float32 [16384], P(('group', 'dev'))
- query_grad: bfloat16 [16384, 1024], P(('group', 'dev'))
- passage_grad: bfloat16 [512, 32, 1024], P(('group', 'dev'))
Inputs may be any that keep to these rules, and one draw needn't show every extreme that they name: `block_ids`: row b names passage block b first (it holds the positives of query block b), then three other passage blocks, all four different.
All inputs are finite; a program needn't handle non-finite values.
Results may differ from a plain program's by a relative error of at most 0.0045.
Values may be sent and summed in bfloat16 or wider, within the bound.
No kernel may reach another device: no remote copies, remote signals or barrier semaphores. Data moves between devices by JAX's collectives and lax.ppermute only.
A program may use at most 64 MiB of HBM per device.

v0:
```python
import jax
import jax.numpy as jnp
from jax import lax
from jax.sharding import PartitionSpec as P

BLOCK = 512
REFS = 4
QB_DEV = 1


SCORE_SCALE = 0.8


def on_device(queries, passages, block_ids, positives):
    feat_width = queries.shape[1]
    own_rows = passages.shape[0]
    block_total = passages.shape[1]
    groups = lax.axis_size("group")
    members = lax.axis_size("dev")
    devices = groups * members
    id_table = block_ids.reshape(devices, QB_DEV, REFS)
    lane_rows = jnp.arange(own_rows, dtype=jnp.int32)
    row_index = jnp.transpose(id_table, (1, 2, 0))[:, :, :, None] + lane_rows * block_total
    flat_rows = row_index.reshape(-1)
    outgoing = jnp.take(passages.reshape(own_rows * block_total, feat_width), flat_rows, axis=0)
    outgoing = outgoing.reshape(QB_DEV, REFS, devices * own_rows, feat_width)
    arrived = lax.all_to_all(outgoing, ("group", "dev"), split_axis=2, concat_axis=2, tiled=True)
    candidate_passages = arrived.reshape(QB_DEV, REFS * BLOCK, feat_width)
    query_block_list = queries.reshape(QB_DEV, BLOCK, feat_width)
    logits = SCORE_SCALE * jnp.einsum(
        "pok,plk->pol", query_block_list, candidate_passages, preferred_element_type=jnp.float32
    )
    highest = jnp.max(logits, axis=2, keepdims=True)
    log_total = highest + jnp.log(jnp.sum(jnp.exp(logits - highest), axis=2, keepdims=True))
    columns = jnp.arange(REFS * BLOCK, dtype=jnp.int32)
    target = positives.reshape(QB_DEV, BLOCK)[:, :, None] == columns
    picked = jnp.sum(jnp.where(target, logits, 0.0), axis=2)
    query_loss = (log_total[:, :, 0] - picked).reshape(-1)
    logits_gradient = (jnp.exp(logits - log_total) - target.astype(jnp.float32)).astype(
        jnp.bfloat16
    )
    query_grad = SCORE_SCALE * jnp.einsum(
        "ouw,owf->ouf", logits_gradient, candidate_passages, preferred_element_type=jnp.float32
    )
    query_grad = query_grad.astype(jnp.bfloat16).reshape(-1, feat_width)
    contribution = SCORE_SCALE * jnp.einsum(
        "fak,fae->fke", logits_gradient, query_block_list, preferred_element_type=jnp.float32
    )
    contribution = contribution.astype(jnp.bfloat16).reshape(
        QB_DEV, REFS, devices * own_rows, feat_width
    )
    returned_rows = lax.all_to_all(
        contribution, ("group", "dev"), split_axis=2, concat_axis=2, tiled=True
    )
    summed = jax.ops.segment_sum(
        returned_rows.reshape(-1, feat_width).astype(jnp.float32),
        flat_rows,
        num_segments=own_rows * block_total,
    )
    passage_grad = summed.reshape(own_rows, block_total, feat_width).astype(jnp.bfloat16)
    return (query_loss, query_grad, passage_grad)


def solution(mesh):
    return jax.shard_map(
        on_device,
        mesh=mesh,
        in_specs=(
            P(("group", "dev"), None),
            P(("group", "dev"), None, None),
            P(),
            P(("group", "dev")),
        ),
        out_specs=(P(("group", "dev")), P(("group", "dev"), None), P(("group", "dev"), None, None)),
        check_vma=False,
    )
```

profile of v0, /device:TPU:0, one launch (start us, length us, event | category | flops | bytes accessed | tf_op | source)
XLA Modules:
  0.0 261.4 jit_solution(5758160825399045099)
XLA Ops:
  0.6 0.0 copy-start
  0.7 0.1 add.84
  0.7 0.8 broadcast_add_fusion
  1.6 0.1 add.91
  1.7 0.8 add.81
  2.5 0.1 add.82
  2.6 0.2 copy.10
  2.8 12.4 %gather_fusion = bf16[2048,1024]{1,0:T(8,128)(2,1)} fusion(bf16[512,1024]{1,0:T(8,128)(2,1)} %bitcast.35, s32[2048]{0:T(1024)S(1)} %broadcast_clamp_fusion), kind=kCustom, calls=%fused_computation | custom fusion | bytes 8396800 | tf_op jit(solution)/shard_map/jit(_take)/gather | solution.py:25
  15.1 6.5 %copy_select_fusion = bf16[1,4,512,1024]{3,1,0,2:T(4,128)(2,1)S(1)} fusion(bf16[1,4,512,1024]{3,2,1,0:T(8,128)(2,1)} %bitcast.36, pred[4,512]{0,1:T(8,128)(4,1)S(1)} %copy.10), kind=kLoop, calls=%fused_computation.14 | loop fusion | flops 2097152 | bytes 8390656 | tf_op jit(solution)/shard_map/jit(_take)/select_n | solution.py:25
  21.6 102.1 %all_to_all.10 = bf16[1,4,512,1024]{3,1,0,2:T(4,128)(2,1)S(1)} all-to-all(bf16[1,4,512,1024]{3,1,0,2:T(4,128)(2,1)S(1)} %copy_select_fusion), channel_id=1, replica_groups=mesh['group'=4,'dev'=8] {'group','dev'}, dimensions={2} | all-to-all | bytes 8388608 | tf_op jit(solution)/shard_map/all_to_all | solution.py:27
  123.7 1.4 copy.12
  125.1 0.0 copy-start.1
  125.1 0.0 copy-done
  125.1 0.0 copy-start.3
  125.1 2.4 multiply_reduce_fusion
  127.6 0.0 copy-done.1
  127.6 0.0 copy-start.2
  127.6 0.0 copy-done.3
  127.6 1.2 fusion.4
  128.8 0.7 fusion.11
  129.5 2.8 %multiply_convert_fusion = bf16[2048,1024]{1,0:T(8,128)(2,1)S(1)} fusion(bf16[512,1024]{1,0:T(8,128)(2,1)S(1)} %copy-done, f32[2048,512]{1,0:T(8,128)S(1)} %get-tuple-element.8, f32[512]{0:T(512)S(1)} %get-tuple-element.6, s32[512]{0:T(512)S(1)} %copy-done.3), kind=kOutput, calls=%fused_computation.4 | convolution fusion | flops 2157969408 | bytes 9441280 | tf_op jit(solution)/shard_map/fak,fae->fke/dot_general | solution.py:46
  132.3 0.0 copy-done.2
  132.3 5.2 %copy.13 = bf16[1,4,512,1024]{3,1,0,2:T(4,128)(2,1)} copy(bf16[1,4,512,1024]{3,2,1,0:T(8,128)(2,1)S(1)} %bitcast.40) | data formatting | bytes 8388608 | tf_op jit(solution)/shard_map/reshape | solution.py:49
  137.5 3.8 %all-to-all-start.1 = ((bf16[1,4,512,1024]{3,1,0,2:T(4,128)(2,1)}), bf16[1,4,512,1024]{3,1,0,2:T(4,128)(2,1)}, u32[]{:S(2)}, u32[]{:S(2)}) async-start(bf16[1,4,512,1024]{3,1,0,2:T(4,128)(2,1)} %copy.13), calls=%async_computation.1 | async-start | bytes 8388608 | tf_op jit(solution)/shard_map/all_to_all | solution.py:52
  141.3 0.1 reshape.188
  141.4 6.9 %multiply_convert_fusion.1 = bf16[512,1024]{1,0:T(8,128)(2,1)} fusion(bf16[2048,1024]{1,0:T(8,128)(2,1)} %bitcast.39, f32[2048,512]{1,0:T(8,128)} %copy-done.2, f32[512]{0:T(512)S(1)} %get-tuple-element.6, s32[512]{0:T(512)S(1)} %copy-done.3), kind=kOutput, calls=%fused_computation.17 | convolution fusion | flops 2154823680 | bytes 9441280 | tf_op jit(solution)/shard_map/ouw,owf->ouf/dot_general | solution.py:42
  148.2 87.9 %all-to-all-done.1 = bf16[1,4,512,1024]{3,1,0,2:T(4,128)(2,1)} async-done(((bf16[1,4,512,1024]{3,1,0,2:T(4,128)(2,1)}), bf16[1,4,512,1024]{3,1,0,2:T(4,128)(2,1)}, u32[]{:S(2)}, u32[]{:S(2)}) %all-to-all-start.1) | async-done | bytes 4194336 | tf_op jit(solution)/shard_map/all_to_all | solution.py:52
  236.1 5.5 %copy.14 = bf16[1,4,512,1024]{3,2,1,0:T(8,128)(2,1)} copy(bf16[1,4,512,1024]{3,1,0,2:T(4,128)(2,1)} %all-to-all-done.1) | data formatting | bytes 8388608 | tf_op jit(solution)/shard_map/all_to_all | solution.py:52
  241.7 18.6 %scatter_custom_fusion = f32[512,1024]{1,0:T(8,128)S(1)} fusion(s32[2048]{0:T(1024)S(1)} %reshape.188, bf16[2048,1024]{1,0:T(8,128)(2,1)} %bitcast.37, f32[]{:T(128)} %constant.26.clone.1), kind=kCustom, calls=%fused_computation.2 | custom fusion | flops 4194304 | bytes 6291460 | tf_op jit(solution)/shard_map/scatter-add | solution.py:55
  260.3 1.1 convert_element_type.34
  (5 shorter events, 0.0 us)
Async XLA Ops:
  0.6 124.5 %copy-start = (bf16[512,1024]{1,0:T(8,128)(2,1)S(1)}, bf16[512,1024]{1,0:T(8,128)(2,1)}, u32[]{:S(2)}) copy-start(bf16[512,1024]{1,0:T(8,128)(2,1)} %param.4) | copy-start | bytes 3145732
  125.1 2.5 copy-start.1
  125.1 2.5 copy-start.3
  127.6 4.7 %copy-start.2 = (f32[2048,512]{1,0:T(8,128)}, f32[2048,512]{1,0:T(8,128)S(1)}, u32[]{:S(2)}) copy-start(f32[2048,512]{1,0:T(8,128)S(1)} %get-tuple-element.8) | copy-start | bytes 12582916
  137.5 98.6 %all-to-all-start.1 = ((bf16[1,4,512,1024]{3,1,0,2:T(4,128)(2,1)}), bf16[1,4,512,1024]{3,1,0,2:T(4,128)(2,1)}, u32[]{:S(2)}, u32[]{:S(2)}) async-start(bf16[1,4,512,1024]{3,1,0,2:T(4,128)(2,1)} %copy.13), calls=%async_computation.1 | async-start | bytes 8388608 | tf_op jit(solution)/shard_map/all_to_all | solution.py:52
where the time goes:
time: 262 us; the launch traced here: 261 us
  blocking collectives  102 us (39%)
  waiting for transfers between devices  87.9 us (34%)
  other arithmetic  29 us (11%)
  local copies, waits for them, and re-layouts  25.8 us (10%)
  matrix products  12.1 us (5%)
  starting transfers between devices  3.78 us (1%)
    all_to_all x1, blocking collectives, on_device(): lax.all_to_all(outgoing, ('group', 'dev'), split_axis=2, concat_axis=2, t...  102 us
    all_to_all x1, waiting for transfers between devices, on_device(): lax.all_to_all(contribution, ('group', 'dev'), split_axis=2, concat_axis=...  87.9 us
    scatter-add x1, other arithmetic, on_device(): jax.ops.segment_sum(returned_rows.reshape(-1, feat_width).astype(jnp.floa...  18.6 us
    gather x1, local copies, waits for them, and re-layouts, on_device(): jnp.take(passages.reshape(own_rows * block_total, feat_width), flat_rows,...  12.4 us
    dot_general x1, matrix products, on_device(): jnp.einsum('ouw,owf->ouf', logits_gradient, candidate_passages, preferred...  6.87 us
    select_n x2, other arithmetic, on_device(): jnp.take(passages.reshape(own_rows * block_total, feat_width), flat_rows,...  6.47 us
    all_to_all x1, local copies, waits for them, and re-layouts, on_device(): lax.all_to_all(contribution, ('group', 'dev'), split_axis=2, concat_axis=...  5.53 us
  transfers between devices with their start and end apart: 1, of which 1 were waited for; matrix products, arithmetic and copies ran while one was open for 3% of the time, Pallas kernels for 0%

commit v1 on v0

v1 whole, which is shorter than its diff:
```python
import functools

import jax
import jax.numpy as jnp
from jax import lax
from jax.experimental import pallas as pl
from jax.experimental.pallas import tpu as pltpu
from jax.sharding import Mesh
from jax.sharding import PartitionSpec as P

SCALE = 0.8
PLANES = 4
BF16 = jnp.bfloat16
F32 = jnp.float32
PLANE = ("group", "rank")
VMEM = pl.BlockSpec(memory_space=pltpu.VMEM)


def params():
    return pltpu.CompilerParams(vmem_limit_bytes=40 << 20)


def gather_kernel(ids, rows_ref, out_ref):
    slab = pl.program_id(0)
    height = rows_ref.shape[1]
    picks = out_ref.shape[1] // height
    for i in range(picks):
        out_ref[0, i * height : (i + 1) * height, :] = rows_ref[ids[slab * picks + i]]


def gather_rows(ids, rows, slabs):
    blocks, height, width = rows.shape
    picks = ids.shape[0] // slabs
    return pl.pallas_call(
        gather_kernel,
        grid_spec=pltpu.PrefetchScalarGridSpec(
            num_scalar_prefetch=1,
            grid=(slabs,),
            in_specs=[pl.BlockSpec((blocks, height, width), lambda s, ids: (0, 0, 0))],
            out_specs=pl.BlockSpec((1, picks * height, width), lambda s, ids: (s, 0, 0)),
        ),
        out_shape=jax.ShapeDtypeStruct((slabs, picks * height, width), rows.dtype),
        compiler_params=params(),
        name="gather_rows",
        cost_estimate=pl.CostEstimate(flops=0, bytes_accessed=6 << 20, transcendentals=0),
    )(ids, rows)


def segment_kernel(with_start, ids, slabs_ref, *refs):
    start_ref = refs[0] if with_start else None
    out_ref, total = refs[-2:]
    slab = pl.program_id(0)
    height = total.shape[1]
    picks = slabs_ref.shape[1] // height

    @pl.when(slab == 0)
    def _():
        if with_start:
            total[...] = start_ref[...].astype(F32)
        else:
            total[...] = jnp.zeros_like(total)

    for i in range(picks):
        n = ids[slab * picks + i]
        total[n] += slabs_ref[0, i * height : (i + 1) * height, :].astype(F32)

    @pl.when(slab == pl.num_programs(0) - 1)
    def _():
        out_ref[...] = total[...].astype(out_ref.dtype)


def segment_rows(ids, slabs, blocks, start=None):
    count, depth, width = slabs.shape
    picks = ids.shape[0] // count
    height = depth // picks
    whole = pl.BlockSpec((blocks, height, width), lambda s, ids: (0, 0, 0))
    extra = [] if start is None else [start]
    return pl.pallas_call(
        functools.partial(segment_kernel, start is not None),
        grid_spec=pltpu.PrefetchScalarGridSpec(
            num_scalar_prefetch=1,
            grid=(count,),
            in_specs=[pl.BlockSpec((1, depth, width), lambda s, ids: (s, 0, 0))] + [whole] * len(extra),
            out_specs=whole,
            scratch_shapes=[pltpu.VMEM((blocks, height, width), F32)],
        ),
        out_shape=jax.ShapeDtypeStruct((blocks, height, width), BF16),
        compiler_params=params(),
        name="segment_rows",
        cost_estimate=pl.CostEstimate(flops=1 << 21, bytes_accessed=6 << 20, transcendentals=0),
    )(ids, slabs, *extra)


def candidates(slabs_ref, q):
    slabs, depth, width = slabs_ref.shape
    half = depth // 2
    return slabs_ref[:, q * half : (q + 1) * half, :].reshape(slabs * half, width)


def hits(shape, target_row):
    return lax.broadcasted_iota(jnp.int32, shape, 0) == target_row


def logits_kernel(queries_ref, others_ref, slabs_ref, target_ref, logits_ref, stats_ref):
    for q, block_ref in enumerate((queries_ref, others_ref)):
        block = lax.dot_general(
            candidates(slabs_ref, q), block_ref[...], (((1,), (1,)), ((), ())), preferred_element_type=F32
        )
        block = SCALE * block
        logits_ref[q] = block
        top = jnp.max(block, axis=0, keepdims=True)
        stats_ref[4 * q : 4 * q + 1, :] = top
        stats_ref[4 * q + 1 : 4 * q + 2, :] = jnp.sum(jnp.exp(block - top), axis=0, keepdims=True)
        hit = hits(block.shape, target_ref[q : q + 1, :])
        stats_ref[4 * q + 2 : 4 * q + 3, :] = jnp.sum(jnp.where(hit, block, 0.0), axis=0, keepdims=True)
        stats_ref[4 * q + 3 : 4 * q + 4, :] = jnp.zeros_like(top)


def half_logits(queries, others, slabs, target):
    size = queries.shape[0]
    rows = slabs.shape[0] * slabs.shape[1] // 2
    return pl.pallas_call(
        logits_kernel,
        in_specs=[VMEM] * 4,
        out_specs=[VMEM] * 2,
        out_shape=[jax.ShapeDtypeStruct((2, rows, size), F32), jax.ShapeDtypeStruct((8, size), F32)],
        compiler_params=params(),
        name="half_logits",
        cost_estimate=pl.CostEstimate(flops=1 << 30, bytes_accessed=6 << 20, transcendentals=1 << 19),
    )(queries, others, slabs, target)


def joined(a, b):
    top = jnp.maximum(a[0], b[0])
    return top, a[1] * jnp.exp(a[0] - top) + b[1] * jnp.exp(b[0] - top), a[2] + b[2]


def stat_rows(ref, q):
    return [ref[4 * q + i : 4 * q + i + 1, :] for i in range(3)]


def log_totals(first_ref, second_ref, partner_first_ref, partner_second_ref):
    out = []
    for q in range(2):
        here = joined(stat_rows(first_ref, q), stat_rows(second_ref, q))
        there = joined(stat_rows(partner_first_ref, 1 - q), stat_rows(partner_second_ref, 1 - q))
        top, total, pick = joined(here, there)
        out.append((top + jnp.log(total), pick))
    return out


def dlogits(logits, log_total, target_row):
    hit = hits(logits.shape, target_row)
    return (jnp.exp(logits - log_total) - jnp.where(hit, 1.0, 0.0)).astype(BF16)


def store_contrib(out_ref, q, piece, block):
    slabs, depth, width = out_ref.shape
    half = depth // 2
    product = SCALE * jnp.dot(piece, block, preferred_element_type=F32)
    out_ref[:, q * half : (q + 1) * half, :] = product.astype(BF16).reshape(slabs, half, width)


def far_kernel(queries_ref, others_ref, logits_ref, target_ref, s0, s1, p0, p1, contrib_ref, dlogits_ref, totals_ref):
    totals = log_totals(s0, s1, p0, p1)
    totals_ref[...] = jnp.zeros_like(totals_ref)
    for q, block_ref in enumerate((queries_ref, others_ref)):
        piece = dlogits(logits_ref[q], totals[q][0], target_ref[q : q + 1, :])
        dlogits_ref[q] = piece
        store_contrib(contrib_ref, q, piece, block_ref[...])
        totals_ref[q : q + 1, :] = totals[q][0]
    totals_ref[2:3, :] = totals[0][0] - totals[0][1]


def far_grads(queries, others, logits, target, stats, slabs):
    size = queries.shape[0]
    rows = logits.shape[1]
    return pl.pallas_call(
        far_kernel,
        in_specs=[VMEM] * 8,
        out_specs=[VMEM] * 3,
        out_shape=[
            jax.ShapeDtypeStruct(slabs.shape, BF16),
            jax.ShapeDtypeStruct((2, rows, size), BF16),
            jax.ShapeDtypeStruct((8, size), F32),
        ],
        compiler_params=params(),
        name="far_grads",
        cost_estimate=pl.CostEstimate(flops=1 << 30, bytes_accessed=8 << 20, transcendentals=1 << 19),
    )(queries, others, logits, target, *stats)


def query_product(near, near_ref, far, far_ref, q):
    dims = (((0,), (0,)), ((), ()))
    total = lax.dot_general(near, candidates(near_ref, q), dims, preferred_element_type=F32)
    total += lax.dot_general(far, candidates(far_ref, q), dims, preferred_element_type=F32)
    return SCALE * total


def other_kernel(logits_ref, target_ref, totals_ref, far_ref, near_slabs_ref, far_slabs_ref, other_ref):
    near = dlogits(logits_ref[1], totals_ref[1:2, :], target_ref[1:2, :])
    other_ref[...] = query_product(near, near_slabs_ref, far_ref[1], far_slabs_ref, 1).astype(BF16)


def other_grads(logits, target, totals, far, near_slabs, far_slabs):
    size, width = logits.shape[2], near_slabs.shape[2]
    return pl.pallas_call(
        other_kernel,
        in_specs=[VMEM] * 6,
        out_specs=VMEM,
        out_shape=jax.ShapeDtypeStruct((size, width), BF16),
        compiler_params=params(),
        name="other_grads",
        cost_estimate=pl.CostEstimate(flops=1 << 30, bytes_accessed=8 << 20, transcendentals=1 << 18),
    )(logits, target, totals, far, near_slabs, far_slabs)


def near_kernel(queries_ref, others_ref, logits_ref, target_ref, totals_ref, far_ref, near_slabs_ref, far_slabs_ref, contrib_ref, own_ref):
    for q, block_ref in enumerate((queries_ref, others_ref)):
        piece = dlogits(logits_ref[q], totals_ref[q : q + 1, :], target_ref[q : q + 1, :])
        store_contrib(contrib_ref, q, piece, block_ref[...])
        if q == 0:
            own_ref[...] = query_product(piece, near_slabs_ref, far_ref[0], far_slabs_ref, 0)


def near_grads(queries, others, logits, target, totals, far, near_slabs, far_slabs):
    return pl.pallas_call(
        near_kernel,
        in_specs=[VMEM] * 8,
        out_specs=[VMEM] * 2,
        out_shape=[
            jax.ShapeDtypeStruct(near_slabs.shape, BF16),
            jax.ShapeDtypeStruct(queries.shape, F32),
        ],
        compiler_params=params(),
        name="near_grads",
        cost_estimate=pl.CostEstimate(flops=1 << 31, bytes_accessed=14 << 20, transcendentals=1 << 19),
    )(queries, others, logits, target, totals, far, near_slabs, far_slabs)


def on_device(queries, passages, block_ids, positives):
    height, blocks, width = passages.shape
    refs = block_ids.shape[1]
    groups, planes, ranks = lax.axis_size("group"), lax.axis_size("z"), lax.axis_size("rank")
    slabs = groups * ranks
    z = lax.axis_index("z")
    to_pair = [(i, i ^ 1) for i in range(planes)]
    across = [(i, (i + planes // 2) % planes) for i in range(planes)]

    own_rows = jnp.transpose(passages, (1, 0, 2))
    pair_rows = lax.ppermute(own_rows, "z", to_pair)
    others = lax.ppermute(queries, "z", across)
    others_positives = lax.ppermute(positives, "z", across)

    table = block_ids.reshape(groups, planes, ranks, refs)
    both = jnp.stack([jnp.take(table, z, axis=1), jnp.take(table, (z + planes // 2) % planes, axis=1)], axis=2)
    ids = both.reshape(-1)

    chosen = jnp.stack([positives, others_positives])
    owner = chosen // height
    place = (owner // (planes * ranks) * ranks + owner % ranks) * (refs * height) + chosen % height
    plane = owner // ranks % planes
    near_target = jnp.where(plane == z, place, -1)
    far_target = jnp.where(plane == z ^ 1, place, -1)

    def exchange(slab_array):
        return lax.all_to_all(slab_array, PLANE, split_axis=0, concat_axis=0, tiled=True)

    near_slabs = exchange(gather_rows(ids, own_rows, slabs))
    far_slabs = exchange(gather_rows(ids, pair_rows, slabs))
    near_logits, near_stats = half_logits(queries, others, near_slabs, near_target)
    far_logits, far_stats = half_logits(queries, others, far_slabs, far_target)
    stats = jnp.concatenate([near_stats, far_stats])
    partner = lax.ppermute(stats, "z", across)
    all_stats = (near_stats, far_stats, partner[:8], partner[8:])

    far_contrib, far_pieces, totals = far_grads(queries, others, far_logits, far_target, all_stats, far_slabs)
    far_back = exchange(far_contrib)
    other_part = other_grads(near_logits, near_target, totals, far_pieces, near_slabs, far_slabs)
    own_part = lax.ppermute(other_part, "z", across)
    near_contrib, own_grad = near_grads(
        queries, others, near_logits, near_target, totals, far_pieces, near_slabs, far_slabs
    )
    near_back = exchange(near_contrib)

    pair_sum = lax.ppermute(segment_rows(ids, far_back, blocks), "z", to_pair)
    query_grad = (own_grad + own_part.astype(F32)).astype(BF16)
    row_sum = segment_rows(ids, near_back, blocks, pair_sum)
    return totals[2], query_grad, jnp.transpose(row_sum, (1, 0, 2))


def solution(mesh):
    groups, members = mesh.devices.shape
    split = Mesh(mesh.devices.reshape(groups, PLANES, members // PLANES), ("group", "z", "rank"))
    rows = ("group", "z", "rank")
    return jax.shard_map(
        on_device,
        mesh=split,
        in_specs=(P(rows, None), P(rows, None, None), P(), P(rows)),
        out_specs=(P(rows), P(rows, None), P(rows, None, None)),
        check_vma=False,
    )
```

time: 262 us -> 212 us (0.81)
  blocking collectives: 102 us -> 0 us
  waiting for transfers between devices: 87.9 us -> 136 us
  Pallas kernels: 0 us -> 28.2 us
  other arithmetic: 29 us -> 1.4 us
  starting transfers between devices: 3.78 us -> 26.6 us
  matrix products: 12.1 us -> 0 us
  local copies, waits for them, and re-layouts: 25.8 us -> 18.3 us
    ppermute x0 -> x6, waiting for transfers between devices: none -> 119 us  [the longest x1 46 us: on_device(): others_positives = lax.ppermute(positives, 'z', across)]
    all_to_all x1 -> x0, blocking collectives: 102 us -> none  [on_device(): lax.all_to_all(outgoing, ('group', 'dev'), split_axis=2, concat_axis=2, t...]
    all_to_all x1 -> x4, waiting for transfers between devices: 87.9 us -> 16.8 us  [exchange(): lax.all_to_all(slab_array, PLANE, split_axis=0, concat_axis=0, tiled=True)]
    pallas_call x0 -> x9, Pallas kernels: none -> 28.2 us  [the longest x2 9.97 us: segment_rows(): pl.pallas_call(functools.partial(segment_kernel, start is not None), grid...]
    scatter-add x1 -> x0, other arithmetic: 18.6 us -> none  [on_device(): jax.ops.segment_sum(returned_rows.reshape(-1, feat_width).astype(jnp.floa...]
    unnamed x8 -> x31, local copies, waits for them, and re-layouts: 0.02 us -> 17.6 us
    all_to_all x1 -> x4, starting transfers between devices: 3.78 us -> 18.5 us  [exchange(): lax.all_to_all(slab_array, PLANE, split_axis=0, concat_axis=0, tiled=True)]
    gather x1 -> x0, local copies, waits for them, and re-layouts: 12.4 us -> none  [on_device(): jnp.take(passages.reshape(own_rows * block_total, feat_width), flat_rows,...]
  transfers between devices with their start and end apart: 1 -> 10, of which waited for: 1 -> 6; matrix products, arithmetic and copies ran while one was open for 3% -> 1% of each run, Pallas kernels for 0% -> 8%
where the time goes in v1:
time: 212 us; the launch traced here: 211 us
  waiting for transfers between devices  136 us (64%)
  Pallas kernels  28.2 us (13%)
  starting transfers between devices  26.6 us (13%)
  local copies, waits for them, and re-layouts  18.3 us (9%)
    ppermute x1, waiting for transfers between devices, on_device(): others_positives = lax.ppermute(positives, 'z', across)  46 us
    ppermute x1, waiting for transfers between devices, on_device(): own_part = lax.ppermute(other_part, 'z', across)  39.9 us
    ppermute x1, waiting for transfers between devices, on_device(): pair_rows = lax.ppermute(own_rows, 'z', to_pair)  24 us
    all_to_all x4, starting transfers between devices, exchange(): lax.all_to_all(slab_array, PLANE, split_axis=0, concat_axis=0, tiled=True)  18.5 us
    unnamed x31, local copies, waits for them, and re-layouts  17.6 us
    all_to_all x4, waiting for transfers between devices, exchange(): lax.all_to_all(slab_array, PLANE, split_axis=0, concat_axis=0, tiled=True)  16.8 us
    pallas_call x2, Pallas kernels, segment_rows(): pl.pallas_call(functools.partial(segment_kernel, start is not None), grid...  9.97 us
    pallas_call x2, Pallas kernels, half_logits(): pl.pallas_call(logits_kernel, in_specs=[VMEM] * 4, out_specs=[VMEM] * 2,...  6.86 us
  transfers between devices with their start and end apart: 10, of which 6 were waited for; matrix products, arithmetic and copies ran while one was open for 1% of the time, Pallas kernels for 8%

profile of v1, /device:TPU:0, one launch (start us, length us, event | category | flops | bytes accessed | tf_op | source)
XLA Modules:
  0.0 211.3 jit_solution(13647180557239877787)
XLA Ops:
  1.5 1.8 copy.12
  4.2 1.3 copy-done.2
  5.5 5.2 %all-to-all-start.1 = ((bf16[8,128,1024]{2,1,0:T(8,128)(2,1)}), bf16[8,128,1024]{2,1,0:T(8,128)(2,1)S(1)}, u32[]{:S(2)}, u32[]{:S(2)}) async-start(bf16[8,128,1024]{2,1,0:T(8,128)(2,1)} %copy-done.2), calls=%async_computation.1 | async-start | bytes 4194304 | tf_op jit(solution)/shard_map/all_to_all | solution.py:267
  10.7 1.6 collective-permute-start.1
  12.3 24.0 %collective-permute-done.1.rows_ref = bf16[32,16,1024]{2,1,0:T(8,128)(2,1)S(1)} collective-permute-done((bf16[32,16,1024]{2,1,0:T(8,128)(2,1)S(1)}, bf16[32,16,1024]{2,1,0:T(8,128)(2,1)S(1)}, u32[]{:S(2)}, u32[]{:S(2)}) %collective-permute-start.1) | collective-permute-done | bytes 1048608 | tf_op jit(solution)/shard_map/ppermute | solution.py:251
  37.1 1.4 copy-done.1
  38.5 4.5 %all-to-all-start = ((bf16[8,128,1024]{2,1,0:T(8,128)(2,1)}), bf16[8,128,1024]{2,1,0:T(8,128)(2,1)}, u32[]{:S(2)}, u32[]{:S(2)}) async-start(bf16[8,128,1024]{2,1,0:T(8,128)(2,1)} %copy-done.1), calls=%async_computation | async-start | bytes 4194304 | tf_op jit(solution)/shard_map/all_to_all | solution.py:267
  42.9 2.7 %collective-permute-start = (bf16[512,1024]{1,0:T(8,128)(2,1)S(1)}, bf16[512,1024]{1,0:T(8,128)(2,1)}, u32[]{:S(2)}, u32[]{:S(2)}) collective-permute-start(bf16[512,1024]{1,0:T(8,128)(2,1)S(1)} %copy-done), channel_id=1, source_target_pairs={{0,4},{2,6},{4,0},{6,2},{1,5},{3,7},{5,1},{7,3},{8,12},{10,14},{12... | collective-permute-start | bytes 3145736 | tf_op jit(solution)/shard_map/ppermute | solution.py:252
  45.9 46.0 %collective-permute-done.2 = s32[512]{0:T(512)S(1)} collective-permute-done((s32[512]{0:T(512)S(1)}, s32[512]{0:T(512)S(1)}, u32[]{:S(2)}, u32[]{:S(2)}) %collective-permute-start.2) | collective-permute-done | bytes 2080 | tf_op jit(solution)/shard_map/ppermute | solution.py:253
  92.0 3.1 %half_logits.3 = (f32[2,512,512]{2,1,0:T(8,128)S(1)}, f32[8,512]{1,0:T(8,128)S(1)}) custom-call(bf16[512,1024]{1,0:T(8,128)(2,1)S(1)} %copy-done, bf16[512,1024]{1,0:T(8,128)(2,1)} %collective-permute-done.others_ref, bf16[8,128,1024]{2,1,0:T(8,128)(2,1)S(1)} %all-to-all-done.1.slabs_ref.near_slabs_ref, s32[2,512]{1,0:T(2,128)S(1)} %get-tuple-element.36.target_ref), custom_call_target="tpu_custom_call" | custom-call | flops 1073741824 | bytes 6291456 | tf_op jit(solution)/shard_map/half_logits/pallas_call | solution.py:122
  95.1 1.3 copy-done.3
  96.4 3.8 %half_logits.2 = (f32[2,512,512]{2,1,0:T(8,128)S(1)}, f32[8,512]{1,0:T(8,128)S(1)}) custom-call(bf16[512,1024]{1,0:T(8,128)(2,1)S(1)} %copy-done, bf16[512,1024]{1,0:T(8,128)(2,1)} %collective-permute-done.others_ref, bf16[8,128,1024]{2,1,0:T(8,128)(2,1)} %all-to-all-done.slabs_ref.far_slabs_ref, s32[2,512]{1,0:T(2,128)S(1)} %compare_select_fusion.3.target_ref), custom_call_target="tpu_custom_call" | custom-call | flops 1073741824 | bytes 6291456 | tf_op jit(solution)/shard_map/half_logits/pallas_call | solution.py:122
  100.3 5.5 %collective-permute-done.3 = f32[16,512]{1,0:T(8,128)S(1)} collective-permute-done((f32[16,512]{1,0:T(8,128)S(1)}, f32[16,512]{1,0:T(8,128)S(1)}, u32[]{:S(2)}, u32[]{:S(2)}) %collective-permute-start.3) | collective-permute-done | bytes 32800 | tf_op jit(solution)/shard_map/ppermute | solution.py:274
  105.8 2.6 %far_grads.1 = (bf16[8,128,1024]{2,1,0:T(8,128)(2,1)S(1)}, bf16[2,512,512]{2,1,0:T(8,128)(2,1)S(1)}, f32[8,512]{1,0:T(8,128)S(1)}) custom-call(bf16[512,1024]{1,0:T(8,128)(2,1)S(1)} %copy-done, bf16[512,1024]{1,0:T(8,128)(2,1)} %collective-permute-done.others_ref, f32[2,512,512]{2,1,0:T(8,128)S(1)} %get-tuple-element.13.logits_ref, ...), custom_call_target="tpu_custom_call" | custom-call | flops 1073741824 | bytes 8388608 | tf_op jit(solution)/shard_map/far_grads/pallas_call | solution.py:178
  109.3 1.4 copy-done.12
  110.7 4.3 %all-to-all-start.3 = ((bf16[8,128,1024]{2,1,0:T(8,128)(2,1)}), bf16[8,128,1024]{2,1,0:T(8,128)(2,1)}, u32[]{:S(2)}, u32[]{:S(2)}) async-start(bf16[8,128,1024]{2,1,0:T(8,128)(2,1)} %copy-done.12), calls=%async_computation.3 | async-start | bytes 4194304 | tf_op jit(solution)/shard_map/all_to_all | solution.py:267
  115.0 1.6 copy-done.4
  116.6 1.2 copy-done.7
  117.8 4.3 %near_grads.1 = (bf16[8,128,1024]{2,1,0:T(8,128)(2,1)S(1)}, f32[512,1024]{1,0:T(8,128)S(1)}) custom-call(bf16[512,1024]{1,0:T(8,128)(2,1)S(1)} %copy-done, bf16[512,1024]{1,0:T(8,128)(2,1)} %collective-permute-done.others_ref, f32[2,512,512]{2,1,0:T(8,128)S(1)} %copy-done.4, s32[2,512]{1,0:T(2,128)S(1)} %get-tuple-element.36.target_ref, ...), custom_call_target="tpu_custom_call" | custom-call | flops 2147483648 | bytes 14680064 | tf_op jit(solution)/shard_map/near_grads/pallas_call | solution.py:227
  122.1 1.4 copy-done.9
  123.5 1.4 copy-done.10
  124.9 16.8 %all-to-all-done.3.slabs_ref = bf16[8,128,1024]{2,1,0:T(8,128)(2,1)} async-done(((bf16[8,128,1024]{2,1,0:T(8,128)(2,1)}), bf16[8,128,1024]{2,1,0:T(8,128)(2,1)}, u32[]{:S(2)}, u32[]{:S(2)}) %all-to-all-start.3) | async-done | bytes 2097184 | tf_op jit(solution)/shard_map/all_to_all | solution.py:267
  141.7 4.5 %all-to-all-start.2 = ((bf16[8,128,1024]{2,1,0:T(8,128)(2,1)}), bf16[8,128,1024]{2,1,0:T(8,128)(2,1)}, u32[]{:S(2)}, u32[]{:S(2)}) async-start(bf16[8,128,1024]{2,1,0:T(8,128)(2,1)} %copy-done.9), calls=%async_computation.2 | async-start | bytes 4194304 | tf_op jit(solution)/shard_map/all_to_all | solution.py:267
  146.2 1.6 copy-done.5
  147.8 2.9 %other_grads.1 = bf16[512,1024]{1,0:T(8,128)(2,1)S(1)} custom-call(f32[2,512,512]{2,1,0:T(8,128)S(1)} %copy-done.5, s32[2,512]{1,0:T(2,128)S(1)} %get-tuple-element.36.target_ref, f32[8,512]{1,0:T(8,128)S(1)} %get-tuple-element.16.totals_ref, bf16[2,512,512]{2,1,0:T(8,128)(2,1)S(1)} %copy-done.8, ...), custom_call_target="tpu_custom_call" | custom-call | flops 1073741824 | bytes 8388608 | tf_op jit(solution)/shard_map/other_grads/pallas_call | solution.py:207
  150.7 5.0 %segment_rows.2 = bf16[32,16,1024]{2,1,0:T(8,128)(2,1)S(1)} custom-call(s32[64]{0:T(128)S(1)} %reshape.14.ids, bf16[8,128,1024]{2,1,0:T(8,128)(2,1)} %all-to-all-done.3.slabs_ref), custom_call_target="tpu_custom_call" | custom-call | flops 2097152 | bytes 6291456 | tf_op jit(solution)/shard_map/segment_rows/pallas_call | solution.py:78
  155.7 3.5 %collective-permute-start.5 = (bf16[32,16,1024]{2,1,0:T(8,128)(2,1)S(1)}, bf16[32,16,1024]{2,1,0:T(8,128)(2,1)S(1)}, u32[]{:S(2)}, u32[]{:S(2)}) collective-permute-start(bf16[32,16,1024]{2,1,0:T(8,128)(2,1)S(1)} %segment_rows.2), channel_id=1, source_target_pairs={{0,2},{2,0},{4,6},{6,4},{1,3},{3,1},{5,7},{7,5},{8,10},{10,8},{12,... | collective-permute-start | bytes 3145736 | tf_op jit(solution)/shard_map/ppermute | solution.py:286
  159.8 39.9 %collective-permute-done.4 = bf16[512,1024]{1,0:T(8,128)(2,1)S(1)} collective-permute-done((bf16[512,1024]{1,0:T(8,128)(2,1)S(1)}, bf16[512,1024]{1,0:T(8,128)(2,1)S(1)}, u32[]{:S(2)}, u32[]{:S(2)}) %collective-permute-start.4) | collective-permute-done | bytes 1048608 | tf_op jit(solution)/shard_map/ppermute | solution.py:280
  199.6 1.3 add_convert_fusion
  201.0 3.8 %collective-permute-done.5.refs_0_ = bf16[32,16,1024]{2,1,0:T(8,128)(2,1)S(1)} collective-permute-done((bf16[32,16,1024]{2,1,0:T(8,128)(2,1)S(1)}, bf16[32,16,1024]{2,1,0:T(8,128)(2,1)S(1)}, u32[]{:S(2)}, u32[]{:S(2)}) %collective-permute-start.5) | collective-permute-done | bytes 1048608 | tf_op jit(solution)/shard_map/ppermute | solution.py:286
  204.8 5.0 %segment_rows.3 = bf16[32,16,1024]{2,1,0:T(8,128)(2,1)S(1)} custom-call(s32[64]{0:T(128)S(1)} %reshape.14.ids, bf16[8,128,1024]{2,1,0:T(8,128)(2,1)} %all-to-all-done.2.slabs_ref, bf16[32,16,1024]{2,1,0:T(8,128)(2,1)S(1)} %collective-permute-done.5.refs_0_), custom_call_target="tpu_custom_call" | custom-call | flops 2097152 | bytes 6291456 | tf_op jit(solution)/shard_map/segment_rows/pallas_call | solution.py:78
  209.8 1.5 copy.10
  (38 shorter events, 4.6 us)
Async XLA Ops:
  4.2 1.4 copy-start.2
  5.5 32.9 %all-to-all-start.1 = ((bf16[8,128,1024]{2,1,0:T(8,128)(2,1)}), bf16[8,128,1024]{2,1,0:T(8,128)(2,1)S(1)}, u32[]{:S(2)}, u32[]{:S(2)}) async-start(bf16[8,128,1024]{2,1,0:T(8,128)(2,1)} %copy-done.2), calls=%async_computation.1 | async-start | bytes 4194304 | tf_op jit(solution)/shard_map/all_to_all | solution.py:267
  10.7 25.6 %collective-permute-start.1 = (bf16[32,16,1024]{2,1,0:T(8,128)(2,1)S(1)}, bf16[32,16,1024]{2,1,0:T(8,128)(2,1)S(1)}, u32[]{:S(2)}, u32[]{:S(2)}) collective-permute-start(bf16[32,16,1024]{2,1,0:T(8,128)(2,1)S(1)} %bitcast.16), channel_id=1, source_target_pairs={{0,2},{2,0},{4,6},{6,4},{1,3},{3,1},{5,7},{7,5},{8,10},{10,8},{12,... | collective-permute-start | bytes 3145736 | tf_op jit(solution)/shard_map/ppermute | solution.py:251
  37.1 1.4 copy-start.1
  38.5 4.5 %copy-start = (bf16[512,1024]{1,0:T(8,128)(2,1)S(1)}, bf16[512,1024]{1,0:T(8,128)(2,1)}, u32[]{:S(2)}) copy-start(bf16[512,1024]{1,0:T(8,128)(2,1)} %queries_ref.7) | copy-start | bytes 3145732
  38.5 7.2 %copy-start.13 = (s32[512]{0:T(512)S(1)}, s32[512]{0:T(512)}, u32[]{:S(2)}) copy-start(s32[512]{0:T(512)} %param.9) | copy-start | bytes 6148
  38.5 58.0 %all-to-all-start = ((bf16[8,128,1024]{2,1,0:T(8,128)(2,1)}), bf16[8,128,1024]{2,1,0:T(8,128)(2,1)}, u32[]{:S(2)}, u32[]{:S(2)}) async-start(bf16[8,128,1024]{2,1,0:T(8,128)(2,1)} %copy-done.1), calls=%async_computation | async-start | bytes 4194304 | tf_op jit(solution)/shard_map/all_to_all | solution.py:267
  42.9 49.1 %collective-permute-start = (bf16[512,1024]{1,0:T(8,128)(2,1)S(1)}, bf16[512,1024]{1,0:T(8,128)(2,1)}, u32[]{:S(2)}, u32[]{:S(2)}) collective-permute-start(bf16[512,1024]{1,0:T(8,128)(2,1)S(1)} %copy-done), channel_id=1, source_target_pairs={{0,4},{2,6},{4,0},{6,2},{1,5},{3,7},{5,1},{7,3},{8,12},{10,14},{12... | collective-permute-start | bytes 3145736 | tf_op jit(solution)/shard_map/ppermute | solution.py:252
  45.6 46.3 %collective-permute-start.2 = (s32[512]{0:T(512)S(1)}, s32[512]{0:T(512)S(1)}, u32[]{:S(2)}, u32[]{:S(2)}) collective-permute-start(s32[512]{0:T(512)S(1)} %copy-done.13), channel_id=1, source_target_pairs={{0,4},{2,6},{4,0},{6,2},{1,5},{3,7},{5,1},{7,3},{8,12},{10,14},{12... | collective-permute-start | bytes 6152 | tf_op jit(solution)/shard_map/ppermute | solution.py:253
  95.1 1.3 copy-start.3
  100.2 5.5 %collective-permute-start.3 = (f32[16,512]{1,0:T(8,128)S(1)}, f32[16,512]{1,0:T(8,128)S(1)}, u32[]{:S(2)}, u32[]{:S(2)}) collective-permute-start(f32[16,512]{1,0:T(8,128)S(1)} %pad_maximum_fusion), channel_id=1, source_target_pairs={{0,4},{2,6},{4,0},{6,2},{1,5},{3,7},{5,1},{7,3},{8,12},{10,14},{12... | collective-permute-start | bytes 98312 | tf_op jit(solution)/shard_map/ppermute | solution.py:274
  108.3 1.0 copy-start.6
  109.3 1.4 copy-start.12
  110.7 31.0 %all-to-all-start.3 = ((bf16[8,128,1024]{2,1,0:T(8,128)(2,1)}), bf16[8,128,1024]{2,1,0:T(8,128)(2,1)}, u32[]{:S(2)}, u32[]{:S(2)}) async-start(bf16[8,128,1024]{2,1,0:T(8,128)(2,1)} %copy-done.12), calls=%async_computation.3 | async-start | bytes 4194304 | tf_op jit(solution)/shard_map/all_to_all | solution.py:267
  115.0 1.6 copy-start.4
  116.6 1.2 copy-start.7
  122.1 1.4 copy-start.9
  123.5 1.4 copy-start.10
  141.7 4.5 %copy-start.8 = (bf16[2,512,512]{2,1,0:T(8,128)(2,1)S(1)}, bf16[2,512,512]{2,1,0:T(8,128)(2,1)}, u32[]{:S(2)}) copy-start(bf16[2,512,512]{2,1,0:T(8,128)(2,1)} %copy-done.6) | copy-start | bytes 3145732
  141.7 59.3 %all-to-all-start.2 = ((bf16[8,128,1024]{2,1,0:T(8,128)(2,1)}), bf16[8,128,1024]{2,1,0:T(8,128)(2,1)}, u32[]{:S(2)}, u32[]{:S(2)}) async-start(bf16[8,128,1024]{2,1,0:T(8,128)(2,1)} %copy-done.9), calls=%async_computation.2 | async-start | bytes 4194304 | tf_op jit(solution)/shard_map/all_to_all | solution.py:267
  146.2 1.6 copy-start.5
  150.7 49.0 %copy-start.11 = (f32[512,1024]{1,0:T(8,128)S(1)}, f32[512,1024]{1,0:T(8,128)}, u32[]{:S(2)}) copy-start(f32[512,1024]{1,0:T(8,128)} %copy-done.10) | copy-start | bytes 6291460
  150.7 49.0 %collective-permute-start.4 = (bf16[512,1024]{1,0:T(8,128)(2,1)S(1)}, bf16[512,1024]{1,0:T(8,128)(2,1)S(1)}, u32[]{:S(2)}, u32[]{:S(2)}) collective-permute-start(bf16[512,1024]{1,0:T(8,128)(2,1)S(1)} %other_grads.1), channel_id=1, source_target_pairs={{0,4},{2,6},{4,0},{6,2},{1,5},{3,7},{5,1},{7,3},{8,12},{10,14},{12... | collective-permute-start | bytes 3145736 | tf_op jit(solution)/shard_map/ppermute | solution.py:280
  155.7 49.0 %collective-permute-start.5 = (bf16[32,16,1024]{2,1,0:T(8,128)(2,1)S(1)}, bf16[32,16,1024]{2,1,0:T(8,128)(2,1)S(1)}, u32[]{:S(2)}, u32[]{:S(2)}) collective-permute-start(bf16[32,16,1024]{2,1,0:T(8,128)(2,1)S(1)} %segment_rows.2), channel_id=1, source_target_pairs={{0,2},{2,0},{4,6},{6,4},{1,3},{3,1},{5,7},{7,5},{8,10},{10,8},{12,... | collective-permute-start | bytes 3145736 | tf_op jit(solution)/shard_map/ppermute | solution.py:286

commit v2 on v0

v2 whole, which is shorter than its diff:
```python
import functools

import jax
import jax.numpy as jnp
from jax import lax
from jax.experimental import pallas as pl
from jax.experimental.pallas import tpu as pltpu
from jax.sharding import Mesh
from jax.sharding import PartitionSpec as P

SCALE = 0.8
PLANES = 4
CHUNKS = 2
EARLY = 4
BF16 = jnp.bfloat16
F32 = jnp.float32
BUSY = 1 << 37
PLANE = ("group", "rank")
ANY = pl.BlockSpec(memory_space=pl.ANY)
HBM = pl.BlockSpec(memory_space=pltpu.HBM)
VMEM = pl.BlockSpec(memory_space=pltpu.VMEM)
SMEM = pl.BlockSpec(memory_space=pltpu.SMEM)


def params():
    return pltpu.CompilerParams(vmem_limit_bytes=28 << 20)


def cost(flops, mib):
    return pl.CostEstimate(flops=flops, bytes_accessed=mib << 20, transcendentals=0)


def in_hbm(array):
    return pltpu.with_memory_space_constraint(array, pltpu.HBM)


def shape(dims, dtype):
    return jax.ShapeDtypeStruct(dims, dtype)


def after_kernel(*refs):
    del refs


def after(array, *others):
    return pl.pallas_call(
        after_kernel,
        in_specs=[ANY] * (1 + len(others)),
        out_specs=ANY,
        out_shape=shape(array.shape, array.dtype),
        input_output_aliases={0: 0},
        name="after",
    )(array, *others)


def gather_kernel(planes, ranks, ids, rows_ref, out_ref, made, left):
    slabs, depth, width = out_ref.shape
    height = rows_ref.shape[1]
    refs = ids.shape[0]
    z = lax.axis_index("z")

    def sent(slab):
        return pltpu.make_async_copy(made.at[slab], out_ref.at[slab], left.at[slab])

    def fill(slab, carry):
        for pick in range(2 * refs):
            there = (z + pick // refs * (planes // 2)) % planes
            owner = (slab // ranks * planes + there) * ranks + slab % ranks
            made[slab, pick * height : (pick + 1) * height, :] = rows_ref[ids[pick % refs, owner]]
        sent(slab).start()
        return carry

    def drain(slab, carry):
        sent(slab).wait()
        return carry

    lax.fori_loop(0, slabs, fill, 0)
    lax.fori_loop(0, slabs, drain, 0)


def gather_rows(ids, rows, slabs, planes, ranks, flops):
    blocks, height, width = rows.shape
    dims = (slabs, 2 * ids.shape[0] * height, width)
    return pl.pallas_call(
        functools.partial(gather_kernel, planes, ranks),
        in_specs=[SMEM, VMEM],
        out_specs=HBM,
        out_shape=pltpu.HBM(dims, BF16),
        scratch_shapes=[pltpu.VMEM(dims, BF16), pltpu.SemaphoreType.DMA((slabs,))],
        compiler_params=params(),
        name="gather_rows",
        cost_estimate=cost(flops, 4),
    )(ids, rows)


def segment_kernel(stripes, with_start, spread_ref, slabs_ref, *refs):
    start_ref = refs[0] if with_start else None
    out_ref, held, result, begun, arrived, left = refs[-6:]
    slabs, depth, width = slabs_ref.shape
    tile = width // stripes
    columns = [pl.ds(t * tile, tile) for t in range(stripes)]
    loads = [
        pltpu.make_async_copy(slabs_ref.at[:, :, columns[t]], held.at[t], arrived.at[t]) for t in range(stripes)
    ]
    for load in loads:
        load.start()
    if with_start:
        first = pltpu.make_async_copy(start_ref, begun, arrived.at[stripes])
        first.start()
        first.wait()
    stores = []
    for t in range(stripes):
        loads[t].wait()
        total = jnp.dot(spread_ref[...], held[t].reshape(slabs * depth, tile), preferred_element_type=F32)
        if with_start:
            total += begun[:, t * tile : (t + 1) * tile].astype(F32)
        result[t] = total.astype(BF16)
        stores.append(pltpu.make_async_copy(result.at[t], out_ref.at[:, columns[t]], left.at[t]))
        stores[t].start()
    for store in stores:
        store.wait()


def segment_rows(spread, slabs, *start):
    stripes = 4
    rows = spread.shape[0]
    count, depth, width = slabs.shape
    tile = width // stripes
    return pl.pallas_call(
        functools.partial(segment_kernel, stripes, len(start) > 0),
        in_specs=[VMEM, HBM] + [HBM] * len(start),
        out_specs=HBM,
        out_shape=pltpu.HBM((rows, width), BF16),
        scratch_shapes=[
            pltpu.VMEM((stripes, count, depth, tile), BF16),
            pltpu.VMEM((stripes, rows, tile), BF16),
            pltpu.VMEM((rows, width) if start else (16, 128), BF16),
            pltpu.SemaphoreType.DMA((stripes + 1,)),
            pltpu.SemaphoreType.DMA((stripes,)),
        ],
        compiler_params=params(),
        name="segment_rows",
        cost_estimate=cost(1 << 30, 4),
    )(spread, slabs, *start)


def candidates(slabs_ref, q, chunk):
    slabs, depth, width = slabs_ref.shape
    part, half = slabs // CHUNKS, depth // 2
    block = slabs_ref[chunk * part : (chunk + 1) * part, q * half : (q + 1) * half, :]
    return block.reshape(part * half, width)


def hits(rows, chunk, target_row):
    row = lax.broadcasted_iota(jnp.int32, (rows, target_row.shape[1]), 0)
    return row + chunk * rows == target_row


def joined(a, b):
    top = jnp.maximum(a[0], b[0])
    return top, a[1] * jnp.exp(a[0] - top) + b[1] * jnp.exp(b[0] - top), a[2] + b[2]


def stat_rows(ref, q):
    return [ref[4 * q + i : 4 * q + i + 1, :] for i in range(3)]


def chunk_rows(ref, chunk):
    rows = ref.shape[1] // CHUNKS
    return slice(chunk * rows, (chunk + 1) * rows)


def place_of(far, planes, ranks, refs, height, chosen):
    owner = chosen // height
    spot = (owner // (planes * ranks) * ranks + owner % ranks) * (refs * height) + chosen % height
    return jnp.where(owner // ranks % planes == lax.axis_index("z") ^ far, spot, -1)


def load_chunks(source, held, arrived):
    part = source.shape[0] // CHUNKS
    loads = []
    for c in range(CHUNKS):
        rows = pl.ds(c * part, part)
        loads.append(pltpu.make_async_copy(source.at[rows], held.at[rows], arrived.at[c]))
        loads[c].start()
    return loads


def logits_body(place, blocks, slabs_ref, chosen_refs, held, arrived, put, target_ref):
    loads = load_chunks(slabs_ref, held, arrived)
    target_ref[...] = jnp.full(target_ref.shape, -1, jnp.int32)
    for q, ref in enumerate(chosen_refs):
        target_ref[q : q + 1, :] = place(ref[...])
    stats = [None, None]
    for c in range(CHUNKS):
        loads[c].wait()
        for q, block_ref in enumerate(blocks):
            block = lax.dot_general(
                candidates(held, q, c), block_ref[...], (((1,), (1,)), ((), ())), preferred_element_type=F32
            )
            block = SCALE * block
            put(q, c, block)
            top = jnp.max(block, axis=0, keepdims=True)
            total = jnp.sum(jnp.exp(block - top), axis=0, keepdims=True)
            hit = hits(block.shape[0], c, target_ref[q : q + 1, :])
            pick = jnp.sum(jnp.where(hit, block, 0.0), axis=0, keepdims=True)
            here = (top, total, pick)
            stats[q] = here if c == 0 else joined(stats[q], here)
    return stats


def put_stats(stats_ref, stats):
    for q in range(2):
        for i in range(3):
            stats_ref[4 * q + i : 4 * q + i + 1, :] = stats[q][i]
        stats_ref[4 * q + 3 : 4 * q + 4, :] = jnp.zeros_like(stats[q][0])


def near_logits_kernel(
    place, queries_ref, low_ref, high_ref, slabs_ref, chosen_ref, chosen_others_ref,
    logits_ref, stats_ref, target_ref, others_ref, held, made, arrived, left,
):
    cut = low_ref.shape[0]
    others_ref[:cut, :] = low_ref[...]
    others_ref[cut:, :] = high_ref[...]
    stores = []

    def put(q, c, block):
        rows = chunk_rows(logits_ref, c)
        made[q, rows, :] = block
        piece = pl.ds(rows.start, rows.stop - rows.start)
        stores.append(pltpu.make_async_copy(made.at[q, piece], logits_ref.at[q, piece], left.at[q, c]))
        stores[-1].start()

    blocks = (queries_ref, others_ref)
    stats = logits_body(place, blocks, slabs_ref, (chosen_ref, chosen_others_ref), held, arrived, put, target_ref)
    put_stats(stats_ref, stats)
    for store in stores:
        store.wait()


def near_half(queries, low, high, slabs, chosen, chosen_others, place):
    size = queries.shape[0]
    rows = slabs.shape[0] * slabs.shape[1] // 2
    return pl.pallas_call(
        functools.partial(near_logits_kernel, place),
        in_specs=[VMEM, VMEM, VMEM, HBM, VMEM, VMEM],
        out_specs=[HBM, VMEM, VMEM, VMEM],
        out_shape=[
            pltpu.HBM((2, rows, size), F32),
            shape((8, size), F32),
            shape((8, size), jnp.int32),
            shape(queries.shape, BF16),
        ],
        scratch_shapes=[
            pltpu.VMEM(slabs.shape, BF16),
            pltpu.VMEM((2, rows, size), F32),
            pltpu.SemaphoreType.DMA((CHUNKS,)),
            pltpu.SemaphoreType.DMA((2, CHUNKS)),
        ],
        compiler_params=params(),
        name="near_half",
        cost_estimate=cost(BUSY, 4),
    )(queries, low, high, slabs, chosen, chosen_others)


def far_logits_kernel(
    place, queries_ref, others_ref, slabs_ref, chosen_ref, chosen_others_ref, near_stats_ref,
    logits_ref, stats_ref, target_ref, held, arrived,
):
    def put(q, c, block):
        logits_ref[q, chunk_rows(logits_ref, c), :] = block

    blocks = (queries_ref, others_ref)
    stats = logits_body(place, blocks, slabs_ref, (chosen_ref, chosen_others_ref), held, arrived, put, target_ref)
    put_stats(stats_ref, [joined(stat_rows(near_stats_ref, q), stats[q]) for q in range(2)])


def far_half(queries, others, slabs, chosen, chosen_others, near_stats, place):
    size = queries.shape[0]
    rows = slabs.shape[0] * slabs.shape[1] // 2
    return pl.pallas_call(
        functools.partial(far_logits_kernel, place),
        in_specs=[VMEM, VMEM, HBM, VMEM, VMEM, VMEM],
        out_specs=[VMEM] * 3,
        out_shape=[shape((2, rows, size), F32), shape((8, size), F32), shape((8, size), jnp.int32)],
        scratch_shapes=[pltpu.VMEM(slabs.shape, BF16), pltpu.SemaphoreType.DMA((CHUNKS,))],
        compiler_params=params(),
        name="far_half",
        cost_estimate=cost(1 << 30, 4),
    )(queries, others, slabs, chosen, chosen_others, near_stats)


def log_totals(here_ref, there_ref):
    out = []
    for q in range(2):
        top, total, pick = joined(stat_rows(here_ref, q), stat_rows(there_ref, 1 - q))
        out.append((top + jnp.log(total), pick))
    return out


def dlogits(logits, log_total, chunk, target_row):
    hit = hits(logits.shape[0], chunk, target_row)
    return (jnp.exp(logits - log_total) - jnp.where(hit, 1.0, 0.0)).astype(BF16)


def send_contrib(made, out_ref, left, chunk, q, piece, block, complete):
    slabs, depth, width = out_ref.shape
    part, half = slabs // CHUNKS, depth // 2
    product = SCALE * jnp.dot(piece, block, preferred_element_type=F32)
    made[chunk, :, q * half : (q + 1) * half, :] = product.astype(BF16).reshape(part, half, width)
    if not complete:
        return []
    store = pltpu.make_async_copy(made.at[chunk], out_ref.at[pl.ds(chunk * part, part)], left.at[chunk])
    store.start()
    return [store]


def contrib_scratch(slabs):
    return [
        pltpu.VMEM((CHUNKS, slabs.shape[0] // CHUNKS) + slabs.shape[1:], BF16),
        pltpu.SemaphoreType.DMA((CHUNKS,)),
    ]


def far_kernel(
    queries_ref, others_ref, logits_ref, target_ref, here_ref, there_ref,
    contrib_ref, dlogits_ref, totals_ref, loss_ref, made, left,
):
    totals = log_totals(here_ref, there_ref)
    stores = []
    for c in range(CHUNKS):
        rows = chunk_rows(logits_ref, c)
        for q, block_ref in enumerate((queries_ref, others_ref)):
            piece = dlogits(logits_ref[q, rows, :], totals[q][0], c, target_ref[q : q + 1, :])
            dlogits_ref[q, rows, :] = piece
            stores += send_contrib(made, contrib_ref, left, c, q, piece, block_ref[...], q == 1)
    totals_ref[...] = jnp.zeros_like(totals_ref)
    for q in range(2):
        totals_ref[q : q + 1, :] = totals[q][0]
    loss_ref[...] = totals[0][0] - totals[0][1]
    for store in stores:
        store.wait()


def far_grads(queries, others, logits, target, here, there, slabs):
    size = queries.shape[0]
    rows = logits.shape[1]
    return pl.pallas_call(
        far_kernel,
        in_specs=[VMEM] * 6,
        out_specs=[HBM, VMEM, VMEM, VMEM],
        out_shape=[
            pltpu.HBM(slabs.shape, BF16),
            shape((2, rows, size), BF16),
            shape((8, size), F32),
            shape((1, size), F32),
        ],
        scratch_shapes=contrib_scratch(slabs),
        compiler_params=params(),
        name="far_grads",
        cost_estimate=cost(1 << 30, 4),
    )(queries, others, logits, target, here, there)


def rest_kernel(
    queries_ref, others_ref, logits_ref, target_ref, totals_ref, far_ref, near_slabs_ref, far_slabs_ref,
    other_ref, contrib_ref, own_ref,
    near, far, logits, other, own, made, near_in, far_in, logits_in, other_out, own_out, left,
):
    dims = (((0,), (0,)), ((), ()))
    scores = []
    for q in (1, 0):
        scores.append(pltpu.make_async_copy(logits_ref.at[q], logits.at[q], logits_in.at[q]))
        scores[-1].start()
    near_loads = load_chunks(near_slabs_ref, near, near_in)
    far_loads = load_chunks(far_slabs_ref, far, far_in)
    stores = []
    for turn, (q, block_ref) in enumerate(((1, others_ref), (0, queries_ref))):
        scores[turn].wait()
        total = None
        for c in range(CHUNKS):
            rows = chunk_rows(logits, c)
            piece = dlogits(logits[q, rows, :], totals_ref[q : q + 1, :], c, target_ref[q : q + 1, :])
            if turn == 0:
                near_loads[c].wait()
                far_loads[c].wait()
            share = lax.dot_general(piece, candidates(near, q, c), dims, preferred_element_type=F32)
            share += lax.dot_general(far_ref[q, rows, :], candidates(far, q, c), dims, preferred_element_type=F32)
            total = share if c == 0 else total + share
            stores += send_contrib(made, contrib_ref, left, c, q, piece, block_ref[...], q == 0)
        if q == 1:
            other[...] = (SCALE * total).astype(BF16)
            stores.append(pltpu.make_async_copy(other, other_ref, other_out))
        else:
            own[...] = SCALE * total
            stores.append(pltpu.make_async_copy(own, own_ref, own_out))
        stores[-1].start()
    for store in stores:
        store.wait()


def rest_grads(queries, others, logits, target, totals, far_pieces, near_slabs, far_slabs):
    chunk_sems = pltpu.SemaphoreType.DMA((CHUNKS,))
    made, left = contrib_scratch(near_slabs)
    return pl.pallas_call(
        rest_kernel,
        in_specs=[VMEM, VMEM, HBM, VMEM, VMEM, VMEM, HBM, HBM],
        out_specs=[HBM] * 3,
        out_shape=[
            pltpu.HBM(queries.shape, BF16),
            pltpu.HBM(near_slabs.shape, BF16),
            pltpu.HBM(queries.shape, F32),
        ],
        scratch_shapes=[
            pltpu.VMEM(near_slabs.shape, BF16),
            pltpu.VMEM(far_slabs.shape, BF16),
            pltpu.VMEM(logits.shape, F32),
            pltpu.VMEM(queries.shape, BF16),
            pltpu.VMEM(queries.shape, F32),
            made,
            chunk_sems,
            chunk_sems,
            pltpu.SemaphoreType.DMA((2,)),
            pltpu.SemaphoreType.DMA,
            pltpu.SemaphoreType.DMA,
            left,
        ],
        compiler_params=params(),
        name="rest_grads",
        cost_estimate=cost(3 << 30, 8),
    )(queries, others, logits, target, totals, far_pieces, near_slabs, far_slabs)


def add_kernel(own_ref, part_ref, out_ref):
    out_ref[...] = (own_ref[...] + part_ref[...].astype(F32)).astype(BF16)


def add_parts(own, part):
    block = pl.BlockSpec((own.shape[0] // 4, own.shape[1]), lambda i: (i, 0))
    return pl.pallas_call(
        add_kernel,
        grid=(4,),
        in_specs=[block] * 2,
        out_specs=block,
        out_shape=shape(own.shape, BF16),
        compiler_params=params(),
        name="add_parts",
        cost_estimate=cost(BUSY, 4),
    )(own, part)


def on_device(queries, passages, block_ids, positives):
    height, blocks, width = passages.shape
    refs = block_ids.shape[1]
    groups, planes, ranks = lax.axis_size("group"), lax.axis_size("z"), lax.axis_size("rank")
    slabs = groups * ranks
    z = lax.axis_index("z")
    to_pair = [(i, i ^ 1) for i in range(planes)]
    across = [(i, (i + planes // 2) % planes) for i in range(planes)]

    def exchange(slab_array):
        return in_hbm(lax.all_to_all(slab_array, PLANE, split_axis=0, concat_axis=0, tiled=True))

    ids = block_ids.T
    early = queries.shape[0] // EARLY
    own_rows = jnp.transpose(passages, (1, 0, 2))
    near_slabs = exchange(gather_rows(ids, own_rows, slabs, planes, ranks, 0))
    pair_rows = lax.ppermute(own_rows, "z", to_pair)
    others_low = lax.ppermute(queries[:early], "z", across)
    others_high = lax.ppermute(after(queries[early:], pair_rows, others_low), "z", across)
    others_positives = lax.ppermute(positives, "z", across)
    far_slabs = exchange(gather_rows(ids, pair_rows, slabs, planes, ranks, BUSY))

    table = block_ids.reshape(groups, planes, ranks, refs)
    both = jnp.stack([jnp.take(table, z, axis=1), jnp.take(table, (z + planes // 2) % planes, axis=1)], axis=2)
    place = (jnp.arange(height, dtype=jnp.int32) * blocks + both.reshape(-1, 1)).reshape(1, -1)
    spread = (jnp.arange(height * blocks, dtype=jnp.int32)[:, None] == place).astype(BF16)

    chosen = positives.reshape(1, -1)
    chosen_others = others_positives.reshape(1, -1)
    near_logits, near_stats, near_target, others = near_half(
        queries,
        others_low,
        others_high,
        near_slabs,
        chosen,
        chosen_others,
        functools.partial(place_of, 0, planes, ranks, refs, height),
    )
    far_logits, stats, far_target = far_half(
        queries,
        others,
        far_slabs,
        chosen,
        chosen_others,
        near_stats,
        functools.partial(place_of, 1, planes, ranks, refs, height),
    )
    partner = lax.ppermute(stats, "z", across)
    far_contrib, far_pieces, totals, loss = far_grads(
        queries, others, far_logits, far_target, stats, partner, far_slabs
    )
    far_back = exchange(far_contrib)
    other_part, near_contrib, own_grad = rest_grads(
        queries, others, in_hbm(near_logits), near_target, totals, far_pieces, near_slabs, far_slabs
    )
    own_part = lax.ppermute(other_part, "z", across)
    far_sum = segment_rows(spread, far_back)
    pair_sum = lax.ppermute(far_sum, "z", to_pair)
    near_back = exchange(after(near_contrib, far_sum))
    query_grad = add_parts(own_grad, own_part)
    row_sum = segment_rows(spread, near_back, in_hbm(pair_sum), in_hbm(query_grad))
    return loss.reshape(-1), query_grad, row_sum.reshape(passages.shape)


def solution(mesh):
    groups, members = mesh.devices.shape
    split = Mesh(mesh.devices.reshape(groups, PLANES, members // PLANES), ("group", "z", "rank"))
    rows = ("group", "z", "rank")
    return jax.shard_map(
        on_device,
        mesh=split,
        in_specs=(P(rows, None), P(rows, None, None), P(), P(rows)),
        out_specs=(P(rows), P(rows, None), P(rows, None, None)),
        check_vma=False,
    )
```

time: 262 us -> 175 us (0.67)
  blocking collectives: 102 us -> 0 us
  Pallas kernels: 0 us -> 33.6 us
  other arithmetic: 29 us -> 0.39 us
  starting transfers between devices: 3.78 us -> 28.2 us
  local copies, waits for them, and re-layouts: 25.8 us -> 8.63 us
  waiting for transfers between devices: 87.9 us -> 102 us
  matrix products: 12.1 us -> 0 us
    all_to_all x1 -> x0, blocking collectives: 102 us -> none  [on_device(): lax.all_to_all(outgoing, ('group', 'dev'), split_axis=2, concat_axis=2, t...]
    ppermute x0 -> x7, waiting for transfers between devices: none -> 83.6 us  [the longest x1 25.9 us: on_device(): lax.ppermute(after(queries[early:], pair_rows, others_low), 'z', across)]
    all_to_all x1 -> x4, waiting for transfers between devices: 87.9 us -> 18.2 us  [exchange(): lax.all_to_all(slab_array, PLANE, split_axis=0, concat_axis=0, tiled=True)]
    pallas_call x0 -> x11, Pallas kernels: none -> 33.6 us  [the longest x2 10.1 us: segment_rows(): pl.pallas_call(functools.partial(segment_kernel, stripes, len(start) > 0)...]
    scatter-add x1 -> x0, other arithmetic: 18.6 us -> none  [on_device(): jax.ops.segment_sum(returned_rows.reshape(-1, feat_width).astype(jnp.floa...]
    all_to_all x1 -> x4, starting transfers between devices: 3.78 us -> 17.8 us  [exchange(): lax.all_to_all(slab_array, PLANE, split_axis=0, concat_axis=0, tiled=True)]
    gather x1 -> x0, local copies, waits for them, and re-layouts: 12.4 us -> none  [on_device(): jnp.take(passages.reshape(own_rows * block_total, feat_width), flat_rows,...]
    dot_general x3 -> x0, matrix products: 12.1 us -> none  [the longest x1 6.87 us: on_device(): jnp.einsum('ouw,owf->ouf', logits_gradient, candidate_passages, preferred...]
  transfers between devices with their start and end apart: 1 -> 11, of which waited for: 1 -> 8; matrix products, arithmetic and copies ran while one was open for 3% -> 1% of each run, Pallas kernels for 0% -> 13%
where the time goes in v2:
time: 175 us; the launch traced here: 174 us
  waiting for transfers between devices  102 us (58%)
  Pallas kernels  33.6 us (19%)
  starting transfers between devices  28.2 us (16%)
  local copies, waits for them, and re-layouts  8.63 us (5%)
    ppermute x1, waiting for transfers between devices, on_device(): lax.ppermute(after(queries[early:], pair_rows, others_low), 'z', across)  25.9 us
    ppermute x1, waiting for transfers between devices, on_device(): own_part = lax.ppermute(other_part, 'z', across)  20.1 us
    all_to_all x4, waiting for transfers between devices, exchange(): lax.all_to_all(slab_array, PLANE, split_axis=0, concat_axis=0, tiled=True)  18.2 us
    all_to_all x4, starting transfers between devices, exchange(): lax.all_to_all(slab_array, PLANE, split_axis=0, concat_axis=0, tiled=True)  17.8 us
    ppermute x1, waiting for transfers between devices, on_device(): others_low = lax.ppermute(queries[:early], 'z', across)  17.1 us
    ppermute x1, waiting for transfers between devices, on_device(): pair_sum = lax.ppermute(far_sum, 'z', to_pair)  15.2 us
    pallas_call x2, Pallas kernels, segment_rows(): pl.pallas_call(functools.partial(segment_kernel, stripes, len(start) > 0)...  10.1 us
    pallas_call x1, Pallas kernels, rest_grads(): pl.pallas_call(rest_kernel, in_specs=[VMEM, VMEM, HBM, VMEM, VMEM, VMEM,...  7.52 us
  transfers between devices with their start and end apart: 11, of which 8 were waited for; matrix products, arithmetic and copies ran while one was open for 1% of the time, Pallas kernels for 13%

profile of v2, /device:TPU:0, one launch (start us, length us, event | category | flops | bytes accessed | tf_op | source)
XLA Modules:
  0.0 173.8 jit_solution(2552184705485855778)
XLA Ops:
  0.7 1.9 %copy.16 = bf16[16,32,1024]{2,0,1:T(8,128)(2,1)S(1)} copy(bf16[16,32,1024]{2,1,0:T(8,128)(2,1)} %param.7) | data formatting | bytes 2097152 | tf_op args[1]
  2.5 3.1 %collective-permute-start.1 = (bf16[32,16,1024]{2,1,0:T(8,128)(2,1)S(1)}, bf16[32,16,1024]{2,1,0:T(8,128)(2,1)S(1)}, u32[]{:S(2)}, u32[]{:S(2)}) collective-permute-start(bf16[32,16,1024]{2,1,0:T(8,128)(2,1)S(1)} %bitcast.15), channel_id=1, source_target_pairs={{0,2},{2,0},{4,6},{6,4},{1,3},{3,1},{5,7},{7,5},{8,10},{10,8},{12,... | collective-permute-start | bytes 3145736 | tf_op jit(solution)/shard_map/ppermute | solution.py:469
  5.6 0.7 slice.6
  6.4 2.6 %collective-permute-start = (bf16[128,1024]{1,0:T(8,128)(2,1)}, bf16[128,1024]{1,0:T(8,128)(2,1)S(1)}, u32[]{:S(2)}, u32[]{:S(2)}) collective-permute-start(bf16[128,1024]{1,0:T(8,128)(2,1)} %slice.6), channel_id=1, source_target_pairs={{0,4},{2,6},{4,0},{6,2},{1,5},{3,7},{5,1},{7,3},{8,12},{10,14},{12... | collective-permute-start | bytes 786440 | tf_op jit(solution)/shard_map/ppermute | solution.py:470
  8.9 2.0 %gather_rows.2 = bf16[8,128,1024]{2,1,0:T(8,128)(2,1)} custom-call(s32[4,32]{1,0:T(4,128)S(1)} %bitcast.17, bf16[32,16,1024]{2,1,0:T(8,128)(2,1)S(1)} %bitcast.16), custom_call_target="tpu_custom_call" | custom-call | bytes 4194304 | tf_op jit(solution)/shard_map/gather_rows/pallas_call | solution.py:84
  11.0 4.4 %all-to-all-start = ((bf16[8,128,1024]{2,1,0:T(8,128)(2,1)}), bf16[8,128,1024]{2,1,0:T(8,128)(2,1)}, u32[]{:S(2)}, u32[]{:S(2)}) async-start(bf16[8,128,1024]{2,1,0:T(8,128)(2,1)} %gather_rows.2), calls=%async_computation | async-start | bytes 4194304 | tf_op jit(solution)/shard_map/all_to_all | solution.py:463
  15.4 0.4 collective-permute-start.3
  15.8 0.9 slice.7.refs_0_
  16.7 17.1 %collective-permute-done.refs_2_.low_ref = bf16[128,1024]{1,0:T(8,128)(2,1)S(1)} collective-permute-done((bf16[128,1024]{1,0:T(8,128)(2,1)}, bf16[128,1024]{1,0:T(8,128)(2,1)S(1)}, u32[]{:S(2)}, u32[]{:S(2)}) %collective-permute-start) | collective-permute-done | bytes 262176 | tf_op jit(solution)/shard_map/ppermute | solution.py:470
  33.8 0.7 collective-permute-done.1.refs_1_.rows_ref
  34.5 1.0 copy-done.1
  35.5 3.3 %collective-permute-start.2 = (bf16[384,1024]{1,0:T(8,128)(2,1)}, bf16[384,1024]{1,0:T(8,128)(2,1)S(1)}, u32[]{:S(2)}, u32[]{:S(2)}) collective-permute-start(bf16[384,1024]{1,0:T(8,128)(2,1)} %after.2), channel_id=1, source_target_pairs={{0,4},{2,6},{4,0},{6,2},{1,5},{3,7},{5,1},{7,3},{8,12},{10,14},{12... | collective-permute-start | bytes 2359304 | tf_op jit(solution)/shard_map/ppermute | solution.py:471
  38.7 1.2 copy-done.2
  40.0 2.0 %gather_rows.3 = bf16[8,128,1024]{2,1,0:T(8,128)(2,1)} custom-call(s32[4,32]{1,0:T(4,128)S(1)} %bitcast.18, bf16[32,16,1024]{2,1,0:T(8,128)(2,1)S(1)} %copy-done.2), custom_call_target="tpu_custom_call" | custom-call | flops 137438953472 | bytes 4194304 | tf_op jit(solution)/shard_map/gather_rows/pallas_call | solution.py:84
  42.0 4.5 %all-to-all-start.1 = ((bf16[8,128,1024]{2,1,0:T(8,128)(2,1)}), bf16[8,128,1024]{2,1,0:T(8,128)(2,1)}, u32[]{:S(2)}, u32[]{:S(2)}) async-start(bf16[8,128,1024]{2,1,0:T(8,128)(2,1)} %gather_rows.3), calls=%async_computation.1 | async-start | bytes 4194304 | tf_op jit(solution)/shard_map/all_to_all | solution.py:463
  46.5 25.9 %collective-permute-done.2.high_ref = bf16[384,1024]{1,0:T(8,128)(2,1)S(1)} collective-permute-done((bf16[384,1024]{1,0:T(8,128)(2,1)}, bf16[384,1024]{1,0:T(8,128)(2,1)S(1)}, u32[]{:S(2)}, u32[]{:S(2)}) %collective-permute-start.2) | collective-permute-done | bytes 786464 | tf_op jit(solution)/shard_map/ppermute | solution.py:471
  72.4 4.1 %near_half.1 = (f32[2,512,512]{2,1,0:T(8,128)}, f32[8,512]{1,0:T(8,128)S(1)}, s32[8,512]{1,0:T(8,128)S(1)}, bf16[512,1024]{1,0:T(8,128)(2,1)S(1)}) custom-call(bf16[512,1024]{1,0:T(8,128)(2,1)S(1)} %copy-done, bf16[128,1024]{1,0:T(8,128)(2,1)S(1)} %copy-done.4, bf16[384,1024]{1,0:T(8,128)(2,1)S(1)} %collective-permute-done.2.high_ref, ...), custom_call_target="tpu_custom_call" | custom-call | flops 137438953472 | bytes 4194304 | tf_op jit(solution)/shard_map/near_half/pallas_call | solution.py:245
  76.6 3.3 %far_half.1 = (f32[2,512,512]{2,1,0:T(8,128)S(1)}, f32[8,512]{1,0:T(8,128)S(1)}, s32[8,512]{1,0:T(8,128)S(1)}) custom-call(bf16[512,1024]{1,0:T(8,128)(2,1)S(1)} %copy-done, bf16[512,1024]{1,0:T(8,128)(2,1)S(1)} %get-tuple-element.18.others_ref, bf16[8,128,1024]{2,1,0:T(8,128)(2,1)} %all-to-all-done.1.slabs_ref.far_slabs_ref, s32[1,512]{1,0:T(1,128)S(1)} %bitcast.20, ...), custom_call_target="tpu_custom_call" | custom-call | flops 1073741824 | bytes 4194304 | tf_op jit(solution)/shard_map/far_half/pallas_call | solution.py:282
  80.0 4.6 %collective-permute-done.4.there_ref = f32[8,512]{1,0:T(8,128)S(1)} collective-permute-done((f32[8,512]{1,0:T(8,128)S(1)}, f32[8,512]{1,0:T(8,128)S(1)}, u32[]{:S(2)}, u32[]{:S(2)}) %collective-permute-start.4) | collective-permute-done | bytes 16416 | tf_op jit(solution)/shard_map/ppermute | solution.py:500
  84.6 3.0 %far_grads.1 = (bf16[8,128,1024]{2,1,0:T(8,128)(2,1)}, bf16[2,512,512]{2,1,0:T(8,128)(2,1)S(1)}, f32[8,512]{1,0:T(8,128)S(1)}, f32[1,512]{1,0:T(1,128)}) custom-call(bf16[512,1024]{1,0:T(8,128)(2,1)S(1)} %copy-done, bf16[512,1024]{1,0:T(8,128)(2,1)S(1)} %get-tuple-element.18.others_ref, f32[2,512,512]{2,1,0:T(8,128)S(1)} %get-tuple-element.20.logits_ref, ...), custom_call_target="tpu_custom_call" | custom-call | flops 1073741824 | bytes 4194304 | tf_op jit(solution)/shard_map/far_grads/pallas_call | solution.py:349
  87.6 4.6 %all-to-all-start.2 = ((bf16[8,128,1024]{2,1,0:T(8,128)(2,1)}), bf16[8,128,1024]{2,1,0:T(8,128)(2,1)}, u32[]{:S(2)}, u32[]{:S(2)}) async-start(bf16[8,128,1024]{2,1,0:T(8,128)(2,1)} %get-tuple-element.31), calls=%async_computation.2 | async-start | bytes 4194304 | tf_op jit(solution)/shard_map/all_to_all | solution.py:463
  92.2 7.5 %rest_grads.1 = (bf16[512,1024]{1,0:T(8,128)(2,1)}, bf16[8,128,1024]{2,1,0:T(8,128)(2,1)}, f32[512,1024]{1,0:T(8,128)}) custom-call(bf16[512,1024]{1,0:T(8,128)(2,1)S(1)} %copy-done, bf16[512,1024]{1,0:T(8,128)(2,1)S(1)} %get-tuple-element.18.others_ref, f32[2,512,512]{2,1,0:T(8,128)} %get-tuple-element.24.logits_ref, ...), custom_call_target="tpu_custom_call" | custom-call | flops 3221225472 | bytes 8388608 | tf_op jit(solution)/shard_map/rest_grads/pallas_call | solution.py:406
  100.5 18.2 %all-to-all-done.2.slabs_ref = bf16[8,128,1024]{2,1,0:T(8,128)(2,1)} async-done(((bf16[8,128,1024]{2,1,0:T(8,128)(2,1)}), bf16[8,128,1024]{2,1,0:T(8,128)(2,1)}, u32[]{:S(2)}, u32[]{:S(2)}) %all-to-all-start.2) | async-done | bytes 2097184 | tf_op jit(solution)/shard_map/all_to_all | solution.py:463
  118.7 4.6 %segment_rows.2.refs_1_ = bf16[512,1024]{1,0:T(8,128)(2,1)} custom-call(bf16[512,1024]{1,0:T(8,128)(2,1)S(1)} %fusion.spread_ref, bf16[8,128,1024]{2,1,0:T(8,128)(2,1)} %all-to-all-done.2.slabs_ref), custom_call_target="tpu_custom_call" | custom-call | flops 1073741824 | bytes 4194304 | tf_op jit(solution)/shard_map/segment_rows/pallas_call | solution.py:129
  123.3 0.9 collective-permute-start.6
  124.2 4.4 %all-to-all-start.3 = ((bf16[8,128,1024]{2,1,0:T(8,128)(2,1)}), bf16[8,128,1024]{2,1,0:T(8,128)(2,1)}, u32[]{:S(2)}, u32[]{:S(2)}) async-start(bf16[8,128,1024]{2,1,0:T(8,128)(2,1)} %after.3), calls=%async_computation.3 | async-start | bytes 4194304 | tf_op jit(solution)/shard_map/all_to_all | solution.py:463
  128.6 20.1 %collective-permute-done.5.part_ref = bf16[512,1024]{1,0:T(8,128)(2,1)S(1)} collective-permute-done((bf16[512,1024]{1,0:T(8,128)(2,1)}, bf16[512,1024]{1,0:T(8,128)(2,1)S(1)}, u32[]{:S(2)}, u32[]{:S(2)}) %collective-permute-start.5) | collective-permute-done | bytes 1048608 | tf_op jit(solution)/shard_map/ppermute | solution.py:508
  148.7 1.6 copy-done.7
  150.3 1.6 add_parts.1.refs_1_
  152.0 15.2 %collective-permute-done.6.refs_0_ = bf16[512,1024]{1,0:T(8,128)(2,1)S(1)} collective-permute-done((bf16[512,1024]{1,0:T(8,128)(2,1)}, bf16[512,1024]{1,0:T(8,128)(2,1)S(1)}, u32[]{:S(2)}, u32[]{:S(2)}) %collective-permute-start.6) | collective-permute-done | bytes 1048608 | tf_op jit(solution)/shard_map/ppermute | solution.py:510
  167.2 1.0 copy-done.8
  168.2 5.4 %segment_rows.3 = bf16[512,1024]{1,0:T(8,128)(2,1)} custom-call(bf16[512,1024]{1,0:T(8,128)(2,1)S(1)} %fusion.spread_ref, bf16[8,128,1024]{2,1,0:T(8,128)(2,1)} %all-to-all-done.3.slabs_ref, bf16[512,1024]{1,0:T(8,128)(2,1)} %copy-done.8, bf16[512,1024]{1,0:T(8,128)(2,1)} %add_parts.1.refs_1_), custom_call_target="tpu_custom_call" | custom-call | flops 1073741824 | bytes 4194304 | tf_op jit(solution)/shard_map/segment_rows/pallas_call | solution.py:129
  (31 shorter events, 0.9 us)
Async XLA Ops:
  0.6 5.0 %copy-start = (bf16[512,1024]{1,0:T(8,128)(2,1)S(1)}, bf16[512,1024]{1,0:T(8,128)(2,1)}, u32[]{:S(2)}) copy-start(bf16[512,1024]{1,0:T(8,128)(2,1)} %queries_ref.7) | copy-start | bytes 3145732
  0.6 8.3 %copy-start.5 = (s32[32,4]{0,1:T(4,128)S(1)}, s32[32,4]{0,1:T(4,128)}, u32[]{:S(2)}) copy-start(s32[32,4]{0,1:T(4,128)} %param.8) | copy-start | bytes 1540
  2.5 31.9 %collective-permute-start.1 = (bf16[32,16,1024]{2,1,0:T(8,128)(2,1)S(1)}, bf16[32,16,1024]{2,1,0:T(8,128)(2,1)S(1)}, u32[]{:S(2)}, u32[]{:S(2)}) collective-permute-start(bf16[32,16,1024]{2,1,0:T(8,128)(2,1)S(1)} %bitcast.15), channel_id=1, source_target_pairs={{0,2},{2,0},{4,6},{6,4},{1,3},{3,1},{5,7},{7,5},{8,10},{10,8},{12,... | collective-permute-start | bytes 3145736 | tf_op jit(solution)/shard_map/ppermute | solution.py:469
  6.4 27.4 %collective-permute-start = (bf16[128,1024]{1,0:T(8,128)(2,1)}, bf16[128,1024]{1,0:T(8,128)(2,1)S(1)}, u32[]{:S(2)}, u32[]{:S(2)}) collective-permute-start(bf16[128,1024]{1,0:T(8,128)(2,1)} %slice.6), channel_id=1, source_target_pairs={{0,4},{2,6},{4,0},{6,2},{1,5},{3,7},{5,1},{7,3},{8,12},{10,14},{12... | collective-permute-start | bytes 786440 | tf_op jit(solution)/shard_map/ppermute | solution.py:470
  11.0 4.4 %copy-start.6 = (s32[512]{0:T(512)S(1)}, s32[512]{0:T(512)}, u32[]{:S(2)}) copy-start(s32[512]{0:T(512)} %param.9) | copy-start | bytes 6148
  11.0 31.0 %all-to-all-start = ((bf16[8,128,1024]{2,1,0:T(8,128)(2,1)}), bf16[8,128,1024]{2,1,0:T(8,128)(2,1)}, u32[]{:S(2)}, u32[]{:S(2)}) async-start(bf16[8,128,1024]{2,1,0:T(8,128)(2,1)} %gather_rows.2), calls=%async_computation | async-start | bytes 4194304 | tf_op jit(solution)/shard_map/all_to_all | solution.py:463
  15.4 31.1 %collective-permute-start.3 = (s32[512]{0:T(512)S(1)}, s32[512]{0:T(512)S(1)}, u32[]{:S(2)}, u32[]{:S(2)}) collective-permute-start(s32[512]{0:T(512)S(1)} %copy-done.6), channel_id=1, source_target_pairs={{0,4},{2,6},{4,0},{6,2},{1,5},{3,7},{5,1},{7,3},{8,12},{10,14},{12... | collective-permute-start | bytes 6152 | tf_op jit(solution)/shard_map/ppermute | solution.py:472
  33.8 0.7 copy-start.3
  34.5 1.0 copy-start.1
  35.5 37.0 %collective-permute-start.2 = (bf16[384,1024]{1,0:T(8,128)(2,1)}, bf16[384,1024]{1,0:T(8,128)(2,1)S(1)}, u32[]{:S(2)}, u32[]{:S(2)}) collective-permute-start(bf16[384,1024]{1,0:T(8,128)(2,1)} %after.2), channel_id=1, source_target_pairs={{0,4},{2,6},{4,0},{6,2},{1,5},{3,7},{5,1},{7,3},{8,12},{10,14},{12... | collective-permute-start | bytes 2359304 | tf_op jit(solution)/shard_map/ppermute | solution.py:471
  38.7 1.2 copy-start.2
  42.0 30.5 %copy-start.4 = (bf16[128,1024]{1,0:T(8,128)(2,1)S(1)}, bf16[128,1024]{1,0:T(8,128)(2,1)}, u32[]{:S(2)}) copy-start(bf16[128,1024]{1,0:T(8,128)(2,1)} %copy-done.3) | copy-start | bytes 786436
  42.0 34.5 %all-to-all-start.1 = ((bf16[8,128,1024]{2,1,0:T(8,128)(2,1)}), bf16[8,128,1024]{2,1,0:T(8,128)(2,1)}, u32[]{:S(2)}, u32[]{:S(2)}) async-start(bf16[8,128,1024]{2,1,0:T(8,128)(2,1)} %gather_rows.3), calls=%async_computation.1 | async-start | bytes 4194304 | tf_op jit(solution)/shard_map/all_to_all | solution.py:463
  79.9 4.7 %collective-permute-start.4 = (f32[8,512]{1,0:T(8,128)S(1)}, f32[8,512]{1,0:T(8,128)S(1)}, u32[]{:S(2)}, u32[]{:S(2)}) collective-permute-start(f32[8,512]{1,0:T(8,128)S(1)} %get-tuple-element.22.here_ref), channel_id=1, source_target_pairs={{0,4},{2,6},{4,0},{6,2},{1,5},{3,7},{5,1},{7,3},{8,12},{10,14},{12... | collective-permute-start | bytes 49160 | tf_op jit(solution)/shard_map/ppermute | solution.py:500
  87.6 31.1 %all-to-all-start.2 = ((bf16[8,128,1024]{2,1,0:T(8,128)(2,1)}), bf16[8,128,1024]{2,1,0:T(8,128)(2,1)}, u32[]{:S(2)}, u32[]{:S(2)}) async-start(bf16[8,128,1024]{2,1,0:T(8,128)(2,1)} %get-tuple-element.31), calls=%async_computation.2 | async-start | bytes 4194304 | tf_op jit(solution)/shard_map/all_to_all | solution.py:463
  99.7 49.0 %collective-permute-start.5 = (bf16[512,1024]{1,0:T(8,128)(2,1)}, bf16[512,1024]{1,0:T(8,128)(2,1)S(1)}, u32[]{:S(2)}, u32[]{:S(2)}) collective-permute-start(bf16[512,1024]{1,0:T(8,128)(2,1)} %get-tuple-element.29), channel_id=1, source_target_pairs={{0,4},{2,6},{4,0},{6,2},{1,5},{3,7},{5,1},{7,3},{8,12},{10,14},{12... | collective-permute-start | bytes 3145736 | tf_op jit(solution)/shard_map/ppermute | solution.py:508
  123.3 43.9 %collective-permute-start.6 = (bf16[512,1024]{1,0:T(8,128)(2,1)}, bf16[512,1024]{1,0:T(8,128)(2,1)S(1)}, u32[]{:S(2)}, u32[]{:S(2)}) collective-permute-start(bf16[512,1024]{1,0:T(8,128)(2,1)} %segment_rows.2.refs_1_), channel_id=1, source_target_pairs={{0,2},{2,0},{4,6},{6,4},{1,3},{3,1},{5,7},{7,5},{8,10},{10,8},{12,... | collective-permute-start | bytes 3145736 | tf_op jit(solution)/shard_map/ppermute | solution.py:510
  124.2 43.0 %all-to-all-start.3 = ((bf16[8,128,1024]{2,1,0:T(8,128)(2,1)}), bf16[8,128,1024]{2,1,0:T(8,128)(2,1)}, u32[]{:S(2)}, u32[]{:S(2)}) async-start(bf16[8,128,1024]{2,1,0:T(8,128)(2,1)} %after.3), calls=%async_computation.3 | async-start | bytes 4194304 | tf_op jit(solution)/shard_map/all_to_all | solution.py:463
  148.7 1.6 copy-start.7
  167.2 1.0 copy-start.8

commit v3 on v2

v3 whole, which is shorter than its diff:
```python
import functools

import jax
import jax.numpy as jnp
from jax import lax
from jax.experimental import pallas as pl
from jax.experimental.pallas import tpu as pltpu
from jax.sharding import Mesh
from jax.sharding import PartitionSpec as P

SCALE = 0.8
PLANES = 4
CHUNKS = 2
EARLY = 4
BF16 = jnp.bfloat16
F32 = jnp.float32
BUSY = 1 << 37
PLANE = ("group", "rank")
ANY = pl.BlockSpec(memory_space=pl.ANY)
HBM = pl.BlockSpec(memory_space=pltpu.HBM)
VMEM = pl.BlockSpec(memory_space=pltpu.VMEM)
SMEM = pl.BlockSpec(memory_space=pltpu.SMEM)


def params():
    return pltpu.CompilerParams(vmem_limit_bytes=28 << 20)


def cost(flops, mib):
    return pl.CostEstimate(flops=flops, bytes_accessed=mib << 20, transcendentals=0)


def in_hbm(array):
    return pltpu.with_memory_space_constraint(array, pltpu.HBM)


def shape(dims, dtype):
    return jax.ShapeDtypeStruct(dims, dtype)


def after_kernel(*refs):
    del refs


def after(array, *others):
    return pl.pallas_call(
        after_kernel,
        in_specs=[ANY] * (1 + len(others)),
        out_specs=ANY,
        out_shape=shape(array.shape, array.dtype),
        input_output_aliases={0: 0},
        name="after",
    )(array, *others)


def split_kernel(source_ref, low_ref, high_ref, held, done):
    cut = low_ref.shape[0]
    parts = [pl.ds(0, cut), pl.ds(cut, source_ref.shape[0] - cut)]
    for i, part in enumerate(parts):
        pltpu.make_async_copy(source_ref.at[part], held.at[part], done.at[i]).start()
    for i, (part, out_ref) in enumerate(zip(parts, (low_ref, high_ref))):
        pltpu.make_async_copy(source_ref.at[part], held.at[part], done.at[i]).wait()
        pltpu.make_async_copy(held.at[part], out_ref, done.at[i]).start()
    for i, (part, out_ref) in enumerate(zip(parts, (low_ref, high_ref))):
        pltpu.make_async_copy(held.at[part], out_ref, done.at[i]).wait()


def split_rows(array, cut):
    rows, width = array.shape
    return pl.pallas_call(
        split_kernel,
        in_specs=[HBM],
        out_specs=[HBM] * 2,
        out_shape=[pltpu.HBM((cut, width), BF16), pltpu.HBM((rows - cut, width), BF16)],
        scratch_shapes=[pltpu.VMEM(array.shape, BF16), pltpu.SemaphoreType.DMA((2,))],
        compiler_params=params(),
        name="split_rows",
        cost_estimate=cost(0, 2),
    )(array)


def gather_kernel(planes, ranks, ids, rows_ref, out_ref, made, left, *held):
    if held:
        load = pltpu.make_async_copy(rows_ref, *held)
        load.start()
        load.wait()
        rows_ref = held[0]
    slabs, depth, width = out_ref.shape
    height = rows_ref.shape[1]
    refs = ids.shape[0]
    z = lax.axis_index("z")

    def sent(slab):
        return pltpu.make_async_copy(made.at[slab], out_ref.at[slab], left.at[slab])

    def fill(slab, carry):
        for pick in range(2 * refs):
            there = (z + pick // refs * (planes // 2)) % planes
            owner = (slab // ranks * planes + there) * ranks + slab % ranks
            made[slab, pick * height : (pick + 1) * height, :] = rows_ref[ids[pick % refs, owner]]
        sent(slab).start()
        return carry

    def drain(slab, carry):
        sent(slab).wait()
        return carry

    lax.fori_loop(0, slabs, fill, 0)
    lax.fori_loop(0, slabs, drain, 0)


def gather_rows(ids, rows, slabs, planes, ranks, flops, arrived):
    blocks, height, width = rows.shape
    held = [pltpu.VMEM(rows.shape, BF16), pltpu.SemaphoreType.DMA] if arrived else []
    dims = (slabs, 2 * ids.shape[0] * height, width)
    return pl.pallas_call(
        functools.partial(gather_kernel, planes, ranks),
        in_specs=[SMEM, HBM if arrived else VMEM],
        out_specs=HBM,
        out_shape=pltpu.HBM(dims, BF16),
        scratch_shapes=[pltpu.VMEM(dims, BF16), pltpu.SemaphoreType.DMA((slabs,))] + held,
        compiler_params=params(),
        name="gather_rows",
        cost_estimate=cost(flops, 4),
    )(ids, rows)


def segment_kernel(stripes, with_start, spread_ref, slabs_ref, *refs):
    start_ref = refs[0] if with_start else None
    out_ref, held, result, begun, arrived, left = refs[-6:]
    slabs, depth, width = slabs_ref.shape
    tile = width // stripes
    columns = [pl.ds(t * tile, tile) for t in range(stripes)]
    loads = [
        pltpu.make_async_copy(slabs_ref.at[:, :, columns[t]], held.at[t], arrived.at[t]) for t in range(stripes)
    ]
    for load in loads:
        load.start()
    if with_start:
        first = pltpu.make_async_copy(start_ref, begun, arrived.at[stripes])
        first.start()
    stores = []
    for t in range(stripes):
        loads[t].wait()
        total = jnp.dot(spread_ref[...], held[t].reshape(slabs * depth, tile), preferred_element_type=F32)
        if with_start:
            if t == 0:
                first.wait()
            total += begun[:, t * tile : (t + 1) * tile].astype(F32)
        result[t] = total.astype(BF16)
        stores.append(pltpu.make_async_copy(result.at[t], out_ref.at[:, columns[t]], left.at[t]))
        stores[t].start()
    for store in stores:
        store.wait()


def segment_rows(spread, slabs, *start):
    stripes = 2
    rows = spread.shape[0]
    count, depth, width = slabs.shape
    tile = width // stripes
    return pl.pallas_call(
        functools.partial(segment_kernel, stripes, len(start) > 0),
        in_specs=[VMEM, HBM] + [HBM] * len(start),
        out_specs=HBM,
        out_shape=pltpu.HBM((rows, width), BF16),
        scratch_shapes=[
            pltpu.VMEM((stripes, count, depth, tile), BF16),
            pltpu.VMEM((stripes, rows, tile), BF16),
            pltpu.VMEM((rows, width) if start else (16, 128), BF16),
            pltpu.SemaphoreType.DMA((stripes + 1,)),
            pltpu.SemaphoreType.DMA((stripes,)),
        ],
        compiler_params=params(),
        name="segment_rows",
        cost_estimate=cost(1 << 30, 4),
    )(spread, slabs, *start)


def candidates(slabs_ref, q, chunk):
    slabs, depth, width = slabs_ref.shape
    part, half = slabs // CHUNKS, depth // 2
    block = slabs_ref[chunk * part : (chunk + 1) * part, q * half : (q + 1) * half, :]
    return block.reshape(part * half, width)


def hits(rows, chunk, target_row):
    row = lax.broadcasted_iota(jnp.int32, (rows, target_row.shape[1]), 0)
    return row + chunk * rows == target_row


def joined(a, b):
    top = jnp.maximum(a[0], b[0])
    return top, a[1] * jnp.exp(a[0] - top) + b[1] * jnp.exp(b[0] - top), a[2] + b[2]


def stat_rows(ref, q):
    return [ref[4 * q + i : 4 * q + i + 1, :] for i in range(3)]


def chunk_rows(ref, chunk):
    rows = ref.shape[1] // CHUNKS
    return slice(chunk * rows, (chunk + 1) * rows)


def place_of(far, planes, ranks, refs, height, chosen):
    owner = chosen // height
    spot = (owner // (planes * ranks) * ranks + owner % ranks) * (refs * height) + chosen % height
    return jnp.where(owner // ranks % planes == lax.axis_index("z") ^ far, spot, -1)


def load(source, held, arrived):
    copy = pltpu.make_async_copy(source, held, arrived)
    copy.start()
    return copy


def part_of(size, chunk):
    return pl.ds(chunk * (size // CHUNKS), size // CHUNKS)


def load_chunks(source, held, arrived):
    parts = [part_of(source.shape[0], c) for c in range(CHUNKS)]
    return [load(source.at[part], held.at[part], arrived.at[c]) for c, part in enumerate(parts)]


def block_logits(block_ref, slab_part, target_row, put):
    stats = None
    for c in range(CHUNKS):
        block = lax.dot_general(slab_part(c), block_ref[...], (((1,), (1,)), ((), ())), preferred_element_type=F32)
        block = SCALE * block
        put(c, block)
        top = jnp.max(block, axis=0, keepdims=True)
        total = jnp.sum(jnp.exp(block - top), axis=0, keepdims=True)
        hit = hits(block.shape[0], c, target_row)
        pick = jnp.sum(jnp.where(hit, block, 0.0), axis=0, keepdims=True)
        here = (top, total, pick)
        stats = here if c == 0 else joined(stats, here)
    return stats


def put_stats(stats_ref, q, stats):
    for i in range(3):
        stats_ref[4 * q + i : 4 * q + i + 1, :] = stats[i]
    stats_ref[4 * q + 3 : 4 * q + 4, :] = jnp.zeros_like(stats[0])


def put_targets(place, target_ref, chosen_ref, chosen_others_ref):
    target_ref[...] = jnp.full(target_ref.shape, -1, jnp.int32)
    target_ref[0:1, :] = place(chosen_ref[...])
    target_ref[1:2, :] = place(chosen_others_ref[...])


def near_logits_kernel(q, place, *refs):
    *block_refs, slabs_ref, chosen_ref, logits_ref, stats_ref, kept_ref, held, made, arrived, came, left = refs
    half = slabs_ref.shape[1] // 2
    picks = pl.ds(q * half, half)
    parts = [part_of(slabs_ref.shape[0], c) for c in range(CHUNKS)]
    loads = [load(slabs_ref.at[part, picks], held.at[part], arrived.at[c]) for c, part in enumerate(parts)]
    if q == 0:
        load(block_refs[0], kept_ref, came).wait()
    else:
        cut = block_refs[0].shape[0]
        kept_ref[:cut, :] = block_refs[0][...]
        kept_ref[cut:, :] = block_refs[1][...]
    stores = []

    def slab_part(c):
        loads[c].wait()
        slabs = held.shape[0] // CHUNKS
        return held[c * slabs : (c + 1) * slabs].reshape(slabs * half, held.shape[2])

    def put(c, block):
        part = part_of(logits_ref.shape[0], c)
        rows = block.shape[0]
        made[c * rows : (c + 1) * rows, :] = block
        stores.append(load(made.at[part], logits_ref.at[part], left.at[c]))

    stats = block_logits(kept_ref, slab_part, place(chosen_ref[...]), put)
    for i in range(3):
        stats_ref[i : i + 1, :] = stats[i]
    stats_ref[3:, :] = jnp.zeros((stats_ref.shape[0] - 3, stats_ref.shape[1]), F32)
    for store in stores:
        store.wait()


def near_half(q, parts, slabs, chosen, place, hint):
    size, width = sum(part.shape[0] for part in parts), slabs.shape[2]
    rows = slabs.shape[0] * slabs.shape[1] // 2
    return pl.pallas_call(
        functools.partial(near_logits_kernel, q, place),
        in_specs=[HBM if q == 0 else VMEM] * len(parts) + [HBM, VMEM],
        out_specs=[HBM, VMEM, VMEM],
        out_shape=[pltpu.HBM((rows, size), F32), shape((8, size), F32), shape((size, width), BF16)],
        scratch_shapes=[
            pltpu.VMEM((slabs.shape[0], slabs.shape[1] // 2, width), BF16),
            pltpu.VMEM((rows, size), F32),
            pltpu.SemaphoreType.DMA((CHUNKS,)),
            pltpu.SemaphoreType.DMA,
            pltpu.SemaphoreType.DMA((CHUNKS,)),
        ],
        compiler_params=params(),
        name="near_half",
        cost_estimate=cost(hint, 4),
    )(*parts, slabs, chosen)


def far_logits_kernel(
    near_place, far_place, queries_ref, others_ref, slabs_ref, chosen_ref, chosen_others_ref, own_stats_ref, other_stats_ref,
    logits_ref, stats_ref, near_target_ref, far_target_ref, held, arrived,
):
    loads = load_chunks(slabs_ref, held, arrived)
    put_targets(near_place, near_target_ref, chosen_ref, chosen_others_ref)
    put_targets(far_place, far_target_ref, chosen_ref, chosen_others_ref)
    for q, (block_ref, near_ref) in enumerate(((queries_ref, own_stats_ref), (others_ref, other_stats_ref))):

        def slab_part(c, q=q):
            if q == 0:
                loads[c].wait()
            return candidates(held, q, c)

        def put(c, block, q=q):
            logits_ref[q, chunk_rows(logits_ref, c), :] = block

        stats = block_logits(block_ref, slab_part, far_target_ref[q : q + 1, :], put)
        put_stats(stats_ref, q, joined(stat_rows(near_ref, 0), stats))


def far_half(queries, others, slabs, chosen, chosen_others, own_stats, other_stats, places):
    size = queries.shape[0]
    rows = slabs.shape[0] * slabs.shape[1] // 2
    return pl.pallas_call(
        functools.partial(far_logits_kernel, *places),
        in_specs=[VMEM, VMEM, HBM, VMEM, VMEM, VMEM, VMEM],
        out_specs=[VMEM] * 4,
        out_shape=[
            shape((2, rows, size), F32),
            shape((8, size), F32),
            shape((8, size), jnp.int32),
            shape((8, size), jnp.int32),
        ],
        scratch_shapes=[pltpu.VMEM(slabs.shape, BF16), pltpu.SemaphoreType.DMA((CHUNKS,))],
        compiler_params=params(),
        name="far_half",
        cost_estimate=cost(1 << 30, 4),
    )(queries, others, slabs, chosen, chosen_others, own_stats, other_stats)


def log_totals(here_ref, there_ref):
    out = []
    for q in range(2):
        top, total, pick = joined(stat_rows(here_ref, q), stat_rows(there_ref, 1 - q))
        out.append((top + jnp.log(total), pick))
    return out


def dlogits(logits, log_total, chunk, target_row):
    hit = hits(logits.shape[0], chunk, target_row)
    return (jnp.exp(logits - log_total) - jnp.where(hit, 1.0, 0.0)).astype(BF16)


def send_contrib(made, out_ref, left, chunk, q, piece, block, complete):
    slabs, depth, width = out_ref.shape
    part, half = slabs // CHUNKS, depth // 2
    product = SCALE * jnp.dot(piece, block, preferred_element_type=F32)
    made[chunk, :, q * half : (q + 1) * half, :] = product.astype(BF16).reshape(part, half, width)
    if not complete:
        return []
    store = pltpu.make_async_copy(made.at[chunk], out_ref.at[pl.ds(chunk * part, part)], left.at[chunk])
    store.start()
    return [store]


def contrib_scratch(slabs):
    return [
        pltpu.VMEM((CHUNKS, slabs.shape[0] // CHUNKS) + slabs.shape[1:], BF16),
        pltpu.SemaphoreType.DMA((CHUNKS,)),
    ]


def load_share(q, logits_ref, near_ref, far_ref, logits, near, far, came):
    rows, slabs, half = logits_ref.shape[0], near_ref.shape[0], near_ref.shape[1] // 2
    picks = pl.ds(q * half, half)
    copies = []
    for c in range(CHUNKS):
        part, some = part_of(rows, c), part_of(slabs, c)
        copies.append(
            [
                load(far_ref.at[some, picks], far.at[some], came.at[0, c]),
                load(logits_ref.at[part], logits.at[part], came.at[1, c]),
                load(near_ref.at[some, picks], near.at[some], came.at[2, c]),
            ]
        )
    return copies


def query_share(copies, far_piece, near_piece, near, far, use):
    dims = (((0,), (0,)), ((), ()))
    slabs, half, width = near.shape
    total = None
    for c in range(CHUNKS):
        some = slice(c * slabs // CHUNKS, (c + 1) * slabs // CHUNKS)
        rows = slabs // CHUNKS * half
        piece = far_piece(c)
        copies[c][0].wait()
        share = lax.dot_general(piece, far[some].reshape(rows, width), dims, preferred_element_type=F32)
        copies[c][1].wait()
        piece = near_piece(c)
        copies[c][2].wait()
        share += lax.dot_general(piece, near[some].reshape(rows, width), dims, preferred_element_type=F32)
        total = share if c == 0 else total + share
        if use is not None:
            use(c, piece)
    return total


def share_scratch(logits, slabs):
    part = (slabs.shape[0], slabs.shape[1] // 2, slabs.shape[2])
    return [
        pltpu.VMEM(logits.shape, F32),
        pltpu.VMEM(part, BF16),
        pltpu.VMEM(part, BF16),
        pltpu.SemaphoreType.DMA((3, CHUNKS)),
    ]


def row_chunk(rows, chunk):
    return slice(chunk * rows // CHUNKS, (chunk + 1) * rows // CHUNKS)


def other_kernel(
    here_ref, there_ref, near_target_ref, far_target_ref, far_logits_ref, near_logits_ref, near_ref, far_ref,
    other_ref, totals_ref, loss_ref, logits, near, far, came, made, left,
):
    copies = load_share(1, near_logits_ref, near_ref, far_ref, logits, near, far, came)
    totals = log_totals(here_ref, there_ref)
    rows = logits.shape[0]

    def far_piece(c):
        return dlogits(far_logits_ref[1, row_chunk(rows, c), :], totals[1][0], c, far_target_ref[1:2, :])

    def near_piece(c):
        return dlogits(logits[row_chunk(rows, c), :], totals[1][0], c, near_target_ref[1:2, :])

    total = query_share(copies, far_piece, near_piece, near, far, None)
    made[...] = (SCALE * total).astype(BF16)
    store = load(made, other_ref, left)
    totals_ref[...] = jnp.zeros_like(totals_ref)
    for q in range(2):
        totals_ref[q : q + 1, :] = totals[q][0]
    loss_ref[...] = totals[0][0] - totals[0][1]
    store.wait()


def other_grads(here, there, near_target, far_target, far_logits, near_logits, near_slabs, far_slabs):
    size, width = far_logits.shape[2], near_slabs.shape[2]
    return pl.pallas_call(
        other_kernel,
        in_specs=[VMEM] * 5 + [HBM] * 3,
        out_specs=[HBM, VMEM, VMEM],
        out_shape=[pltpu.HBM((size, width), BF16), shape((8, size), F32), shape((1, size), F32)],
        scratch_shapes=share_scratch(near_logits, near_slabs)
        + [pltpu.VMEM((size, width), BF16), pltpu.SemaphoreType.DMA],
        compiler_params=params(),
        name="other_grads",
        cost_estimate=cost(1 << 30, 8),
    )(here, there, near_target, far_target, far_logits, near_logits, near_slabs, far_slabs)


def far_kernel(
    queries_ref, others_ref, logits_ref, target_ref, totals_ref, wait_ref,
    contrib_ref, pieces_ref, made, left, pieces, pieces_out,
):
    del wait_ref
    stores = []
    for c in range(CHUNKS):
        rows = chunk_rows(logits_ref, c)
        for q, block_ref in enumerate((queries_ref, others_ref)):
            piece = dlogits(logits_ref[q, rows, :], totals_ref[q : q + 1, :], c, target_ref[q : q + 1, :])
            if q == 0:
                pieces[rows, :] = piece
                part = part_of(logits_ref.shape[1], c)
                stores.append(load(pieces.at[part], pieces_ref.at[part], pieces_out.at[c]))
            stores += send_contrib(made, contrib_ref, left, c, q, piece, block_ref[...], q == 1)
    for store in stores:
        store.wait()


def far_grads(queries, others, logits, target, totals, wait, slabs):
    size = queries.shape[0]
    rows = logits.shape[1]
    return pl.pallas_call(
        far_kernel,
        in_specs=[VMEM] * 5 + [ANY],
        out_specs=[HBM] * 2,
        out_shape=[pltpu.HBM(slabs.shape, BF16), pltpu.HBM((rows, size), BF16)],
        scratch_shapes=contrib_scratch(slabs)
        + [pltpu.VMEM((rows, size), BF16), pltpu.SemaphoreType.DMA((CHUNKS,))],
        compiler_params=params(),
        name="far_grads",
        cost_estimate=cost(1 << 30, 4),
    )(queries, others, logits, target, totals, wait)


def near_kernel(
    queries_ref, others_ref, target_ref, totals_ref, own_logits_ref, other_logits_ref, pieces_ref, near_ref, far_ref,
    contrib_ref, own_ref, logits, near, far, came, pieces, begun, score, scored, own, own_out, made, left,
):
    first = load(pieces_ref, pieces, begun)
    copies = load_share(0, own_logits_ref, near_ref, far_ref, logits, near, far, came)
    other_scores = load(other_logits_ref, score, scored)
    rows = logits.shape[0]
    first.wait()

    def far_piece(c):
        return pieces[row_chunk(rows, c), :]

    def near_piece(c):
        return dlogits(logits[row_chunk(rows, c), :], totals_ref[0:1, :], c, target_ref[0:1, :])

    def use(c, piece):
        send_contrib(made, contrib_ref, left, c, 0, piece, queries_ref[...], False)

    total = query_share(copies, far_piece, near_piece, near, far, use)
    own[...] = SCALE * total
    stores = [load(own, own_ref, own_out)]
    other_scores.wait()
    for c in range(CHUNKS):
        piece = dlogits(score[row_chunk(rows, c), :], totals_ref[1:2, :], c, target_ref[1:2, :])
        stores += send_contrib(made, contrib_ref, left, c, 1, piece, others_ref[...], True)
    for store in stores:
        store.wait()


def near_grads(queries, others, target, totals, own_logits, other_logits, pieces, near_slabs, far_slabs):
    return pl.pallas_call(
        near_kernel,
        in_specs=[VMEM] * 4 + [HBM] * 5,
        out_specs=[HBM] * 2,
        out_shape=[pltpu.HBM(near_slabs.shape, BF16), pltpu.HBM(queries.shape, F32)],
        scratch_shapes=share_scratch(own_logits, near_slabs)
        + [pltpu.VMEM(pieces.shape, BF16), pltpu.SemaphoreType.DMA]
        + [pltpu.VMEM(own_logits.shape, F32), pltpu.SemaphoreType.DMA]
        + [pltpu.VMEM(queries.shape, F32), pltpu.SemaphoreType.DMA]
        + contrib_scratch(near_slabs),
        compiler_params=params(),
        name="near_grads",
        cost_estimate=cost(BUSY, 8),
    )(queries, others, target, totals, own_logits, other_logits, pieces, near_slabs, far_slabs)


def add_kernel(own_ref, part_ref, out_ref):
    out_ref[...] = (own_ref[...] + part_ref[...].astype(F32)).astype(BF16)


def add_parts(own, part):
    block = pl.BlockSpec((own.shape[0] // 4, own.shape[1]), lambda i: (i, 0))
    return pl.pallas_call(
        add_kernel,
        grid=(4,),
        in_specs=[block] * 2,
        out_specs=block,
        out_shape=shape(own.shape, BF16),
        compiler_params=params(),
        name="add_parts",
        cost_estimate=cost(BUSY, 4),
    )(own, part)


def on_device(queries, passages, block_ids, positives):
    height, blocks, width = passages.shape
    refs = block_ids.shape[1]
    groups, planes, ranks = lax.axis_size("group"), lax.axis_size("z"), lax.axis_size("rank")
    slabs = groups * ranks
    z = lax.axis_index("z")
    to_pair = [(i, i ^ 1) for i in range(planes)]
    across = [(i, (i + planes // 2) % planes) for i in range(planes)]

    def exchange(slab_array):
        return in_hbm(lax.all_to_all(slab_array, PLANE, split_axis=0, concat_axis=0, tiled=True))

    ids = block_ids.T
    early = queries.shape[0] // EARLY
    own_rows = jnp.transpose(passages, (1, 0, 2))
    near_slabs = exchange(gather_rows(ids, own_rows, slabs, planes, ranks, 0, False))
    pair_rows = in_hbm(lax.ppermute(own_rows, "z", to_pair))
    low, high = split_rows(in_hbm(queries), early)
    others_low = lax.ppermute(low, "z", across)
    others_high = lax.ppermute(after(high, pair_rows, others_low), "z", across)
    others_positives = lax.ppermute(positives, "z", across)
    far_slabs = exchange(gather_rows(ids, pair_rows, slabs, planes, ranks, BUSY, True))

    table = block_ids.reshape(groups, planes, ranks, refs)
    both = jnp.stack([jnp.take(table, z, axis=1), jnp.take(table, (z + planes // 2) % planes, axis=1)], axis=2)
    place = (jnp.arange(height, dtype=jnp.int32) * blocks + both.reshape(-1, 1)).reshape(1, -1)
    spread = (jnp.arange(height * blocks, dtype=jnp.int32)[:, None] == place).astype(BF16)

    chosen = positives.reshape(1, -1)
    chosen_others = others_positives.reshape(1, -1)
    places = [functools.partial(place_of, far, planes, ranks, refs, height) for far in range(2)]
    own_logits, own_stats, own = near_half(0, [in_hbm(queries)], near_slabs, chosen, places[0], BUSY)
    other_logits, other_stats, others = near_half(
        1, [others_low, others_high], near_slabs, chosen_others, places[0], BUSY
    )
    far_logits, stats, near_target, far_target = far_half(
        own, others, far_slabs, chosen, chosen_others, own_stats, other_stats, places
    )
    partner = lax.ppermute(stats, "z", across)
    own_logits, other_logits = in_hbm(own_logits), in_hbm(other_logits)
    other_part, totals, loss = other_grads(
        stats, partner, near_target, far_target, far_logits, other_logits, near_slabs, far_slabs
    )
    far_contrib, pieces = far_grads(own, others, far_logits, far_target, totals, other_part, far_slabs)
    far_back = exchange(far_contrib)
    near_contrib, own_grad = near_grads(
        own, others, near_target, totals, own_logits, other_logits, in_hbm(pieces), near_slabs, far_slabs
    )
    own_part = lax.ppermute(other_part, "z", across)
    far_sum = segment_rows(spread, far_back)
    pair_sum = lax.ppermute(far_sum, "z", to_pair)
    near_back = exchange(near_contrib)
    query_grad = add_parts(own_grad, own_part)
    row_sum = segment_rows(spread, near_back, in_hbm(pair_sum), in_hbm(query_grad))
    return loss.reshape(-1), query_grad, row_sum.reshape(passages.shape)


def solution(mesh):
    groups, members = mesh.devices.shape
    split = Mesh(mesh.devices.reshape(groups, PLANES, members // PLANES), ("group", "z", "rank"))
    rows = ("group", "z", "rank")
    return jax.shard_map(
        on_device,
        mesh=split,
        in_specs=(P(rows, None), P(rows, None, None), P(), P(rows)),
        out_specs=(P(rows), P(rows, None), P(rows, None, None)),
        check_vma=False,
    )
```

time: 175 us -> 164 us (0.937)
  waiting for transfers between devices: 102 us -> 82.7 us
  Pallas kernels: 33.6 us -> 44.5 us
  local copies, waits for them, and re-layouts: 8.63 us -> 5.23 us
    ppermute x1, waiting for transfers between devices: 20.1 us -> 0.09 us  [on_device(): own_part = lax.ppermute(other_part, 'z', across)]
    all_to_all x4, waiting for transfers between devices: 18.2 us -> 35.7 us  [exchange(): lax.all_to_all(slab_array, PLANE, split_axis=0, concat_axis=0, tiled=True)]
    ppermute x1, waiting for transfers between devices: 15.2 us -> 4.96 us  [on_device(): pair_sum = lax.ppermute(far_sum, 'z', to_pair)]
    pallas_call x4 -> x7, Pallas kernels: 18 us -> 28 us  [the longest x2 8.48 us: near_half(): pl.pallas_call(functools.partial(near_logits_kernel, q, place), in_specs=...]
    ppermute x3, waiting for transfers between devices: 43.6 us -> 37.6 us  [the longest x1 20.6 us: on_device(): others_high = lax.ppermute(after(high, pair_rows, others_low), 'z', across)]
    ppermute x1, starting transfers between devices: 0.94 us -> 3.84 us  [on_device(): pair_sum = lax.ppermute(far_sum, 'z', to_pair)]
    unnamed x20 -> x18, local copies, waits for them, and re-layouts: 6.81 us -> 4.46 us
    pallas_call x2, Pallas kernels: 10.1 us -> 7.76 us  [segment_rows(): pl.pallas_call(functools.partial(segment_kernel, stripes, len(start) > 0)...]
  transfers between devices with their start and end apart: 11 -> 11, of which waited for: 8 -> 8; matrix products, arithmetic and copies ran while one was open for 1% -> 1% of each run, Pallas kernels for 13% -> 19%
where the time goes in v3:
time: 164 us; the launch traced here: 163 us
  waiting for transfers between devices  82.7 us (50%)
  Pallas kernels  44.5 us (27%)
  starting transfers between devices  29.5 us (18%)
  local copies, waits for them, and re-layouts  5.23 us (3%)
    all_to_all x4, waiting for transfers between devices, exchange(): lax.all_to_all(slab_array, PLANE, split_axis=0, concat_axis=0, tiled=True)  35.7 us
    ppermute x1, waiting for transfers between devices, on_device(): others_high = lax.ppermute(after(high, pair_rows, others_low), 'z', across)  20.6 us
    ppermute x1, waiting for transfers between devices, on_device(): others_low = lax.ppermute(low, 'z', across)  16.3 us
    all_to_all x4, starting transfers between devices, exchange(): lax.all_to_all(slab_array, PLANE, split_axis=0, concat_axis=0, tiled=True)  16.2 us
    pallas_call x2, Pallas kernels, near_half(): pl.pallas_call(functools.partial(near_logits_kernel, q, place), in_specs=...  8.48 us
    pallas_call x2, Pallas kernels, segment_rows(): pl.pallas_call(functools.partial(segment_kernel, stripes, len(start) > 0)...  7.76 us
    pallas_call x1, Pallas kernels, near_grads(): pl.pallas_call(near_kernel, in_specs=[VMEM] * 4 + [HBM] * 5, out_specs=[H...  6.3 us
    pallas_call x2, Pallas kernels, gather_rows(): pl.pallas_call(functools.partial(gather_kernel, planes, ranks), in_specs=...  5.27 us
  transfers between devices with their start and end apart: 11, of which 8 were waited for; matrix products, arithmetic and copies ran while one was open for 1% of the time, Pallas kernels for 19%

profile of v3, /device:TPU:0, one launch (start us, length us, event | category | flops | bytes accessed | tf_op | source)
XLA Modules:
  0.0 163.4 jit_solution(12167038556185088950)
XLA Ops:
  0.6 1.8 %copy.15 = bf16[16,32,1024]{2,0,1:T(8,128)(2,1)S(1)} copy(bf16[16,32,1024]{2,1,0:T(8,128)(2,1)} %param.7) | data formatting | bytes 2097152 | tf_op args[1]
  2.5 3.1 %collective-permute-start.1 = (bf16[32,16,1024]{2,1,0:T(8,128)(2,1)S(1)}, bf16[32,16,1024]{2,1,0:T(8,128)(2,1)}, u32[]{:S(2)}, u32[]{:S(2)}) collective-permute-start(bf16[32,16,1024]{2,1,0:T(8,128)(2,1)S(1)} %bitcast.15), channel_id=1, source_target_pairs={{0,2},{2,0},{4,6},{6,4},{1,3},{3,1},{5,7},{7,5},{8,10},{10,8},{12,... | collective-permute-start | bytes 3145736 | tf_op jit(solution)/shard_map/ppermute | solution.py:586
  5.5 2.0 %gather_rows.2 = bf16[8,128,1024]{2,1,0:T(8,128)(2,1)} custom-call(s32[4,32]{1,0:T(4,128)S(1)} %bitcast.17, bf16[32,16,1024]{2,1,0:T(8,128)(2,1)S(1)} %bitcast.16), custom_call_target="tpu_custom_call" | custom-call | bytes 4194304 | tf_op jit(solution)/shard_map/gather_rows/pallas_call | solution.py:116
  7.6 3.7 %all-to-all-start = ((bf16[8,128,1024]{2,1,0:T(8,128)(2,1)}), bf16[8,128,1024]{2,1,0:T(8,128)(2,1)S(1)}, u32[]{:S(2)}, u32[]{:S(2)}) async-start(bf16[8,128,1024]{2,1,0:T(8,128)(2,1)} %gather_rows.2), calls=%async_computation | async-start | bytes 4194304 | tf_op jit(solution)/shard_map/all_to_all | solution.py:580
  11.3 2.1 %split_rows.1 = (bf16[128,1024]{1,0:T(8,128)(2,1)}, bf16[384,1024]{1,0:T(8,128)(2,1)}) custom-call(bf16[512,1024]{1,0:T(8,128)(2,1)} %source_ref.1), custom_call_target="tpu_custom_call" | custom-call | bytes 2097152 | tf_op jit(solution)/shard_map/split_rows/pallas_call | solution.py:70
  13.4 2.7 %collective-permute-start = (bf16[128,1024]{1,0:T(8,128)(2,1)}, bf16[128,1024]{1,0:T(8,128)(2,1)S(1)}, u32[]{:S(2)}, u32[]{:S(2)}) collective-permute-start(bf16[128,1024]{1,0:T(8,128)(2,1)} %get-tuple-element.24), channel_id=1, source_target_pairs={{0,4},{2,6},{4,0},{6,2},{1,5},{3,7},{5,1},{7,3},{8,12},{10,14},{12... | collective-permute-start | bytes 786440 | tf_op jit(solution)/shard_map/ppermute | solution.py:588
  16.1 0.3 collective-permute-start.3
  16.7 0.7 add.38
  17.4 16.3 %collective-permute-done.refs_2_.refs_0_ = bf16[128,1024]{1,0:T(8,128)(2,1)S(1)} collective-permute-done((bf16[128,1024]{1,0:T(8,128)(2,1)}, bf16[128,1024]{1,0:T(8,128)(2,1)S(1)}, u32[]{:S(2)}, u32[]{:S(2)}) %collective-permute-start) | collective-permute-done | bytes 262176 | tf_op jit(solution)/shard_map/ppermute | solution.py:588
  33.7 0.8 collective-permute-done.1.refs_1_.rows_ref
  34.5 3.2 %collective-permute-start.2 = (bf16[384,1024]{1,0:T(8,128)(2,1)}, bf16[384,1024]{1,0:T(8,128)(2,1)}, u32[]{:S(2)}, u32[]{:S(2)}) collective-permute-start(bf16[384,1024]{1,0:T(8,128)(2,1)} %after.1), channel_id=1, source_target_pairs={{0,4},{2,6},{4,0},{6,2},{1,5},{3,7},{5,1},{7,3},{8,12},{10,14},{12... | collective-permute-start | bytes 2359304 | tf_op jit(solution)/shard_map/ppermute | solution.py:589
  37.7 3.2 %gather_rows.3 = bf16[8,128,1024]{2,1,0:T(8,128)(2,1)} custom-call(s32[4,32]{1,0:T(4,128)S(1)} %bitcast.18, bf16[32,16,1024]{2,1,0:T(8,128)(2,1)} %collective-permute-done.1.refs_1_.rows_ref), custom_call_target="tpu_custom_call" | custom-call | flops 137438953472 | bytes 4194304 | tf_op jit(solution)/shard_map/gather_rows/pallas_call | solution.py:116
  41.0 1.3 copy-done.5
  42.2 4.4 %all-to-all-start.1 = ((bf16[8,128,1024]{2,1,0:T(8,128)(2,1)}), bf16[8,128,1024]{2,1,0:T(8,128)(2,1)}, u32[]{:S(2)}, u32[]{:S(2)}) async-start(bf16[8,128,1024]{2,1,0:T(8,128)(2,1)} %gather_rows.3), calls=%async_computation.1 | async-start | bytes 4194304 | tf_op jit(solution)/shard_map/all_to_all | solution.py:580
  46.6 4.3 %near_half.2 = (f32[512,512]{1,0:T(8,128)}, f32[8,512]{1,0:T(8,128)S(1)}, bf16[512,1024]{1,0:T(8,128)(2,1)S(1)}) custom-call(bf16[512,1024]{1,0:T(8,128)(2,1)} %source_ref.1, bf16[8,128,1024]{2,1,0:T(8,128)(2,1)} %copy-done.5, s32[1,512]{1,0:T(1,128)} %bitcast.2.refs_2_.chosen_ref), custom_call_target="tpu_custom_call" | custom-call | flops 137438953472 | bytes 4194304 | tf_op jit(solution)/shard_map/near_half/pallas_call | solution.py:290
  50.9 20.6 %collective-permute-done.2.refs_1_ = bf16[384,1024]{1,0:T(8,128)(2,1)} collective-permute-done((bf16[384,1024]{1,0:T(8,128)(2,1)}, bf16[384,1024]{1,0:T(8,128)(2,1)}, u32[]{:S(2)}, u32[]{:S(2)}) %collective-permute-start.2) | collective-permute-done | bytes 786464 | tf_op jit(solution)/shard_map/ppermute | solution.py:589
  71.5 4.2 %near_half.3 = (f32[512,512]{1,0:T(8,128)}, f32[8,512]{1,0:T(8,128)S(1)}, bf16[512,1024]{1,0:T(8,128)(2,1)S(1)}) custom-call(bf16[128,1024]{1,0:T(8,128)(2,1)S(1)} %copy-done.2, bf16[384,1024]{1,0:T(8,128)(2,1)} %collective-permute-done.2.refs_1_, bf16[8,128,1024]{2,1,0:T(8,128)(2,1)} %copy-done.5, s32[1,512]{1,0:T(1,128)} %bitcast.3.refs_3_.chosen_others_ref), custom_call_target="tpu_custom_call" | custom-call | flops 137438953472 | bytes 4194304 | tf_op jit(solution)/shard_map/near_half/pallas_call | solution.py:290
  75.7 4.0 %far_half.1 = (f32[2,512,512]{2,1,0:T(8,128)S(1)}, f32[8,512]{1,0:T(8,128)S(1)}, s32[8,512]{1,0:T(8,128)S(1)}, s32[8,512]{1,0:T(8,128)S(1)}) custom-call(bf16[512,1024]{1,0:T(8,128)(2,1)S(1)} %get-tuple-element.23.queries_ref, bf16[512,1024]{1,0:T(8,128)(2,1)S(1)} %get-tuple-element.26.others_ref, bf16[8,128,1024]{2,1,0:T(8,128)(2,1)} %all-to-all-done.1.slabs_ref.far_ref, ...), custom_call_target="tpu_custom_call" | custom-call | flops 1073741824 | bytes 4194304 | tf_op jit(solution)/shard_map/far_half/pallas_call | solution.py:332
  80.1 4.3 %collective-permute-done.4.there_ref = f32[8,512]{1,0:T(8,128)S(1)} collective-permute-done((f32[8,512]{1,0:T(8,128)S(1)}, f32[8,512]{1,0:T(8,128)S(1)}, u32[]{:S(2)}, u32[]{:S(2)}) %collective-permute-start.4) | collective-permute-done | bytes 16416 | tf_op jit(solution)/shard_map/ppermute | solution.py:608
  84.4 4.8 %other_grads.1 = (bf16[512,1024]{1,0:T(8,128)(2,1)}, f32[8,512]{1,0:T(8,128)S(1)}, f32[1,512]{1,0:T(1,128)}) custom-call(f32[8,512]{1,0:T(8,128)S(1)} %get-tuple-element.29.here_ref, f32[8,512]{1,0:T(8,128)S(1)} %collective-permute-done.4.there_ref, s32[8,512]{1,0:T(8,128)S(1)} %get-tuple-element.30.near_target_ref.target_ref, ...), custom_call_target="tpu_custom_call" | custom-call | flops 1073741824 | bytes 8388608 | tf_op jit(solution)/shard_map/other_grads/pallas_call | solution.py:457
  89.3 1.2 copy-done
  90.5 2.4 %far_grads.1 = (bf16[8,128,1024]{2,1,0:T(8,128)(2,1)}, bf16[512,512]{1,0:T(8,128)(2,1)}) custom-call(bf16[512,1024]{1,0:T(8,128)(2,1)S(1)} %get-tuple-element.23.queries_ref, bf16[512,1024]{1,0:T(8,128)(2,1)S(1)} %get-tuple-element.26.others_ref, f32[2,512,512]{2,1,0:T(8,128)S(1)} %get-tuple-element.32.far_logits_ref.logits_ref, ...), custom_call_target="tpu_custom_call" | custom-call | flops 1073741824 | bytes 4194304 | tf_op jit(solution)/shard_map/far_grads/pallas_call | solution.py:492
  92.9 4.6 %all-to-all-start.3 = ((bf16[8,128,1024]{2,1,0:T(8,128)(2,1)}), bf16[8,128,1024]{2,1,0:T(8,128)(2,1)}, u32[]{:S(2)}, u32[]{:S(2)}) async-start(bf16[8,128,1024]{2,1,0:T(8,128)(2,1)} %get-tuple-element.41), calls=%async_computation.3 | async-start | bytes 4194304 | tf_op jit(solution)/shard_map/all_to_all | solution.py:580
  97.5 6.3 %near_grads.1 = (bf16[8,128,1024]{2,1,0:T(8,128)(2,1)}, f32[512,1024]{1,0:T(8,128)}) custom-call(bf16[512,1024]{1,0:T(8,128)(2,1)S(1)} %get-tuple-element.23.queries_ref, bf16[512,1024]{1,0:T(8,128)(2,1)S(1)} %get-tuple-element.26.others_ref, s32[8,512]{1,0:T(8,128)S(1)} %get-tuple-element.30.near_target_ref.target_ref, ...), custom_call_target="tpu_custom_call" | custom-call | flops 137438953472 | bytes 8388608 | tf_op jit(solution)/shard_map/near_grads/pallas_call | solution.py:536
  103.8 20.2 %all-to-all-done.3.slabs_ref = bf16[8,128,1024]{2,1,0:T(8,128)(2,1)} async-done(((bf16[8,128,1024]{2,1,0:T(8,128)(2,1)}), bf16[8,128,1024]{2,1,0:T(8,128)(2,1)}, u32[]{:S(2)}, u32[]{:S(2)}) %all-to-all-start.3) | async-done | bytes 2097184 | tf_op jit(solution)/shard_map/all_to_all | solution.py:580
  124.0 3.6 %all-to-all-start.2 = ((bf16[8,128,1024]{2,1,0:T(8,128)(2,1)}), bf16[8,128,1024]{2,1,0:T(8,128)(2,1)S(1)}, u32[]{:S(2)}, u32[]{:S(2)}) async-start(bf16[8,128,1024]{2,1,0:T(8,128)(2,1)} %get-tuple-element.40), calls=%async_computation.2 | async-start | bytes 4194304 | tf_op jit(solution)/shard_map/all_to_all | solution.py:580
  127.6 3.6 %segment_rows.2 = bf16[512,1024]{1,0:T(8,128)(2,1)} custom-call(bf16[512,1024]{1,0:T(8,128)(2,1)S(1)} %fusion.spread_ref, bf16[8,128,1024]{2,1,0:T(8,128)(2,1)} %all-to-all-done.3.slabs_ref), custom_call_target="tpu_custom_call" | custom-call | flops 1073741824 | bytes 4194304 | tf_op jit(solution)/shard_map/segment_rows/pallas_call | solution.py:162
  131.2 3.8 %collective-permute-start.6 = (bf16[512,1024]{1,0:T(8,128)(2,1)}, bf16[512,1024]{1,0:T(8,128)(2,1)}, u32[]{:S(2)}, u32[]{:S(2)}) collective-permute-start(bf16[512,1024]{1,0:T(8,128)(2,1)} %segment_rows.2), channel_id=1, source_target_pairs={{0,2},{2,0},{4,6},{6,4},{1,3},{3,1},{5,7},{7,5},{8,10},{10,8},{12,... | collective-permute-start | bytes 3145736 | tf_op jit(solution)/shard_map/ppermute | solution.py:620
  135.2 3.5 %add_parts.1.refs_1_ = bf16[512,1024]{1,0:T(8,128)(2,1)} custom-call(f32[512,1024]{1,0:T(8,128)S(1)} %copy-done.4, bf16[512,1024]{1,0:T(8,128)(2,1)} %collective-permute-done.5.part_ref), custom_call_target="tpu_custom_call" | custom-call | flops 137438953472 | bytes 4194304 | tf_op jit(solution)/shard_map/add_parts/pallas_call | solution.py:558
  138.6 15.5 %all-to-all-done.2.slabs_ref = bf16[8,128,1024]{2,1,0:T(8,128)(2,1)S(1)} async-done(((bf16[8,128,1024]{2,1,0:T(8,128)(2,1)}), bf16[8,128,1024]{2,1,0:T(8,128)(2,1)S(1)}, u32[]{:S(2)}, u32[]{:S(2)}) %all-to-all-start.2) | async-done | bytes 2097184 | tf_op jit(solution)/shard_map/all_to_all | solution.py:580
  154.1 5.0 %collective-permute-done.6.refs_0_ = bf16[512,1024]{1,0:T(8,128)(2,1)} collective-permute-done((bf16[512,1024]{1,0:T(8,128)(2,1)}, bf16[512,1024]{1,0:T(8,128)(2,1)}, u32[]{:S(2)}, u32[]{:S(2)}) %collective-permute-start.6) | collective-permute-done | bytes 1048608 | tf_op jit(solution)/shard_map/ppermute | solution.py:620
  159.1 4.1 %segment_rows.3 = bf16[512,1024]{1,0:T(8,128)(2,1)} custom-call(bf16[512,1024]{1,0:T(8,128)(2,1)S(1)} %fusion.spread_ref, bf16[8,128,1024]{2,1,0:T(8,128)(2,1)} %copy-done.6, bf16[512,1024]{1,0:T(8,128)(2,1)} %collective-permute-done.6.refs_0_, bf16[512,1024]{1,0:T(8,128)(2,1)} %add_parts.1.refs_1_), custom_call_target="tpu_custom_call" | custom-call | flops 1073741824 | bytes 4194304 | tf_op jit(solution)/shard_map/segment_rows/pallas_call | solution.py:162
  (29 shorter events, 0.8 us)
Async XLA Ops:
  0.6 4.9 %copy-start.3 = (s32[32,4]{0,1:T(4,128)S(1)}, s32[32,4]{0,1:T(4,128)}, u32[]{:S(2)}) copy-start(s32[32,4]{0,1:T(4,128)} %param.8) | copy-start | bytes 1540
  2.5 32.0 %collective-permute-start.1 = (bf16[32,16,1024]{2,1,0:T(8,128)(2,1)S(1)}, bf16[32,16,1024]{2,1,0:T(8,128)(2,1)}, u32[]{:S(2)}, u32[]{:S(2)}) collective-permute-start(bf16[32,16,1024]{2,1,0:T(8,128)(2,1)S(1)} %bitcast.15), channel_id=1, source_target_pairs={{0,2},{2,0},{4,6},{6,4},{1,3},{3,1},{5,7},{7,5},{8,10},{10,8},{12,... | collective-permute-start | bytes 3145736 | tf_op jit(solution)/shard_map/ppermute | solution.py:586
  7.6 33.4 %all-to-all-start = ((bf16[8,128,1024]{2,1,0:T(8,128)(2,1)}), bf16[8,128,1024]{2,1,0:T(8,128)(2,1)S(1)}, u32[]{:S(2)}, u32[]{:S(2)}) async-start(bf16[8,128,1024]{2,1,0:T(8,128)(2,1)} %gather_rows.2), calls=%async_computation | async-start | bytes 4194304 | tf_op jit(solution)/shard_map/all_to_all | solution.py:580
  13.4 20.3 %collective-permute-start = (bf16[128,1024]{1,0:T(8,128)(2,1)}, bf16[128,1024]{1,0:T(8,128)(2,1)S(1)}, u32[]{:S(2)}, u32[]{:S(2)}) collective-permute-start(bf16[128,1024]{1,0:T(8,128)(2,1)} %get-tuple-element.24), channel_id=1, source_target_pairs={{0,4},{2,6},{4,0},{6,2},{1,5},{3,7},{5,1},{7,3},{8,12},{10,14},{12... | collective-permute-start | bytes 786440 | tf_op jit(solution)/shard_map/ppermute | solution.py:588
  16.1 34.8 %collective-permute-start.3 = (s32[512]{0:T(512)}, s32[512]{0:T(512)}, u32[]{:S(2)}, u32[]{:S(2)}) collective-permute-start(s32[512]{0:T(512)} %param.9), channel_id=1, source_target_pairs={{0,4},{2,6},{4,0},{6,2},{1,5},{3,7},{5,1},{7,3},{8,12},{10,14},{12... | collective-permute-start | bytes 6152 | tf_op jit(solution)/shard_map/ppermute | solution.py:590
  33.7 0.8 copy-start.1
  34.5 37.0 %collective-permute-start.2 = (bf16[384,1024]{1,0:T(8,128)(2,1)}, bf16[384,1024]{1,0:T(8,128)(2,1)}, u32[]{:S(2)}, u32[]{:S(2)}) collective-permute-start(bf16[384,1024]{1,0:T(8,128)(2,1)} %after.1), channel_id=1, source_target_pairs={{0,4},{2,6},{4,0},{6,2},{1,5},{3,7},{5,1},{7,3},{8,12},{10,14},{12... | collective-permute-start | bytes 2359304 | tf_op jit(solution)/shard_map/ppermute | solution.py:589
  40.9 1.3 copy-start.5
  42.2 33.4 %all-to-all-start.1 = ((bf16[8,128,1024]{2,1,0:T(8,128)(2,1)}), bf16[8,128,1024]{2,1,0:T(8,128)(2,1)}, u32[]{:S(2)}, u32[]{:S(2)}) async-start(bf16[8,128,1024]{2,1,0:T(8,128)(2,1)} %gather_rows.3), calls=%async_computation.1 | async-start | bytes 4194304 | tf_op jit(solution)/shard_map/all_to_all | solution.py:580
  46.6 24.9 %copy-start.2 = (bf16[128,1024]{1,0:T(8,128)(2,1)S(1)}, bf16[128,1024]{1,0:T(8,128)(2,1)}, u32[]{:S(2)}) copy-start(bf16[128,1024]{1,0:T(8,128)(2,1)} %copy-done.1) | copy-start | bytes 786436
  75.7 4.1 %copy-start.7 = (s32[1024]{0:T(1024)S(1)}, s32[1024]{0:T(1024)}, u32[]{:S(2)}) copy-start(s32[1024]{0:T(1024)} %add.38) | copy-start | bytes 12292
  79.7 4.7 %collective-permute-start.4 = (f32[8,512]{1,0:T(8,128)S(1)}, f32[8,512]{1,0:T(8,128)S(1)}, u32[]{:S(2)}, u32[]{:S(2)}) collective-permute-start(f32[8,512]{1,0:T(8,128)S(1)} %get-tuple-element.29.here_ref), channel_id=1, source_target_pairs={{0,4},{2,6},{4,0},{6,2},{1,5},{3,7},{5,1},{7,3},{8,12},{10,14},{12... | collective-permute-start | bytes 49160 | tf_op jit(solution)/shard_map/ppermute | solution.py:608
  89.2 46.0 %collective-permute-start.5 = (bf16[512,1024]{1,0:T(8,128)(2,1)}, bf16[512,1024]{1,0:T(8,128)(2,1)}, u32[]{:S(2)}, u32[]{:S(2)}) collective-permute-start(bf16[512,1024]{1,0:T(8,128)(2,1)} %get-tuple-element.37.wait_ref), channel_id=1, source_target_pairs={{0,4},{2,6},{4,0},{6,2},{1,5},{3,7},{5,1},{7,3},{8,12},{10,14},{12... | collective-permute-start | bytes 3145736 | tf_op jit(solution)/shard_map/ppermute | solution.py:618
  89.3 1.3 copy-start
  92.9 31.0 %all-to-all-start.3 = ((bf16[8,128,1024]{2,1,0:T(8,128)(2,1)}), bf16[8,128,1024]{2,1,0:T(8,128)(2,1)}, u32[]{:S(2)}, u32[]{:S(2)}) async-start(bf16[8,128,1024]{2,1,0:T(8,128)(2,1)} %get-tuple-element.41), calls=%async_computation.3 | async-start | bytes 4194304 | tf_op jit(solution)/shard_map/all_to_all | solution.py:580
  124.0 30.2 %all-to-all-start.2 = ((bf16[8,128,1024]{2,1,0:T(8,128)(2,1)}), bf16[8,128,1024]{2,1,0:T(8,128)(2,1)S(1)}, u32[]{:S(2)}, u32[]{:S(2)}) async-start(bf16[8,128,1024]{2,1,0:T(8,128)(2,1)} %get-tuple-element.40), calls=%async_computation.2 | async-start | bytes 4194304 | tf_op jit(solution)/shard_map/all_to_all | solution.py:580
  127.6 7.6 %copy-start.4 = (f32[512,1024]{1,0:T(8,128)S(1)}, f32[512,1024]{1,0:T(8,128)}, u32[]{:S(2)}) copy-start(f32[512,1024]{1,0:T(8,128)} %get-tuple-element.39.own_ref) | copy-start | bytes 6291460
  131.2 27.9 %collective-permute-start.6 = (bf16[512,1024]{1,0:T(8,128)(2,1)}, bf16[512,1024]{1,0:T(8,128)(2,1)}, u32[]{:S(2)}, u32[]{:S(2)}) collective-permute-start(bf16[512,1024]{1,0:T(8,128)(2,1)} %segment_rows.2), channel_id=1, source_target_pairs={{0,2},{2,0},{4,6},{6,4},{1,3},{3,1},{5,7},{7,5},{8,10},{10,8},{12,... | collective-permute-start | bytes 3145736 | tf_op jit(solution)/shard_map/ppermute | solution.py:620
  154.1 5.0 %copy-start.6 = (bf16[8,128,1024]{2,1,0:T(8,128)(2,1)}, bf16[8,128,1024]{2,1,0:T(8,128)(2,1)S(1)}, u32[]{:S(2)}) copy-start(bf16[8,128,1024]{2,1,0:T(8,128)(2,1)S(1)} %all-to-all-done.2.slabs_ref) | copy-start | bytes 6291460

commit v4 on v3

--- a/solution.py
+++ b/solution.py
@@ -79,12 +79,7 @@
     )(array)
 
 
-def gather_kernel(planes, ranks, ids, rows_ref, out_ref, made, left, *held):
-    if held:
-        load = pltpu.make_async_copy(rows_ref, *held)
-        load.start()
-        load.wait()
-        rows_ref = held[0]
+def gather_kernel(planes, ranks, ids, rows_ref, out_ref, made, left):
     slabs, depth, width = out_ref.shape
     height = rows_ref.shape[1]
     refs = ids.shape[0]
@@ -109,16 +104,15 @@
     lax.fori_loop(0, slabs, drain, 0)
 
 
-def gather_rows(ids, rows, slabs, planes, ranks, flops, arrived):
+def gather_rows(ids, rows, slabs, planes, ranks, flops):
     blocks, height, width = rows.shape
-    held = [pltpu.VMEM(rows.shape, BF16), pltpu.SemaphoreType.DMA] if arrived else []
     dims = (slabs, 2 * ids.shape[0] * height, width)
     return pl.pallas_call(
         functools.partial(gather_kernel, planes, ranks),
-        in_specs=[SMEM, HBM if arrived else VMEM],
+        in_specs=[SMEM, VMEM],
         out_specs=HBM,
         out_shape=pltpu.HBM(dims, BF16),
-        scratch_shapes=[pltpu.VMEM(dims, BF16), pltpu.SemaphoreType.DMA((slabs,))] + held,
+        scratch_shapes=[pltpu.VMEM(dims, BF16), pltpu.SemaphoreType.DMA((slabs,))],
         compiler_params=params(),
         name="gather_rows",
         cost_estimate=cost(flops, 4),
@@ -126,55 +120,48 @@
 
 
 def segment_kernel(stripes, with_start, spread_ref, slabs_ref, *refs):
-    start_ref = refs[0] if with_start else None
-    out_ref, held, result, begun, arrived, left = refs[-6:]
+    out_ref, held, result, begun, arrived, came, left = refs[-7:]
     slabs, depth, width = slabs_ref.shape
     tile = width // stripes
     columns = [pl.ds(t * tile, tile) for t in range(stripes)]
-    loads = [
-        pltpu.make_async_copy(slabs_ref.at[:, :, columns[t]], held.at[t], arrived.at[t]) for t in range(stripes)
-    ]
-    for load in loads:
-        load.start()
+    loads = [load(slabs_ref.at[:, :, columns[t]], held.at[t], arrived.at[t]) for t in range(stripes)]
     if with_start:
-        first = pltpu.make_async_copy(start_ref, begun, arrived.at[stripes])
-        first.start()
+        starts = [load(refs[0].at[:, columns[t]], begun.at[t], came.at[t]) for t in range(stripes)]
     stores = []
     for t in range(stripes):
         loads[t].wait()
         total = jnp.dot(spread_ref[...], held[t].reshape(slabs * depth, tile), preferred_element_type=F32)
         if with_start:
-            if t == 0:
-                first.wait()
-            total += begun[:, t * tile : (t + 1) * tile].astype(F32)
+            starts[t].wait()
+            total += begun[t].astype(F32)
         result[t] = total.astype(BF16)
-        stores.append(pltpu.make_async_copy(result.at[t], out_ref.at[:, columns[t]], left.at[t]))
-        stores[t].start()
+        stores.append(load(result.at[t], out_ref.at[:, columns[t]], left.at[t]))
     for store in stores:
         store.wait()
 
 
-def segment_rows(spread, slabs, *start):
+def segment_rows(spread, slabs, start=None, wait=None):
     stripes = 2
     rows = spread.shape[0]
     count, depth, width = slabs.shape
     tile = width // stripes
-    return pl.pallas_call(
-        functools.partial(segment_kernel, stripes, len(start) > 0),
-        in_specs=[VMEM, HBM] + [HBM] * len(start),
+    extra = [array for array in (start, wait) if array is not None]
+    sems = pltpu.SemaphoreType.DMA((stripes,))
+    return pl.pallas_call(
+        functools.partial(segment_kernel, stripes, start is not None),
+        in_specs=[VMEM, ANY] + [ANY] * len(extra),
         out_specs=HBM,
         out_shape=pltpu.HBM((rows, width), BF16),
         scratch_shapes=[
             pltpu.VMEM((stripes, count, depth, tile), BF16),
             pltpu.VMEM((stripes, rows, tile), BF16),
-            pltpu.VMEM((rows, width) if start else (16, 128), BF16),
-            pltpu.SemaphoreType.DMA((stripes + 1,)),
-            pltpu.SemaphoreType.DMA((stripes,)),
-        ],
+            pltpu.VMEM((stripes, rows, tile), BF16),
+        ]
+        + [sems] * 3,
         compiler_params=params(),
         name="segment_rows",
         cost_estimate=cost(1 << 30, 4),
-    )(spread, slabs, *start)
+    )(spread, slabs, *extra)
 
 
 def candidates(slabs_ref, q, chunk):
@@ -245,51 +232,49 @@
     stats_ref[4 * q + 3 : 4 * q + 4, :] = jnp.zeros_like(stats[0])
 
 
+def held_rows(held, chunk):
+    slabs = held.shape[0] // CHUNKS
+    return held[chunk * slabs : (chunk + 1) * slabs].reshape(slabs * held.shape[1], held.shape[2])
+
+
+def row_chunk(rows, chunk):
+    return slice(chunk * rows // CHUNKS, (chunk + 1) * rows // CHUNKS)
+
+
 def put_targets(place, target_ref, chosen_ref, chosen_others_ref):
     target_ref[...] = jnp.full(target_ref.shape, -1, jnp.int32)
     target_ref[0:1, :] = place(chosen_ref[...])
     target_ref[1:2, :] = place(chosen_others_ref[...])
 
 
-def near_logits_kernel(q, place, *refs):
-    *block_refs, slabs_ref, chosen_ref, logits_ref, stats_ref, kept_ref, held, made, arrived, came, left = refs
+def own_kernel(place, queries_ref, slabs_ref, chosen_ref, logits_ref, stats_ref, kept_ref, held, made, arrived, came, left):
     half = slabs_ref.shape[1] // 2
-    picks = pl.ds(q * half, half)
-    parts = [part_of(slabs_ref.shape[0], c) for c in range(CHUNKS)]
-    loads = [load(slabs_ref.at[part, picks], held.at[part], arrived.at[c]) for c, part in enumerate(parts)]
-    if q == 0:
-        load(block_refs[0], kept_ref, came).wait()
-    else:
-        cut = block_refs[0].shape[0]
-        kept_ref[:cut, :] = block_refs[0][...]
-        kept_ref[cut:, :] = block_refs[1][...]
+    loads = load_chunks(slabs_ref.at[:, pl.ds(0, half)], held, arrived)
+    load(queries_ref, kept_ref, came).wait()
     stores = []
 
     def slab_part(c):
         loads[c].wait()
-        slabs = held.shape[0] // CHUNKS
-        return held[c * slabs : (c + 1) * slabs].reshape(slabs * half, held.shape[2])
+        return held_rows(held, c)
 
     def put(c, block):
         part = part_of(logits_ref.shape[0], c)
-        rows = block.shape[0]
-        made[c * rows : (c + 1) * rows, :] = block
+        made[row_chunk(made.shape[0], c), :] = block
         stores.append(load(made.at[part], logits_ref.at[part], left.at[c]))
 
     stats = block_logits(kept_ref, slab_part, place(chosen_ref[...]), put)
-    for i in range(3):
-        stats_ref[i : i + 1, :] = stats[i]
-    stats_ref[3:, :] = jnp.zeros((stats_ref.shape[0] - 3, stats_ref.shape[1]), F32)
+    put_stats(stats_ref, 0, stats)
+    put_stats(stats_ref, 1, stats)
     for store in stores:
         store.wait()
 
 
-def near_half(q, parts, slabs, chosen, place, hint):
-    size, width = sum(part.shape[0] for part in parts), slabs.shape[2]
+def own_half(queries, slabs, chosen, place):
+    size, width = queries.shape
     rows = slabs.shape[0] * slabs.shape[1] // 2
     return pl.pallas_call(
-        functools.partial(near_logits_kernel, q, place),
-        in_specs=[HBM if q == 0 else VMEM] * len(parts) + [HBM, VMEM],
+        functools.partial(own_kernel, place),
+        in_specs=[HBM, HBM, VMEM],
         out_specs=[HBM, VMEM, VMEM],
         out_shape=[pltpu.HBM((rows, size), F32), shape((8, size), F32), shape((size, width), BF16)],
         scratch_shapes=[
@@ -300,50 +285,84 @@
             pltpu.SemaphoreType.DMA((CHUNKS,)),
         ],
         compiler_params=params(),
-        name="near_half",
-        cost_estimate=cost(hint, 4),
-    )(*parts, slabs, chosen)
-
-
-def far_logits_kernel(
-    near_place, far_place, queries_ref, others_ref, slabs_ref, chosen_ref, chosen_others_ref, own_stats_ref, other_stats_ref,
-    logits_ref, stats_ref, near_target_ref, far_target_ref, held, arrived,
+        name="own_half",
+        cost_estimate=cost(BUSY, 4),
+    )(queries, slabs, chosen)
+
+
+def rest_kernel(
+    near_place, far_place, queries_ref, low_ref, high_ref, near_ref, far_ref, chosen_ref, chosen_others_ref, own_stats_ref,
+    other_logits_ref, saved_ref, far_logits_ref, stats_ref, near_target_ref, far_target_ref, others_ref, near_rows, far_rows,
+    held, near_in, far_in, held_in, left, came,
 ):
-    loads = load_chunks(slabs_ref, held, arrived)
+    half = near_ref.shape[1] // 2
+    cut = low_ref.shape[0]
+    size = others_ref.shape[0]
+    whole = [
+        load(low_ref, others_ref.at[pl.ds(0, cut)], came.at[0]),
+        load(high_ref, others_ref.at[pl.ds(cut, size - cut)], came.at[1]),
+    ]
+    near_loads = load_chunks(near_ref.at[:, pl.ds(half, half)], near_rows, near_in)
+    held_loads = load_chunks(far_ref.at[:, pl.ds(0, half)], held, held_in)
+    far_loads = load_chunks(far_ref.at[:, pl.ds(half, half)], far_rows, far_in)
     put_targets(near_place, near_target_ref, chosen_ref, chosen_others_ref)
     put_targets(far_place, far_target_ref, chosen_ref, chosen_others_ref)
-    for q, (block_ref, near_ref) in enumerate(((queries_ref, own_stats_ref), (others_ref, other_stats_ref))):
-
-        def slab_part(c, q=q):
-            if q == 0:
-                loads[c].wait()
-            return candidates(held, q, c)
-
-        def put(c, block, q=q):
-            logits_ref[q, chunk_rows(logits_ref, c), :] = block
-
-        stats = block_logits(block_ref, slab_part, far_target_ref[q : q + 1, :], put)
-        put_stats(stats_ref, q, joined(stat_rows(near_ref, 0), stats))
-
-
-def far_half(queries, others, slabs, chosen, chosen_others, own_stats, other_stats, places):
-    size = queries.shape[0]
-    rows = slabs.shape[0] * slabs.shape[1] // 2
-    return pl.pallas_call(
-        functools.partial(far_logits_kernel, *places),
-        in_specs=[VMEM, VMEM, HBM, VMEM, VMEM, VMEM, VMEM],
-        out_specs=[VMEM] * 4,
+    stores = []
+
+    def part(loads, rows):
+        def get(c):
+            loads[c].wait()
+            return held_rows(rows, c)
+
+        return get
+
+    def put_near(c, block):
+        rows = part_of(other_logits_ref.shape[0], c)
+        other_logits_ref[row_chunk(other_logits_ref.shape[0], c), :] = block
+        stores.append(load(other_logits_ref.at[rows], saved_ref.at[rows], left.at[c]))
+
+    def put_far(q):
+        def put(c, block):
+            far_logits_ref[q, chunk_rows(far_logits_ref, c), :] = block
+
+        return put
+
+    for copy in whole:
+        copy.wait()
+    near = block_logits(others_ref, part(near_loads, near_rows), near_target_ref[1:2, :], put_near)
+    own = block_logits(queries_ref, part(held_loads, held), far_target_ref[0:1, :], put_far(0))
+    put_stats(stats_ref, 0, joined(stat_rows(own_stats_ref, 0), own))
+    far = block_logits(others_ref, part(far_loads, far_rows), far_target_ref[1:2, :], put_far(1))
+    put_stats(stats_ref, 1, joined(near, far))
+    for store in stores:
+        store.wait()
+
+
+def rest_half(queries, low, high, near_slabs, far_slabs, chosen, chosen_others, own_stats, places):
+    size, width = queries.shape
+    rows = near_slabs.shape[0] * near_slabs.shape[1] // 2
+    part = (near_slabs.shape[0], near_slabs.shape[1] // 2, width)
+    chunk_sems = pltpu.SemaphoreType.DMA((CHUNKS,))
+    return pl.pallas_call(
+        functools.partial(rest_kernel, *places),
+        in_specs=[VMEM] + [ANY] * 2 + [HBM] * 2 + [VMEM] * 3,
+        out_specs=[VMEM, HBM] + [VMEM] * 7,
         out_shape=[
+            shape((rows, size), F32),
+            pltpu.HBM((rows, size), F32),
             shape((2, rows, size), F32),
             shape((8, size), F32),
             shape((8, size), jnp.int32),
             shape((8, size), jnp.int32),
+            shape((size, width), BF16),
+            shape(part, BF16),
+            shape(part, BF16),
         ],
-        scratch_shapes=[pltpu.VMEM(slabs.shape, BF16), pltpu.SemaphoreType.DMA((CHUNKS,))],
-        compiler_params=params(),
-        name="far_half",
-        cost_estimate=cost(1 << 30, 4),
-    )(queries, others, slabs, chosen, chosen_others, own_stats, other_stats)
+        scratch_shapes=[pltpu.VMEM(part, BF16)] + [chunk_sems] * 4 + [pltpu.SemaphoreType.DMA((2,))],
+        compiler_params=params(),
+        name="rest_half",
+        cost_estimate=cost(3 << 29, 8),
+    )(queries, low, high, near_slabs, far_slabs, chosen, chosen_others, own_stats)
 
 
 def log_totals(here_ref, there_ref):
@@ -424,47 +443,78 @@
     ]
 
 
-def row_chunk(rows, chunk):
-    return slice(chunk * rows // CHUNKS, (chunk + 1) * rows // CHUNKS)
-
-
-def other_kernel(
-    here_ref, there_ref, near_target_ref, far_target_ref, far_logits_ref, near_logits_ref, near_ref, far_ref,
-    other_ref, totals_ref, loss_ref, logits, near, far, came, made, left,
-):
-    copies = load_share(1, near_logits_ref, near_ref, far_ref, logits, near, far, came)
+def early_kernel(stats_ref, near_target_ref, far_target_ref, near_logits_ref, far_logits_ref, near_ref, far_ref, sums_ref, hit_ref):
+    dims = (((0,), (0,)), ((), ()))
+    top = stats_ref[4:5, :]
+    rows = near_logits_ref.shape[0]
+    for c in range(CHUNKS):
+        part = row_chunk(rows, c)
+        for i, (score, target_ref, slab_ref) in enumerate(
+            ((near_logits_ref[part, :], near_target_ref, near_ref), (far_logits_ref[1, part, :], far_target_ref, far_ref))
+        ):
+            block = held_rows(slab_ref, c)
+            weight = jnp.exp(score - top).astype(BF16)
+            hit = jnp.where(hits(score.shape[0], c, target_ref[1:2, :]), 1.0, 0.0).astype(BF16)
+            product = lax.dot_general(weight, block, dims, preferred_element_type=F32)
+            picked = lax.dot_general(hit, block, dims, preferred_element_type=F32)
+            if c == 0 and i == 0:
+                sums_ref[...] = product
+                hit_ref[...] = picked
+            else:
+                sums_ref[...] += product
+                hit_ref[...] += picked
+
+
+def early_grads(stats, near_target, far_target, near_logits, far_logits, near_rows, far_rows):
+    size, width = near_logits.shape[1], near_rows.shape[2]
+    return pl.pallas_call(
+        early_kernel,
+        in_specs=[VMEM] * 7,
+        out_specs=[VMEM] * 2,
+        out_shape=[shape((size, width), F32)] * 2,
+        compiler_params=params(),
+        name="early_grads",
+        cost_estimate=cost(BUSY, 4),
+    )(stats, near_target, far_target, near_logits, far_logits, near_rows, far_rows)
+
+
+def other_kernel(here_ref, there_ref, near_target_ref, far_target_ref, sums_ref, hit_ref, other_ref, totals_ref, loss_ref, made, left):
     totals = log_totals(here_ref, there_ref)
-    rows = logits.shape[0]
-
-    def far_piece(c):
-        return dlogits(far_logits_ref[1, row_chunk(rows, c), :], totals[1][0], c, far_target_ref[1:2, :])
-
-    def near_piece(c):
-        return dlogits(logits[row_chunk(rows, c), :], totals[1][0], c, near_target_ref[1:2, :])
-
-    total = query_share(copies, far_piece, near_piece, near, far, None)
-    made[...] = (SCALE * total).astype(BF16)
-    store = load(made, other_ref, left)
+    total = totals[1][0]
+    top, _, pick = stat_rows(here_ref, 1)
+    held = jnp.maximum(near_target_ref[1:2, :], far_target_ref[1:2, :]) >= 0
+    scale = jnp.exp(top - total)
+    counted = scale * jnp.exp(jnp.where(held, pick - top, 0.0)).astype(BF16).astype(F32)
+    wanted = (jnp.exp(jnp.where(held, pick - total, 0.0)) - 1.0).astype(BF16).astype(F32)
+    rows = [scale, jnp.where(held, wanted - counted, 0.0)]
+    columns = jnp.transpose(jnp.concatenate(rows + [jnp.zeros_like(scale)] * 6, axis=0))
+    stores = []
+    for c in range(CHUNKS):
+        part = row_chunk(made.shape[0], c)
+        share = columns[part, 0:1] * sums_ref[part, :] + columns[part, 1:2] * hit_ref[part, :]
+        made[part, :] = (SCALE * share).astype(BF16)
+        some = part_of(made.shape[0], c)
+        stores.append(load(made.at[some], other_ref.at[some], left.at[c]))
     totals_ref[...] = jnp.zeros_like(totals_ref)
     for q in range(2):
         totals_ref[q : q + 1, :] = totals[q][0]
     loss_ref[...] = totals[0][0] - totals[0][1]
-    store.wait()
-
-
-def other_grads(here, there, near_target, far_target, far_logits, near_logits, near_slabs, far_slabs):
-    size, width = far_logits.shape[2], near_slabs.shape[2]
+    for store in stores:
+        store.wait()
+
+
+def other_grads(here, there, near_target, far_target, sums, hit):
+    size, width = sums.shape
     return pl.pallas_call(
         other_kernel,
-        in_specs=[VMEM] * 5 + [HBM] * 3,
+        in_specs=[VMEM] * 6,
         out_specs=[HBM, VMEM, VMEM],
         out_shape=[pltpu.HBM((size, width), BF16), shape((8, size), F32), shape((1, size), F32)],
-        scratch_shapes=share_scratch(near_logits, near_slabs)
-        + [pltpu.VMEM((size, width), BF16), pltpu.SemaphoreType.DMA],
+        scratch_shapes=[pltpu.VMEM((size, width), BF16), pltpu.SemaphoreType.DMA((CHUNKS,))],
         compiler_params=params(),
         name="other_grads",
-        cost_estimate=cost(1 << 30, 8),
-    )(here, there, near_target, far_target, far_logits, near_logits, near_slabs, far_slabs)
+        cost_estimate=cost(1 << 20, 4),
+    )(here, there, near_target, far_target, sums, hit)
 
 
 def far_kernel(
@@ -549,22 +599,37 @@
     )(queries, others, target, totals, own_logits, other_logits, pieces, near_slabs, far_slabs)
 
 
-def add_kernel(own_ref, part_ref, out_ref):
-    out_ref[...] = (own_ref[...] + part_ref[...].astype(F32)).astype(BF16)
-
-
-def add_parts(own, part):
-    block = pl.BlockSpec((own.shape[0] // 4, own.shape[1]), lambda i: (i, 0))
+def add_kernel(own_ref, part_ref, *refs):
+    out_ref, own, part, made, own_in, part_in, left = refs[-7:]
+    pieces = [part_of(own.shape[0], c) for c in range(CHUNKS)]
+    loads = [
+        (load(own_ref.at[p], own.at[p], own_in.at[c]), load(part_ref.at[p], part.at[p], part_in.at[c]))
+        for c, p in enumerate(pieces)
+    ]
+    stores = []
+    for c, p in enumerate(pieces):
+        for copy in loads[c]:
+            copy.wait()
+        rows = row_chunk(own.shape[0], c)
+        made[rows, :] = (own[rows, :] + part[rows, :].astype(F32)).astype(BF16)
+        stores.append(load(made.at[p], out_ref.at[p], left.at[c]))
+    for store in stores:
+        store.wait()
+
+
+def add_parts(own, part, hint, *waits):
+    chunk_sems = pltpu.SemaphoreType.DMA((CHUNKS,))
     return pl.pallas_call(
         add_kernel,
-        grid=(4,),
-        in_specs=[block] * 2,
-        out_specs=block,
-        out_shape=shape(own.shape, BF16),
+        in_specs=[HBM] * 2 + [ANY] * len(waits),
+        out_specs=HBM,
+        out_shape=pltpu.HBM(own.shape, BF16),
+        scratch_shapes=[pltpu.VMEM(own.shape, F32), pltpu.VMEM(own.shape, BF16), pltpu.VMEM(own.shape, BF16)]
+        + [chunk_sems] * 3,
         compiler_params=params(),
         name="add_parts",
-        cost_estimate=cost(BUSY, 4),
-    )(own, part)
+        cost_estimate=cost(hint, 4),
+    )(in_hbm(own), in_hbm(part), *waits)
 
 
 def on_device(queries, passages, block_ids, positives):
@@ -577,18 +642,18 @@
     across = [(i, (i + planes // 2) % planes) for i in range(planes)]
 
     def exchange(slab_array):
-        return in_hbm(lax.all_to_all(slab_array, PLANE, split_axis=0, concat_axis=0, tiled=True))
+        return lax.all_to_all(slab_array, PLANE, split_axis=0, concat_axis=0, tiled=True)
 
     ids = block_ids.T
     early = queries.shape[0] // EARLY
     own_rows = jnp.transpose(passages, (1, 0, 2))
-    near_slabs = exchange(gather_rows(ids, own_rows, slabs, planes, ranks, 0, False))
-    pair_rows = in_hbm(lax.ppermute(own_rows, "z", to_pair))
+    near_slabs = in_hbm(exchange(gather_rows(ids, own_rows, slabs, planes, ranks, 0)))
+    pair_rows = lax.ppermute(own_rows, "z", to_pair)
     low, high = split_rows(in_hbm(queries), early)
-    others_low = lax.ppermute(low, "z", across)
-    others_high = lax.ppermute(after(high, pair_rows, others_low), "z", across)
+    others_low = in_hbm(lax.ppermute(low, "z", across))
+    others_high = lax.ppermute(after(high, others_low), "z", across)
     others_positives = lax.ppermute(positives, "z", across)
-    far_slabs = exchange(gather_rows(ids, pair_rows, slabs, planes, ranks, BUSY, True))
+    far_slabs = in_hbm(exchange(gather_rows(ids, pair_rows, slabs, planes, ranks, BUSY)))
 
     table = block_ids.reshape(groups, planes, ranks, refs)
     both = jnp.stack([jnp.take(table, z, axis=1), jnp.take(table, (z + planes // 2) % planes, axis=1)], axis=2)
@@ -598,20 +663,16 @@
     chosen = positives.reshape(1, -1)
     chosen_others = others_positives.reshape(1, -1)
     places = [functools.partial(place_of, far, planes, ranks, refs, height) for far in range(2)]
-    own_logits, own_stats, own = near_half(0, [in_hbm(queries)], near_slabs, chosen, places[0], BUSY)
-    other_logits, other_stats, others = near_half(
-        1, [others_low, others_high], near_slabs, chosen_others, places[0], BUSY
-    )
-    far_logits, stats, near_target, far_target = far_half(
-        own, others, far_slabs, chosen, chosen_others, own_stats, other_stats, places
+    own_logits, own_stats, own = own_half(in_hbm(queries), near_slabs, chosen, places[0])
+    other_logits, saved_logits, far_logits, stats, near_target, far_target, others, near_rows, far_rows = rest_half(
+        own, others_low, others_high, near_slabs, far_slabs, chosen, chosen_others, own_stats, places
     )
     partner = lax.ppermute(stats, "z", across)
-    own_logits, other_logits = in_hbm(own_logits), in_hbm(other_logits)
-    other_part, totals, loss = other_grads(
-        stats, partner, near_target, far_target, far_logits, other_logits, near_slabs, far_slabs
-    )
-    far_contrib, pieces = far_grads(own, others, far_logits, far_target, totals, other_part, far_slabs)
-    far_back = exchange(far_contrib)
+    sums, hit = early_grads(stats, near_target, far_target, other_logits, far_logits, near_rows, far_rows)
+    other_part, totals, loss = other_grads(stats, partner, near_target, far_target, sums, hit)
+    own_logits, other_logits = in_hbm(own_logits), in_hbm(saved_logits)
+    far_contrib, pieces = far_grads(own, others, far_logits, far_target, totals, in_hbm(other_part), far_slabs)
+    far_back = in_hbm(exchange(far_contrib))
     near_contrib, own_grad = near_grads(
         own, others, near_target, totals, own_logits, other_logits, in_hbm(pieces), near_slabs, far_slabs
     )
@@ -619,8 +680,8 @@
     far_sum = segment_rows(spread, far_back)
     pair_sum = lax.ppermute(far_sum, "z", to_pair)
     near_back = exchange(near_contrib)
-    query_grad = add_parts(own_grad, own_part)
-    row_sum = segment_rows(spread, near_back, in_hbm(pair_sum), in_hbm(query_grad))
+    query_grad = add_parts(own_grad, own_part, BUSY, in_hbm(far_sum))
+    row_sum = segment_rows(spread, near_back, pair_sum, in_hbm(query_grad))
     return loss.reshape(-1), query_grad, row_sum.reshape(passages.shape)
 
 

time: 164 us -> 158 us (0.963)
  Pallas kernels: 44.5 us -> 39.9 us
  local copies, waits for them, and re-layouts: 5.23 us -> 2.77 us
    pallas_call x7, Pallas kernels: 28.5 us -> 25.2 us  [the longest x2 7.28 us: segment_rows(): pl.pallas_call(functools.partial(segment_kernel, stripes, start is not No...]
    ppermute x1, waiting for transfers between devices: 4.32 us -> 1.64 us  [on_device(): partner = lax.ppermute(stats, 'z', across)]
    ppermute x1, waiting for transfers between devices: 0.09 us -> 2.45 us  [on_device(): own_part = lax.ppermute(other_part, 'z', across)]
    unnamed x18 -> x6, local copies, waits for them, and re-layouts: 4.46 us -> 2.6 us
  transfers between devices with their start and end apart: 11 -> 11, of which waited for: 8 -> 7; matrix products, arithmetic and copies ran while one was open for 1% -> 0% of each run, Pallas kernels for 19% -> 18%
where the time goes in v4:
time: 158 us; the launch traced here: 157 us
  waiting for transfers between devices  83.1 us (53%)
  Pallas kernels  39.9 us (25%)
  starting transfers between devices  30 us (19%)
  local copies, waits for them, and re-layouts  2.77 us (2%)
    all_to_all x4, waiting for transfers between devices, exchange(): lax.all_to_all(slab_array, PLANE, split_axis=0, concat_axis=0, tiled=True)  35.7 us
    ppermute x1, waiting for transfers between devices, on_device(): others_high = lax.ppermute(after(high, others_low), 'z', across)  23.2 us
    all_to_all x4, starting transfers between devices, exchange(): lax.all_to_all(slab_array, PLANE, split_axis=0, concat_axis=0, tiled=True)  16.9 us
    ppermute x1, waiting for transfers between devices, on_device(): others_low = in_hbm(lax.ppermute(low, 'z', across))  16 us
    pallas_call x2, Pallas kernels, segment_rows(): pl.pallas_call(functools.partial(segment_kernel, stripes, start is not No...  7.28 us
    pallas_call x1, Pallas kernels, rest_half(): pl.pallas_call(functools.partial(rest_kernel, *places), in_specs=[VMEM] +...  6.29 us
    pallas_call x1, Pallas kernels, near_grads(): pl.pallas_call(near_kernel, in_specs=[VMEM] * 4 + [HBM] * 5, out_specs=[H...  6.28 us
    pallas_call x1, Pallas kernels, own_half(): pl.pallas_call(functools.partial(own_kernel, place), in_specs=[HBM, HBM,...  4.26 us
  transfers between devices with their start and end apart: 11, of which 7 were waited for; matrix products, arithmetic and copies ran while one was open for 0% of the time, Pallas kernels for 18%

profile of v4, /device:TPU:0, one launch (start us, length us, event | category | flops | bytes accessed | tf_op | source)
XLA Modules:
  0.0 157.2 jit_solution(6021797836096599109)
XLA Ops:
  0.6 1.8 %copy.15 = bf16[16,32,1024]{2,0,1:T(8,128)(2,1)S(1)} copy(bf16[16,32,1024]{2,1,0:T(8,128)(2,1)} %param.7) | data formatting | bytes 2097152 | tf_op args[1]
  2.5 3.1 %collective-permute-start.2 = (bf16[32,16,1024]{2,1,0:T(8,128)(2,1)S(1)}, bf16[32,16,1024]{2,1,0:T(8,128)(2,1)S(1)}, u32[]{:S(2)}, u32[]{:S(2)}) collective-permute-start(bf16[32,16,1024]{2,1,0:T(8,128)(2,1)S(1)} %bitcast.15), channel_id=1, source_target_pairs={{0,2},{2,0},{4,6},{6,4},{1,3},{3,1},{5,7},{7,5},{8,10},{10,8},{12,... | collective-permute-start | bytes 3145736 | tf_op jit(solution)/shard_map/ppermute | solution.py:651
  5.5 2.0 %gather_rows.2 = bf16[8,128,1024]{2,1,0:T(8,128)(2,1)} custom-call(s32[4,32]{1,0:T(4,128)S(1)} %bitcast.17, bf16[32,16,1024]{2,1,0:T(8,128)(2,1)S(1)} %bitcast.16), custom_call_target="tpu_custom_call" | custom-call | bytes 4194304 | tf_op jit(solution)/shard_map/gather_rows/pallas_call | solution.py:110
  7.5 4.4 %all-to-all-start = ((bf16[8,128,1024]{2,1,0:T(8,128)(2,1)}), bf16[8,128,1024]{2,1,0:T(8,128)(2,1)}, u32[]{:S(2)}, u32[]{:S(2)}) async-start(bf16[8,128,1024]{2,1,0:T(8,128)(2,1)} %gather_rows.2), calls=%async_computation | async-start | bytes 4194304 | tf_op jit(solution)/shard_map/all_to_all | solution.py:645
  11.9 2.1 %split_rows.1 = (bf16[128,1024]{1,0:T(8,128)(2,1)}, bf16[384,1024]{1,0:T(8,128)(2,1)}) custom-call(bf16[512,1024]{1,0:T(8,128)(2,1)} %source_ref.1), custom_call_target="tpu_custom_call" | custom-call | bytes 2097152 | tf_op jit(solution)/shard_map/split_rows/pallas_call | solution.py:70
  14.0 2.7 %collective-permute-start = (bf16[128,1024]{1,0:T(8,128)(2,1)}, bf16[128,1024]{1,0:T(8,128)(2,1)S(1)}, u32[]{:S(2)}, u32[]{:S(2)}) collective-permute-start(bf16[128,1024]{1,0:T(8,128)(2,1)} %get-tuple-element.28), channel_id=1, source_target_pairs={{0,4},{2,6},{4,0},{6,2},{1,5},{3,7},{5,1},{7,3},{8,12},{10,14},{12... | collective-permute-start | bytes 786440 | tf_op jit(solution)/shard_map/ppermute | solution.py:653
  16.7 0.3 collective-permute-start.3
  17.7 16.0 %collective-permute-done.refs_1_.low_ref = bf16[128,1024]{1,0:T(8,128)(2,1)S(1)} collective-permute-done((bf16[128,1024]{1,0:T(8,128)(2,1)}, bf16[128,1024]{1,0:T(8,128)(2,1)S(1)}, u32[]{:S(2)}, u32[]{:S(2)}) %collective-permute-start) | collective-permute-done | bytes 262176 | tf_op jit(solution)/shard_map/ppermute | solution.py:653
  33.7 0.7 copy-done.1
  34.4 3.3 %collective-permute-start.1 = (bf16[384,1024]{1,0:T(8,128)(2,1)}, bf16[384,1024]{1,0:T(8,128)(2,1)}, u32[]{:S(2)}, u32[]{:S(2)}) collective-permute-start(bf16[384,1024]{1,0:T(8,128)(2,1)} %after.1), channel_id=1, source_target_pairs={{0,4},{2,6},{4,0},{6,2},{1,5},{3,7},{5,1},{7,3},{8,12},{10,14},{12... | collective-permute-start | bytes 2359304 | tf_op jit(solution)/shard_map/ppermute | solution.py:654
  37.7 2.0 %gather_rows.3 = bf16[8,128,1024]{2,1,0:T(8,128)(2,1)} custom-call(s32[4,32]{1,0:T(4,128)S(1)} %bitcast.18, bf16[32,16,1024]{2,1,0:T(8,128)(2,1)S(1)} %collective-permute-done.2.rows_ref), custom_call_target="tpu_custom_call" | custom-call | flops 137438953472 | bytes 4194304 | tf_op jit(solution)/shard_map/gather_rows/pallas_call | solution.py:110
  39.7 4.4 %all-to-all-start.1 = ((bf16[8,128,1024]{2,1,0:T(8,128)(2,1)}), bf16[8,128,1024]{2,1,0:T(8,128)(2,1)}, u32[]{:S(2)}, u32[]{:S(2)}) async-start(bf16[8,128,1024]{2,1,0:T(8,128)(2,1)} %gather_rows.3), calls=%async_computation.1 | async-start | bytes 4194304 | tf_op jit(solution)/shard_map/all_to_all | solution.py:645
  44.1 4.3 %own_half.1 = (f32[512,512]{1,0:T(8,128)}, f32[8,512]{1,0:T(8,128)S(1)}, bf16[512,1024]{1,0:T(8,128)(2,1)S(1)}) custom-call(bf16[512,1024]{1,0:T(8,128)(2,1)} %source_ref.1, bf16[8,128,1024]{2,1,0:T(8,128)(2,1)} %all-to-all-done.slabs_ref.near_ref, s32[1,512]{1,0:T(1,128)} %bitcast.2.chosen_ref), custom_call_target="tpu_custom_call" | custom-call | flops 137438953472 | bytes 4194304 | tf_op jit(solution)/shard_map/own_half/pallas_call | solution.py:275
  48.4 23.2 %collective-permute-done.1.high_ref = bf16[384,1024]{1,0:T(8,128)(2,1)} collective-permute-done((bf16[384,1024]{1,0:T(8,128)(2,1)}, bf16[384,1024]{1,0:T(8,128)(2,1)}, u32[]{:S(2)}, u32[]{:S(2)}) %collective-permute-start.1) | collective-permute-done | bytes 786464 | tf_op jit(solution)/shard_map/ppermute | solution.py:654
  71.6 6.3 %rest_half.1 = (f32[512,512]{1,0:T(8,128)S(1)}, f32[512,512]{1,0:T(8,128)}, f32[2,512,512]{2,1,0:T(8,128)S(1)}, f32[8,512]{1,0:T(8,128)S(1)}, s32[8,512]{1,0:T(8...) custom-call(bf16[512,1024]{1,0:T(8,128)(2,1)S(1)} %get-tuple-element, ...), custom_call_target="tpu_custom_call" | custom-call | flops 1610612736 | bytes 8388608 | tf_op jit(solution)/shard_map/rest_half/pallas_call | solution.py:346
  77.9 0.6 collective-permute-start.4
  78.5 2.4 %early_grads.1 = (f32[512,1024]{1,0:T(8,128)S(1)}, f32[512,1024]{1,0:T(8,128)S(1)}) custom-call(f32[8,512]{1,0:T(8,128)S(1)} %get-tuple-element.31.stats_ref.here_ref, s32[8,512]{1,0:T(8,128)S(1)} %get-tuple-element.32.near_target_ref.target_ref, s32[8,512]{1,0:T(8,128)S(1)} %get-tuple-element.33.far_target_ref.target_ref, ...), custom_call_target="tpu_custom_call" | custom-call | flops 137438953472 | bytes 4194304 | tf_op jit(solution)/shard_map/early_grads/pallas_call | solution.py:470
  81.0 1.6 %collective-permute-done.4.there_ref = f32[8,512]{1,0:T(8,128)S(1)} collective-permute-done((f32[8,512]{1,0:T(8,128)S(1)}, f32[8,512]{1,0:T(8,128)S(1)}, u32[]{:S(2)}, u32[]{:S(2)}) %collective-permute-start.4) | collective-permute-done | bytes 16416 | tf_op jit(solution)/shard_map/ppermute | solution.py:670
  82.6 2.1 %other_grads.1 = (bf16[512,1024]{1,0:T(8,128)(2,1)}, f32[8,512]{1,0:T(8,128)S(1)}, f32[1,512]{1,0:T(1,128)}) custom-call(f32[8,512]{1,0:T(8,128)S(1)} %get-tuple-element.31.stats_ref.here_ref, f32[8,512]{1,0:T(8,128)S(1)} %collective-permute-done.4.there_ref, s32[8,512]{1,0:T(8,128)S(1)} %get-tuple-element.32.near_target_ref.target_ref, ...), custom_call_target="tpu_custom_call" | custom-call | flops 1048576 | bytes 4194304 | tf_op jit(solution)/shard_map/other_grads/pallas_call | solution.py:508
  84.8 0.8 collective-permute-start.5
  85.6 2.4 %far_grads.1 = (bf16[8,128,1024]{2,1,0:T(8,128)(2,1)}, bf16[512,512]{1,0:T(8,128)(2,1)}) custom-call(bf16[512,1024]{1,0:T(8,128)(2,1)S(1)} %get-tuple-element.27.queries_ref, bf16[512,1024]{1,0:T(8,128)(2,1)S(1)} %get-tuple-element.41.others_ref, f32[2,512,512]{2,1,0:T(8,128)S(1)} %get-tuple-element.35.far_logits_ref.logits_ref, ...), custom_call_target="tpu_custom_call" | custom-call | flops 1073741824 | bytes 4194304 | tf_op jit(solution)/shard_map/far_grads/pallas_call | solution.py:542
  87.9 4.5 %all-to-all-start.2 = ((bf16[8,128,1024]{2,1,0:T(8,128)(2,1)}), bf16[8,128,1024]{2,1,0:T(8,128)(2,1)}, u32[]{:S(2)}, u32[]{:S(2)}) async-start(bf16[8,128,1024]{2,1,0:T(8,128)(2,1)} %get-tuple-element.48), calls=%async_computation.2 | async-start | bytes 4194304 | tf_op jit(solution)/shard_map/all_to_all | solution.py:645
  92.5 6.3 %near_grads.1 = (bf16[8,128,1024]{2,1,0:T(8,128)(2,1)}, f32[512,1024]{1,0:T(8,128)}) custom-call(bf16[512,1024]{1,0:T(8,128)(2,1)S(1)} %get-tuple-element.27.queries_ref, bf16[512,1024]{1,0:T(8,128)(2,1)S(1)} %get-tuple-element.41.others_ref, s32[8,512]{1,0:T(8,128)S(1)} %get-tuple-element.32.near_target_ref.target_ref, ...), custom_call_target="tpu_custom_call" | custom-call | flops 137438953472 | bytes 8388608 | tf_op jit(solution)/shard_map/near_grads/pallas_call | solution.py:586
  98.8 20.2 %all-to-all-done.2.slabs_ref = bf16[8,128,1024]{2,1,0:T(8,128)(2,1)} async-done(((bf16[8,128,1024]{2,1,0:T(8,128)(2,1)}), bf16[8,128,1024]{2,1,0:T(8,128)(2,1)}, u32[]{:S(2)}, u32[]{:S(2)}) %all-to-all-start.2) | async-done | bytes 2097184 | tf_op jit(solution)/shard_map/all_to_all | solution.py:645
  119.0 3.6 %all-to-all-start.3 = ((bf16[8,128,1024]{2,1,0:T(8,128)(2,1)}), bf16[8,128,1024]{2,1,0:T(8,128)(2,1)S(1)}, u32[]{:S(2)}, u32[]{:S(2)}) async-start(bf16[8,128,1024]{2,1,0:T(8,128)(2,1)} %get-tuple-element.49), calls=%async_computation.3 | async-start | bytes 4194304 | tf_op jit(solution)/shard_map/all_to_all | solution.py:645
  122.6 3.5 %segment_rows.2.refs_0_ = bf16[512,1024]{1,0:T(8,128)(2,1)} custom-call(bf16[512,1024]{1,0:T(8,128)(2,1)S(1)} %fusion.spread_ref, bf16[8,128,1024]{2,1,0:T(8,128)(2,1)} %all-to-all-done.2.slabs_ref), custom_call_target="tpu_custom_call" | custom-call | flops 1073741824 | bytes 4194304 | tf_op jit(solution)/shard_map/segment_rows/pallas_call | solution.py:150
  126.1 2.4 %collective-permute-start.6 = (bf16[512,1024]{1,0:T(8,128)(2,1)}, bf16[512,1024]{1,0:T(8,128)(2,1)}, u32[]{:S(2)}, u32[]{:S(2)}) collective-permute-start(bf16[512,1024]{1,0:T(8,128)(2,1)} %segment_rows.2.refs_0_), channel_id=1, source_target_pairs={{0,2},{2,0},{4,6},{6,4},{1,3},{3,1},{5,7},{7,5},{8,10},{10,8},{12,... | collective-permute-start | bytes 3145736 | tf_op jit(solution)/shard_map/ppermute | solution.py:681
  128.5 2.4 %collective-permute-done.5.part_ref = bf16[512,1024]{1,0:T(8,128)(2,1)} collective-permute-done((bf16[512,1024]{1,0:T(8,128)(2,1)}, bf16[512,1024]{1,0:T(8,128)(2,1)}, u32[]{:S(2)}, u32[]{:S(2)}) %collective-permute-start.5) | collective-permute-done | bytes 1048608 | tf_op jit(solution)/shard_map/ppermute | solution.py:679
  130.9 2.8 %add_parts.1.refs_1_ = bf16[512,1024]{1,0:T(8,128)(2,1)} custom-call(f32[512,1024]{1,0:T(8,128)} %get-tuple-element.47.own_ref, bf16[512,1024]{1,0:T(8,128)(2,1)} %collective-permute-done.5.part_ref, bf16[512,1024]{1,0:T(8,128)(2,1)} %segment_rows.2.refs_0_), custom_call_target="tpu_custom_call" | custom-call | flops 137438953472 | bytes 4194304 | tf_op jit(solution)/shard_map/add_parts/pallas_call | solution.py:622
  133.7 15.5 %all-to-all-done.3.slabs_ref = bf16[8,128,1024]{2,1,0:T(8,128)(2,1)S(1)} async-done(((bf16[8,128,1024]{2,1,0:T(8,128)(2,1)}), bf16[8,128,1024]{2,1,0:T(8,128)(2,1)S(1)}, u32[]{:S(2)}, u32[]{:S(2)}) %all-to-all-start.3) | async-done | bytes 2097184 | tf_op jit(solution)/shard_map/all_to_all | solution.py:645
  149.2 4.1 %collective-permute-done.6.refs_0_ = bf16[512,1024]{1,0:T(8,128)(2,1)} collective-permute-done((bf16[512,1024]{1,0:T(8,128)(2,1)}, bf16[512,1024]{1,0:T(8,128)(2,1)}, u32[]{:S(2)}, u32[]{:S(2)}) %collective-permute-start.6) | collective-permute-done | bytes 1048608 | tf_op jit(solution)/shard_map/ppermute | solution.py:681
  153.3 3.8 %segment_rows.3 = bf16[512,1024]{1,0:T(8,128)(2,1)} custom-call(bf16[512,1024]{1,0:T(8,128)(2,1)S(1)} %fusion.spread_ref, bf16[8,128,1024]{2,1,0:T(8,128)(2,1)S(1)} %all-to-all-done.3.slabs_ref, bf16[512,1024]{1,0:T(8,128)(2,1)} %collective-permute-done.6.refs_0_, bf16[512,1024]{1,0:T(8,128)(2,1)} %add_parts.1.refs_1_), custom_call_target="tpu_custom_call" | custom-call | flops 1073741824 | bytes 4194304 | tf_op jit(solution)/shard_map/segment_rows/pallas_call | solution.py:150
  (17 shorter events, 0.7 us)
Async XLA Ops:
  0.6 4.9 %copy-start = (s32[32,4]{0,1:T(4,128)S(1)}, s32[32,4]{0,1:T(4,128)}, u32[]{:S(2)}) copy-start(s32[32,4]{0,1:T(4,128)} %param.8) | copy-start | bytes 1540
  2.5 35.2 %collective-permute-start.2 = (bf16[32,16,1024]{2,1,0:T(8,128)(2,1)S(1)}, bf16[32,16,1024]{2,1,0:T(8,128)(2,1)S(1)}, u32[]{:S(2)}, u32[]{:S(2)}) collective-permute-start(bf16[32,16,1024]{2,1,0:T(8,128)(2,1)S(1)} %bitcast.15), channel_id=1, source_target_pairs={{0,2},{2,0},{4,6},{6,4},{1,3},{3,1},{5,7},{7,5},{8,10},{10,8},{12,... | collective-permute-start | bytes 3145736 | tf_op jit(solution)/shard_map/ppermute | solution.py:651
  7.5 32.2 %all-to-all-start = ((bf16[8,128,1024]{2,1,0:T(8,128)(2,1)}), bf16[8,128,1024]{2,1,0:T(8,128)(2,1)}, u32[]{:S(2)}, u32[]{:S(2)}) async-start(bf16[8,128,1024]{2,1,0:T(8,128)(2,1)} %gather_rows.2), calls=%async_computation | async-start | bytes 4194304 | tf_op jit(solution)/shard_map/all_to_all | solution.py:645
  14.0 19.7 %collective-permute-start = (bf16[128,1024]{1,0:T(8,128)(2,1)}, bf16[128,1024]{1,0:T(8,128)(2,1)S(1)}, u32[]{:S(2)}, u32[]{:S(2)}) collective-permute-start(bf16[128,1024]{1,0:T(8,128)(2,1)} %get-tuple-element.28), channel_id=1, source_target_pairs={{0,4},{2,6},{4,0},{6,2},{1,5},{3,7},{5,1},{7,3},{8,12},{10,14},{12... | collective-permute-start | bytes 786440 | tf_op jit(solution)/shard_map/ppermute | solution.py:653
  16.7 31.6 %collective-permute-start.3 = (s32[512]{0:T(512)}, s32[512]{0:T(512)}, u32[]{:S(2)}, u32[]{:S(2)}) collective-permute-start(s32[512]{0:T(512)} %param.9), channel_id=1, source_target_pairs={{0,4},{2,6},{4,0},{6,2},{1,5},{3,7},{5,1},{7,3},{8,12},{10,14},{12... | collective-permute-start | bytes 6152 | tf_op jit(solution)/shard_map/ppermute | solution.py:655
  33.7 0.7 copy-start.1
  34.4 37.2 %collective-permute-start.1 = (bf16[384,1024]{1,0:T(8,128)(2,1)}, bf16[384,1024]{1,0:T(8,128)(2,1)}, u32[]{:S(2)}, u32[]{:S(2)}) collective-permute-start(bf16[384,1024]{1,0:T(8,128)(2,1)} %after.1), channel_id=1, source_target_pairs={{0,4},{2,6},{4,0},{6,2},{1,5},{3,7},{5,1},{7,3},{8,12},{10,14},{12... | collective-permute-start | bytes 2359304 | tf_op jit(solution)/shard_map/ppermute | solution.py:654
  39.7 31.9 %all-to-all-start.1 = ((bf16[8,128,1024]{2,1,0:T(8,128)(2,1)}), bf16[8,128,1024]{2,1,0:T(8,128)(2,1)}, u32[]{:S(2)}, u32[]{:S(2)}) async-start(bf16[8,128,1024]{2,1,0:T(8,128)(2,1)} %gather_rows.3), calls=%async_computation.1 | async-start | bytes 4194304 | tf_op jit(solution)/shard_map/all_to_all | solution.py:645
  77.9 4.7 %collective-permute-start.4 = (f32[8,512]{1,0:T(8,128)S(1)}, f32[8,512]{1,0:T(8,128)S(1)}, u32[]{:S(2)}, u32[]{:S(2)}) collective-permute-start(f32[8,512]{1,0:T(8,128)S(1)} %get-tuple-element.31.stats_ref.here_ref), channel_id=1, source_target_pairs={{0,4},{2,6},{4,0},{6,2},{1,5},{3,7},{5,1},{7,3},{8,12},{10,14},{12... | collective-permute-start | bytes 49160 | tf_op jit(solution)/shard_map/ppermute | solution.py:670
  84.8 46.1 %collective-permute-start.5 = (bf16[512,1024]{1,0:T(8,128)(2,1)}, bf16[512,1024]{1,0:T(8,128)(2,1)}, u32[]{:S(2)}, u32[]{:S(2)}) collective-permute-start(bf16[512,1024]{1,0:T(8,128)(2,1)} %get-tuple-element.45.wait_ref), channel_id=1, source_target_pairs={{0,4},{2,6},{4,0},{6,2},{1,5},{3,7},{5,1},{7,3},{8,12},{10,14},{12... | collective-permute-start | bytes 3145736 | tf_op jit(solution)/shard_map/ppermute | solution.py:679
  87.9 31.0 %all-to-all-start.2 = ((bf16[8,128,1024]{2,1,0:T(8,128)(2,1)}), bf16[8,128,1024]{2,1,0:T(8,128)(2,1)}, u32[]{:S(2)}, u32[]{:S(2)}) async-start(bf16[8,128,1024]{2,1,0:T(8,128)(2,1)} %get-tuple-element.48), calls=%async_computation.2 | async-start | bytes 4194304 | tf_op jit(solution)/shard_map/all_to_all | solution.py:645
  119.0 30.2 %all-to-all-start.3 = ((bf16[8,128,1024]{2,1,0:T(8,128)(2,1)}), bf16[8,128,1024]{2,1,0:T(8,128)(2,1)S(1)}, u32[]{:S(2)}, u32[]{:S(2)}) async-start(bf16[8,128,1024]{2,1,0:T(8,128)(2,1)} %get-tuple-element.49), calls=%async_computation.3 | async-start | bytes 4194304 | tf_op jit(solution)/shard_map/all_to_all | solution.py:645
  126.1 27.2 %collective-permute-start.6 = (bf16[512,1024]{1,0:T(8,128)(2,1)}, bf16[512,1024]{1,0:T(8,128)(2,1)}, u32[]{:S(2)}, u32[]{:S(2)}) collective-permute-start(bf16[512,1024]{1,0:T(8,128)(2,1)} %segment_rows.2.refs_0_), channel_id=1, source_target_pairs={{0,2},{2,0},{4,6},{6,4},{1,3},{3,1},{5,7},{7,5},{8,10},{10,8},{12,... | collective-permute-start | bytes 3145736 | tf_op jit(solution)/shard_map/ppermute | solution.py:681

commit v5 on v4

--- a/solution.py
+++ b/solution.py
@@ -10,7 +10,7 @@
 
 SCALE = 0.8
 PLANES = 4
-CHUNKS = 2
+CHUNKS = 1
 EARLY = 4
 BF16 = jnp.bfloat16
 F32 = jnp.float32
@@ -119,48 +119,77 @@
     )(ids, rows)
 
 
-def segment_kernel(stripes, with_start, spread_ref, slabs_ref, *refs):
-    out_ref, held, result, begun, arrived, came, left = refs[-7:]
+def select_kernel(spread_ref, rows_ref, out_ref, made, left):
+    slabs, depth, width = out_ref.shape
+    part = slabs // 2
+    stores = []
+    for c in range(2):
+        some = slice(c * part, (c + 1) * part)
+        lanes = slice(c * part * depth, (c + 1) * part * depth)
+        product = lax.dot_general(
+            spread_ref[:, lanes], rows_ref[...], (((0,), (0,)), ((), ())), preferred_element_type=F32
+        )
+        made[some] = product.astype(BF16).reshape(part, depth, width)
+        some = pl.ds(c * part, part)
+        stores.append(load(made.at[some], out_ref.at[some], left.at[c]))
+    for store in stores:
+        store.wait()
+
+
+def select_rows(spread, rows, slabs):
+    dims = (slabs, spread.shape[1] // slabs, rows.shape[1])
+    return pl.pallas_call(
+        select_kernel,
+        in_specs=[VMEM, VMEM],
+        out_specs=HBM,
+        out_shape=pltpu.HBM(dims, BF16),
+        scratch_shapes=[pltpu.VMEM(dims, BF16), pltpu.SemaphoreType.DMA((2,))],
+        compiler_params=params(),
+        name="select_rows",
+        cost_estimate=cost(BUSY, 4),
+    )(spread, rows)
+
+
+def segment_kernel(stripes, spread_ref, slabs_ref, *refs):
+    out_ref, held, result, arrived, left = refs[-5:]
     slabs, depth, width = slabs_ref.shape
     tile = width // stripes
     columns = [pl.ds(t * tile, tile) for t in range(stripes)]
     loads = [load(slabs_ref.at[:, :, columns[t]], held.at[t], arrived.at[t]) for t in range(stripes)]
-    if with_start:
-        starts = [load(refs[0].at[:, columns[t]], begun.at[t], came.at[t]) for t in range(stripes)]
     stores = []
     for t in range(stripes):
         loads[t].wait()
         total = jnp.dot(spread_ref[...], held[t].reshape(slabs * depth, tile), preferred_element_type=F32)
-        if with_start:
-            starts[t].wait()
-            total += begun[t].astype(F32)
-        result[t] = total.astype(BF16)
-        stores.append(load(result.at[t], out_ref.at[:, columns[t]], left.at[t]))
+        if out_ref.dtype == F32:
+            out_ref[:, t * tile : (t + 1) * tile] = total
+        else:
+            result[t] = total.astype(BF16)
+            stores.append(load(result.at[t], out_ref.at[:, columns[t]], left.at[t]))
     for store in stores:
         store.wait()
 
 
-def segment_rows(spread, slabs, start=None, wait=None):
+def segment_rows(spread, slabs, wait=None):
     stripes = 2
     rows = spread.shape[0]
     count, depth, width = slabs.shape
     tile = width // stripes
-    extra = [array for array in (start, wait) if array is not None]
+    extra = [] if wait is None else [wait]
     sems = pltpu.SemaphoreType.DMA((stripes,))
     return pl.pallas_call(
-        functools.partial(segment_kernel, stripes, start is not None),
+        functools.partial(segment_kernel, stripes),
         in_specs=[VMEM, ANY] + [ANY] * len(extra),
-        out_specs=HBM,
-        out_shape=pltpu.HBM((rows, width), BF16),
+        out_specs=VMEM if extra else HBM,
+        out_shape=shape((rows, width), F32) if extra else pltpu.HBM((rows, width), BF16),
         scratch_shapes=[
             pltpu.VMEM((stripes, count, depth, tile), BF16),
             pltpu.VMEM((stripes, rows, tile), BF16),
-            pltpu.VMEM((stripes, rows, tile), BF16),
-        ]
-        + [sems] * 3,
+            sems,
+            sems,
+        ],
         compiler_params=params(),
         name="segment_rows",
-        cost_estimate=cost(1 << 30, 4),
+        cost_estimate=cost(BUSY if extra else 1 << 30, 4),
     )(spread, slabs, *extra)
 
 
@@ -601,35 +630,40 @@
 
 def add_kernel(own_ref, part_ref, *refs):
     out_ref, own, part, made, own_in, part_in, left = refs[-7:]
-    pieces = [part_of(own.shape[0], c) for c in range(CHUNKS)]
-    loads = [
-        (load(own_ref.at[p], own.at[p], own_in.at[c]), load(part_ref.at[p], part.at[p], part_in.at[c]))
-        for c, p in enumerate(pieces)
-    ]
+    pieces = [pl.ds(i * (part.shape[0] // 4), part.shape[0] // 4) for i in range(4)]
+    halves = [load(part_ref.at[p], part.at[p], part_in.at[i]) for i, p in enumerate(pieces)]
+    if own.shape == part.shape:
+        sums = [load(own_ref.at[p], own.at[p], own_in.at[i]) for i, p in enumerate(pieces)]
+        own_ref = own
     stores = []
-    for c, p in enumerate(pieces):
-        for copy in loads[c]:
-            copy.wait()
-        rows = row_chunk(own.shape[0], c)
-        made[rows, :] = (own[rows, :] + part[rows, :].astype(F32)).astype(BF16)
-        stores.append(load(made.at[p], out_ref.at[p], left.at[c]))
+    for i, p in enumerate(pieces):
+        halves[i].wait()
+        if own_ref is own:
+            sums[i].wait()
+        rows = slice(p.start, p.start + p.size)
+        made[rows, :] = (own_ref[rows, :] + part[rows, :].astype(F32)).astype(BF16)
+        stores.append(load(made.at[p], out_ref.at[p], left.at[i]))
     for store in stores:
         store.wait()
 
 
 def add_parts(own, part, hint, *waits):
-    chunk_sems = pltpu.SemaphoreType.DMA((CHUNKS,))
+    sems = pltpu.SemaphoreType.DMA((4,))
     return pl.pallas_call(
         add_kernel,
-        in_specs=[HBM] * 2 + [ANY] * len(waits),
+        in_specs=[HBM if waits else VMEM, ANY] + [ANY] * len(waits),
         out_specs=HBM,
         out_shape=pltpu.HBM(own.shape, BF16),
-        scratch_shapes=[pltpu.VMEM(own.shape, F32), pltpu.VMEM(own.shape, BF16), pltpu.VMEM(own.shape, BF16)]
-        + [chunk_sems] * 3,
+        scratch_shapes=[
+            pltpu.VMEM(own.shape if waits else (8, 128), F32),
+            pltpu.VMEM(own.shape, BF16),
+            pltpu.VMEM(own.shape, BF16),
+        ]
+        + [sems] * 3,
         compiler_params=params(),
         name="add_parts",
         cost_estimate=cost(hint, 4),
-    )(in_hbm(own), in_hbm(part), *waits)
+    )(in_hbm(own) if waits else own, part, *waits)
 
 
 def on_device(queries, passages, block_ids, positives):
@@ -648,17 +682,17 @@
     early = queries.shape[0] // EARLY
     own_rows = jnp.transpose(passages, (1, 0, 2))
     near_slabs = in_hbm(exchange(gather_rows(ids, own_rows, slabs, planes, ranks, 0)))
-    pair_rows = lax.ppermute(own_rows, "z", to_pair)
+    pair_rows = lax.ppermute(passages.reshape(height * blocks, width), "z", to_pair)
     low, high = split_rows(in_hbm(queries), early)
     others_low = in_hbm(lax.ppermute(low, "z", across))
     others_high = lax.ppermute(after(high, others_low), "z", across)
     others_positives = lax.ppermute(positives, "z", across)
-    far_slabs = in_hbm(exchange(gather_rows(ids, pair_rows, slabs, planes, ranks, BUSY)))
 
     table = block_ids.reshape(groups, planes, ranks, refs)
     both = jnp.stack([jnp.take(table, z, axis=1), jnp.take(table, (z + planes // 2) % planes, axis=1)], axis=2)
     place = (jnp.arange(height, dtype=jnp.int32) * blocks + both.reshape(-1, 1)).reshape(1, -1)
     spread = (jnp.arange(height * blocks, dtype=jnp.int32)[:, None] == place).astype(BF16)
+    far_slabs = in_hbm(exchange(select_rows(spread, pair_rows, slabs)))
 
     chosen = positives.reshape(1, -1)
     chosen_others = others_positives.reshape(1, -1)
@@ -681,7 +715,8 @@
     pair_sum = lax.ppermute(far_sum, "z", to_pair)
     near_back = exchange(near_contrib)
     query_grad = add_parts(own_grad, own_part, BUSY, in_hbm(far_sum))
-    row_sum = segment_rows(spread, near_back, pair_sum, in_hbm(query_grad))
+    near_sum = segment_rows(spread, near_back, in_hbm(query_grad))
+    row_sum = add_parts(near_sum, pair_sum, 1 << 20)
     return loss.reshape(-1), query_grad, row_sum.reshape(passages.shape)
 
 

time: 158 us -> 154 us (0.975)
  waiting for transfers between devices: 83.1 us -> 78.2 us
  starting transfers between devices: 30 us -> 32 us
    ppermute x1, waiting for transfers between devices: 4.13 us -> 1.05 us  [on_device(): pair_sum = lax.ppermute(far_sum, 'z', to_pair)]
    all_to_all x4, waiting for transfers between devices: 35.7 us -> 38.2 us  [exchange(): lax.all_to_all(slab_array, PLANE, split_axis=0, concat_axis=0, tiled=True)]
    pallas_call x3 -> x5, Pallas kernels: 10 us -> 12.2 us  [the longest x2 5.2 us: segment_rows(): pl.pallas_call(functools.partial(segment_kernel, stripes), in_specs=[VMEM...]
    pallas_call x2 -> x1, Pallas kernels: 4 us -> 1.98 us  [gather_rows(): pl.pallas_call(functools.partial(gather_kernel, planes, ranks), in_specs=...]
    ppermute x1, starting transfers between devices: 0.63 us -> 2.37 us  [on_device(): partner = lax.ppermute(stats, 'z', across)]
    ppermute x1, waiting for transfers between devices: 1.64 us -> 0.01 us  [on_device(): partner = lax.ppermute(stats, 'z', across)]
    ppermute x1, waiting for transfers between devices: 16 us -> 14.3 us  [on_device(): others_low = in_hbm(lax.ppermute(low, 'z', across))]
  transfers between devices with their start and end apart: 11 -> 11, of which waited for: 7 -> 7; matrix products, arithmetic and copies ran while one was open for 0% -> 2% of each run, Pallas kernels for 18% -> 19%
where the time goes in v5:
time: 154 us
  waiting for transfers between devices  78.2 us (51%)
  Pallas kernels  39.3 us (26%)
  starting transfers between devices  32 us (21%)
  local copies, waits for them, and re-layouts  2.8 us (2%)
    all_to_all x4, waiting for transfers between devices, exchange(): lax.all_to_all(slab_array, PLANE, split_axis=0, concat_axis=0, tiled=True)  38.2 us
    ppermute x1, waiting for transfers between devices, on_device(): others_high = lax.ppermute(after(high, others_low), 'z', across)  22.8 us
    all_to_all x4, starting transfers between devices, exchange(): lax.all_to_all(slab_array, PLANE, split_axis=0, concat_axis=0, tiled=True)  17 us
    ppermute x1, waiting for transfers between devices, on_device(): others_low = in_hbm(lax.ppermute(low, 'z', across))  14.3 us
    pallas_call x1, Pallas kernels, near_grads(): pl.pallas_call(near_kernel, in_specs=[VMEM] * 4 + [HBM] * 5, out_specs=[H...  6.17 us
    pallas_call x1, Pallas kernels, rest_half(): pl.pallas_call(functools.partial(rest_kernel, *places), in_specs=[VMEM] +...  5.48 us
    pallas_call x2, Pallas kernels, segment_rows(): pl.pallas_call(functools.partial(segment_kernel, stripes), in_specs=[VMEM...  5.2 us
    pallas_call x2, Pallas kernels, add_parts(): pl.pallas_call(add_kernel, in_specs=[HBM if waits else VMEM, ANY] + [ANY]...  4.74 us
  transfers between devices with their start and end apart: 11, of which 7 were waited for; matrix products, arithmetic and copies ran while one was open for 2% of the time, Pallas kernels for 19%

profile of v5, /device:TPU:0, one launch (start us, length us, event | category | flops | bytes accessed | tf_op | source)
XLA Modules:
  0.0 153.7 jit_solution(1228474517626445125)
XLA Ops:
  0.6 3.1 %collective-permute-start.2 = (bf16[512,1024]{1,0:T(8,128)(2,1)}, bf16[512,1024]{1,0:T(8,128)(2,1)S(1)}, u32[]{:S(2)}, u32[]{:S(2)}) collective-permute-start(bf16[512,1024]{1,0:T(8,128)(2,1)} %bitcast.18), channel_id=1, source_target_pairs={{0,2},{2,0},{4,6},{6,4},{1,3},{3,1},{5,7},{7,5},{8,10},{10,8},{12,... | collective-permute-start | bytes 3145736 | tf_op jit(solution)/shard_map/ppermute | solution.py:685
  3.7 1.8 %copy.15 = bf16[16,32,1024]{2,0,1:T(8,128)(2,1)S(1)} copy(bf16[16,32,1024]{2,1,0:T(8,128)(2,1)} %param.7) | data formatting | bytes 2097152 | tf_op args[1]
  5.6 2.0 %gather_rows.1 = bf16[8,128,1024]{2,1,0:T(8,128)(2,1)} custom-call(s32[4,32]{1,0:T(4,128)S(1)} %bitcast.17, bf16[32,16,1024]{2,1,0:T(8,128)(2,1)S(1)} %bitcast.16), custom_call_target="tpu_custom_call" | custom-call | bytes 4194304 | tf_op jit(solution)/shard_map/gather_rows/pallas_call | solution.py:110
  7.6 4.4 %all-to-all-start = ((bf16[8,128,1024]{2,1,0:T(8,128)(2,1)}), bf16[8,128,1024]{2,1,0:T(8,128)(2,1)}, u32[]{:S(2)}, u32[]{:S(2)}) async-start(bf16[8,128,1024]{2,1,0:T(8,128)(2,1)} %gather_rows.1), calls=%async_computation | async-start | bytes 4194304 | tf_op jit(solution)/shard_map/all_to_all | solution.py:679
  11.9 2.1 %split_rows.1 = (bf16[128,1024]{1,0:T(8,128)(2,1)}, bf16[384,1024]{1,0:T(8,128)(2,1)}) custom-call(bf16[512,1024]{1,0:T(8,128)(2,1)} %source_ref.1), custom_call_target="tpu_custom_call" | custom-call | bytes 2097152 | tf_op jit(solution)/shard_map/split_rows/pallas_call | solution.py:70
  14.1 2.7 %collective-permute-start = (bf16[128,1024]{1,0:T(8,128)(2,1)}, bf16[128,1024]{1,0:T(8,128)(2,1)S(1)}, u32[]{:S(2)}, u32[]{:S(2)}) collective-permute-start(bf16[128,1024]{1,0:T(8,128)(2,1)} %get-tuple-element.28), channel_id=1, source_target_pairs={{0,4},{2,6},{4,0},{6,2},{1,5},{3,7},{5,1},{7,3},{8,12},{10,14},{12... | collective-permute-start | bytes 786440 | tf_op jit(solution)/shard_map/ppermute | solution.py:687
  16.7 0.3 collective-permute-start.3
  17.8 14.3 %collective-permute-done.refs_1_.low_ref = bf16[128,1024]{1,0:T(8,128)(2,1)S(1)} collective-permute-done((bf16[128,1024]{1,0:T(8,128)(2,1)}, bf16[128,1024]{1,0:T(8,128)(2,1)S(1)}, u32[]{:S(2)}, u32[]{:S(2)}) %collective-permute-start) | collective-permute-done | bytes 262176 | tf_op jit(solution)/shard_map/ppermute | solution.py:687
  32.1 0.7 copy-done.3
  32.8 3.3 %collective-permute-start.1 = (bf16[384,1024]{1,0:T(8,128)(2,1)}, bf16[384,1024]{1,0:T(8,128)(2,1)}, u32[]{:S(2)}, u32[]{:S(2)}) collective-permute-start(bf16[384,1024]{1,0:T(8,128)(2,1)} %after.1), channel_id=1, source_target_pairs={{0,4},{2,6},{4,0},{6,2},{1,5},{3,7},{5,1},{7,3},{8,12},{10,14},{12... | collective-permute-start | bytes 2359304 | tf_op jit(solution)/shard_map/ppermute | solution.py:688
  36.1 2.3 %select_rows.1 = bf16[8,128,1024]{2,1,0:T(8,128)(2,1)} custom-call(bf16[512,1024]{1,0:T(8,128)(2,1)S(1)} %fusion.spread_ref, bf16[512,1024]{1,0:T(8,128)(2,1)S(1)} %collective-permute-done.2.rows_ref), custom_call_target="tpu_custom_call" | custom-call | flops 137438953472 | bytes 4194304 | tf_op jit(solution)/shard_map/select_rows/pallas_call | solution.py:141
  38.6 4.4 %all-to-all-start.1 = ((bf16[8,128,1024]{2,1,0:T(8,128)(2,1)}), bf16[8,128,1024]{2,1,0:T(8,128)(2,1)}, u32[]{:S(2)}, u32[]{:S(2)}) async-start(bf16[8,128,1024]{2,1,0:T(8,128)(2,1)} %select_rows.1), calls=%async_computation.1 | async-start | bytes 4194304 | tf_op jit(solution)/shard_map/all_to_all | solution.py:679
  42.9 4.1 %own_half.1 = (f32[512,512]{1,0:T(8,128)}, f32[8,512]{1,0:T(8,128)S(1)}, bf16[512,1024]{1,0:T(8,128)(2,1)S(1)}) custom-call(bf16[512,1024]{1,0:T(8,128)(2,1)} %source_ref.1, bf16[8,128,1024]{2,1,0:T(8,128)(2,1)} %all-to-all-done.slabs_ref.near_ref, s32[1,512]{1,0:T(1,128)} %bitcast.2.chosen_ref), custom_call_target="tpu_custom_call" | custom-call | flops 137438953472 | bytes 4194304 | tf_op jit(solution)/shard_map/own_half/pallas_call | solution.py:304
  47.1 22.8 %collective-permute-done.1.high_ref = bf16[384,1024]{1,0:T(8,128)(2,1)} collective-permute-done((bf16[384,1024]{1,0:T(8,128)(2,1)}, bf16[384,1024]{1,0:T(8,128)(2,1)}, u32[]{:S(2)}, u32[]{:S(2)}) %collective-permute-start.1) | collective-permute-done | bytes 786464 | tf_op jit(solution)/shard_map/ppermute | solution.py:688
  69.9 5.5 %rest_half.1 = (f32[512,512]{1,0:T(8,128)S(1)}, f32[512,512]{1,0:T(8,128)}, f32[2,512,512]{2,1,0:T(8,128)S(1)}, f32[8,512]{1,0:T(8,128)S(1)}, s32[8,512]{1,0:T(8...) custom-call(bf16[512,1024]{1,0:T(8,128)(2,1)S(1)} %get-tuple-element, ...), custom_call_target="tpu_custom_call" | custom-call | flops 1610612736 | bytes 8388608 | tf_op jit(solution)/shard_map/rest_half/pallas_call | solution.py:375
  75.4 2.4 %collective-permute-start.4 = (f32[8,512]{1,0:T(8,128)S(1)}, f32[8,512]{1,0:T(8,128)S(1)}, u32[]{:S(2)}, u32[]{:S(2)}) collective-permute-start(f32[8,512]{1,0:T(8,128)S(1)} %get-tuple-element.31.stats_ref.here_ref), channel_id=1, source_target_pairs={{0,4},{2,6},{4,0},{6,2},{1,5},{3,7},{5,1},{7,3},{8,12},{10,14},{12... | collective-permute-start | bytes 49160 | tf_op jit(solution)/shard_map/ppermute | solution.py:704
  77.7 2.4 %early_grads.1 = (f32[512,1024]{1,0:T(8,128)S(1)}, f32[512,1024]{1,0:T(8,128)S(1)}) custom-call(f32[8,512]{1,0:T(8,128)S(1)} %get-tuple-element.31.stats_ref.here_ref, s32[8,512]{1,0:T(8,128)S(1)} %get-tuple-element.32.near_target_ref.target_ref, s32[8,512]{1,0:T(8,128)S(1)} %get-tuple-element.33.far_target_ref.target_ref, ...), custom_call_target="tpu_custom_call" | custom-call | flops 137438953472 | bytes 4194304 | tf_op jit(solution)/shard_map/early_grads/pallas_call | solution.py:499
  80.1 2.2 %other_grads.1 = (bf16[512,1024]{1,0:T(8,128)(2,1)}, f32[8,512]{1,0:T(8,128)S(1)}, f32[1,512]{1,0:T(1,128)}) custom-call(f32[8,512]{1,0:T(8,128)S(1)} %get-tuple-element.31.stats_ref.here_ref, f32[8,512]{1,0:T(8,128)S(1)} %collective-permute-done.4.there_ref, s32[8,512]{1,0:T(8,128)S(1)} %get-tuple-element.32.near_target_ref.target_ref, ...), custom_call_target="tpu_custom_call" | custom-call | flops 1048576 | bytes 4194304 | tf_op jit(solution)/shard_map/other_grads/pallas_call | solution.py:537
  82.3 2.3 %collective-permute-start.5 = (bf16[512,1024]{1,0:T(8,128)(2,1)}, bf16[512,1024]{1,0:T(8,128)(2,1)}, u32[]{:S(2)}, u32[]{:S(2)}) collective-permute-start(bf16[512,1024]{1,0:T(8,128)(2,1)} %get-tuple-element.45.wait_ref), channel_id=1, source_target_pairs={{0,4},{2,6},{4,0},{6,2},{1,5},{3,7},{5,1},{7,3},{8,12},{10,14},{12... | collective-permute-start | bytes 3145736 | tf_op jit(solution)/shard_map/ppermute | solution.py:713
  84.6 2.7 %far_grads.1 = (bf16[8,128,1024]{2,1,0:T(8,128)(2,1)}, bf16[512,512]{1,0:T(8,128)(2,1)}) custom-call(bf16[512,1024]{1,0:T(8,128)(2,1)S(1)} %get-tuple-element.27.queries_ref, bf16[512,1024]{1,0:T(8,128)(2,1)S(1)} %get-tuple-element.41.others_ref, f32[2,512,512]{2,1,0:T(8,128)S(1)} %get-tuple-element.35.far_logits_ref.logits_ref, ...), custom_call_target="tpu_custom_call" | custom-call | flops 1073741824 | bytes 4194304 | tf_op jit(solution)/shard_map/far_grads/pallas_call | solution.py:571
  87.3 4.5 %all-to-all-start.2 = ((bf16[8,128,1024]{2,1,0:T(8,128)(2,1)}), bf16[8,128,1024]{2,1,0:T(8,128)(2,1)}, u32[]{:S(2)}, u32[]{:S(2)}) async-start(bf16[8,128,1024]{2,1,0:T(8,128)(2,1)} %get-tuple-element.48), calls=%async_computation.2 | async-start | bytes 4194304 | tf_op jit(solution)/shard_map/all_to_all | solution.py:679
  91.8 6.2 %near_grads.1 = (bf16[8,128,1024]{2,1,0:T(8,128)(2,1)}, f32[512,1024]{1,0:T(8,128)}) custom-call(bf16[512,1024]{1,0:T(8,128)(2,1)S(1)} %get-tuple-element.27.queries_ref, bf16[512,1024]{1,0:T(8,128)(2,1)S(1)} %get-tuple-element.41.others_ref, s32[8,512]{1,0:T(8,128)S(1)} %get-tuple-element.32.near_target_ref.target_ref, ...), custom_call_target="tpu_custom_call" | custom-call | flops 137438953472 | bytes 8388608 | tf_op jit(solution)/shard_map/near_grads/pallas_call | solution.py:615
  98.0 20.3 %all-to-all-done.2.slabs_ref = bf16[8,128,1024]{2,1,0:T(8,128)(2,1)} async-done(((bf16[8,128,1024]{2,1,0:T(8,128)(2,1)}), bf16[8,128,1024]{2,1,0:T(8,128)(2,1)}, u32[]{:S(2)}, u32[]{:S(2)}) %all-to-all-start.2) | async-done | bytes 2097184 | tf_op jit(solution)/shard_map/all_to_all | solution.py:679
  118.3 3.7 %all-to-all-start.3 = ((bf16[8,128,1024]{2,1,0:T(8,128)(2,1)}), bf16[8,128,1024]{2,1,0:T(8,128)(2,1)S(1)}, u32[]{:S(2)}, u32[]{:S(2)}) async-start(bf16[8,128,1024]{2,1,0:T(8,128)(2,1)} %get-tuple-element.49), calls=%async_computation.3 | async-start | bytes 4194304 | tf_op jit(solution)/shard_map/all_to_all | solution.py:679
  122.1 3.5 %segment_rows.2.refs_0_ = bf16[512,1024]{1,0:T(8,128)(2,1)} custom-call(bf16[512,1024]{1,0:T(8,128)(2,1)S(1)} %copy-done.1, bf16[8,128,1024]{2,1,0:T(8,128)(2,1)} %all-to-all-done.2.slabs_ref), custom_call_target="tpu_custom_call" | custom-call | flops 1073741824 | bytes 4194304 | tf_op jit(solution)/shard_map/segment_rows/pallas_call | solution.py:179
  125.6 0.9 collective-permute-start.6
  126.5 1.7 %collective-permute-done.5.part_ref = bf16[512,1024]{1,0:T(8,128)(2,1)} collective-permute-done((bf16[512,1024]{1,0:T(8,128)(2,1)}, bf16[512,1024]{1,0:T(8,128)(2,1)}, u32[]{:S(2)}, u32[]{:S(2)}) %collective-permute-start.5) | collective-permute-done | bytes 1048608 | tf_op jit(solution)/shard_map/ppermute | solution.py:713
  128.2 2.7 %add_parts.2.refs_0_ = bf16[512,1024]{1,0:T(8,128)(2,1)} custom-call(f32[512,1024]{1,0:T(8,128)} %get-tuple-element.47.own_ref, bf16[512,1024]{1,0:T(8,128)(2,1)} %collective-permute-done.5.part_ref, bf16[512,1024]{1,0:T(8,128)(2,1)} %segment_rows.2.refs_0_), custom_call_target="tpu_custom_call" | custom-call | flops 137438953472 | bytes 4194304 | tf_op jit(solution)/shard_map/add_parts/pallas_call | solution.py:652
  130.9 17.7 %all-to-all-done.3.slabs_ref = bf16[8,128,1024]{2,1,0:T(8,128)(2,1)S(1)} async-done(((bf16[8,128,1024]{2,1,0:T(8,128)(2,1)}), bf16[8,128,1024]{2,1,0:T(8,128)(2,1)S(1)}, u32[]{:S(2)}, u32[]{:S(2)}) %all-to-all-start.3) | async-done | bytes 2097184 | tf_op jit(solution)/shard_map/all_to_all | solution.py:679
  148.6 1.7 %segment_rows.3.own_ref = f32[512,1024]{1,0:T(8,128)S(1)} custom-call(bf16[512,1024]{1,0:T(8,128)(2,1)S(1)} %copy-done.1, bf16[8,128,1024]{2,1,0:T(8,128)(2,1)S(1)} %all-to-all-done.3.slabs_ref, bf16[512,1024]{1,0:T(8,128)(2,1)} %add_parts.2.refs_0_), custom_call_target="tpu_custom_call" | custom-call | flops 137438953472 | bytes 4194304 | tf_op jit(solution)/shard_map/segment_rows/pallas_call | solution.py:179
  150.4 1.1 collective-permute-done.6.part_ref
  151.4 2.1 %add_parts.3 = bf16[512,1024]{1,0:T(8,128)(2,1)} custom-call(f32[512,1024]{1,0:T(8,128)S(1)} %segment_rows.3.own_ref, bf16[512,1024]{1,0:T(8,128)(2,1)} %collective-permute-done.6.part_ref), custom_call_target="tpu_custom_call" | custom-call | flops 1048576 | bytes 4194304 | tf_op jit(solution)/shard_map/add_parts/pallas_call | solution.py:652
  (22 shorter events, 0.9 us)
Async XLA Ops:
  0.6 4.9 %copy-start.2 = (s32[32,4]{0,1:T(4,128)S(1)}, s32[32,4]{0,1:T(4,128)}, u32[]{:S(2)}) copy-start(s32[32,4]{0,1:T(4,128)} %param.8) | copy-start | bytes 1540
  0.6 35.4 %collective-permute-start.2 = (bf16[512,1024]{1,0:T(8,128)(2,1)}, bf16[512,1024]{1,0:T(8,128)(2,1)S(1)}, u32[]{:S(2)}, u32[]{:S(2)}) collective-permute-start(bf16[512,1024]{1,0:T(8,128)(2,1)} %bitcast.18), channel_id=1, source_target_pairs={{0,2},{2,0},{4,6},{6,4},{1,3},{3,1},{5,7},{7,5},{8,10},{10,8},{12,... | collective-permute-start | bytes 3145736 | tf_op jit(solution)/shard_map/ppermute | solution.py:685
  7.6 31.0 %all-to-all-start = ((bf16[8,128,1024]{2,1,0:T(8,128)(2,1)}), bf16[8,128,1024]{2,1,0:T(8,128)(2,1)}, u32[]{:S(2)}, u32[]{:S(2)}) async-start(bf16[8,128,1024]{2,1,0:T(8,128)(2,1)} %gather_rows.1), calls=%async_computation | async-start | bytes 4194304 | tf_op jit(solution)/shard_map/all_to_all | solution.py:679
  14.1 18.0 %collective-permute-start = (bf16[128,1024]{1,0:T(8,128)(2,1)}, bf16[128,1024]{1,0:T(8,128)(2,1)S(1)}, u32[]{:S(2)}, u32[]{:S(2)}) collective-permute-start(bf16[128,1024]{1,0:T(8,128)(2,1)} %get-tuple-element.28), channel_id=1, source_target_pairs={{0,4},{2,6},{4,0},{6,2},{1,5},{3,7},{5,1},{7,3},{8,12},{10,14},{12... | collective-permute-start | bytes 786440 | tf_op jit(solution)/shard_map/ppermute | solution.py:687
  16.7 30.3 %collective-permute-start.3 = (s32[512]{0:T(512)}, s32[512]{0:T(512)}, u32[]{:S(2)}, u32[]{:S(2)}) collective-permute-start(s32[512]{0:T(512)} %param.9), channel_id=1, source_target_pairs={{0,4},{2,6},{4,0},{6,2},{1,5},{3,7},{5,1},{7,3},{8,12},{10,14},{12... | collective-permute-start | bytes 6152 | tf_op jit(solution)/shard_map/ppermute | solution.py:689
  17.7 20.6 %copy-start = (bf16[512,1024]{1,0:T(8,128)(2,1)}, bf16[512,1024]{1,0:T(8,128)(2,1)S(1)}, u32[]{:S(2)}) copy-start(bf16[512,1024]{1,0:T(8,128)(2,1)S(1)} %fusion.spread_ref) | copy-start | bytes 3145732
  32.1 0.7 copy-start.3
  32.8 37.1 %collective-permute-start.1 = (bf16[384,1024]{1,0:T(8,128)(2,1)}, bf16[384,1024]{1,0:T(8,128)(2,1)}, u32[]{:S(2)}, u32[]{:S(2)}) collective-permute-start(bf16[384,1024]{1,0:T(8,128)(2,1)} %after.1), channel_id=1, source_target_pairs={{0,4},{2,6},{4,0},{6,2},{1,5},{3,7},{5,1},{7,3},{8,12},{10,14},{12... | collective-permute-start | bytes 2359304 | tf_op jit(solution)/shard_map/ppermute | solution.py:688
  38.6 31.3 %all-to-all-start.1 = ((bf16[8,128,1024]{2,1,0:T(8,128)(2,1)}), bf16[8,128,1024]{2,1,0:T(8,128)(2,1)}, u32[]{:S(2)}, u32[]{:S(2)}) async-start(bf16[8,128,1024]{2,1,0:T(8,128)(2,1)} %select_rows.1), calls=%async_computation.1 | async-start | bytes 4194304 | tf_op jit(solution)/shard_map/all_to_all | solution.py:679
  75.4 4.8 %collective-permute-start.4 = (f32[8,512]{1,0:T(8,128)S(1)}, f32[8,512]{1,0:T(8,128)S(1)}, u32[]{:S(2)}, u32[]{:S(2)}) collective-permute-start(f32[8,512]{1,0:T(8,128)S(1)} %get-tuple-element.31.stats_ref.here_ref), channel_id=1, source_target_pairs={{0,4},{2,6},{4,0},{6,2},{1,5},{3,7},{5,1},{7,3},{8,12},{10,14},{12... | collective-permute-start | bytes 49160 | tf_op jit(solution)/shard_map/ppermute | solution.py:704
  82.3 45.9 %collective-permute-start.5 = (bf16[512,1024]{1,0:T(8,128)(2,1)}, bf16[512,1024]{1,0:T(8,128)(2,1)}, u32[]{:S(2)}, u32[]{:S(2)}) collective-permute-start(bf16[512,1024]{1,0:T(8,128)(2,1)} %get-tuple-element.45.wait_ref), channel_id=1, source_target_pairs={{0,4},{2,6},{4,0},{6,2},{1,5},{3,7},{5,1},{7,3},{8,12},{10,14},{12... | collective-permute-start | bytes 3145736 | tf_op jit(solution)/shard_map/ppermute | solution.py:713
  87.3 31.0 %all-to-all-start.2 = ((bf16[8,128,1024]{2,1,0:T(8,128)(2,1)}), bf16[8,128,1024]{2,1,0:T(8,128)(2,1)}, u32[]{:S(2)}, u32[]{:S(2)}) async-start(bf16[8,128,1024]{2,1,0:T(8,128)(2,1)} %get-tuple-element.48), calls=%async_computation.2 | async-start | bytes 4194304 | tf_op jit(solution)/shard_map/all_to_all | solution.py:679
  118.3 3.7 %copy-start.1 = (bf16[512,1024]{1,0:T(8,128)(2,1)S(1)}, bf16[512,1024]{1,0:T(8,128)(2,1)}, u32[]{:S(2)}) copy-start(bf16[512,1024]{1,0:T(8,128)(2,1)} %copy-done) | copy-start | bytes 3145732
  118.3 30.3 %all-to-all-start.3 = ((bf16[8,128,1024]{2,1,0:T(8,128)(2,1)}), bf16[8,128,1024]{2,1,0:T(8,128)(2,1)S(1)}, u32[]{:S(2)}, u32[]{:S(2)}) async-start(bf16[8,128,1024]{2,1,0:T(8,128)(2,1)} %get-tuple-element.49), calls=%async_computation.3 | async-start | bytes 4194304 | tf_op jit(solution)/shard_map/all_to_all | solution.py:679
  125.6 25.9 %collective-permute-start.6 = (bf16[512,1024]{1,0:T(8,128)(2,1)}, bf16[512,1024]{1,0:T(8,128)(2,1)}, u32[]{:S(2)}, u32[]{:S(2)}) collective-permute-start(bf16[512,1024]{1,0:T(8,128)(2,1)} %segment_rows.2.refs_0_), channel_id=1, source_target_pairs={{0,2},{2,0},{4,6},{6,4},{1,3},{3,1},{5,7},{7,5},{8,10},{10,8},{12,... | collective-permute-start | bytes 3145736 | tf_op jit(solution)/shard_map/ppermute | solution.py:715

commit v6 on v5

--- a/solution.py
+++ b/solution.py
@@ -11,7 +11,6 @@
 SCALE = 0.8
 PLANES = 4
 CHUNKS = 1
-EARLY = 4
 BF16 = jnp.bfloat16
 F32 = jnp.float32
 BUSY = 1 << 37
@@ -45,7 +44,7 @@
 def after(array, *others):
     return pl.pallas_call(
         after_kernel,
-        in_specs=[ANY] * (1 + len(others)),
+        in_specs=[ANY] + [VMEM] * len(others),
         out_specs=ANY,
         out_shape=shape(array.shape, array.dtype),
         input_output_aliases={0: 0},
@@ -150,16 +149,62 @@
     )(spread, rows)
 
 
-def segment_kernel(stripes, spread_ref, slabs_ref, *refs):
+def plane_place(ranks):
+    return lax.axis_index("group") * ranks + lax.axis_index("rank")
+
+
+def join_kernel(kept_ref, *refs):
+    chips, depth, _ = kept_ref.shape
+    given_refs = refs[:chips]
+    *out_refs, held, arrived, left = refs[chips:]
+    for g in range(chips):
+        load(kept_ref.at[g], held.at[g, pl.ds(0, depth)], arrived.at[g, 0])
+        load(given_refs[g], held.at[g, pl.ds(depth, depth)], arrived.at[g, 1])
+    for g in range(chips):
+        pltpu.make_async_copy(kept_ref.at[g], held.at[g, pl.ds(0, depth)], arrived.at[g, 0]).wait()
+        pltpu.make_async_copy(given_refs[g], held.at[g, pl.ds(depth, depth)], arrived.at[g, 1]).wait()
+        load(held.at[g], out_refs[g], left.at[g])
+    for g in range(chips):
+        pltpu.make_async_copy(held.at[g], out_refs[g], left.at[g]).wait()
+
+
+def join_cores(kept, given):
+    chips, depth, width = kept.shape
+    return pl.pallas_call(
+        join_kernel,
+        in_specs=[HBM] + [ANY] * chips,
+        out_specs=[HBM] * chips,
+        out_shape=[pltpu.HBM((2 * depth, width), BF16)] * chips,
+        scratch_shapes=[
+            pltpu.VMEM((chips, 2 * depth, width), BF16),
+            pltpu.SemaphoreType.DMA((chips, 2)),
+            pltpu.SemaphoreType.DMA((chips,)),
+        ],
+        compiler_params=params(),
+        name="join_cores",
+        cost_estimate=cost(1 << 20, 4),
+    )(kept, *given)
+
+
+def segment_kernel(stripes, arrays, spread_ref, *refs):
+    slab_refs = refs[:arrays]
     out_ref, held, result, arrived, left = refs[-5:]
-    slabs, depth, width = slabs_ref.shape
-    tile = width // stripes
+    tile = out_ref.shape[1] // stripes
+    depth = held.shape[1] // arrays
     columns = [pl.ds(t * tile, tile) for t in range(stripes)]
-    loads = [load(slabs_ref.at[:, :, columns[t]], held.at[t], arrived.at[t]) for t in range(stripes)]
+    loads = [
+        Several(
+            [
+                load(ref.at[:, columns[t]], held.at[t, pl.ds(i * depth, depth)], arrived.at[t, i])
+                for i, ref in enumerate(slab_refs)
+            ]
+        )
+        for t in range(stripes)
+    ]
     stores = []
     for t in range(stripes):
         loads[t].wait()
-        total = jnp.dot(spread_ref[...], held[t].reshape(slabs * depth, tile), preferred_element_type=F32)
+        total = jnp.dot(spread_ref[...], held[t], preferred_element_type=F32)
         if out_ref.dtype == F32:
             out_ref[:, t * tile : (t + 1) * tile] = total
         else:
@@ -169,28 +214,36 @@
         store.wait()
 
 
-def segment_rows(spread, slabs, wait=None):
+class Several:
+    def __init__(self, copies):
+        self.copies = copies
+
+    def wait(self):
+        for copy in self.copies:
+            copy.wait()
+
+
+def segment_rows(spread, arrays, wait=None):
     stripes = 2
-    rows = spread.shape[0]
-    count, depth, width = slabs.shape
+    rows, depth = spread.shape
+    width = arrays[0].shape[-1]
     tile = width // stripes
     extra = [] if wait is None else [wait]
-    sems = pltpu.SemaphoreType.DMA((stripes,))
-    return pl.pallas_call(
-        functools.partial(segment_kernel, stripes),
-        in_specs=[VMEM, ANY] + [ANY] * len(extra),
+    return pl.pallas_call(
+        functools.partial(segment_kernel, stripes, len(arrays)),
+        in_specs=[VMEM] + [ANY] * (len(arrays) + len(extra)),
         out_specs=VMEM if extra else HBM,
         out_shape=shape((rows, width), F32) if extra else pltpu.HBM((rows, width), BF16),
         scratch_shapes=[
-            pltpu.VMEM((stripes, count, depth, tile), BF16),
+            pltpu.VMEM((stripes, depth, tile), BF16),
             pltpu.VMEM((stripes, rows, tile), BF16),
-            sems,
-            sems,
+            pltpu.SemaphoreType.DMA((stripes, len(arrays))),
+            pltpu.SemaphoreType.DMA((stripes,)),
         ],
         compiler_params=params(),
         name="segment_rows",
         cost_estimate=cost(BUSY if extra else 1 << 30, 4),
-    )(spread, slabs, *extra)
+    )(spread, *arrays, *extra)
 
 
 def candidates(slabs_ref, q, chunk):
@@ -327,12 +380,12 @@
     half = near_ref.shape[1] // 2
     cut = low_ref.shape[0]
     size = others_ref.shape[0]
+    held_loads = load_chunks(far_ref.at[:, pl.ds(0, half)], held, held_in)
     whole = [
         load(low_ref, others_ref.at[pl.ds(0, cut)], came.at[0]),
         load(high_ref, others_ref.at[pl.ds(cut, size - cut)], came.at[1]),
     ]
     near_loads = load_chunks(near_ref.at[:, pl.ds(half, half)], near_rows, near_in)
-    held_loads = load_chunks(far_ref.at[:, pl.ds(0, half)], held, held_in)
     far_loads = load_chunks(far_ref.at[:, pl.ds(half, half)], far_rows, far_in)
     put_targets(near_place, near_target_ref, chosen_ref, chosen_others_ref)
     put_targets(far_place, far_target_ref, chosen_ref, chosen_others_ref)
@@ -356,11 +409,11 @@
 
         return put
 
+    own = block_logits(queries_ref, part(held_loads, held), far_target_ref[0:1, :], put_far(0))
+    put_stats(stats_ref, 0, joined(stat_rows(own_stats_ref, 0), own))
     for copy in whole:
         copy.wait()
     near = block_logits(others_ref, part(near_loads, near_rows), near_target_ref[1:2, :], put_near)
-    own = block_logits(queries_ref, part(held_loads, held), far_target_ref[0:1, :], put_far(0))
-    put_stats(stats_ref, 0, joined(stat_rows(own_stats_ref, 0), own))
     far = block_logits(others_ref, part(far_loads, far_rows), far_target_ref[1:2, :], put_far(1))
     put_stats(stats_ref, 1, joined(near, far))
     for store in stores:
@@ -518,11 +571,12 @@
     rows = [scale, jnp.where(held, wanted - counted, 0.0)]
     columns = jnp.transpose(jnp.concatenate(rows + [jnp.zeros_like(scale)] * 6, axis=0))
     stores = []
-    for c in range(CHUNKS):
-        part = row_chunk(made.shape[0], c)
+    size = made.shape[0] // 4
+    for c in range(4):
+        part = slice(c * size, (c + 1) * size)
         share = columns[part, 0:1] * sums_ref[part, :] + columns[part, 1:2] * hit_ref[part, :]
         made[part, :] = (SCALE * share).astype(BF16)
-        some = part_of(made.shape[0], c)
+        some = pl.ds(c * size, size)
         stores.append(load(made.at[some], other_ref.at[some], left.at[c]))
     totals_ref[...] = jnp.zeros_like(totals_ref)
     for q in range(2):
@@ -539,7 +593,7 @@
         in_specs=[VMEM] * 6,
         out_specs=[HBM, VMEM, VMEM],
         out_shape=[pltpu.HBM((size, width), BF16), shape((8, size), F32), shape((1, size), F32)],
-        scratch_shapes=[pltpu.VMEM((size, width), BF16), pltpu.SemaphoreType.DMA((CHUNKS,))],
+        scratch_shapes=[pltpu.VMEM((size, width), BF16), pltpu.SemaphoreType.DMA((4,))],
         compiler_params=params(),
         name="other_grads",
         cost_estimate=cost(1 << 20, 4),
@@ -551,16 +605,17 @@
     contrib_ref, pieces_ref, made, left, pieces, pieces_out,
 ):
     del wait_ref
+    slabs, depth, width = contrib_ref.shape
+    half = depth // 2
     stores = []
-    for c in range(CHUNKS):
-        rows = chunk_rows(logits_ref, c)
-        for q, block_ref in enumerate((queries_ref, others_ref)):
-            piece = dlogits(logits_ref[q, rows, :], totals_ref[q : q + 1, :], c, target_ref[q : q + 1, :])
-            if q == 0:
-                pieces[rows, :] = piece
-                part = part_of(logits_ref.shape[1], c)
-                stores.append(load(pieces.at[part], pieces_ref.at[part], pieces_out.at[c]))
-            stores += send_contrib(made, contrib_ref, left, c, q, piece, block_ref[...], q == 1)
+    for q, block_ref in enumerate((queries_ref, others_ref)):
+        piece = dlogits(logits_ref[q], totals_ref[q : q + 1, :], 0, target_ref[q : q + 1, :])
+        if q == 0:
+            pieces[...] = piece
+            stores.append(load(pieces, pieces_ref, pieces_out))
+        product = SCALE * jnp.dot(piece, block_ref[...], preferred_element_type=F32)
+        made[q] = product.astype(BF16).reshape(slabs, half, width)
+        stores.append(load(made.at[q], contrib_ref.at[:, pl.ds(q * half, half)], left.at[q]))
     for store in stores:
         store.wait()
 
@@ -568,13 +623,18 @@
 def far_grads(queries, others, logits, target, totals, wait, slabs):
     size = queries.shape[0]
     rows = logits.shape[1]
+    count, depth, width = slabs.shape
     return pl.pallas_call(
         far_kernel,
         in_specs=[VMEM] * 5 + [ANY],
         out_specs=[HBM] * 2,
         out_shape=[pltpu.HBM(slabs.shape, BF16), pltpu.HBM((rows, size), BF16)],
-        scratch_shapes=contrib_scratch(slabs)
-        + [pltpu.VMEM((rows, size), BF16), pltpu.SemaphoreType.DMA((CHUNKS,))],
+        scratch_shapes=[
+            pltpu.VMEM((2, count, depth // 2, width), BF16),
+            pltpu.SemaphoreType.DMA((2,)),
+            pltpu.VMEM((rows, size), BF16),
+            pltpu.SemaphoreType.DMA,
+        ],
         compiler_params=params(),
         name="far_grads",
         cost_estimate=cost(1 << 30, 4),
@@ -582,46 +642,59 @@
 
 
 def near_kernel(
-    queries_ref, others_ref, target_ref, totals_ref, own_logits_ref, other_logits_ref, pieces_ref, near_ref, far_ref,
-    contrib_ref, own_ref, logits, near, far, came, pieces, begun, score, scored, own, own_out, made, left,
+    ranks, queries_ref, others_ref, target_ref, totals_ref, own_logits_ref, other_logits_ref, pieces_ref, near_ref, far_ref,
+    kept_ref, *refs,
 ):
+    *given_refs, own_ref, logits, near, far, came, pieces, begun, score, scored, own, own_out, made, left = refs
     first = load(pieces_ref, pieces, begun)
     copies = load_share(0, own_logits_ref, near_ref, far_ref, logits, near, far, came)
     other_scores = load(other_logits_ref, score, scored)
-    rows = logits.shape[0]
+    slabs, depth, width = made.shape
+    half = depth // 2
+
+    def store_part(q, piece, block_ref):
+        product = SCALE * jnp.dot(piece, block_ref[...], preferred_element_type=F32)
+        made[:, q * half : (q + 1) * half, :] = product.astype(BF16).reshape(slabs, half, width)
+
+    other_scores.wait()
+    store_part(1, dlogits(score[...], totals_ref[1:2, :], 0, target_ref[1:2, :]), others_ref)
     first.wait()
 
     def far_piece(c):
-        return pieces[row_chunk(rows, c), :]
+        return pieces[row_chunk(logits.shape[0], c), :]
 
     def near_piece(c):
-        return dlogits(logits[row_chunk(rows, c), :], totals_ref[0:1, :], c, target_ref[0:1, :])
+        return dlogits(logits[row_chunk(logits.shape[0], c), :], totals_ref[0:1, :], c, target_ref[0:1, :])
 
     def use(c, piece):
-        send_contrib(made, contrib_ref, left, c, 0, piece, queries_ref[...], False)
+        store_part(0, piece, queries_ref)
 
     total = query_share(copies, far_piece, near_piece, near, far, use)
+    place = plane_place(ranks)
+    stores = []
+    for s in range(slabs):
+        out_ref = given_refs[s // 2] if s % 2 else kept_ref.at[s // 2]
+        stores.append(load(made.at[place ^ s], out_ref, left.at[s]))
     own[...] = SCALE * total
-    stores = [load(own, own_ref, own_out)]
-    other_scores.wait()
-    for c in range(CHUNKS):
-        piece = dlogits(score[row_chunk(rows, c), :], totals_ref[1:2, :], c, target_ref[1:2, :])
-        stores += send_contrib(made, contrib_ref, left, c, 1, piece, others_ref[...], True)
+    stores.append(load(own, own_ref, own_out))
     for store in stores:
         store.wait()
 
 
-def near_grads(queries, others, target, totals, own_logits, other_logits, pieces, near_slabs, far_slabs):
-    return pl.pallas_call(
-        near_kernel,
+def near_grads(queries, others, target, totals, own_logits, other_logits, pieces, near_slabs, far_slabs, ranks):
+    slabs, depth, width = near_slabs.shape
+    kept = pltpu.HBM((slabs // 2, depth, width), BF16)
+    given = [pltpu.HBM((depth, width), BF16)] * (slabs // 2)
+    return pl.pallas_call(
+        functools.partial(near_kernel, ranks),
         in_specs=[VMEM] * 4 + [HBM] * 5,
-        out_specs=[HBM] * 2,
-        out_shape=[pltpu.HBM(near_slabs.shape, BF16), pltpu.HBM(queries.shape, F32)],
+        out_specs=[HBM] * (2 + slabs // 2),
+        out_shape=[kept, *given, pltpu.HBM(queries.shape, F32)],
         scratch_shapes=share_scratch(own_logits, near_slabs)
         + [pltpu.VMEM(pieces.shape, BF16), pltpu.SemaphoreType.DMA]
         + [pltpu.VMEM(own_logits.shape, F32), pltpu.SemaphoreType.DMA]
         + [pltpu.VMEM(queries.shape, F32), pltpu.SemaphoreType.DMA]
-        + contrib_scratch(near_slabs),
+        + [pltpu.VMEM(near_slabs.shape, BF16), pltpu.SemaphoreType.DMA((slabs,))],
         compiler_params=params(),
         name="near_grads",
         cost_estimate=cost(BUSY, 8),
@@ -679,23 +752,26 @@
         return lax.all_to_all(slab_array, PLANE, split_axis=0, concat_axis=0, tiled=True)
 
     ids = block_ids.T
-    early = queries.shape[0] // EARLY
+    early = queries.shape[0] * 3 // 8
     own_rows = jnp.transpose(passages, (1, 0, 2))
     near_slabs = in_hbm(exchange(gather_rows(ids, own_rows, slabs, planes, ranks, 0)))
     pair_rows = lax.ppermute(passages.reshape(height * blocks, width), "z", to_pair)
     low, high = split_rows(in_hbm(queries), early)
-    others_low = in_hbm(lax.ppermute(low, "z", across))
-    others_high = lax.ppermute(after(high, others_low), "z", across)
-    others_positives = lax.ppermute(positives, "z", across)
+    others_low = lax.ppermute(low, "z", across)
+    others_positives = lax.ppermute(positives, "z", across).reshape(1, -1)
+    others_high = lax.ppermute(after(high, others_positives), "z", across)
 
     table = block_ids.reshape(groups, planes, ranks, refs)
     both = jnp.stack([jnp.take(table, z, axis=1), jnp.take(table, (z + planes // 2) % planes, axis=1)], axis=2)
     place = (jnp.arange(height, dtype=jnp.int32) * blocks + both.reshape(-1, 1)).reshape(1, -1)
     spread = (jnp.arange(height * blocks, dtype=jnp.int32)[:, None] == place).astype(BF16)
+    by_shift = jnp.take(both.reshape(slabs, -1), plane_place(ranks) ^ jnp.arange(slabs), axis=0)
+    near_place = (jnp.arange(height, dtype=jnp.int32) * blocks + by_shift.reshape(-1, 1)).reshape(1, -1)
+    near_spread = (jnp.arange(height * blocks, dtype=jnp.int32)[:, None] == near_place).astype(BF16)
     far_slabs = in_hbm(exchange(select_rows(spread, pair_rows, slabs)))
 
     chosen = positives.reshape(1, -1)
-    chosen_others = others_positives.reshape(1, -1)
+    chosen_others = others_positives
     places = [functools.partial(place_of, far, planes, ranks, refs, height) for far in range(2)]
     own_logits, own_stats, own = own_half(in_hbm(queries), near_slabs, chosen, places[0])
     other_logits, saved_logits, far_logits, stats, near_target, far_target, others, near_rows, far_rows = rest_half(
@@ -706,16 +782,20 @@
     other_part, totals, loss = other_grads(stats, partner, near_target, far_target, sums, hit)
     own_logits, other_logits = in_hbm(own_logits), in_hbm(saved_logits)
     far_contrib, pieces = far_grads(own, others, far_logits, far_target, totals, in_hbm(other_part), far_slabs)
-    far_back = in_hbm(exchange(far_contrib))
-    near_contrib, own_grad = near_grads(
-        own, others, near_target, totals, own_logits, other_logits, in_hbm(pieces), near_slabs, far_slabs
+    far_back = in_hbm(exchange(far_contrib).reshape(-1, width))
+    kept, *given, own_grad = near_grads(
+        own, others, near_target, totals, own_logits, other_logits, in_hbm(pieces), near_slabs, far_slabs, ranks
     )
+    joined = join_cores(kept, [lax.ppermute(array, PLANE, [(i, i ^ 1) for i in range(slabs)]) for array in given])
     own_part = lax.ppermute(other_part, "z", across)
-    far_sum = segment_rows(spread, far_back)
+    far_sum = segment_rows(spread, [far_back])
     pair_sum = lax.ppermute(far_sum, "z", to_pair)
-    near_back = exchange(near_contrib)
+    near_back = [
+        lax.ppermute(array, PLANE, [(i, i ^ (2 * g)) for i in range(slabs)]) if g else array
+        for g, array in enumerate(joined)
+    ]
     query_grad = add_parts(own_grad, own_part, BUSY, in_hbm(far_sum))
-    near_sum = segment_rows(spread, near_back, in_hbm(query_grad))
+    near_sum = segment_rows(near_spread, near_back, in_hbm(query_grad))
     row_sum = add_parts(near_sum, pair_sum, 1 << 20)
     return loss.reshape(-1), query_grad, row_sum.reshape(passages.shape)
 

time: 154 us -> 153 us (level)
  waiting for transfers between devices: 78.2 us -> 69.2 us
  Pallas kernels: 39.3 us -> 41.4 us
  local copies, waits for them, and re-layouts: 2.8 us -> 4.72 us
    all_to_all x4 -> x3, waiting for transfers between devices: 38.2 us -> 14.8 us  [exchange(): lax.all_to_all(slab_array, PLANE, split_axis=0, concat_axis=0, tiled=True)]
    ppermute x1, waiting for transfers between devices: 1.05 us -> 7.13 us  [on_device(): pair_sum = lax.ppermute(far_sum, 'z', to_pair)]
    ppermute x3 -> x10, starting transfers between devices: 6.28 us -> 11 us  [the longest x3 3.55 us: on_device(): lax.ppermute(array, PLANE, [(i, i ^ 2 * g) for i in range(slabs)])]
    pallas_call x4 -> x5, Pallas kernels: 11.4 us -> 15.5 us  [the longest x1 7.2 us: near_grads(): pl.pallas_call(functools.partial(near_kernel, ranks), in_specs=[VMEM] * 4...]
    all_to_all x4 -> x3, starting transfers between devices: 17 us -> 13.3 us  [exchange(): lax.all_to_all(slab_array, PLANE, split_axis=0, concat_axis=0, tiled=True)]
    ppermute x1, waiting for transfers between devices: 0.01 us -> 3.48 us  [on_device(): lax.ppermute(passages.reshape(height * blocks, width), 'z', to_pair)]
    ppermute x1, waiting for transfers between devices: 1.72 us -> 4.6 us  [on_device(): own_part = lax.ppermute(other_part, 'z', across)]
    ppermute x3 -> x10, waiting for transfers between devices: 37.2 us -> 39.2 us  [the longest x1 19.5 us: on_device(): others_high = lax.ppermute(after(high, others_positives), 'z', across)]
  transfers between devices with their start and end apart: 11 -> 17, of which waited for: 7 -> 13; matrix products, arithmetic and copies ran while one was open for 2% -> 3% of each run, Pallas kernels for 19% -> 22%
where the time goes in v6:
time: 153 us; the launch traced here: 151 us
  waiting for transfers between devices  69.2 us (45%)
  Pallas kernels  41.4 us (27%)
  starting transfers between devices  33.5 us (22%)
  local copies, waits for them, and re-layouts  4.72 us (3%)
    ppermute x1, waiting for transfers between devices, on_device(): others_high = lax.ppermute(after(high, others_positives), 'z', across)  19.5 us
    all_to_all x3, waiting for transfers between devices, exchange(): lax.all_to_all(slab_array, PLANE, split_axis=0, concat_axis=0, tiled=True)  14.8 us
    all_to_all x3, starting transfers between devices, exchange(): lax.all_to_all(slab_array, PLANE, split_axis=0, concat_axis=0, tiled=True)  13.3 us
    ppermute x3, waiting for transfers between devices, on_device(): lax.ppermute(array, PLANE, [(i, i ^ 2 * g) for i in range(slabs)])  9.93 us
    ppermute x1, waiting for transfers between devices, on_device(): others_positives = lax.ppermute(positives, 'z', across).reshape(1, -1)  8.35 us
    pallas_call x1, Pallas kernels, near_grads(): pl.pallas_call(functools.partial(near_kernel, ranks), in_specs=[VMEM] * 4...  7.2 us
    ppermute x1, waiting for transfers between devices, on_device(): pair_sum = lax.ppermute(far_sum, 'z', to_pair)  7.13 us
    pallas_call x2, Pallas kernels, segment_rows(): pl.pallas_call(functools.partial(segment_kernel, stripes, len(arrays)), i...  6.02 us
  transfers between devices with their start and end apart: 17, of which 13 were waited for; matrix products, arithmetic and copies ran while one was open for 3% of the time, Pallas kernels for 22%

profile of v6, /device:TPU:0, one launch (start us, length us, event | category | flops | bytes accessed | tf_op | source)
XLA Modules:
  0.0 151.4 jit_solution(7439769549958479382)
XLA Ops:
  0.6 3.1 %collective-permute-start.3 = (bf16[512,1024]{1,0:T(8,128)(2,1)}, bf16[512,1024]{1,0:T(8,128)(2,1)S(1)}, u32[]{:S(2)}, u32[]{:S(2)}) collective-permute-start(bf16[512,1024]{1,0:T(8,128)(2,1)} %bitcast.25), channel_id=1, source_target_pairs={{0,2},{2,0},{4,6},{6,4},{1,3},{3,1},{5,7},{7,5},{8,10},{10,8},{12,... | collective-permute-start | bytes 3145736 | tf_op jit(solution)/shard_map/ppermute | solution.py:758
  3.7 1.8 %copy.17 = bf16[16,32,1024]{2,0,1:T(8,128)(2,1)S(1)} copy(bf16[16,32,1024]{2,1,0:T(8,128)(2,1)} %param.7) | data formatting | bytes 2097152 | tf_op args[1]
  5.6 2.0 %gather_rows.1 = bf16[8,128,1024]{2,1,0:T(8,128)(2,1)} custom-call(s32[4,32]{1,0:T(4,128)S(1)} %bitcast.22, bf16[32,16,1024]{2,1,0:T(8,128)(2,1)S(1)} %bitcast.19), custom_call_target="tpu_custom_call" | custom-call | bytes 4194304 | tf_op jit(solution)/shard_map/gather_rows/pallas_call | solution.py:109
  7.6 4.4 %all-to-all-start = ((bf16[8,128,1024]{2,1,0:T(8,128)(2,1)}), bf16[8,128,1024]{2,1,0:T(8,128)(2,1)}, u32[]{:S(2)}, u32[]{:S(2)}) async-start(bf16[8,128,1024]{2,1,0:T(8,128)(2,1)} %gather_rows.1), calls=%async_computation | async-start | bytes 4194304 | tf_op jit(solution)/shard_map/all_to_all | solution.py:752
  12.0 2.7 %collective-permute-start.1 = (s32[512]{0:T(512)S(1)}, s32[512]{0:T(512)S(1)}, u32[]{:S(2)}, u32[]{:S(2)}) collective-permute-start(s32[512]{0:T(512)S(1)} %copy-done.6), channel_id=1, source_target_pairs={{0,4},{2,6},{4,0},{6,2},{1,5},{3,7},{5,1},{7,3},{8,12},{10,14},{12... | collective-permute-start | bytes 6152 | tf_op jit(solution)/shard_map/ppermute | solution.py:761
  14.6 2.1 %split_rows.1 = (bf16[192,1024]{1,0:T(8,128)(2,1)}, bf16[320,1024]{1,0:T(8,128)(2,1)}) custom-call(bf16[512,1024]{1,0:T(8,128)(2,1)} %source_ref.1), custom_call_target="tpu_custom_call" | custom-call | bytes 2097152 | tf_op jit(solution)/shard_map/split_rows/pallas_call | solution.py:69
  19.3 8.4 %collective-permute-done.1 = s32[512]{0:T(512)S(1)} collective-permute-done((s32[512]{0:T(512)S(1)}, s32[512]{0:T(512)S(1)}, u32[]{:S(2)}, u32[]{:S(2)}) %collective-permute-start.1) | collective-permute-done | bytes 2080 | tf_op jit(solution)/shard_map/ppermute | solution.py:761
  28.9 3.3 %collective-permute-start.2 = (bf16[320,1024]{1,0:T(8,128)(2,1)}, bf16[320,1024]{1,0:T(8,128)(2,1)}, u32[]{:S(2)}, u32[]{:S(2)}) collective-permute-start(bf16[320,1024]{1,0:T(8,128)(2,1)} %after.1), channel_id=1, source_target_pairs={{0,4},{2,6},{4,0},{6,2},{1,5},{3,7},{5,1},{7,3},{8,12},{10,14},{12... | collective-permute-start | bytes 1966088 | tf_op jit(solution)/shard_map/ppermute | solution.py:762
  32.2 3.5 %collective-permute-done.3.rows_ref = bf16[512,1024]{1,0:T(8,128)(2,1)S(1)} collective-permute-done((bf16[512,1024]{1,0:T(8,128)(2,1)}, bf16[512,1024]{1,0:T(8,128)(2,1)S(1)}, u32[]{:S(2)}, u32[]{:S(2)}) %collective-permute-start.3) | collective-permute-done | bytes 1048608 | tf_op jit(solution)/shard_map/ppermute | solution.py:758
  35.7 2.3 %select_rows.1 = bf16[8,128,1024]{2,1,0:T(8,128)(2,1)} custom-call(bf16[512,1024]{1,0:T(8,128)(2,1)S(1)} %fusion.spread_ref, bf16[512,1024]{1,0:T(8,128)(2,1)S(1)} %collective-permute-done.3.rows_ref), custom_call_target="tpu_custom_call" | custom-call | flops 137438953472 | bytes 4194304 | tf_op jit(solution)/shard_map/select_rows/pallas_call | solution.py:140
  38.6 4.4 %all-to-all-start.1 = ((bf16[8,128,1024]{2,1,0:T(8,128)(2,1)}), bf16[8,128,1024]{2,1,0:T(8,128)(2,1)}, u32[]{:S(2)}, u32[]{:S(2)}) async-start(bf16[8,128,1024]{2,1,0:T(8,128)(2,1)} %select_rows.1), calls=%async_computation.1 | async-start | bytes 4194304 | tf_op jit(solution)/shard_map/all_to_all | solution.py:752
  43.0 3.4 %own_half.1 = (f32[512,512]{1,0:T(8,128)}, f32[8,512]{1,0:T(8,128)S(1)}, bf16[512,1024]{1,0:T(8,128)(2,1)S(1)}) custom-call(bf16[512,1024]{1,0:T(8,128)(2,1)} %source_ref.1, bf16[8,128,1024]{2,1,0:T(8,128)(2,1)} %all-to-all-done.slabs_ref.near_ref, s32[1,512]{1,0:T(1,128)S(1)} %bitcast.23), custom_call_target="tpu_custom_call" | custom-call | flops 137438953472 | bytes 4194304 | tf_op jit(solution)/shard_map/own_half/pallas_call | solution.py:357
  46.5 19.5 %collective-permute-done.2.high_ref = bf16[320,1024]{1,0:T(8,128)(2,1)} collective-permute-done((bf16[320,1024]{1,0:T(8,128)(2,1)}, bf16[320,1024]{1,0:T(8,128)(2,1)}, u32[]{:S(2)}, u32[]{:S(2)}) %collective-permute-start.2) | collective-permute-done | bytes 655392 | tf_op jit(solution)/shard_map/ppermute | solution.py:762
  66.0 3.7 %all-to-all-done.1.far_ref = bf16[8,128,1024]{2,1,0:T(8,128)(2,1)} async-done(((bf16[8,128,1024]{2,1,0:T(8,128)(2,1)}), bf16[8,128,1024]{2,1,0:T(8,128)(2,1)}, u32[]{:S(2)}, u32[]{:S(2)}) %all-to-all-start.1) | async-done | bytes 2097184 | tf_op jit(solution)/shard_map/all_to_all | solution.py:752
  69.7 4.5 %rest_half.1 = (f32[512,512]{1,0:T(8,128)S(1)}, f32[512,512]{1,0:T(8,128)}, f32[2,512,512]{2,1,0:T(8,128)S(1)}, f32[8,512]{1,0:T(8,128)S(1)}, s32[8,512]{1,0:T(8...) custom-call(bf16[512,1024]{1,0:T(8,128)(2,1)S(1)} %get-tuple-element, ...), custom_call_target="tpu_custom_call" | custom-call | flops 1610612736 | bytes 8388608 | tf_op jit(solution)/shard_map/rest_half/pallas_call | solution.py:428
  74.1 2.7 %collective-permute-start.4 = (f32[8,512]{1,0:T(8,128)S(1)}, f32[8,512]{1,0:T(8,128)S(1)}, u32[]{:S(2)}, u32[]{:S(2)}) collective-permute-start(f32[8,512]{1,0:T(8,128)S(1)} %get-tuple-element.39.stats_ref.here_ref), channel_id=1, source_target_pairs={{0,4},{2,6},{4,0},{6,2},{1,5},{3,7},{5,1},{7,3},{8,12},{10,14},{12... | collective-permute-start | bytes 49160 | tf_op jit(solution)/shard_map/ppermute | solution.py:780
  76.8 2.4 %early_grads.1 = (f32[512,1024]{1,0:T(8,128)S(1)}, f32[512,1024]{1,0:T(8,128)S(1)}) custom-call(f32[8,512]{1,0:T(8,128)S(1)} %get-tuple-element.39.stats_ref.here_ref, s32[8,512]{1,0:T(8,128)S(1)} %get-tuple-element.40.near_target_ref.target_ref, s32[8,512]{1,0:T(8,128)S(1)} %get-tuple-element.41.far_target_ref.target_ref, ...), custom_call_target="tpu_custom_call" | custom-call | flops 137438953472 | bytes 4194304 | tf_op jit(solution)/shard_map/early_grads/pallas_call | solution.py:552
  79.2 2.1 %other_grads.1 = (bf16[512,1024]{1,0:T(8,128)(2,1)}, f32[8,512]{1,0:T(8,128)S(1)}, f32[1,512]{1,0:T(1,128)}) custom-call(f32[8,512]{1,0:T(8,128)S(1)} %get-tuple-element.39.stats_ref.here_ref, f32[8,512]{1,0:T(8,128)S(1)} %collective-permute-done.4.there_ref, s32[8,512]{1,0:T(8,128)S(1)} %get-tuple-element.40.near_target_ref.target_ref, ...), custom_call_target="tpu_custom_call" | custom-call | flops 1048576 | bytes 4194304 | tf_op jit(solution)/shard_map/other_grads/pallas_call | solution.py:591
  81.3 2.3 %collective-permute-start.5 = (bf16[512,1024]{1,0:T(8,128)(2,1)}, bf16[512,1024]{1,0:T(8,128)(2,1)}, u32[]{:S(2)}, u32[]{:S(2)}) collective-permute-start(bf16[512,1024]{1,0:T(8,128)(2,1)} %get-tuple-element.53.wait_ref), channel_id=1, source_target_pairs={{0,4},{2,6},{4,0},{6,2},{1,5},{3,7},{5,1},{7,3},{8,12},{10,14},{12... | collective-permute-start | bytes 3145736 | tf_op jit(solution)/shard_map/ppermute | solution.py:790
  83.6 2.4 %far_grads.1 = (bf16[8,128,1024]{2,1,0:T(8,128)(2,1)}, bf16[512,512]{1,0:T(8,128)(2,1)}) custom-call(bf16[512,1024]{1,0:T(8,128)(2,1)S(1)} %get-tuple-element.35.queries_ref, bf16[512,1024]{1,0:T(8,128)(2,1)S(1)} %get-tuple-element.49.others_ref, f32[2,512,512]{2,1,0:T(8,128)S(1)} %get-tuple-element.43.far_logits_ref.logits_ref, ...), custom_call_target="tpu_custom_call" | custom-call | flops 1073741824 | bytes 4194304 | tf_op jit(solution)/shard_map/far_grads/pallas_call | solution.py:627
  86.0 4.5 %all-to-all-start.2 = ((bf16[8,128,1024]{2,1,0:T(8,128)(2,1)}), bf16[8,128,1024]{2,1,0:T(8,128)(2,1)}, u32[]{:S(2)}, u32[]{:S(2)}) async-start(bf16[8,128,1024]{2,1,0:T(8,128)(2,1)} %get-tuple-element.56), calls=%async_computation.2 | async-start | bytes 4194304 | tf_op jit(solution)/shard_map/all_to_all | solution.py:752
  90.5 7.2 %near_grads.1 = (bf16[4,128,1024]{2,1,0:T(8,128)(2,1)}, bf16[128,1024]{1,0:T(8,128)(2,1)}, bf16[128,1024]{1,0:T(8,128)(2,1)}, bf16[128,1024]{1,0:T(8,128)(2,1)},...) custom-call(bf16[512,1024]{1,0:T(8,128)(2,1)S(1)} %get-tuple-element.35.queries_ref, ...), custom_call_target="tpu_custom_call" | custom-call | flops 137438953472 | bytes 8388608 | tf_op jit(solution)/shard_map/near_grads/pallas_call | solution.py:688
  101.9 1.6 %join_cores.1 = (bf16[256,1024]{1,0:T(8,128)(2,1)}, bf16[256,1024]{1,0:T(8,128)(2,1)}, bf16[256,1024]{1,0:T(8,128)(2,1)}, bf16[256,1024]{1,0:T(8,128)(2,1)}) custom-call(bf16[4,128,1024]{2,1,0:T(8,128)(2,1)S(1)} %copy-done.2, bf16[128,1024]{1,0:T(8,128)(2,1)S(1)} %collective-permute-done.6.refs_0_, bf16[128,1024]{1,0:T(8,128)(2,1)S(1)} %collective-permute-done.7.refs_1_, ...), custom_call_target="tpu_custom_call" | custom-call | flops 1048576 | bytes 4194304 | tf_op jit(solution)/shard_map/join_cores/pallas_call | solution.py:173
  103.5 1.8 %collective-permute-start.10 = (bf16[256,1024]{1,0:T(8,128)(2,1)}, bf16[256,1024]{1,0:T(8,128)(2,1)S(1)}, u32[]{:S(2)}, u32[]{:S(2)}) collective-permute-start(bf16[256,1024]{1,0:T(8,128)(2,1)} %get-tuple-element.63), channel_id=1, source_target_pairs={{0,8},{1,9},{8,0},{9,1},{16,24},{17,25},{24,16},{25,17},{2,10},{3,... | collective-permute-start | bytes 1572872 | tf_op jit(solution)/shard_map/ppermute | solution.py:794
  107.0 10.4 %all-to-all-done.2 = bf16[8,128,1024]{2,1,0:T(8,128)(2,1)} async-done(((bf16[8,128,1024]{2,1,0:T(8,128)(2,1)}), bf16[8,128,1024]{2,1,0:T(8,128)(2,1)}, u32[]{:S(2)}, u32[]{:S(2)}) %all-to-all-start.2) | async-done | bytes 2097184 | tf_op jit(solution)/shard_map/all_to_all | solution.py:752
  117.5 3.5 %segment_rows.2.refs_0_ = bf16[512,1024]{1,0:T(8,128)(2,1)} custom-call(bf16[512,1024]{1,0:T(8,128)(2,1)S(1)} %copy-done.1, bf16[1024,1024]{1,0:T(8,128)(2,1)} %bitcast.11.refs_0_), custom_call_target="tpu_custom_call" | custom-call | flops 1073741824 | bytes 4194304 | tf_op jit(solution)/shard_map/segment_rows/pallas_call | solution.py:232
  122.2 4.6 %collective-permute-done.5.part_ref = bf16[512,1024]{1,0:T(8,128)(2,1)} collective-permute-done((bf16[512,1024]{1,0:T(8,128)(2,1)}, bf16[512,1024]{1,0:T(8,128)(2,1)}, u32[]{:S(2)}, u32[]{:S(2)}) %collective-permute-start.5) | collective-permute-done | bytes 1048608 | tf_op jit(solution)/shard_map/ppermute | solution.py:790
  126.8 2.7 %add_parts.2.refs_4_ = bf16[512,1024]{1,0:T(8,128)(2,1)} custom-call(f32[512,1024]{1,0:T(8,128)} %get-tuple-element.55.own_ref, bf16[512,1024]{1,0:T(8,128)(2,1)} %collective-permute-done.5.part_ref, bf16[512,1024]{1,0:T(8,128)(2,1)} %segment_rows.2.refs_0_), custom_call_target="tpu_custom_call" | custom-call | flops 137438953472 | bytes 4194304 | tf_op jit(solution)/shard_map/add_parts/pallas_call | solution.py:725
  129.6 9.9 %collective-permute-done.12.refs_3_ = bf16[256,1024]{1,0:T(8,128)(2,1)} collective-permute-done((bf16[256,1024]{1,0:T(8,128)(2,1)}, bf16[256,1024]{1,0:T(8,128)(2,1)}, u32[]{:S(2)}, u32[]{:S(2)}) %collective-permute-start.12) | collective-permute-done | bytes 524320 | tf_op jit(solution)/shard_map/ppermute | solution.py:794
  139.5 2.5 %segment_rows.3.own_ref = f32[512,1024]{1,0:T(8,128)S(1)} custom-call(bf16[512,1024]{1,0:T(8,128)(2,1)S(1)} %fusion.1.spread_ref, bf16[256,1024]{1,0:T(8,128)(2,1)S(1)} %copy-done.7, bf16[256,1024]{1,0:T(8,128)(2,1)S(1)} %collective-permute-done.10.refs_1_, bf16[256,1024]{1,0:T(8,128)(2,1)S(1)} %collective-permute-done.11.refs_2_, ...), custom_call_target="tpu_custom_call" | custom-call | flops 137438953472 | bytes 4194304 | tf_op jit(solution)/shard_map/segment_rows/pallas_call | solution.py:232
  142.0 7.1 %collective-permute-done.13.part_ref = bf16[512,1024]{1,0:T(8,128)(2,1)} collective-permute-done((bf16[512,1024]{1,0:T(8,128)(2,1)}, bf16[512,1024]{1,0:T(8,128)(2,1)}, u32[]{:S(2)}, u32[]{:S(2)}) %collective-permute-start.13) | collective-permute-done | bytes 1048608 | tf_op jit(solution)/shard_map/ppermute | solution.py:792
  149.2 2.1 %add_parts.3 = bf16[512,1024]{1,0:T(8,128)(2,1)} custom-call(f32[512,1024]{1,0:T(8,128)S(1)} %segment_rows.3.own_ref, bf16[512,1024]{1,0:T(8,128)(2,1)} %collective-permute-done.13.part_ref), custom_call_target="tpu_custom_call" | custom-call | flops 1048576 | bytes 4194304 | tf_op jit(solution)/shard_map/add_parts/pallas_call | solution.py:725
  (54 shorter events, 11.5 us)
Async XLA Ops:
  0.6 4.9 %copy-start.5 = (s32[32,4]{0,1:T(4,128)S(1)}, s32[32,4]{0,1:T(4,128)}, u32[]{:S(2)}) copy-start(s32[32,4]{0,1:T(4,128)} %param.8) | copy-start | bytes 1540
  0.6 35.0 %collective-permute-start.3 = (bf16[512,1024]{1,0:T(8,128)(2,1)}, bf16[512,1024]{1,0:T(8,128)(2,1)S(1)}, u32[]{:S(2)}, u32[]{:S(2)}) collective-permute-start(bf16[512,1024]{1,0:T(8,128)(2,1)} %bitcast.25), channel_id=1, source_target_pairs={{0,2},{2,0},{4,6},{6,4},{1,3},{3,1},{5,7},{7,5},{8,10},{10,8},{12,... | collective-permute-start | bytes 3145736 | tf_op jit(solution)/shard_map/ppermute | solution.py:758
  7.6 4.4 %copy-start.6 = (s32[512]{0:T(512)S(1)}, s32[512]{0:T(512)}, u32[]{:S(2)}) copy-start(s32[512]{0:T(512)} %param.9) | copy-start | bytes 6148
  7.6 31.0 %all-to-all-start = ((bf16[8,128,1024]{2,1,0:T(8,128)(2,1)}), bf16[8,128,1024]{2,1,0:T(8,128)(2,1)}, u32[]{:S(2)}, u32[]{:S(2)}) async-start(bf16[8,128,1024]{2,1,0:T(8,128)(2,1)} %gather_rows.1), calls=%async_computation | async-start | bytes 4194304 | tf_op jit(solution)/shard_map/all_to_all | solution.py:752
  12.0 15.6 %collective-permute-start.1 = (s32[512]{0:T(512)S(1)}, s32[512]{0:T(512)S(1)}, u32[]{:S(2)}, u32[]{:S(2)}) collective-permute-start(s32[512]{0:T(512)S(1)} %copy-done.6), channel_id=1, source_target_pairs={{0,4},{2,6},{4,0},{6,2},{1,5},{3,7},{5,1},{7,3},{8,12},{10,14},{12... | collective-permute-start | bytes 6152 | tf_op jit(solution)/shard_map/ppermute | solution.py:761
  16.7 29.8 %collective-permute-start = (bf16[192,1024]{1,0:T(8,128)(2,1)}, bf16[192,1024]{1,0:T(8,128)(2,1)}, u32[]{:S(2)}, u32[]{:S(2)}) collective-permute-start(bf16[192,1024]{1,0:T(8,128)(2,1)} %get-tuple-element.36), channel_id=1, source_target_pairs={{0,4},{2,6},{4,0},{6,2},{1,5},{3,7},{5,1},{7,3},{8,12},{10,14},{12... | collective-permute-start | bytes 1179656 | tf_op jit(solution)/shard_map/ppermute | solution.py:760
  19.2 18.7 %copy-start = (bf16[512,1024]{1,0:T(8,128)(2,1)}, bf16[512,1024]{1,0:T(8,128)(2,1)S(1)}, u32[]{:S(2)}) copy-start(bf16[512,1024]{1,0:T(8,128)(2,1)S(1)} %fusion.spread_ref) | copy-start | bytes 3145732
  27.6 0.6 copy-start.3
  28.9 37.1 %collective-permute-start.2 = (bf16[320,1024]{1,0:T(8,128)(2,1)}, bf16[320,1024]{1,0:T(8,128)(2,1)}, u32[]{:S(2)}, u32[]{:S(2)}) collective-permute-start(bf16[320,1024]{1,0:T(8,128)(2,1)} %after.1), channel_id=1, source_target_pairs={{0,4},{2,6},{4,0},{6,2},{1,5},{3,7},{5,1},{7,3},{8,12},{10,14},{12... | collective-permute-start | bytes 1966088 | tf_op jit(solution)/shard_map/ppermute | solution.py:762
  38.6 31.0 %all-to-all-start.1 = ((bf16[8,128,1024]{2,1,0:T(8,128)(2,1)}), bf16[8,128,1024]{2,1,0:T(8,128)(2,1)}, u32[]{:S(2)}, u32[]{:S(2)}) async-start(bf16[8,128,1024]{2,1,0:T(8,128)(2,1)} %select_rows.1), calls=%async_computation.1 | async-start | bytes 4194304 | tf_op jit(solution)/shard_map/all_to_all | solution.py:752
  43.0 26.7 %copy-start.4 = (s32[512]{0:T(512)S(1)}, s32[512]{0:T(512)}, u32[]{:S(2)}) copy-start(s32[512]{0:T(512)} %copy-done.3) | copy-start | bytes 6148
  74.1 5.1 %collective-permute-start.4 = (f32[8,512]{1,0:T(8,128)S(1)}, f32[8,512]{1,0:T(8,128)S(1)}, u32[]{:S(2)}, u32[]{:S(2)}) collective-permute-start(f32[8,512]{1,0:T(8,128)S(1)} %get-tuple-element.39.stats_ref.here_ref), channel_id=1, source_target_pairs={{0,4},{2,6},{4,0},{6,2},{1,5},{3,7},{5,1},{7,3},{8,12},{10,14},{12... | collective-permute-start | bytes 49160 | tf_op jit(solution)/shard_map/ppermute | solution.py:780
  81.3 45.5 %collective-permute-start.5 = (bf16[512,1024]{1,0:T(8,128)(2,1)}, bf16[512,1024]{1,0:T(8,128)(2,1)}, u32[]{:S(2)}, u32[]{:S(2)}) collective-permute-start(bf16[512,1024]{1,0:T(8,128)(2,1)} %get-tuple-element.53.wait_ref), channel_id=1, source_target_pairs={{0,4},{2,6},{4,0},{6,2},{1,5},{3,7},{5,1},{7,3},{8,12},{10,14},{12... | collective-permute-start | bytes 3145736 | tf_op jit(solution)/shard_map/ppermute | solution.py:790
  86.0 31.5 %all-to-all-start.2 = ((bf16[8,128,1024]{2,1,0:T(8,128)(2,1)}), bf16[8,128,1024]{2,1,0:T(8,128)(2,1)}, u32[]{:S(2)}, u32[]{:S(2)}) async-start(bf16[8,128,1024]{2,1,0:T(8,128)(2,1)} %get-tuple-element.56), calls=%async_computation.2 | async-start | bytes 4194304 | tf_op jit(solution)/shard_map/all_to_all | solution.py:752
  90.5 8.3 %copy-start.8 = (s32[64,16]{1,0:T(8,128)S(1)}, s32[64,16]{1,0:T(8,128)}, u32[]{:S(2)}) copy-start(s32[64,16]{1,0:T(8,128)} %get-tuple-element.79) | copy-start | bytes 12292
  97.7 19.8 %copy-start.1 = (bf16[512,1024]{1,0:T(8,128)(2,1)S(1)}, bf16[512,1024]{1,0:T(8,128)(2,1)}, u32[]{:S(2)}) copy-start(bf16[512,1024]{1,0:T(8,128)(2,1)} %copy-done) | copy-start | bytes 3145732
  97.7 1.8 %collective-permute-start.6 = (bf16[128,1024]{1,0:T(8,128)(2,1)}, bf16[128,1024]{1,0:T(8,128)(2,1)S(1)}, u32[]{:S(2)}, u32[]{:S(2)}) collective-permute-start(bf16[128,1024]{1,0:T(8,128)(2,1)} %get-tuple-element.58), channel_id=1, source_target_pairs={{0,1},{1,0},{8,9},{9,8},{16,17},{17,16},{24,25},{25,24},{2,3},{3,2... | collective-permute-start | bytes 786440 | tf_op jit(solution)/shard_map/ppermute | solution.py:789
  98.0 1.9 %collective-permute-start.7 = (bf16[128,1024]{1,0:T(8,128)(2,1)}, bf16[128,1024]{1,0:T(8,128)(2,1)S(1)}, u32[]{:S(2)}, u32[]{:S(2)}) collective-permute-start(bf16[128,1024]{1,0:T(8,128)(2,1)} %get-tuple-element.59), channel_id=1, source_target_pairs={{0,1},{1,0},{8,9},{9,8},{16,17},{17,16},{24,25},{25,24},{2,3},{3,2... | collective-permute-start | bytes 786440 | tf_op jit(solution)/shard_map/ppermute | solution.py:789
  98.3 2.0 %collective-permute-start.8 = (bf16[128,1024]{1,0:T(8,128)(2,1)}, bf16[128,1024]{1,0:T(8,128)(2,1)S(1)}, u32[]{:S(2)}, u32[]{:S(2)}) collective-permute-start(bf16[128,1024]{1,0:T(8,128)(2,1)} %get-tuple-element.60), channel_id=1, source_target_pairs={{0,1},{1,0},{8,9},{9,8},{16,17},{17,16},{24,25},{25,24},{2,3},{3,2... | collective-permute-start | bytes 786440 | tf_op jit(solution)/shard_map/ppermute | solution.py:789
  98.5 2.2 %collective-permute-start.9 = (bf16[128,1024]{1,0:T(8,128)(2,1)}, bf16[128,1024]{1,0:T(8,128)(2,1)S(1)}, u32[]{:S(2)}, u32[]{:S(2)}) collective-permute-start(bf16[128,1024]{1,0:T(8,128)(2,1)} %get-tuple-element.61), channel_id=1, source_target_pairs={{0,1},{1,0},{8,9},{9,8},{16,17},{17,16},{24,25},{25,24},{2,3},{3,2... | collective-permute-start | bytes 786440 | tf_op jit(solution)/shard_map/ppermute | solution.py:789
  100.7 1.2 copy-start.2
  103.5 26.0 %collective-permute-start.10 = (bf16[256,1024]{1,0:T(8,128)(2,1)}, bf16[256,1024]{1,0:T(8,128)(2,1)S(1)}, u32[]{:S(2)}, u32[]{:S(2)}) collective-permute-start(bf16[256,1024]{1,0:T(8,128)(2,1)} %get-tuple-element.63), channel_id=1, source_target_pairs={{0,8},{1,9},{8,0},{9,1},{16,24},{17,25},{24,16},{25,17},{2,10},{3,... | collective-permute-start | bytes 1572872 | tf_op jit(solution)/shard_map/ppermute | solution.py:794
  105.3 24.3 %collective-permute-start.11 = (bf16[256,1024]{1,0:T(8,128)(2,1)}, bf16[256,1024]{1,0:T(8,128)(2,1)S(1)}, u32[]{:S(2)}, u32[]{:S(2)}) collective-permute-start(bf16[256,1024]{1,0:T(8,128)(2,1)} %get-tuple-element.64), channel_id=1, source_target_pairs={{0,16},{1,17},{8,24},{9,25},{16,0},{17,1},{24,8},{25,9},{2,18},{3,... | collective-permute-start | bytes 1572872 | tf_op jit(solution)/shard_map/ppermute | solution.py:794
  106.8 32.7 %collective-permute-start.12 = (bf16[256,1024]{1,0:T(8,128)(2,1)}, bf16[256,1024]{1,0:T(8,128)(2,1)}, u32[]{:S(2)}, u32[]{:S(2)}) collective-permute-start(bf16[256,1024]{1,0:T(8,128)(2,1)} %get-tuple-element.65), channel_id=1, source_target_pairs={{0,24},{1,25},{8,16},{9,17},{16,8},{17,9},{24,0},{25,1},{2,26},{3,... | collective-permute-start | bytes 1572872 | tf_op jit(solution)/shard_map/ppermute | solution.py:794
  121.0 28.2 %collective-permute-start.13 = (bf16[512,1024]{1,0:T(8,128)(2,1)}, bf16[512,1024]{1,0:T(8,128)(2,1)}, u32[]{:S(2)}, u32[]{:S(2)}) collective-permute-start(bf16[512,1024]{1,0:T(8,128)(2,1)} %segment_rows.2.refs_0_), channel_id=1, source_target_pairs={{0,2},{2,0},{4,6},{6,4},{1,3},{3,1},{5,7},{7,5},{8,10},{10,8},{12,... | collective-permute-start | bytes 3145736 | tf_op jit(solution)/shard_map/ppermute | solution.py:792
  126.8 12.7 %copy-start.7 = (bf16[256,1024]{1,0:T(8,128)(2,1)S(1)}, bf16[256,1024]{1,0:T(8,128)(2,1)}, u32[]{:S(2)}) copy-start(bf16[256,1024]{1,0:T(8,128)(2,1)} %get-tuple-element.62.refs_0_) | copy-start | bytes 1572868

commit v7 on v6

--- a/solution.py
+++ b/solution.py
@@ -41,10 +41,10 @@
     del refs
 
 
-def after(array, *others):
+def after(array, *others, where=VMEM):
     return pl.pallas_call(
         after_kernel,
-        in_specs=[ANY] + [VMEM] * len(others),
+        in_specs=[ANY] + [where] * len(others),
         out_specs=ANY,
         out_shape=shape(array.shape, array.dtype),
         input_output_aliases={0: 0},
@@ -52,28 +52,26 @@
     )(array, *others)
 
 
-def split_kernel(source_ref, low_ref, high_ref, held, done):
-    cut = low_ref.shape[0]
-    parts = [pl.ds(0, cut), pl.ds(cut, source_ref.shape[0] - cut)]
-    for i, part in enumerate(parts):
-        pltpu.make_async_copy(source_ref.at[part], held.at[part], done.at[i]).start()
-    for i, (part, out_ref) in enumerate(zip(parts, (low_ref, high_ref))):
-        pltpu.make_async_copy(source_ref.at[part], held.at[part], done.at[i]).wait()
-        pltpu.make_async_copy(held.at[part], out_ref, done.at[i]).start()
-    for i, (part, out_ref) in enumerate(zip(parts, (low_ref, high_ref))):
-        pltpu.make_async_copy(held.at[part], out_ref, done.at[i]).wait()
-
-
-def split_rows(array, cut):
-    rows, width = array.shape
-    return pl.pallas_call(
-        split_kernel,
+def copy_kernel(source_ref, out_ref, held, done):
+    pieces = [pl.ds(i * (held.shape[0] // 4), held.shape[0] // 4) for i in range(4)]
+    loads = [load(source_ref.at[p], held.at[p], done.at[0, i]) for i, p in enumerate(pieces)]
+    stores = []
+    for i, p in enumerate(pieces):
+        loads[i].wait()
+        stores.append(load(held.at[p], out_ref.at[p], done.at[1, i]))
+    for store in stores:
+        store.wait()
+
+
+def copy_rows(array):
+    return pl.pallas_call(
+        copy_kernel,
         in_specs=[HBM],
-        out_specs=[HBM] * 2,
-        out_shape=[pltpu.HBM((cut, width), BF16), pltpu.HBM((rows - cut, width), BF16)],
-        scratch_shapes=[pltpu.VMEM(array.shape, BF16), pltpu.SemaphoreType.DMA((2,))],
-        compiler_params=params(),
-        name="split_rows",
+        out_specs=HBM,
+        out_shape=pltpu.HBM(array.shape, BF16),
+        scratch_shapes=[pltpu.VMEM(array.shape, BF16), pltpu.SemaphoreType.DMA((2, 4))],
+        compiler_params=params(),
+        name="copy_rows",
         cost_estimate=cost(0, 2),
     )(array)
 
@@ -89,7 +87,7 @@
 
     def fill(slab, carry):
         for pick in range(2 * refs):
-            there = (z + pick // refs * (planes // 2)) % planes
+            there = z if pick < refs else planes - 1 - z
             owner = (slab // ranks * planes + there) * ranks + slab % ranks
             made[slab, pick * height : (pick + 1) * height, :] = rows_ref[ids[pick % refs, owner]]
         sent(slab).start()
@@ -373,18 +371,24 @@
 
 
 def rest_kernel(
-    near_place, far_place, queries_ref, low_ref, high_ref, near_ref, far_ref, chosen_ref, chosen_others_ref, own_stats_ref,
+    near_place, far_place, queries_ref, inner_ref, outer_ref, near_ref, far_ref, chosen_ref, chosen_others_ref, own_stats_ref,
     other_logits_ref, saved_ref, far_logits_ref, stats_ref, near_target_ref, far_target_ref, others_ref, near_rows, far_rows,
     held, near_in, far_in, held_in, left, came,
 ):
     half = near_ref.shape[1] // 2
-    cut = low_ref.shape[0]
-    size = others_ref.shape[0]
     held_loads = load_chunks(far_ref.at[:, pl.ds(0, half)], held, held_in)
-    whole = [
-        load(low_ref, others_ref.at[pl.ds(0, cut)], came.at[0]),
-        load(high_ref, others_ref.at[pl.ds(cut, size - cut)], came.at[1]),
-    ]
+    z = lax.axis_index("z")
+    inner = (z > 0) & (z < lax.axis_size("z") - 1)
+
+    @pl.when(inner)
+    def _():
+        load(inner_ref, others_ref, came)
+
+    @pl.when(jnp.logical_not(inner))
+    def _():
+        load(outer_ref, others_ref, came)
+
+    whole = [pltpu.make_async_copy(outer_ref, others_ref, came)]
     near_loads = load_chunks(near_ref.at[:, pl.ds(half, half)], near_rows, near_in)
     far_loads = load_chunks(far_ref.at[:, pl.ds(half, half)], far_rows, far_in)
     put_targets(near_place, near_target_ref, chosen_ref, chosen_others_ref)
@@ -420,7 +424,7 @@
         store.wait()
 
 
-def rest_half(queries, low, high, near_slabs, far_slabs, chosen, chosen_others, own_stats, places):
+def rest_half(queries, inner, outer, near_slabs, far_slabs, chosen, chosen_others, own_stats, places):
     size, width = queries.shape
     rows = near_slabs.shape[0] * near_slabs.shape[1] // 2
     part = (near_slabs.shape[0], near_slabs.shape[1] // 2, width)
@@ -440,11 +444,11 @@
             shape(part, BF16),
             shape(part, BF16),
         ],
-        scratch_shapes=[pltpu.VMEM(part, BF16)] + [chunk_sems] * 4 + [pltpu.SemaphoreType.DMA((2,))],
+        scratch_shapes=[pltpu.VMEM(part, BF16)] + [chunk_sems] * 4 + [pltpu.SemaphoreType.DMA],
         compiler_params=params(),
         name="rest_half",
         cost_estimate=cost(3 << 29, 8),
-    )(queries, low, high, near_slabs, far_slabs, chosen, chosen_others, own_stats)
+    )(queries, inner, outer, near_slabs, far_slabs, chosen, chosen_others, own_stats)
 
 
 def log_totals(here_ref, there_ref):
@@ -746,36 +750,37 @@
     slabs = groups * ranks
     z = lax.axis_index("z")
     to_pair = [(i, i ^ 1) for i in range(planes)]
-    across = [(i, (i + planes // 2) % planes) for i in range(planes)]
+    across = [(i, planes - 1 - i) for i in range(planes)]
 
     def exchange(slab_array):
         return lax.all_to_all(slab_array, PLANE, split_axis=0, concat_axis=0, tiled=True)
 
     ids = block_ids.T
-    early = queries.shape[0] * 3 // 8
     own_rows = jnp.transpose(passages, (1, 0, 2))
     near_slabs = in_hbm(exchange(gather_rows(ids, own_rows, slabs, planes, ranks, 0)))
     pair_rows = lax.ppermute(passages.reshape(height * blocks, width), "z", to_pair)
-    low, high = split_rows(in_hbm(queries), early)
-    others_low = lax.ppermute(low, "z", across)
+    inner = [pair for pair in across if 0 < pair[0] < planes - 1]
+    outer = [pair for pair in across if pair not in inner]
+    others_inner = lax.ppermute(queries, "z", inner)
     others_positives = lax.ppermute(positives, "z", across).reshape(1, -1)
-    others_high = lax.ppermute(after(high, others_positives), "z", across)
 
     table = block_ids.reshape(groups, planes, ranks, refs)
-    both = jnp.stack([jnp.take(table, z, axis=1), jnp.take(table, (z + planes // 2) % planes, axis=1)], axis=2)
+    both = jnp.stack([jnp.take(table, z, axis=1), jnp.take(table, planes - 1 - z, axis=1)], axis=2)
     place = (jnp.arange(height, dtype=jnp.int32) * blocks + both.reshape(-1, 1)).reshape(1, -1)
     spread = (jnp.arange(height * blocks, dtype=jnp.int32)[:, None] == place).astype(BF16)
     by_shift = jnp.take(both.reshape(slabs, -1), plane_place(ranks) ^ jnp.arange(slabs), axis=0)
     near_place = (jnp.arange(height, dtype=jnp.int32) * blocks + by_shift.reshape(-1, 1)).reshape(1, -1)
     near_spread = (jnp.arange(height * blocks, dtype=jnp.int32)[:, None] == near_place).astype(BF16)
-    far_slabs = in_hbm(exchange(select_rows(spread, pair_rows, slabs)))
+    far_sent = select_rows(spread, pair_rows, slabs)
+    others_outer = lax.ppermute(after(copy_rows(in_hbm(queries)), in_hbm(far_sent), where=HBM), "z", outer)
+    far_slabs = in_hbm(exchange(far_sent))
 
     chosen = positives.reshape(1, -1)
     chosen_others = others_positives
     places = [functools.partial(place_of, far, planes, ranks, refs, height) for far in range(2)]
     own_logits, own_stats, own = own_half(in_hbm(queries), near_slabs, chosen, places[0])
     other_logits, saved_logits, far_logits, stats, near_target, far_target, others, near_rows, far_rows = rest_half(
-        own, others_low, others_high, near_slabs, far_slabs, chosen, chosen_others, own_stats, places
+        own, others_inner, others_outer, near_slabs, far_slabs, chosen, chosen_others, own_stats, places
     )
     partner = lax.ppermute(stats, "z", across)
     sums, hit = early_grads(stats, near_target, far_target, other_logits, far_logits, near_rows, far_rows)

time: 153 us -> 148 us (0.967)
  waiting for transfers between devices: 69.2 us -> 60.8 us
  starting transfers between devices: 33.5 us -> 36 us
    all_to_all x3, waiting for transfers between devices: 14.8 us -> 23.8 us  [exchange(): lax.all_to_all(slab_array, PLANE, split_axis=0, concat_axis=0, tiled=True)]
    ppermute x1, waiting for transfers between devices: 8.35 us -> 0.01 us  [on_device(): others_positives = lax.ppermute(positives, 'z', across).reshape(1, -1)]
    ppermute x2, waiting for transfers between devices: 19.5 us -> 11.7 us  [the longest x1 11.7 us: on_device(): lax.ppermute(after(copy_rows(in_hbm(queries)), in_hbm(far_sent), where=HB...]
    ppermute x1, waiting for transfers between devices: 7.13 us -> 0.66 us  [on_device(): pair_sum = lax.ppermute(far_sum, 'z', to_pair)]
    ppermute x3, waiting for transfers between devices: 9.93 us -> 15.7 us  [on_device(): lax.ppermute(array, PLANE, [(i, i ^ 2 * g) for i in range(slabs)])]
    ppermute x1, waiting for transfers between devices: 4.6 us -> 0.01 us  [on_device(): own_part = lax.ppermute(other_part, 'z', across)]
    ppermute x2, starting transfers between devices: 3.72 us -> 7.33 us  [the longest x1 5.71 us: on_device(): lax.ppermute(after(copy_rows(in_hbm(queries)), in_hbm(far_sent), where=HB...]
    ppermute x1, waiting for transfers between devices: 3.48 us -> 6.88 us  [on_device(): lax.ppermute(passages.reshape(height * blocks, width), 'z', to_pair)]
where the time goes in v7:
time: 148 us; the launch traced here: 146 us
  waiting for transfers between devices  60.8 us (41%)
  Pallas kernels  41.9 us (28%)
  starting transfers between devices  36 us (24%)
  local copies, waits for them, and re-layouts  5.09 us (3%)
    all_to_all x3, waiting for transfers between devices, exchange(): lax.all_to_all(slab_array, PLANE, split_axis=0, concat_axis=0, tiled=True)  23.8 us
    ppermute x3, waiting for transfers between devices, on_device(): lax.ppermute(array, PLANE, [(i, i ^ 2 * g) for i in range(slabs)])  15.7 us
    all_to_all x3, starting transfers between devices, exchange(): lax.all_to_all(slab_array, PLANE, split_axis=0, concat_axis=0, tiled=True)  13.3 us
    ppermute x1, waiting for transfers between devices, on_device(): lax.ppermute(after(copy_rows(in_hbm(queries)), in_hbm(far_sent), where=HB...  11.7 us
    pallas_call x1, Pallas kernels, near_grads(): pl.pallas_call(functools.partial(near_kernel, ranks), in_specs=[VMEM] * 4...  7.19 us
    ppermute x1, waiting for transfers between devices, on_device(): lax.ppermute(passages.reshape(height * blocks, width), 'z', to_pair)  6.88 us
    pallas_call x2, Pallas kernels, segment_rows(): pl.pallas_call(functools.partial(segment_kernel, stripes, len(arrays)), i...  5.98 us
    ppermute x1, starting transfers between devices, on_device(): lax.ppermute(after(copy_rows(in_hbm(queries)), in_hbm(far_sent), where=HB...  5.71 us
  transfers between devices with their start and end apart: 17, of which 13 were waited for; matrix products, arithmetic and copies ran while one was open for 3% of the time, Pallas kernels for 22%

profile of v7, /device:TPU:0, one launch (start us, length us, event | category | flops | bytes accessed | tf_op | source)
XLA Modules:
  0.0 146.3 jit_solution(186216370273799246)
XLA Ops:
  0.6 3.1 %collective-permute-start.1 = (bf16[512,1024]{1,0:T(8,128)(2,1)}, bf16[512,1024]{1,0:T(8,128)(2,1)S(1)}, u32[]{:S(2)}, u32[]{:S(2)}) collective-permute-start(bf16[512,1024]{1,0:T(8,128)(2,1)} %bitcast.21), channel_id=1, source_target_pairs={{0,2},{2,0},{4,6},{6,4},{1,3},{3,1},{5,7},{7,5},{8,10},{10,8},{12,... | collective-permute-start | bytes 3145736 | tf_op jit(solution)/shard_map/ppermute | solution.py:761
  3.7 1.8 %copy.17 = bf16[16,32,1024]{2,0,1:T(8,128)(2,1)S(1)} copy(bf16[16,32,1024]{2,1,0:T(8,128)(2,1)} %param.7) | data formatting | bytes 2097152 | tf_op args[1]
  5.6 2.0 %gather_rows.1 = bf16[8,128,1024]{2,1,0:T(8,128)(2,1)} custom-call(s32[4,32]{1,0:T(4,128)S(1)} %bitcast.20, bf16[32,16,1024]{2,1,0:T(8,128)(2,1)S(1)} %bitcast.19), custom_call_target="tpu_custom_call" | custom-call | bytes 4194304 | tf_op jit(solution)/shard_map/gather_rows/pallas_call | solution.py:107
  7.6 4.4 %all-to-all-start = ((bf16[8,128,1024]{2,1,0:T(8,128)(2,1)}), bf16[8,128,1024]{2,1,0:T(8,128)(2,1)}, u32[]{:S(2)}, u32[]{:S(2)}) async-start(bf16[8,128,1024]{2,1,0:T(8,128)(2,1)} %gather_rows.1), calls=%async_computation | async-start | bytes 4194304 | tf_op jit(solution)/shard_map/all_to_all | solution.py:756
  12.0 1.6 %collective-permute-start = (bf16[512,1024]{1,0:T(8,128)(2,1)}, bf16[512,1024]{1,0:T(8,128)(2,1)}, u32[]{:S(2)}, u32[]{:S(2)}) collective-permute-start(bf16[512,1024]{1,0:T(8,128)(2,1)} %source_ref.1), channel_id=1, source_target_pairs={{2,4},{4,2},{3,5},{5,3},{10,12},{12,10},{11,13},{13,11},{18,20},{2... | collective-permute-start | bytes 3145736 | tf_op jit(solution)/shard_map/ppermute | solution.py:764
  13.6 2.5 %collective-permute-start.3 = (s32[512]{0:T(512)}, s32[512]{0:T(512)}, u32[]{:S(2)}, u32[]{:S(2)}) collective-permute-start(s32[512]{0:T(512)} %param.9), channel_id=1, source_target_pairs={{0,6},{2,4},{4,2},{6,0},{1,7},{3,5},{5,3},{7,1},{8,14},{10,12},{12... | collective-permute-start | bytes 6152 | tf_op jit(solution)/shard_map/ppermute | solution.py:765
  16.4 2.0 %copy_rows.1.refs_0_ = bf16[512,1024]{1,0:T(8,128)(2,1)} custom-call(bf16[512,1024]{1,0:T(8,128)(2,1)} %source_ref.1), custom_call_target="tpu_custom_call" | custom-call | bytes 2097152 | tf_op jit(solution)/shard_map/copy_rows/pallas_call | solution.py:67
  20.2 6.9 %collective-permute-done.1.rows_ref = bf16[512,1024]{1,0:T(8,128)(2,1)S(1)} collective-permute-done((bf16[512,1024]{1,0:T(8,128)(2,1)}, bf16[512,1024]{1,0:T(8,128)(2,1)S(1)}, u32[]{:S(2)}, u32[]{:S(2)}) %collective-permute-start.1) | collective-permute-done | bytes 1048608 | tf_op jit(solution)/shard_map/ppermute | solution.py:761
  27.1 2.3 %select_rows.1.refs_1_ = bf16[8,128,1024]{2,1,0:T(8,128)(2,1)} custom-call(bf16[512,1024]{1,0:T(8,128)(2,1)S(1)} %fusion.spread_ref, bf16[512,1024]{1,0:T(8,128)(2,1)S(1)} %collective-permute-done.1.rows_ref), custom_call_target="tpu_custom_call" | custom-call | flops 137438953472 | bytes 4194304 | tf_op jit(solution)/shard_map/select_rows/pallas_call | solution.py:138
  30.4 5.7 %collective-permute-start.2 = (bf16[512,1024]{1,0:T(8,128)(2,1)}, bf16[512,1024]{1,0:T(8,128)(2,1)S(1)}, u32[]{:S(2)}, u32[]{:S(2)}) collective-permute-start(bf16[512,1024]{1,0:T(8,128)(2,1)} %after.1), channel_id=1, source_target_pairs={{0,6},{6,0},{1,7},{7,1},{8,14},{14,8},{9,15},{15,9},{16,22},{22,16... | collective-permute-start | bytes 3145736 | tf_op jit(solution)/shard_map/ppermute | solution.py:775
  36.1 2.5 %all-to-all-done.slabs_ref.near_ref = bf16[8,128,1024]{2,1,0:T(8,128)(2,1)} async-done(((bf16[8,128,1024]{2,1,0:T(8,128)(2,1)}), bf16[8,128,1024]{2,1,0:T(8,128)(2,1)}, u32[]{:S(2)}, u32[]{:S(2)}) %all-to-all-start) | async-done | bytes 2097184 | tf_op jit(solution)/shard_map/all_to_all | solution.py:756
  38.6 4.4 %all-to-all-start.1 = ((bf16[8,128,1024]{2,1,0:T(8,128)(2,1)}), bf16[8,128,1024]{2,1,0:T(8,128)(2,1)}, u32[]{:S(2)}, u32[]{:S(2)}) async-start(bf16[8,128,1024]{2,1,0:T(8,128)(2,1)} %select_rows.1.refs_1_), calls=%async_computation.1 | async-start | bytes 4194304 | tf_op jit(solution)/shard_map/all_to_all | solution.py:756
  43.0 4.1 %own_half.1 = (f32[512,512]{1,0:T(8,128)}, f32[8,512]{1,0:T(8,128)S(1)}, bf16[512,1024]{1,0:T(8,128)(2,1)S(1)}) custom-call(bf16[512,1024]{1,0:T(8,128)(2,1)} %source_ref.1, bf16[8,128,1024]{2,1,0:T(8,128)(2,1)} %all-to-all-done.slabs_ref.near_ref, s32[1,512]{1,0:T(1,128)} %bitcast.2.chosen_ref), custom_call_target="tpu_custom_call" | custom-call | flops 137438953472 | bytes 4194304 | tf_op jit(solution)/shard_map/own_half/pallas_call | solution.py:355
  47.2 11.7 %collective-permute-done.2.outer_ref = bf16[512,1024]{1,0:T(8,128)(2,1)S(1)} collective-permute-done((bf16[512,1024]{1,0:T(8,128)(2,1)}, bf16[512,1024]{1,0:T(8,128)(2,1)S(1)}, u32[]{:S(2)}, u32[]{:S(2)}) %collective-permute-start.2) | collective-permute-done | bytes 1048608 | tf_op jit(solution)/shard_map/ppermute | solution.py:775
  58.8 10.8 %all-to-all-done.1.far_ref = bf16[8,128,1024]{2,1,0:T(8,128)(2,1)} async-done(((bf16[8,128,1024]{2,1,0:T(8,128)(2,1)}), bf16[8,128,1024]{2,1,0:T(8,128)(2,1)}, u32[]{:S(2)}, u32[]{:S(2)}) %all-to-all-start.1) | async-done | bytes 2097184 | tf_op jit(solution)/shard_map/all_to_all | solution.py:756
  69.7 5.1 %rest_half.1 = (f32[512,512]{1,0:T(8,128)S(1)}, f32[512,512]{1,0:T(8,128)}, f32[2,512,512]{2,1,0:T(8,128)S(1)}, f32[8,512]{1,0:T(8,128)S(1)}, s32[8,512]{1,0:T(8...) custom-call(bf16[512,1024]{1,0:T(8,128)(2,1)S(1)} %get-tuple-element, ...), custom_call_target="tpu_custom_call" | custom-call | flops 1610612736 | bytes 8388608 | tf_op jit(solution)/shard_map/rest_half/pallas_call | solution.py:432
  74.8 2.5 %collective-permute-start.4 = (f32[8,512]{1,0:T(8,128)S(1)}, f32[8,512]{1,0:T(8,128)S(1)}, u32[]{:S(2)}, u32[]{:S(2)}) collective-permute-start(f32[8,512]{1,0:T(8,128)S(1)} %get-tuple-element.35.stats_ref.here_ref), channel_id=1, source_target_pairs={{0,6},{2,4},{4,2},{6,0},{1,7},{3,5},{5,3},{7,1},{8,14},{10,12},{12... | collective-permute-start | bytes 49160 | tf_op jit(solution)/shard_map/ppermute | solution.py:785
  77.4 2.4 %early_grads.1 = (f32[512,1024]{1,0:T(8,128)S(1)}, f32[512,1024]{1,0:T(8,128)S(1)}) custom-call(f32[8,512]{1,0:T(8,128)S(1)} %get-tuple-element.35.stats_ref.here_ref, s32[8,512]{1,0:T(8,128)S(1)} %get-tuple-element.36.near_target_ref.target_ref, s32[8,512]{1,0:T(8,128)S(1)} %get-tuple-element.37.far_target_ref.target_ref, ...), custom_call_target="tpu_custom_call" | custom-call | flops 137438953472 | bytes 4194304 | tf_op jit(solution)/shard_map/early_grads/pallas_call | solution.py:556
  80.4 2.0 %other_grads.1 = (bf16[512,1024]{1,0:T(8,128)(2,1)}, f32[8,512]{1,0:T(8,128)S(1)}, f32[1,512]{1,0:T(1,128)}) custom-call(f32[8,512]{1,0:T(8,128)S(1)} %get-tuple-element.35.stats_ref.here_ref, f32[8,512]{1,0:T(8,128)S(1)} %collective-permute-done.4.there_ref, s32[8,512]{1,0:T(8,128)S(1)} %get-tuple-element.36.near_target_ref.target_ref, ...), custom_call_target="tpu_custom_call" | custom-call | flops 1048576 | bytes 4194304 | tf_op jit(solution)/shard_map/other_grads/pallas_call | solution.py:595
  82.4 2.6 %collective-permute-start.5 = (bf16[512,1024]{1,0:T(8,128)(2,1)}, bf16[512,1024]{1,0:T(8,128)(2,1)}, u32[]{:S(2)}, u32[]{:S(2)}) collective-permute-start(bf16[512,1024]{1,0:T(8,128)(2,1)} %get-tuple-element.49.wait_ref), channel_id=1, source_target_pairs={{0,6},{2,4},{4,2},{6,0},{1,7},{3,5},{5,3},{7,1},{8,14},{10,12},{12... | collective-permute-start | bytes 3145736 | tf_op jit(solution)/shard_map/ppermute | solution.py:795
  85.0 2.3 %far_grads.1 = (bf16[8,128,1024]{2,1,0:T(8,128)(2,1)}, bf16[512,512]{1,0:T(8,128)(2,1)}) custom-call(bf16[512,1024]{1,0:T(8,128)(2,1)S(1)} %get-tuple-element.33.queries_ref, bf16[512,1024]{1,0:T(8,128)(2,1)S(1)} %get-tuple-element.45.others_ref, f32[2,512,512]{2,1,0:T(8,128)S(1)} %get-tuple-element.39.far_logits_ref.logits_ref, ...), custom_call_target="tpu_custom_call" | custom-call | flops 1073741824 | bytes 4194304 | tf_op jit(solution)/shard_map/far_grads/pallas_call | solution.py:631
  87.3 4.5 %all-to-all-start.2 = ((bf16[8,128,1024]{2,1,0:T(8,128)(2,1)}), bf16[8,128,1024]{2,1,0:T(8,128)(2,1)}, u32[]{:S(2)}, u32[]{:S(2)}) async-start(bf16[8,128,1024]{2,1,0:T(8,128)(2,1)} %get-tuple-element.52), calls=%async_computation.2 | async-start | bytes 4194304 | tf_op jit(solution)/shard_map/all_to_all | solution.py:756
  91.9 7.2 %near_grads.1 = (bf16[4,128,1024]{2,1,0:T(8,128)(2,1)}, bf16[128,1024]{1,0:T(8,128)(2,1)}, bf16[128,1024]{1,0:T(8,128)(2,1)}, bf16[128,1024]{1,0:T(8,128)(2,1)},...) custom-call(bf16[512,1024]{1,0:T(8,128)(2,1)S(1)} %get-tuple-element.33.queries_ref, ...), custom_call_target="tpu_custom_call" | custom-call | flops 137438953472 | bytes 8388608 | tf_op jit(solution)/shard_map/near_grads/pallas_call | solution.py:692
  103.3 1.6 %join_cores.1 = (bf16[256,1024]{1,0:T(8,128)(2,1)}, bf16[256,1024]{1,0:T(8,128)(2,1)}, bf16[256,1024]{1,0:T(8,128)(2,1)}, bf16[256,1024]{1,0:T(8,128)(2,1)}) custom-call(bf16[4,128,1024]{2,1,0:T(8,128)(2,1)S(1)} %copy-done.2, bf16[128,1024]{1,0:T(8,128)(2,1)S(1)} %collective-permute-done.6.refs_0_, bf16[128,1024]{1,0:T(8,128)(2,1)S(1)} %collective-permute-done.7.refs_1_, ...), custom_call_target="tpu_custom_call" | custom-call | flops 1048576 | bytes 4194304 | tf_op jit(solution)/shard_map/join_cores/pallas_call | solution.py:171
  104.9 1.8 %collective-permute-start.10 = (bf16[256,1024]{1,0:T(8,128)(2,1)}, bf16[256,1024]{1,0:T(8,128)(2,1)S(1)}, u32[]{:S(2)}, u32[]{:S(2)}) collective-permute-start(bf16[256,1024]{1,0:T(8,128)(2,1)} %get-tuple-element.59), channel_id=1, source_target_pairs={{0,8},{1,9},{8,0},{9,1},{16,24},{17,25},{24,16},{25,17},{2,10},{3,... | collective-permute-start | bytes 1572872 | tf_op jit(solution)/shard_map/ppermute | solution.py:799
  108.4 10.4 %all-to-all-done.2 = bf16[8,128,1024]{2,1,0:T(8,128)(2,1)} async-done(((bf16[8,128,1024]{2,1,0:T(8,128)(2,1)}), bf16[8,128,1024]{2,1,0:T(8,128)(2,1)}, u32[]{:S(2)}, u32[]{:S(2)}) %all-to-all-start.2) | async-done | bytes 2097184 | tf_op jit(solution)/shard_map/all_to_all | solution.py:756
  118.9 3.5 %segment_rows.2.refs_0_ = bf16[512,1024]{1,0:T(8,128)(2,1)} custom-call(bf16[512,1024]{1,0:T(8,128)(2,1)S(1)} %copy-done.1, bf16[1024,1024]{1,0:T(8,128)(2,1)} %bitcast.11.refs_0_), custom_call_target="tpu_custom_call" | custom-call | flops 1073741824 | bytes 4194304 | tf_op jit(solution)/shard_map/segment_rows/pallas_call | solution.py:230
  122.5 2.7 %add_parts.2.refs_4_ = bf16[512,1024]{1,0:T(8,128)(2,1)} custom-call(f32[512,1024]{1,0:T(8,128)} %get-tuple-element.51.own_ref, bf16[512,1024]{1,0:T(8,128)(2,1)} %collective-permute-done.5.part_ref, bf16[512,1024]{1,0:T(8,128)(2,1)} %segment_rows.2.refs_0_), custom_call_target="tpu_custom_call" | custom-call | flops 137438953472 | bytes 4194304 | tf_op jit(solution)/shard_map/add_parts/pallas_call | solution.py:729
  125.2 3.9 %collective-permute-done.10.refs_1_ = bf16[256,1024]{1,0:T(8,128)(2,1)S(1)} collective-permute-done((bf16[256,1024]{1,0:T(8,128)(2,1)}, bf16[256,1024]{1,0:T(8,128)(2,1)S(1)}, u32[]{:S(2)}, u32[]{:S(2)}) %collective-permute-start.10) | collective-permute-done | bytes 524320 | tf_op jit(solution)/shard_map/ppermute | solution.py:799
  129.1 11.8 %collective-permute-done.12.refs_3_ = bf16[256,1024]{1,0:T(8,128)(2,1)} collective-permute-done((bf16[256,1024]{1,0:T(8,128)(2,1)}, bf16[256,1024]{1,0:T(8,128)(2,1)}, u32[]{:S(2)}, u32[]{:S(2)}) %collective-permute-start.12) | collective-permute-done | bytes 524320 | tf_op jit(solution)/shard_map/ppermute | solution.py:799
  140.9 2.5 %segment_rows.3.own_ref = f32[512,1024]{1,0:T(8,128)S(1)} custom-call(bf16[512,1024]{1,0:T(8,128)(2,1)S(1)} %fusion.1.spread_ref, bf16[256,1024]{1,0:T(8,128)(2,1)S(1)} %copy-done.4, bf16[256,1024]{1,0:T(8,128)(2,1)S(1)} %collective-permute-done.10.refs_1_, bf16[256,1024]{1,0:T(8,128)(2,1)S(1)} %collective-permute-done.11.refs_2_, ...), custom_call_target="tpu_custom_call" | custom-call | flops 137438953472 | bytes 4194304 | tf_op jit(solution)/shard_map/segment_rows/pallas_call | solution.py:230
  144.1 2.1 %add_parts.3 = bf16[512,1024]{1,0:T(8,128)(2,1)} custom-call(f32[512,1024]{1,0:T(8,128)S(1)} %segment_rows.3.own_ref, bf16[512,1024]{1,0:T(8,128)(2,1)} %collective-permute-done.13.part_ref), custom_call_target="tpu_custom_call" | custom-call | flops 1048576 | bytes 4194304 | tf_op jit(solution)/shard_map/add_parts/pallas_call | solution.py:729
  (48 shorter events, 10.4 us)
Async XLA Ops:
  0.6 4.9 %copy-start.3 = (s32[32,4]{0,1:T(4,128)S(1)}, s32[32,4]{0,1:T(4,128)}, u32[]{:S(2)}) copy-start(s32[32,4]{0,1:T(4,128)} %param.8) | copy-start | bytes 1540
  0.6 26.5 %collective-permute-start.1 = (bf16[512,1024]{1,0:T(8,128)(2,1)}, bf16[512,1024]{1,0:T(8,128)(2,1)S(1)}, u32[]{:S(2)}, u32[]{:S(2)}) collective-permute-start(bf16[512,1024]{1,0:T(8,128)(2,1)} %bitcast.21), channel_id=1, source_target_pairs={{0,2},{2,0},{4,6},{6,4},{1,3},{3,1},{5,7},{7,5},{8,10},{10,8},{12,... | collective-permute-start | bytes 3145736 | tf_op jit(solution)/shard_map/ppermute | solution.py:761
  7.6 31.0 %all-to-all-start = ((bf16[8,128,1024]{2,1,0:T(8,128)(2,1)}), bf16[8,128,1024]{2,1,0:T(8,128)(2,1)}, u32[]{:S(2)}, u32[]{:S(2)}) async-start(bf16[8,128,1024]{2,1,0:T(8,128)(2,1)} %gather_rows.1), calls=%async_computation | async-start | bytes 4194304 | tf_op jit(solution)/shard_map/all_to_all | solution.py:756
  12.0 35.2 %collective-permute-start = (bf16[512,1024]{1,0:T(8,128)(2,1)}, bf16[512,1024]{1,0:T(8,128)(2,1)}, u32[]{:S(2)}, u32[]{:S(2)}) collective-permute-start(bf16[512,1024]{1,0:T(8,128)(2,1)} %source_ref.1), channel_id=1, source_target_pairs={{2,4},{4,2},{3,5},{5,3},{10,12},{12,10},{11,13},{13,11},{18,20},{2... | collective-permute-start | bytes 3145736 | tf_op jit(solution)/shard_map/ppermute | solution.py:764
  13.6 33.5 %collective-permute-start.3 = (s32[512]{0:T(512)}, s32[512]{0:T(512)}, u32[]{:S(2)}, u32[]{:S(2)}) collective-permute-start(s32[512]{0:T(512)} %param.9), channel_id=1, source_target_pairs={{0,6},{2,4},{4,2},{6,0},{1,7},{3,5},{5,3},{7,1},{8,14},{10,12},{12... | collective-permute-start | bytes 6152 | tf_op jit(solution)/shard_map/ppermute | solution.py:765
  29.4 1.0 copy-start
  30.4 28.4 %collective-permute-start.2 = (bf16[512,1024]{1,0:T(8,128)(2,1)}, bf16[512,1024]{1,0:T(8,128)(2,1)S(1)}, u32[]{:S(2)}, u32[]{:S(2)}) collective-permute-start(bf16[512,1024]{1,0:T(8,128)(2,1)} %after.1), channel_id=1, source_target_pairs={{0,6},{6,0},{1,7},{7,1},{8,14},{14,8},{9,15},{15,9},{16,22},{22,16... | collective-permute-start | bytes 3145736 | tf_op jit(solution)/shard_map/ppermute | solution.py:775
  38.6 31.0 %all-to-all-start.1 = ((bf16[8,128,1024]{2,1,0:T(8,128)(2,1)}), bf16[8,128,1024]{2,1,0:T(8,128)(2,1)}, u32[]{:S(2)}, u32[]{:S(2)}) async-start(bf16[8,128,1024]{2,1,0:T(8,128)(2,1)} %select_rows.1.refs_1_), calls=%async_computation.1 | async-start | bytes 4194304 | tf_op jit(solution)/shard_map/all_to_all | solution.py:756
  74.8 5.6 %collective-permute-start.4 = (f32[8,512]{1,0:T(8,128)S(1)}, f32[8,512]{1,0:T(8,128)S(1)}, u32[]{:S(2)}, u32[]{:S(2)}) collective-permute-start(f32[8,512]{1,0:T(8,128)S(1)} %get-tuple-element.35.stats_ref.here_ref), channel_id=1, source_target_pairs={{0,6},{2,4},{4,2},{6,0},{1,7},{3,5},{5,3},{7,1},{8,14},{10,12},{12... | collective-permute-start | bytes 49160 | tf_op jit(solution)/shard_map/ppermute | solution.py:785
  82.4 40.0 %collective-permute-start.5 = (bf16[512,1024]{1,0:T(8,128)(2,1)}, bf16[512,1024]{1,0:T(8,128)(2,1)}, u32[]{:S(2)}, u32[]{:S(2)}) collective-permute-start(bf16[512,1024]{1,0:T(8,128)(2,1)} %get-tuple-element.49.wait_ref), channel_id=1, source_target_pairs={{0,6},{2,4},{4,2},{6,0},{1,7},{3,5},{5,3},{7,1},{8,14},{10,12},{12... | collective-permute-start | bytes 3145736 | tf_op jit(solution)/shard_map/ppermute | solution.py:795
  87.3 31.5 %all-to-all-start.2 = ((bf16[8,128,1024]{2,1,0:T(8,128)(2,1)}), bf16[8,128,1024]{2,1,0:T(8,128)(2,1)}, u32[]{:S(2)}, u32[]{:S(2)}) async-start(bf16[8,128,1024]{2,1,0:T(8,128)(2,1)} %get-tuple-element.52), calls=%async_computation.2 | async-start | bytes 4194304 | tf_op jit(solution)/shard_map/all_to_all | solution.py:756
  91.9 8.3 %copy-start.5 = (s32[64,16]{1,0:T(8,128)S(1)}, s32[64,16]{1,0:T(8,128)}, u32[]{:S(2)}) copy-start(s32[64,16]{1,0:T(8,128)} %get-tuple-element.75) | copy-start | bytes 12292
  99.1 19.8 %copy-start.1 = (bf16[512,1024]{1,0:T(8,128)(2,1)S(1)}, bf16[512,1024]{1,0:T(8,128)(2,1)}, u32[]{:S(2)}) copy-start(bf16[512,1024]{1,0:T(8,128)(2,1)} %copy-done) | copy-start | bytes 3145732
  99.1 1.8 %collective-permute-start.6 = (bf16[128,1024]{1,0:T(8,128)(2,1)}, bf16[128,1024]{1,0:T(8,128)(2,1)S(1)}, u32[]{:S(2)}, u32[]{:S(2)}) collective-permute-start(bf16[128,1024]{1,0:T(8,128)(2,1)} %get-tuple-element.54), channel_id=1, source_target_pairs={{0,1},{1,0},{8,9},{9,8},{16,17},{17,16},{24,25},{25,24},{2,3},{3,2... | collective-permute-start | bytes 786440 | tf_op jit(solution)/shard_map/ppermute | solution.py:794
  99.4 1.9 %collective-permute-start.7 = (bf16[128,1024]{1,0:T(8,128)(2,1)}, bf16[128,1024]{1,0:T(8,128)(2,1)S(1)}, u32[]{:S(2)}, u32[]{:S(2)}) collective-permute-start(bf16[128,1024]{1,0:T(8,128)(2,1)} %get-tuple-element.55), channel_id=1, source_target_pairs={{0,1},{1,0},{8,9},{9,8},{16,17},{17,16},{24,25},{25,24},{2,3},{3,2... | collective-permute-start | bytes 786440 | tf_op jit(solution)/shard_map/ppermute | solution.py:794
  99.7 2.0 %collective-permute-start.8 = (bf16[128,1024]{1,0:T(8,128)(2,1)}, bf16[128,1024]{1,0:T(8,128)(2,1)S(1)}, u32[]{:S(2)}, u32[]{:S(2)}) collective-permute-start(bf16[128,1024]{1,0:T(8,128)(2,1)} %get-tuple-element.56), channel_id=1, source_target_pairs={{0,1},{1,0},{8,9},{9,8},{16,17},{17,16},{24,25},{25,24},{2,3},{3,2... | collective-permute-start | bytes 786440 | tf_op jit(solution)/shard_map/ppermute | solution.py:794
  99.9 2.2 %collective-permute-start.9 = (bf16[128,1024]{1,0:T(8,128)(2,1)}, bf16[128,1024]{1,0:T(8,128)(2,1)S(1)}, u32[]{:S(2)}, u32[]{:S(2)}) collective-permute-start(bf16[128,1024]{1,0:T(8,128)(2,1)} %get-tuple-element.57), channel_id=1, source_target_pairs={{0,1},{1,0},{8,9},{9,8},{16,17},{17,16},{24,25},{25,24},{2,3},{3,2... | collective-permute-start | bytes 786440 | tf_op jit(solution)/shard_map/ppermute | solution.py:794
  102.0 1.2 copy-start.2
  104.9 24.2 %collective-permute-start.10 = (bf16[256,1024]{1,0:T(8,128)(2,1)}, bf16[256,1024]{1,0:T(8,128)(2,1)S(1)}, u32[]{:S(2)}, u32[]{:S(2)}) collective-permute-start(bf16[256,1024]{1,0:T(8,128)(2,1)} %get-tuple-element.59), channel_id=1, source_target_pairs={{0,8},{1,9},{8,0},{9,1},{16,24},{17,25},{24,16},{25,17},{2,10},{3,... | collective-permute-start | bytes 1572872 | tf_op jit(solution)/shard_map/ppermute | solution.py:799
  106.7 22.4 %collective-permute-start.11 = (bf16[256,1024]{1,0:T(8,128)(2,1)}, bf16[256,1024]{1,0:T(8,128)(2,1)S(1)}, u32[]{:S(2)}, u32[]{:S(2)}) collective-permute-start(bf16[256,1024]{1,0:T(8,128)(2,1)} %get-tuple-element.60), channel_id=1, source_target_pairs={{0,16},{1,17},{8,24},{9,25},{16,0},{17,1},{24,8},{25,9},{2,18},{3,... | collective-permute-start | bytes 1572872 | tf_op jit(solution)/shard_map/ppermute | solution.py:799
  108.1 32.7 %collective-permute-start.12 = (bf16[256,1024]{1,0:T(8,128)(2,1)}, bf16[256,1024]{1,0:T(8,128)(2,1)}, u32[]{:S(2)}, u32[]{:S(2)}) collective-permute-start(bf16[256,1024]{1,0:T(8,128)(2,1)} %get-tuple-element.61), channel_id=1, source_target_pairs={{0,24},{1,25},{8,16},{9,17},{16,8},{17,9},{24,0},{25,1},{2,26},{3,... | collective-permute-start | bytes 1572872 | tf_op jit(solution)/shard_map/ppermute | solution.py:799
  122.4 21.7 %collective-permute-start.13 = (bf16[512,1024]{1,0:T(8,128)(2,1)}, bf16[512,1024]{1,0:T(8,128)(2,1)}, u32[]{:S(2)}, u32[]{:S(2)}) collective-permute-start(bf16[512,1024]{1,0:T(8,128)(2,1)} %segment_rows.2.refs_0_), channel_id=1, source_target_pairs={{0,2},{2,0},{4,6},{6,4},{1,3},{3,1},{5,7},{7,5},{8,10},{10,8},{12,... | collective-permute-start | bytes 3145736 | tf_op jit(solution)/shard_map/ppermute | solution.py:797
  122.4 18.4 %copy-start.4 = (bf16[256,1024]{1,0:T(8,128)(2,1)S(1)}, bf16[256,1024]{1,0:T(8,128)(2,1)}, u32[]{:S(2)}) copy-start(bf16[256,1024]{1,0:T(8,128)(2,1)} %get-tuple-element.58.refs_0_) | copy-start | bytes 1572868

commit v8 on v7

--- a/solution.py
+++ b/solution.py
@@ -564,9 +564,9 @@
     )(stats, near_target, far_target, near_logits, far_logits, near_rows, far_rows)
 
 
-def other_kernel(here_ref, there_ref, near_target_ref, far_target_ref, sums_ref, hit_ref, other_ref, totals_ref, loss_ref, made, left):
-    totals = log_totals(here_ref, there_ref)
-    total = totals[1][0]
+def other_kernel(here_ref, totals_ref, near_target_ref, far_target_ref, sums_ref, hit_ref, wait_ref, other_ref, made, left):
+    del wait_ref
+    total = totals_ref[1:2, :]
     top, _, pick = stat_rows(here_ref, 1)
     held = jnp.maximum(near_target_ref[1:2, :], far_target_ref[1:2, :]) >= 0
     scale = jnp.exp(top - total)
@@ -582,38 +582,39 @@
         made[part, :] = (SCALE * share).astype(BF16)
         some = pl.ds(c * size, size)
         stores.append(load(made.at[some], other_ref.at[some], left.at[c]))
+    for store in stores:
+        store.wait()
+
+
+def other_grads(here, totals, near_target, far_target, sums, hit, wait):
+    size, width = sums.shape
+    return pl.pallas_call(
+        other_kernel,
+        in_specs=[VMEM] * 6 + [HBM],
+        out_specs=HBM,
+        out_shape=pltpu.HBM((size, width), BF16),
+        scratch_shapes=[pltpu.VMEM((size, width), BF16), pltpu.SemaphoreType.DMA((4,))],
+        compiler_params=params(),
+        name="other_grads",
+        cost_estimate=cost(1 << 20, 4),
+    )(here, totals, near_target, far_target, sums, hit, wait)
+
+
+def far_kernel(
+    queries_ref, others_ref, logits_ref, target_ref, here_ref, there_ref, wait_ref,
+    contrib_ref, pieces_ref, totals_ref, loss_ref, made, left, pieces, pieces_out,
+):
+    del wait_ref
+    totals = log_totals(here_ref, there_ref)
     totals_ref[...] = jnp.zeros_like(totals_ref)
     for q in range(2):
         totals_ref[q : q + 1, :] = totals[q][0]
     loss_ref[...] = totals[0][0] - totals[0][1]
-    for store in stores:
-        store.wait()
-
-
-def other_grads(here, there, near_target, far_target, sums, hit):
-    size, width = sums.shape
-    return pl.pallas_call(
-        other_kernel,
-        in_specs=[VMEM] * 6,
-        out_specs=[HBM, VMEM, VMEM],
-        out_shape=[pltpu.HBM((size, width), BF16), shape((8, size), F32), shape((1, size), F32)],
-        scratch_shapes=[pltpu.VMEM((size, width), BF16), pltpu.SemaphoreType.DMA((4,))],
-        compiler_params=params(),
-        name="other_grads",
-        cost_estimate=cost(1 << 20, 4),
-    )(here, there, near_target, far_target, sums, hit)
-
-
-def far_kernel(
-    queries_ref, others_ref, logits_ref, target_ref, totals_ref, wait_ref,
-    contrib_ref, pieces_ref, made, left, pieces, pieces_out,
-):
-    del wait_ref
     slabs, depth, width = contrib_ref.shape
     half = depth // 2
     stores = []
     for q, block_ref in enumerate((queries_ref, others_ref)):
-        piece = dlogits(logits_ref[q], totals_ref[q : q + 1, :], 0, target_ref[q : q + 1, :])
+        piece = dlogits(logits_ref[q], totals[q][0], 0, target_ref[q : q + 1, :])
         if q == 0:
             pieces[...] = piece
             stores.append(load(pieces, pieces_ref, pieces_out))
@@ -624,15 +625,20 @@
         store.wait()
 
 
-def far_grads(queries, others, logits, target, totals, wait, slabs):
+def far_grads(queries, others, logits, target, here, there, wait, slabs):
     size = queries.shape[0]
     rows = logits.shape[1]
     count, depth, width = slabs.shape
     return pl.pallas_call(
         far_kernel,
-        in_specs=[VMEM] * 5 + [ANY],
-        out_specs=[HBM] * 2,
-        out_shape=[pltpu.HBM(slabs.shape, BF16), pltpu.HBM((rows, size), BF16)],
+        in_specs=[VMEM] * 7,
+        out_specs=[HBM] * 2 + [VMEM] * 2,
+        out_shape=[
+            pltpu.HBM(slabs.shape, BF16),
+            pltpu.HBM((rows, size), BF16),
+            shape((8, size), F32),
+            shape((1, size), F32),
+        ],
         scratch_shapes=[
             pltpu.VMEM((2, count, depth // 2, width), BF16),
             pltpu.SemaphoreType.DMA((2,)),
@@ -642,7 +648,7 @@
         compiler_params=params(),
         name="far_grads",
         cost_estimate=cost(1 << 30, 4),
-    )(queries, others, logits, target, totals, wait)
+    )(queries, others, logits, target, here, there, wait)
 
 
 def near_kernel(
@@ -701,7 +707,7 @@
         + [pltpu.VMEM(near_slabs.shape, BF16), pltpu.SemaphoreType.DMA((slabs,))],
         compiler_params=params(),
         name="near_grads",
-        cost_estimate=cost(BUSY, 8),
+        cost_estimate=cost(2 << 30, 8),
     )(queries, others, target, totals, own_logits, other_logits, pieces, near_slabs, far_slabs)
 
 
@@ -784,12 +790,15 @@
     )
     partner = lax.ppermute(stats, "z", across)
     sums, hit = early_grads(stats, near_target, far_target, other_logits, far_logits, near_rows, far_rows)
-    other_part, totals, loss = other_grads(stats, partner, near_target, far_target, sums, hit)
     own_logits, other_logits = in_hbm(own_logits), in_hbm(saved_logits)
-    far_contrib, pieces = far_grads(own, others, far_logits, far_target, totals, in_hbm(other_part), far_slabs)
+    far_contrib, pieces, totals, loss = far_grads(
+        own, others, far_logits, far_target, stats, partner, hit, far_slabs
+    )
+    pieces = in_hbm(pieces)
+    other_part = other_grads(stats, totals, near_target, far_target, sums, hit, pieces)
     far_back = in_hbm(exchange(far_contrib).reshape(-1, width))
     kept, *given, own_grad = near_grads(
-        own, others, near_target, totals, own_logits, other_logits, in_hbm(pieces), near_slabs, far_slabs, ranks
+        own, others, near_target, totals, own_logits, other_logits, pieces, near_slabs, far_slabs, ranks
     )
     joined = join_cores(kept, [lax.ppermute(array, PLANE, [(i, i ^ 1) for i in range(slabs)]) for array in given])
     own_part = lax.ppermute(other_part, "z", across)

time: 148 us -> 144 us (0.973)
  waiting for transfers between devices: 60.8 us -> 56.1 us
  local copies, waits for them, and re-layouts: 5.09 us -> 6.69 us
    all_to_all x3, waiting for transfers between devices: 23.8 us -> 18.2 us  [exchange(): lax.all_to_all(slab_array, PLANE, split_axis=0, concat_axis=0, tiled=True)]
    unnamed x14 -> x22, local copies, waits for them, and re-layouts: 4.13 us -> 5.73 us
  transfers between devices with their start and end apart: 17 -> 17, of which waited for: 13 -> 15; matrix products, arithmetic and copies ran while one was open for 3% -> 3% of each run, Pallas kernels for 22% -> 22%
where the time goes in v8:
time: 144 us; the launch traced here: 143 us
  waiting for transfers between devices  56.1 us (39%)
  Pallas kernels  41.9 us (29%)
  starting transfers between devices  36 us (25%)
  local copies, waits for them, and re-layouts  6.69 us (5%)
    all_to_all x3, waiting for transfers between devices, exchange(): lax.all_to_all(slab_array, PLANE, split_axis=0, concat_axis=0, tiled=True)  18.2 us
    ppermute x3, waiting for transfers between devices, on_device(): lax.ppermute(array, PLANE, [(i, i ^ 2 * g) for i in range(slabs)])  15.5 us
    all_to_all x3, starting transfers between devices, exchange(): lax.all_to_all(slab_array, PLANE, split_axis=0, concat_axis=0, tiled=True)  13.3 us
    ppermute x1, waiting for transfers between devices, on_device(): lax.ppermute(after(copy_rows(in_hbm(queries)), in_hbm(far_sent), where=HB...  11.7 us
    pallas_call x1, Pallas kernels, near_grads(): pl.pallas_call(functools.partial(near_kernel, ranks), in_specs=[VMEM] * 4...  7.18 us
    ppermute x1, waiting for transfers between devices, on_device(): lax.ppermute(passages.reshape(height * blocks, width), 'z', to_pair)  6.88 us
    pallas_call x2, Pallas kernels, segment_rows(): pl.pallas_call(functools.partial(segment_kernel, stripes, len(arrays)), i...  5.98 us
    unnamed x22, local copies, waits for them, and re-layouts  5.73 us
  transfers between devices with their start and end apart: 17, of which 15 were waited for; matrix products, arithmetic and copies ran while one was open for 3% of the time, Pallas kernels for 22%

profile of v8, /device:TPU:0, one launch (start us, length us, event | category | flops | bytes accessed | tf_op | source)
XLA Modules:
  0.0 143.2 jit_solution(4027342386262953565)
XLA Ops:
  0.6 3.1 %collective-permute-start.1 = (bf16[512,1024]{1,0:T(8,128)(2,1)}, bf16[512,1024]{1,0:T(8,128)(2,1)S(1)}, u32[]{:S(2)}, u32[]{:S(2)}) collective-permute-start(bf16[512,1024]{1,0:T(8,128)(2,1)} %bitcast.21), channel_id=1, source_target_pairs={{0,2},{2,0},{4,6},{6,4},{1,3},{3,1},{5,7},{7,5},{8,10},{10,8},{12,... | collective-permute-start | bytes 3145736 | tf_op jit(solution)/shard_map/ppermute | solution.py:767
  3.7 1.8 %copy.17 = bf16[16,32,1024]{2,0,1:T(8,128)(2,1)S(1)} copy(bf16[16,32,1024]{2,1,0:T(8,128)(2,1)} %param.7) | data formatting | bytes 2097152 | tf_op args[1]
  5.6 2.0 %gather_rows.1 = bf16[8,128,1024]{2,1,0:T(8,128)(2,1)} custom-call(s32[4,32]{1,0:T(4,128)S(1)} %bitcast.20, bf16[32,16,1024]{2,1,0:T(8,128)(2,1)S(1)} %bitcast.19), custom_call_target="tpu_custom_call" | custom-call | bytes 4194304 | tf_op jit(solution)/shard_map/gather_rows/pallas_call | solution.py:107
  7.6 4.4 %all-to-all-start = ((bf16[8,128,1024]{2,1,0:T(8,128)(2,1)}), bf16[8,128,1024]{2,1,0:T(8,128)(2,1)}, u32[]{:S(2)}, u32[]{:S(2)}) async-start(bf16[8,128,1024]{2,1,0:T(8,128)(2,1)} %gather_rows.1), calls=%async_computation | async-start | bytes 4194304 | tf_op jit(solution)/shard_map/all_to_all | solution.py:762
  12.0 1.6 %collective-permute-start = (bf16[512,1024]{1,0:T(8,128)(2,1)}, bf16[512,1024]{1,0:T(8,128)(2,1)}, u32[]{:S(2)}, u32[]{:S(2)}) collective-permute-start(bf16[512,1024]{1,0:T(8,128)(2,1)} %source_ref.1), channel_id=1, source_target_pairs={{2,4},{4,2},{3,5},{5,3},{10,12},{12,10},{11,13},{13,11},{18,20},{2... | collective-permute-start | bytes 3145736 | tf_op jit(solution)/shard_map/ppermute | solution.py:770
  13.6 2.5 %collective-permute-start.3 = (s32[512]{0:T(512)}, s32[512]{0:T(512)}, u32[]{:S(2)}, u32[]{:S(2)}) collective-permute-start(s32[512]{0:T(512)} %param.9), channel_id=1, source_target_pairs={{0,6},{2,4},{4,2},{6,0},{1,7},{3,5},{5,3},{7,1},{8,14},{10,12},{12... | collective-permute-start | bytes 6152 | tf_op jit(solution)/shard_map/ppermute | solution.py:771
  16.4 2.0 %copy_rows.1.refs_0_ = bf16[512,1024]{1,0:T(8,128)(2,1)} custom-call(bf16[512,1024]{1,0:T(8,128)(2,1)} %source_ref.1), custom_call_target="tpu_custom_call" | custom-call | bytes 2097152 | tf_op jit(solution)/shard_map/copy_rows/pallas_call | solution.py:67
  20.2 6.9 %collective-permute-done.1.rows_ref = bf16[512,1024]{1,0:T(8,128)(2,1)S(1)} collective-permute-done((bf16[512,1024]{1,0:T(8,128)(2,1)}, bf16[512,1024]{1,0:T(8,128)(2,1)S(1)}, u32[]{:S(2)}, u32[]{:S(2)}) %collective-permute-start.1) | collective-permute-done | bytes 1048608 | tf_op jit(solution)/shard_map/ppermute | solution.py:767
  27.1 2.3 %select_rows.1.refs_1_ = bf16[8,128,1024]{2,1,0:T(8,128)(2,1)} custom-call(bf16[512,1024]{1,0:T(8,128)(2,1)S(1)} %fusion.spread_ref, bf16[512,1024]{1,0:T(8,128)(2,1)S(1)} %collective-permute-done.1.rows_ref), custom_call_target="tpu_custom_call" | custom-call | flops 137438953472 | bytes 4194304 | tf_op jit(solution)/shard_map/select_rows/pallas_call | solution.py:138
  30.4 5.7 %collective-permute-start.2 = (bf16[512,1024]{1,0:T(8,128)(2,1)}, bf16[512,1024]{1,0:T(8,128)(2,1)S(1)}, u32[]{:S(2)}, u32[]{:S(2)}) collective-permute-start(bf16[512,1024]{1,0:T(8,128)(2,1)} %after.1), channel_id=1, source_target_pairs={{0,6},{6,0},{1,7},{7,1},{8,14},{14,8},{9,15},{15,9},{16,22},{22,16... | collective-permute-start | bytes 3145736 | tf_op jit(solution)/shard_map/ppermute | solution.py:781
  36.1 2.5 %all-to-all-done.slabs_ref.near_ref = bf16[8,128,1024]{2,1,0:T(8,128)(2,1)} async-done(((bf16[8,128,1024]{2,1,0:T(8,128)(2,1)}), bf16[8,128,1024]{2,1,0:T(8,128)(2,1)}, u32[]{:S(2)}, u32[]{:S(2)}) %all-to-all-start) | async-done | bytes 2097184 | tf_op jit(solution)/shard_map/all_to_all | solution.py:762
  38.6 4.4 %all-to-all-start.1 = ((bf16[8,128,1024]{2,1,0:T(8,128)(2,1)}), bf16[8,128,1024]{2,1,0:T(8,128)(2,1)}, u32[]{:S(2)}, u32[]{:S(2)}) async-start(bf16[8,128,1024]{2,1,0:T(8,128)(2,1)} %select_rows.1.refs_1_), calls=%async_computation.1 | async-start | bytes 4194304 | tf_op jit(solution)/shard_map/all_to_all | solution.py:762
  43.0 4.1 %own_half.1 = (f32[512,512]{1,0:T(8,128)}, f32[8,512]{1,0:T(8,128)S(1)}, bf16[512,1024]{1,0:T(8,128)(2,1)S(1)}) custom-call(bf16[512,1024]{1,0:T(8,128)(2,1)} %source_ref.1, bf16[8,128,1024]{2,1,0:T(8,128)(2,1)} %all-to-all-done.slabs_ref.near_ref, s32[1,512]{1,0:T(1,128)} %bitcast.2.chosen_ref), custom_call_target="tpu_custom_call" | custom-call | flops 137438953472 | bytes 4194304 | tf_op jit(solution)/shard_map/own_half/pallas_call | solution.py:355
  47.2 11.7 %collective-permute-done.2.outer_ref = bf16[512,1024]{1,0:T(8,128)(2,1)S(1)} collective-permute-done((bf16[512,1024]{1,0:T(8,128)(2,1)}, bf16[512,1024]{1,0:T(8,128)(2,1)S(1)}, u32[]{:S(2)}, u32[]{:S(2)}) %collective-permute-start.2) | collective-permute-done | bytes 1048608 | tf_op jit(solution)/shard_map/ppermute | solution.py:781
  58.8 10.8 %all-to-all-done.1.far_ref = bf16[8,128,1024]{2,1,0:T(8,128)(2,1)} async-done(((bf16[8,128,1024]{2,1,0:T(8,128)(2,1)}), bf16[8,128,1024]{2,1,0:T(8,128)(2,1)}, u32[]{:S(2)}, u32[]{:S(2)}) %all-to-all-start.1) | async-done | bytes 2097184 | tf_op jit(solution)/shard_map/all_to_all | solution.py:762
  69.7 5.2 %rest_half.1 = (f32[512,512]{1,0:T(8,128)S(1)}, f32[512,512]{1,0:T(8,128)}, f32[2,512,512]{2,1,0:T(8,128)S(1)}, f32[8,512]{1,0:T(8,128)S(1)}, s32[8,512]{1,0:T(8...) custom-call(bf16[512,1024]{1,0:T(8,128)(2,1)S(1)} %get-tuple-element, ...), custom_call_target="tpu_custom_call" | custom-call | flops 1610612736 | bytes 8388608 | tf_op jit(solution)/shard_map/rest_half/pallas_call | solution.py:432
  74.8 2.5 %collective-permute-start.4 = (f32[8,512]{1,0:T(8,128)S(1)}, f32[8,512]{1,0:T(8,128)S(1)}, u32[]{:S(2)}, u32[]{:S(2)}) collective-permute-start(f32[8,512]{1,0:T(8,128)S(1)} %get-tuple-element.37.stats_ref.here_ref), channel_id=1, source_target_pairs={{0,6},{2,4},{4,2},{6,0},{1,7},{3,5},{5,3},{7,1},{8,14},{10,12},{12... | collective-permute-start | bytes 49160 | tf_op jit(solution)/shard_map/ppermute | solution.py:791
  77.4 2.4 %early_grads.1 = (f32[512,1024]{1,0:T(8,128)S(1)}, f32[512,1024]{1,0:T(8,128)S(1)}) custom-call(f32[8,512]{1,0:T(8,128)S(1)} %get-tuple-element.37.stats_ref.here_ref, s32[8,512]{1,0:T(8,128)S(1)} %get-tuple-element.38.near_target_ref.target_ref, s32[8,512]{1,0:T(8,128)S(1)} %get-tuple-element.36.far_target_ref.target_ref, ...), custom_call_target="tpu_custom_call" | custom-call | flops 137438953472 | bytes 4194304 | tf_op jit(solution)/shard_map/early_grads/pallas_call | solution.py:556
  80.4 2.9 %far_grads.1 = (bf16[8,128,1024]{2,1,0:T(8,128)(2,1)}, bf16[512,512]{1,0:T(8,128)(2,1)}, f32[8,512]{1,0:T(8,128)S(1)}, f32[1,512]{1,0:T(1,128)}) custom-call(bf16[512,1024]{1,0:T(8,128)(2,1)S(1)} %get-tuple-element.32.queries_ref, bf16[512,1024]{1,0:T(8,128)(2,1)S(1)} %get-tuple-element.34.others_ref, ...), custom_call_target="tpu_custom_call" | custom-call | flops 1073741824 | bytes 4194304 | tf_op jit(solution)/shard_map/far_grads/pallas_call | solution.py:632
  83.4 4.5 %all-to-all-start.2 = ((bf16[8,128,1024]{2,1,0:T(8,128)(2,1)}), bf16[8,128,1024]{2,1,0:T(8,128)(2,1)}, u32[]{:S(2)}, u32[]{:S(2)}) async-start(bf16[8,128,1024]{2,1,0:T(8,128)(2,1)} %get-tuple-element.50), calls=%async_computation.2 | async-start | bytes 4194304 | tf_op jit(solution)/shard_map/all_to_all | solution.py:762
  87.9 1.6 %copy-done.5 = f32[512,1024]{1,0:T(8,128)S(1)} copy-done((f32[512,1024]{1,0:T(8,128)S(1)}, f32[512,1024]{1,0:T(8,128)}, u32[]{:S(2)}) %copy-start.5) | copy-done | bytes 2097176
  91.0 2.5 %collective-permute-start.5 = (bf16[512,1024]{1,0:T(8,128)(2,1)}, bf16[512,1024]{1,0:T(8,128)(2,1)}, u32[]{:S(2)}, u32[]{:S(2)}) collective-permute-start(bf16[512,1024]{1,0:T(8,128)(2,1)} %other_grads.1), channel_id=1, source_target_pairs={{0,6},{2,4},{4,2},{6,0},{1,7},{3,5},{5,3},{7,1},{8,14},{10,12},{12... | collective-permute-start | bytes 3145736 | tf_op jit(solution)/shard_map/ppermute | solution.py:804
  93.5 7.2 %near_grads.1 = (bf16[4,128,1024]{2,1,0:T(8,128)(2,1)}, bf16[128,1024]{1,0:T(8,128)(2,1)}, bf16[128,1024]{1,0:T(8,128)(2,1)}, bf16[128,1024]{1,0:T(8,128)(2,1)},...) custom-call(bf16[512,1024]{1,0:T(8,128)(2,1)S(1)} %get-tuple-element.32.queries_ref, bf16[512,1024]{1,0:T(8,128)(2,1)S(1)} %copy-done.1, ...), custom_call_target="tpu_custom_call" | custom-call | flops 2147483648 | bytes 8388608 | tf_op jit(solution)/shard_map/near_grads/pallas_call | solution.py:698
  104.9 1.6 %join_cores.1 = (bf16[256,1024]{1,0:T(8,128)(2,1)}, bf16[256,1024]{1,0:T(8,128)(2,1)}, bf16[256,1024]{1,0:T(8,128)(2,1)}, bf16[256,1024]{1,0:T(8,128)(2,1)}) custom-call(bf16[4,128,1024]{2,1,0:T(8,128)(2,1)S(1)} %copy-done.6, bf16[128,1024]{1,0:T(8,128)(2,1)S(1)} %collective-permute-done.6.refs_0_, bf16[128,1024]{1,0:T(8,128)(2,1)S(1)} %collective-permute-done.7.refs_1_, ...), custom_call_target="tpu_custom_call" | custom-call | flops 1048576 | bytes 4194304 | tf_op jit(solution)/shard_map/join_cores/pallas_call | solution.py:171
  106.5 1.8 %collective-permute-start.10 = (bf16[256,1024]{1,0:T(8,128)(2,1)}, bf16[256,1024]{1,0:T(8,128)(2,1)S(1)}, u32[]{:S(2)}, u32[]{:S(2)}) collective-permute-start(bf16[256,1024]{1,0:T(8,128)(2,1)} %get-tuple-element.57), channel_id=1, source_target_pairs={{0,8},{1,9},{8,0},{9,1},{16,24},{17,25},{24,16},{25,17},{2,10},{3,... | collective-permute-start | bytes 1572872 | tf_op jit(solution)/shard_map/ppermute | solution.py:808
  110.0 4.9 %all-to-all-done.2 = bf16[8,128,1024]{2,1,0:T(8,128)(2,1)} async-done(((bf16[8,128,1024]{2,1,0:T(8,128)(2,1)}), bf16[8,128,1024]{2,1,0:T(8,128)(2,1)}, u32[]{:S(2)}, u32[]{:S(2)}) %all-to-all-start.2) | async-done | bytes 2097184 | tf_op jit(solution)/shard_map/all_to_all | solution.py:762
  114.9 3.5 %segment_rows.2.refs_0_ = bf16[512,1024]{1,0:T(8,128)(2,1)} custom-call(bf16[512,1024]{1,0:T(8,128)(2,1)S(1)} %copy-done.3, bf16[1024,1024]{1,0:T(8,128)(2,1)} %bitcast.11.refs_0_), custom_call_target="tpu_custom_call" | custom-call | flops 1073741824 | bytes 4194304 | tf_op jit(solution)/shard_map/segment_rows/pallas_call | solution.py:230
  118.6 2.7 %add_parts.2.refs_4_ = bf16[512,1024]{1,0:T(8,128)(2,1)} custom-call(f32[512,1024]{1,0:T(8,128)} %get-tuple-element.48.own_ref, bf16[512,1024]{1,0:T(8,128)(2,1)} %collective-permute-done.5.part_ref, bf16[512,1024]{1,0:T(8,128)(2,1)} %segment_rows.2.refs_0_), custom_call_target="tpu_custom_call" | custom-call | flops 137438953472 | bytes 4194304 | tf_op jit(solution)/shard_map/add_parts/pallas_call | solution.py:735
  121.4 3.7 %collective-permute-done.10.refs_1_ = bf16[256,1024]{1,0:T(8,128)(2,1)S(1)} collective-permute-done((bf16[256,1024]{1,0:T(8,128)(2,1)}, bf16[256,1024]{1,0:T(8,128)(2,1)S(1)}, u32[]{:S(2)}, u32[]{:S(2)}) %collective-permute-start.10) | collective-permute-done | bytes 524320 | tf_op jit(solution)/shard_map/ppermute | solution.py:808
  126.0 11.0 %collective-permute-done.12.refs_3_ = bf16[256,1024]{1,0:T(8,128)(2,1)} collective-permute-done((bf16[256,1024]{1,0:T(8,128)(2,1)}, bf16[256,1024]{1,0:T(8,128)(2,1)}, u32[]{:S(2)}, u32[]{:S(2)}) %collective-permute-start.12) | collective-permute-done | bytes 524320 | tf_op jit(solution)/shard_map/ppermute | solution.py:808
  136.9 2.5 %segment_rows.3.own_ref = f32[512,1024]{1,0:T(8,128)S(1)} custom-call(bf16[512,1024]{1,0:T(8,128)(2,1)S(1)} %fusion.1.spread_ref, bf16[256,1024]{1,0:T(8,128)(2,1)S(1)} %copy-done.8, bf16[256,1024]{1,0:T(8,128)(2,1)S(1)} %collective-permute-done.10.refs_1_, bf16[256,1024]{1,0:T(8,128)(2,1)S(1)} %collective-permute-done.11.refs_2_, ...), custom_call_target="tpu_custom_call" | custom-call | flops 137438953472 | bytes 4194304 | tf_op jit(solution)/shard_map/segment_rows/pallas_call | solution.py:230
  141.0 2.1 %add_parts.3 = bf16[512,1024]{1,0:T(8,128)(2,1)} custom-call(f32[512,1024]{1,0:T(8,128)S(1)} %segment_rows.3.own_ref, bf16[512,1024]{1,0:T(8,128)(2,1)} %collective-permute-done.13.part_ref), custom_call_target="tpu_custom_call" | custom-call | flops 1048576 | bytes 4194304 | tf_op jit(solution)/shard_map/add_parts/pallas_call | solution.py:735
  (56 shorter events, 13.7 us)
Async XLA Ops:
  0.6 4.9 %copy-start.7 = (s32[32,4]{0,1:T(4,128)S(1)}, s32[32,4]{0,1:T(4,128)}, u32[]{:S(2)}) copy-start(s32[32,4]{0,1:T(4,128)} %param.8) | copy-start | bytes 1540
  0.6 26.5 %collective-permute-start.1 = (bf16[512,1024]{1,0:T(8,128)(2,1)}, bf16[512,1024]{1,0:T(8,128)(2,1)S(1)}, u32[]{:S(2)}, u32[]{:S(2)}) collective-permute-start(bf16[512,1024]{1,0:T(8,128)(2,1)} %bitcast.21), channel_id=1, source_target_pairs={{0,2},{2,0},{4,6},{6,4},{1,3},{3,1},{5,7},{7,5},{8,10},{10,8},{12,... | collective-permute-start | bytes 3145736 | tf_op jit(solution)/shard_map/ppermute | solution.py:767
  7.6 31.0 %all-to-all-start = ((bf16[8,128,1024]{2,1,0:T(8,128)(2,1)}), bf16[8,128,1024]{2,1,0:T(8,128)(2,1)}, u32[]{:S(2)}, u32[]{:S(2)}) async-start(bf16[8,128,1024]{2,1,0:T(8,128)(2,1)} %gather_rows.1), calls=%async_computation | async-start | bytes 4194304 | tf_op jit(solution)/shard_map/all_to_all | solution.py:762
  12.0 35.2 %collective-permute-start = (bf16[512,1024]{1,0:T(8,128)(2,1)}, bf16[512,1024]{1,0:T(8,128)(2,1)}, u32[]{:S(2)}, u32[]{:S(2)}) collective-permute-start(bf16[512,1024]{1,0:T(8,128)(2,1)} %source_ref.1), channel_id=1, source_target_pairs={{2,4},{4,2},{3,5},{5,3},{10,12},{12,10},{11,13},{13,11},{18,20},{2... | collective-permute-start | bytes 3145736 | tf_op jit(solution)/shard_map/ppermute | solution.py:770
  13.6 33.5 %collective-permute-start.3 = (s32[512]{0:T(512)}, s32[512]{0:T(512)}, u32[]{:S(2)}, u32[]{:S(2)}) collective-permute-start(s32[512]{0:T(512)} %param.9), channel_id=1, source_target_pairs={{0,6},{2,4},{4,2},{6,0},{1,7},{3,5},{5,3},{7,1},{8,14},{10,12},{12... | collective-permute-start | bytes 6152 | tf_op jit(solution)/shard_map/ppermute | solution.py:771
  29.4 1.0 copy-start.2
  30.4 28.5 %collective-permute-start.2 = (bf16[512,1024]{1,0:T(8,128)(2,1)}, bf16[512,1024]{1,0:T(8,128)(2,1)S(1)}, u32[]{:S(2)}, u32[]{:S(2)}) collective-permute-start(bf16[512,1024]{1,0:T(8,128)(2,1)} %after.1), channel_id=1, source_target_pairs={{0,6},{6,0},{1,7},{7,1},{8,14},{14,8},{9,15},{15,9},{16,22},{22,16... | collective-permute-start | bytes 3145736 | tf_op jit(solution)/shard_map/ppermute | solution.py:781
  38.6 31.0 %all-to-all-start.1 = ((bf16[8,128,1024]{2,1,0:T(8,128)(2,1)}), bf16[8,128,1024]{2,1,0:T(8,128)(2,1)}, u32[]{:S(2)}, u32[]{:S(2)}) async-start(bf16[8,128,1024]{2,1,0:T(8,128)(2,1)} %select_rows.1.refs_1_), calls=%async_computation.1 | async-start | bytes 4194304 | tf_op jit(solution)/shard_map/all_to_all | solution.py:762
  74.8 5.6 %copy-start = (bf16[512,1024]{1,0:T(8,128)(2,1)}, bf16[512,1024]{1,0:T(8,128)(2,1)S(1)}, u32[]{:S(2)}) copy-start(bf16[512,1024]{1,0:T(8,128)(2,1)S(1)} %get-tuple-element.34.others_ref) | copy-start | bytes 3145732
  74.8 5.6 %collective-permute-start.4 = (f32[8,512]{1,0:T(8,128)S(1)}, f32[8,512]{1,0:T(8,128)S(1)}, u32[]{:S(2)}, u32[]{:S(2)}) collective-permute-start(f32[8,512]{1,0:T(8,128)S(1)} %get-tuple-element.37.stats_ref.here_ref), channel_id=1, source_target_pairs={{0,6},{2,4},{4,2},{6,0},{1,7},{3,5},{5,3},{7,1},{8,14},{10,12},{12... | collective-permute-start | bytes 49160 | tf_op jit(solution)/shard_map/ppermute | solution.py:791
  79.8 3.6 %copy-start.4 = (f32[512,1024]{1,0:T(8,128)}, f32[512,1024]{1,0:T(8,128)S(1)}, u32[]{:S(2)}) copy-start(f32[512,1024]{1,0:T(8,128)S(1)} %get-tuple-element.49.sums_ref) | copy-start | bytes 6291460
  83.4 31.5 %all-to-all-start.2 = ((bf16[8,128,1024]{2,1,0:T(8,128)(2,1)}), bf16[8,128,1024]{2,1,0:T(8,128)(2,1)}, u32[]{:S(2)}, u32[]{:S(2)}) async-start(bf16[8,128,1024]{2,1,0:T(8,128)(2,1)} %get-tuple-element.50), calls=%async_computation.2 | async-start | bytes 4194304 | tf_op jit(solution)/shard_map/all_to_all | solution.py:762
  87.9 1.6 %copy-start.5 = (f32[512,1024]{1,0:T(8,128)S(1)}, f32[512,1024]{1,0:T(8,128)}, u32[]{:S(2)}) copy-start(f32[512,1024]{1,0:T(8,128)} %copy-done.4) | copy-start | bytes 6291460
  89.5 4.0 %copy-start.1 = (bf16[512,1024]{1,0:T(8,128)(2,1)S(1)}, bf16[512,1024]{1,0:T(8,128)(2,1)}, u32[]{:S(2)}) copy-start(bf16[512,1024]{1,0:T(8,128)(2,1)} %copy-done) | copy-start | bytes 3145732
  91.0 27.6 %collective-permute-start.5 = (bf16[512,1024]{1,0:T(8,128)(2,1)}, bf16[512,1024]{1,0:T(8,128)(2,1)}, u32[]{:S(2)}, u32[]{:S(2)}) collective-permute-start(bf16[512,1024]{1,0:T(8,128)(2,1)} %other_grads.1), channel_id=1, source_target_pairs={{0,6},{2,4},{4,2},{6,0},{1,7},{3,5},{5,3},{7,1},{8,14},{10,12},{12... | collective-permute-start | bytes 3145736 | tf_op jit(solution)/shard_map/ppermute | solution.py:804
  93.5 8.3 %copy-start.9 = (s32[64,16]{1,0:T(8,128)S(1)}, s32[64,16]{1,0:T(8,128)}, u32[]{:S(2)}) copy-start(s32[64,16]{1,0:T(8,128)} %get-tuple-element.73) | copy-start | bytes 12292
  100.7 14.2 %copy-start.3 = (bf16[512,1024]{1,0:T(8,128)(2,1)S(1)}, bf16[512,1024]{1,0:T(8,128)(2,1)}, u32[]{:S(2)}) copy-start(bf16[512,1024]{1,0:T(8,128)(2,1)} %copy-done.2) | copy-start | bytes 3145732
  100.7 1.8 %collective-permute-start.6 = (bf16[128,1024]{1,0:T(8,128)(2,1)}, bf16[128,1024]{1,0:T(8,128)(2,1)S(1)}, u32[]{:S(2)}, u32[]{:S(2)}) collective-permute-start(bf16[128,1024]{1,0:T(8,128)(2,1)} %get-tuple-element.52), channel_id=1, source_target_pairs={{0,1},{1,0},{8,9},{9,8},{16,17},{17,16},{24,25},{25,24},{2,3},{3,2... | collective-permute-start | bytes 786440 | tf_op jit(solution)/shard_map/ppermute | solution.py:803
  100.8 2.1 %collective-permute-start.7 = (bf16[128,1024]{1,0:T(8,128)(2,1)}, bf16[128,1024]{1,0:T(8,128)(2,1)S(1)}, u32[]{:S(2)}, u32[]{:S(2)}) collective-permute-start(bf16[128,1024]{1,0:T(8,128)(2,1)} %get-tuple-element.53), channel_id=1, source_target_pairs={{0,1},{1,0},{8,9},{9,8},{16,17},{17,16},{24,25},{25,24},{2,3},{3,2... | collective-permute-start | bytes 786440 | tf_op jit(solution)/shard_map/ppermute | solution.py:803
  101.3 2.0 %collective-permute-start.8 = (bf16[128,1024]{1,0:T(8,128)(2,1)}, bf16[128,1024]{1,0:T(8,128)(2,1)S(1)}, u32[]{:S(2)}, u32[]{:S(2)}) collective-permute-start(bf16[128,1024]{1,0:T(8,128)(2,1)} %get-tuple-element.54), channel_id=1, source_target_pairs={{0,1},{1,0},{8,9},{9,8},{16,17},{17,16},{24,25},{25,24},{2,3},{3,2... | collective-permute-start | bytes 786440 | tf_op jit(solution)/shard_map/ppermute | solution.py:803
  101.4 2.3 %collective-permute-start.9 = (bf16[128,1024]{1,0:T(8,128)(2,1)}, bf16[128,1024]{1,0:T(8,128)(2,1)S(1)}, u32[]{:S(2)}, u32[]{:S(2)}) collective-permute-start(bf16[128,1024]{1,0:T(8,128)(2,1)} %get-tuple-element.55), channel_id=1, source_target_pairs={{0,1},{1,0},{8,9},{9,8},{16,17},{17,16},{24,25},{25,24},{2,3},{3,2... | collective-permute-start | bytes 786440 | tf_op jit(solution)/shard_map/ppermute | solution.py:803
  103.7 1.2 copy-start.6
  106.5 18.6 %collective-permute-start.10 = (bf16[256,1024]{1,0:T(8,128)(2,1)}, bf16[256,1024]{1,0:T(8,128)(2,1)S(1)}, u32[]{:S(2)}, u32[]{:S(2)}) collective-permute-start(bf16[256,1024]{1,0:T(8,128)(2,1)} %get-tuple-element.57), channel_id=1, source_target_pairs={{0,8},{1,9},{8,0},{9,1},{16,24},{17,25},{24,16},{25,17},{2,10},{3,... | collective-permute-start | bytes 1572872 | tf_op jit(solution)/shard_map/ppermute | solution.py:808
  108.3 17.7 %collective-permute-start.11 = (bf16[256,1024]{1,0:T(8,128)(2,1)}, bf16[256,1024]{1,0:T(8,128)(2,1)S(1)}, u32[]{:S(2)}, u32[]{:S(2)}) collective-permute-start(bf16[256,1024]{1,0:T(8,128)(2,1)} %get-tuple-element.58), channel_id=1, source_target_pairs={{0,16},{1,17},{8,24},{9,25},{16,0},{17,1},{24,8},{25,9},{2,18},{3,... | collective-permute-start | bytes 1572872 | tf_op jit(solution)/shard_map/ppermute | solution.py:808
  109.8 27.1 %collective-permute-start.12 = (bf16[256,1024]{1,0:T(8,128)(2,1)}, bf16[256,1024]{1,0:T(8,128)(2,1)}, u32[]{:S(2)}, u32[]{:S(2)}) collective-permute-start(bf16[256,1024]{1,0:T(8,128)(2,1)} %get-tuple-element.59), channel_id=1, source_target_pairs={{0,24},{1,25},{8,16},{9,17},{16,8},{17,9},{24,0},{25,1},{2,26},{3,... | collective-permute-start | bytes 1572872 | tf_op jit(solution)/shard_map/ppermute | solution.py:808
  118.4 22.6 %collective-permute-start.13 = (bf16[512,1024]{1,0:T(8,128)(2,1)}, bf16[512,1024]{1,0:T(8,128)(2,1)}, u32[]{:S(2)}, u32[]{:S(2)}) collective-permute-start(bf16[512,1024]{1,0:T(8,128)(2,1)} %segment_rows.2.refs_0_), channel_id=1, source_target_pairs={{0,2},{2,0},{4,6},{6,4},{1,3},{3,1},{5,7},{7,5},{8,10},{10,8},{12,... | collective-permute-start | bytes 3145736 | tf_op jit(solution)/shard_map/ppermute | solution.py:806
  118.6 18.3 %copy-start.8 = (bf16[256,1024]{1,0:T(8,128)(2,1)S(1)}, bf16[256,1024]{1,0:T(8,128)(2,1)}, u32[]{:S(2)}) copy-start(bf16[256,1024]{1,0:T(8,128)(2,1)} %get-tuple-element.56.refs_0_) | copy-start | bytes 1572868

commit v9 on v8

--- a/solution.py
+++ b/solution.py
@@ -370,13 +370,11 @@
     )(queries, slabs, chosen)
 
 
-def rest_kernel(
-    near_place, far_place, queries_ref, inner_ref, outer_ref, near_ref, far_ref, chosen_ref, chosen_others_ref, own_stats_ref,
-    other_logits_ref, saved_ref, far_logits_ref, stats_ref, near_target_ref, far_target_ref, others_ref, near_rows, far_rows,
-    held, near_in, far_in, held_in, left, came,
+def other_half_kernel(
+    place, inner_ref, outer_ref, near_ref, chosen_ref,
+    logits_ref, saved_ref, stats_ref, others_ref, near_rows, near_in, left, came,
 ):
     half = near_ref.shape[1] // 2
-    held_loads = load_chunks(far_ref.at[:, pl.ds(0, half)], held, held_in)
     z = lax.axis_index("z")
     inner = (z > 0) & (z < lax.axis_size("z") - 1)
 
@@ -389,11 +387,54 @@
         load(outer_ref, others_ref, came)
 
     whole = [pltpu.make_async_copy(outer_ref, others_ref, came)]
-    near_loads = load_chunks(near_ref.at[:, pl.ds(half, half)], near_rows, near_in)
+    near_load = load(near_ref.at[:, pl.ds(half, half)], near_rows, near_in)
+    stores = []
+
+    def put(c, block):
+        logits_ref[...] = block
+        stores.append(load(logits_ref, saved_ref, left))
+
+    for copy in whole:
+        copy.wait()
+    near_load.wait()
+    stats = block_logits(others_ref, lambda c: held_rows(near_rows, c), place(chosen_ref[...]), put)
+    put_stats(stats_ref, 0, stats)
+    put_stats(stats_ref, 1, stats)
+    for store in stores:
+        store.wait()
+
+
+def other_half(inner, outer, near_slabs, chosen, place):
+    size, width = inner.shape
+    rows = near_slabs.shape[0] * near_slabs.shape[1] // 2
+    part = (near_slabs.shape[0], near_slabs.shape[1] // 2, width)
+    return pl.pallas_call(
+        functools.partial(other_half_kernel, place),
+        in_specs=[ANY] * 2 + [HBM, VMEM],
+        out_specs=[VMEM, HBM] + [VMEM] * 3,
+        out_shape=[
+            shape((rows, size), F32),
+            pltpu.HBM((rows, size), F32),
+            shape((8, size), F32),
+            shape((size, width), BF16),
+            shape(part, BF16),
+        ],
+        scratch_shapes=[pltpu.SemaphoreType.DMA] * 3,
+        compiler_params=params(),
+        name="other_half",
+        cost_estimate=cost(BUSY, 8),
+    )(inner, outer, near_slabs, chosen)
+
+
+def rest_kernel(
+    near_place, far_place, queries_ref, others_ref, far_ref, chosen_ref, chosen_others_ref, own_stats_ref, other_stats_ref,
+    far_logits_ref, stats_ref, near_target_ref, far_target_ref, far_rows, held, far_in, held_in,
+):
+    half = far_ref.shape[1] // 2
+    held_loads = load_chunks(far_ref.at[:, pl.ds(0, half)], held, held_in)
     far_loads = load_chunks(far_ref.at[:, pl.ds(half, half)], far_rows, far_in)
     put_targets(near_place, near_target_ref, chosen_ref, chosen_others_ref)
     put_targets(far_place, far_target_ref, chosen_ref, chosen_others_ref)
-    stores = []
 
     def part(loads, rows):
         def get(c):
@@ -402,11 +443,6 @@
 
         return get
 
-    def put_near(c, block):
-        rows = part_of(other_logits_ref.shape[0], c)
-        other_logits_ref[row_chunk(other_logits_ref.shape[0], c), :] = block
-        stores.append(load(other_logits_ref.at[rows], saved_ref.at[rows], left.at[c]))
-
     def put_far(q):
         def put(c, block):
             far_logits_ref[q, chunk_rows(far_logits_ref, c), :] = block
@@ -415,40 +451,31 @@
 
     own = block_logits(queries_ref, part(held_loads, held), far_target_ref[0:1, :], put_far(0))
     put_stats(stats_ref, 0, joined(stat_rows(own_stats_ref, 0), own))
-    for copy in whole:
-        copy.wait()
-    near = block_logits(others_ref, part(near_loads, near_rows), near_target_ref[1:2, :], put_near)
     far = block_logits(others_ref, part(far_loads, far_rows), far_target_ref[1:2, :], put_far(1))
-    put_stats(stats_ref, 1, joined(near, far))
-    for store in stores:
-        store.wait()
-
-
-def rest_half(queries, inner, outer, near_slabs, far_slabs, chosen, chosen_others, own_stats, places):
+    put_stats(stats_ref, 1, joined(stat_rows(other_stats_ref, 0), far))
+
+
+def rest_half(queries, others, far_slabs, chosen, chosen_others, own_stats, other_stats, places):
     size, width = queries.shape
-    rows = near_slabs.shape[0] * near_slabs.shape[1] // 2
-    part = (near_slabs.shape[0], near_slabs.shape[1] // 2, width)
+    rows = far_slabs.shape[0] * far_slabs.shape[1] // 2
+    part = (far_slabs.shape[0], far_slabs.shape[1] // 2, width)
     chunk_sems = pltpu.SemaphoreType.DMA((CHUNKS,))
     return pl.pallas_call(
         functools.partial(rest_kernel, *places),
-        in_specs=[VMEM] + [ANY] * 2 + [HBM] * 2 + [VMEM] * 3,
-        out_specs=[VMEM, HBM] + [VMEM] * 7,
+        in_specs=[VMEM] * 2 + [HBM] + [VMEM] * 4,
+        out_specs=[VMEM] * 5,
         out_shape=[
-            shape((rows, size), F32),
-            pltpu.HBM((rows, size), F32),
             shape((2, rows, size), F32),
             shape((8, size), F32),
             shape((8, size), jnp.int32),
             shape((8, size), jnp.int32),
-            shape((size, width), BF16),
-            shape(part, BF16),
             shape(part, BF16),
         ],
-        scratch_shapes=[pltpu.VMEM(part, BF16)] + [chunk_sems] * 4 + [pltpu.SemaphoreType.DMA],
+        scratch_shapes=[pltpu.VMEM(part, BF16)] + [chunk_sems] * 2,
         compiler_params=params(),
         name="rest_half",
         cost_estimate=cost(3 << 29, 8),
-    )(queries, inner, outer, near_slabs, far_slabs, chosen, chosen_others, own_stats)
+    )(queries, others, far_slabs, chosen, chosen_others, own_stats, other_stats)
 
 
 def log_totals(here_ref, there_ref):
@@ -785,8 +812,11 @@
     chosen_others = others_positives
     places = [functools.partial(place_of, far, planes, ranks, refs, height) for far in range(2)]
     own_logits, own_stats, own = own_half(in_hbm(queries), near_slabs, chosen, places[0])
-    other_logits, saved_logits, far_logits, stats, near_target, far_target, others, near_rows, far_rows = rest_half(
-        own, others_inner, others_outer, near_slabs, far_slabs, chosen, chosen_others, own_stats, places
+    other_logits, saved_logits, other_stats, others, near_rows = other_half(
+        others_inner, others_outer, near_slabs, chosen_others, places[0]
+    )
+    far_logits, stats, near_target, far_target, far_rows = rest_half(
+        own, others, far_slabs, chosen, chosen_others, own_stats, other_stats, places
     )
     partner = lax.ppermute(stats, "z", across)
     sums, hit = early_grads(stats, near_target, far_target, other_logits, far_logits, near_rows, far_rows)

time: 144 us -> 144 us (level)
  waiting for transfers between devices: 56.1 us -> 50.3 us
  Pallas kernels: 41.9 us -> 44.9 us
  local copies, waits for them, and re-layouts: 6.69 us -> 8.68 us
    all_to_all x3, waiting for transfers between devices: 18.2 us -> 12.4 us  [exchange(): lax.all_to_all(slab_array, PLANE, split_axis=0, concat_axis=0, tiled=True)]
    pallas_call x1 -> x2, Pallas kernels: 5.16 us -> 8.04 us  [the longest x1 4.2 us: rest_half(): pl.pallas_call(functools.partial(rest_kernel, *places), in_specs=[VMEM] *...]
    unnamed x22 -> x32, local copies, waits for them, and re-layouts: 5.73 us -> 7.72 us
  transfers between devices with their start and end apart: 17 -> 17, of which waited for: 15 -> 15; matrix products, arithmetic and copies ran while one was open for 3% -> 3% of each run, Pallas kernels for 22% -> 25%
where the time goes in v9:
time: 144 us; the launch traced here: 142 us
  waiting for transfers between devices  50.3 us (35%)
  Pallas kernels  44.9 us (31%)
  starting transfers between devices  36 us (25%)
  local copies, waits for them, and re-layouts  8.68 us (6%)
    ppermute x3, waiting for transfers between devices, on_device(): lax.ppermute(array, PLANE, [(i, i ^ 2 * g) for i in range(slabs)])  15.5 us
    all_to_all x3, starting transfers between devices, exchange(): lax.all_to_all(slab_array, PLANE, split_axis=0, concat_axis=0, tiled=True)  13.3 us
    all_to_all x3, waiting for transfers between devices, exchange(): lax.all_to_all(slab_array, PLANE, split_axis=0, concat_axis=0, tiled=True)  12.4 us
    ppermute x1, waiting for transfers between devices, on_device(): lax.ppermute(after(copy_rows(in_hbm(queries)), in_hbm(far_sent), where=HB...  11.7 us
    unnamed x32, local copies, waits for them, and re-layouts  7.72 us
    pallas_call x1, Pallas kernels, near_grads(): pl.pallas_call(functools.partial(near_kernel, ranks), in_specs=[VMEM] * 4...  7.16 us
    ppermute x1, waiting for transfers between devices, on_device(): lax.ppermute(passages.reshape(height * blocks, width), 'z', to_pair)  6.81 us
    pallas_call x2, Pallas kernels, segment_rows(): pl.pallas_call(functools.partial(segment_kernel, stripes, len(arrays)), i...  5.98 us
  transfers between devices with their start and end apart: 17, of which 15 were waited for; matrix products, arithmetic and copies ran while one was open for 3% of the time, Pallas kernels for 25%

profile of v9, /device:TPU:0, one launch (start us, length us, event | category | flops | bytes accessed | tf_op | source)
XLA Modules:
  0.0 142.3 jit_solution(4548186126914999006)
XLA Ops:
  0.6 3.1 %collective-permute-start.1 = (bf16[512,1024]{1,0:T(8,128)(2,1)}, bf16[512,1024]{1,0:T(8,128)(2,1)S(1)}, u32[]{:S(2)}, u32[]{:S(2)}) collective-permute-start(bf16[512,1024]{1,0:T(8,128)(2,1)} %bitcast.21), channel_id=1, source_target_pairs={{0,2},{2,0},{4,6},{6,4},{1,3},{3,1},{5,7},{7,5},{8,10},{10,8},{12,... | collective-permute-start | bytes 3145736 | tf_op jit(solution)/shard_map/ppermute | solution.py:794
  3.7 1.8 %copy.17 = bf16[16,32,1024]{2,0,1:T(8,128)(2,1)S(1)} copy(bf16[16,32,1024]{2,1,0:T(8,128)(2,1)} %param.7) | data formatting | bytes 2097152 | tf_op args[1]
  5.6 2.1 %gather_rows.1 = bf16[8,128,1024]{2,1,0:T(8,128)(2,1)} custom-call(s32[4,32]{1,0:T(4,128)S(1)} %bitcast.20, bf16[32,16,1024]{2,1,0:T(8,128)(2,1)S(1)} %bitcast.19), custom_call_target="tpu_custom_call" | custom-call | bytes 4194304 | tf_op jit(solution)/shard_map/gather_rows/pallas_call | solution.py:107
  7.6 4.4 %all-to-all-start = ((bf16[8,128,1024]{2,1,0:T(8,128)(2,1)}), bf16[8,128,1024]{2,1,0:T(8,128)(2,1)}, u32[]{:S(2)}, u32[]{:S(2)}) async-start(bf16[8,128,1024]{2,1,0:T(8,128)(2,1)} %gather_rows.1), calls=%async_computation | async-start | bytes 4194304 | tf_op jit(solution)/shard_map/all_to_all | solution.py:789
  12.0 2.5 %collective-permute-start.3 = (s32[512]{0:T(512)}, s32[512]{0:T(512)}, u32[]{:S(2)}, u32[]{:S(2)}) collective-permute-start(s32[512]{0:T(512)} %param.9), channel_id=1, source_target_pairs={{0,6},{2,4},{4,2},{6,0},{1,7},{3,5},{5,3},{7,1},{8,14},{10,12},{12... | collective-permute-start | bytes 6152 | tf_op jit(solution)/shard_map/ppermute | solution.py:798
  14.6 1.6 %collective-permute-start = (bf16[512,1024]{1,0:T(8,128)(2,1)}, bf16[512,1024]{1,0:T(8,128)(2,1)}, u32[]{:S(2)}, u32[]{:S(2)}) collective-permute-start(bf16[512,1024]{1,0:T(8,128)(2,1)} %source_ref.1), channel_id=1, source_target_pairs={{2,4},{4,2},{3,5},{5,3},{10,12},{12,10},{11,13},{13,11},{18,20},{2... | collective-permute-start | bytes 3145736 | tf_op jit(solution)/shard_map/ppermute | solution.py:797
  16.5 2.0 %copy_rows.1.refs_0_ = bf16[512,1024]{1,0:T(8,128)(2,1)} custom-call(bf16[512,1024]{1,0:T(8,128)(2,1)} %source_ref.1), custom_call_target="tpu_custom_call" | custom-call | bytes 2097152 | tf_op jit(solution)/shard_map/copy_rows/pallas_call | solution.py:67
  20.3 6.8 %collective-permute-done.1.rows_ref = bf16[512,1024]{1,0:T(8,128)(2,1)S(1)} collective-permute-done((bf16[512,1024]{1,0:T(8,128)(2,1)}, bf16[512,1024]{1,0:T(8,128)(2,1)S(1)}, u32[]{:S(2)}, u32[]{:S(2)}) %collective-permute-start.1) | collective-permute-done | bytes 1048608 | tf_op jit(solution)/shard_map/ppermute | solution.py:794
  27.1 2.3 %select_rows.1.refs_1_ = bf16[8,128,1024]{2,1,0:T(8,128)(2,1)} custom-call(bf16[512,1024]{1,0:T(8,128)(2,1)S(1)} %fusion.spread_ref, bf16[512,1024]{1,0:T(8,128)(2,1)S(1)} %collective-permute-done.1.rows_ref), custom_call_target="tpu_custom_call" | custom-call | flops 137438953472 | bytes 4194304 | tf_op jit(solution)/shard_map/select_rows/pallas_call | solution.py:138
  30.4 5.7 %collective-permute-start.2 = (bf16[512,1024]{1,0:T(8,128)(2,1)}, bf16[512,1024]{1,0:T(8,128)(2,1)S(1)}, u32[]{:S(2)}, u32[]{:S(2)}) collective-permute-start(bf16[512,1024]{1,0:T(8,128)(2,1)} %after.1), channel_id=1, source_target_pairs={{0,6},{6,0},{1,7},{7,1},{8,14},{14,8},{9,15},{15,9},{16,22},{22,16... | collective-permute-start | bytes 3145736 | tf_op jit(solution)/shard_map/ppermute | solution.py:808
  36.1 2.6 %all-to-all-done.slabs_ref.near_ref = bf16[8,128,1024]{2,1,0:T(8,128)(2,1)} async-done(((bf16[8,128,1024]{2,1,0:T(8,128)(2,1)}), bf16[8,128,1024]{2,1,0:T(8,128)(2,1)}, u32[]{:S(2)}, u32[]{:S(2)}) %all-to-all-start) | async-done | bytes 2097184 | tf_op jit(solution)/shard_map/all_to_all | solution.py:789
  38.7 4.3 %all-to-all-start.1 = ((bf16[8,128,1024]{2,1,0:T(8,128)(2,1)}), bf16[8,128,1024]{2,1,0:T(8,128)(2,1)}, u32[]{:S(2)}, u32[]{:S(2)}) async-start(bf16[8,128,1024]{2,1,0:T(8,128)(2,1)} %select_rows.1.refs_1_), calls=%async_computation.1 | async-start | bytes 4194304 | tf_op jit(solution)/shard_map/all_to_all | solution.py:789
  43.0 4.1 %own_half.1 = (f32[512,512]{1,0:T(8,128)}, f32[8,512]{1,0:T(8,128)S(1)}, bf16[512,1024]{1,0:T(8,128)(2,1)S(1)}) custom-call(bf16[512,1024]{1,0:T(8,128)(2,1)} %source_ref.1, bf16[8,128,1024]{2,1,0:T(8,128)(2,1)} %all-to-all-done.slabs_ref.near_ref, s32[1,512]{1,0:T(1,128)} %bitcast.2.chosen_ref), custom_call_target="tpu_custom_call" | custom-call | flops 137438953472 | bytes 4194304 | tf_op jit(solution)/shard_map/own_half/pallas_call | solution.py:355
  47.2 11.7 %collective-permute-done.2.outer_ref = bf16[512,1024]{1,0:T(8,128)(2,1)S(1)} collective-permute-done((bf16[512,1024]{1,0:T(8,128)(2,1)}, bf16[512,1024]{1,0:T(8,128)(2,1)S(1)}, u32[]{:S(2)}, u32[]{:S(2)}) %collective-permute-start.2) | collective-permute-done | bytes 1048608 | tf_op jit(solution)/shard_map/ppermute | solution.py:808
  58.8 3.8 %other_half.1 = (f32[512,512]{1,0:T(8,128)S(1)}, f32[512,512]{1,0:T(8,128)}, f32[8,512]{1,0:T(8,128)S(1)}, bf16[512,1024]{1,0:T(8,128)(2,1)S(1)}, bf16[8,64,1024]{2,1,0:T(8,128)(2,1)S(1)}) custom-call(bf16[512,1024]{1,0:T(8,128)(2,1)} %collective-permute-done.inner_ref, bf16[512,1024]{1,0:T(8,128)(2,1)S(1)} %collective-permute-done.2.outer_ref, ...), custom_call_target="tpu_custom_call" | custom-call | flops 137438953472 | bytes 8388608 | tf_op jit(solution)/shard_map/other_half/pallas_call | solution.py:411
  64.7 5.0 %all-to-all-done.1.far_ref = bf16[8,128,1024]{2,1,0:T(8,128)(2,1)} async-done(((bf16[8,128,1024]{2,1,0:T(8,128)(2,1)}), bf16[8,128,1024]{2,1,0:T(8,128)(2,1)}, u32[]{:S(2)}, u32[]{:S(2)}) %all-to-all-start.1) | async-done | bytes 2097184 | tf_op jit(solution)/shard_map/all_to_all | solution.py:789
  69.7 4.2 %rest_half.1 = (f32[2,512,512]{2,1,0:T(8,128)S(1)}, f32[8,512]{1,0:T(8,128)S(1)}, s32[8,512]{1,0:T(8,128)S(1)}, s32[8,512]{1,0:T(8,128)S(1)}, bf16[8,64,1024]{2,1,0:T(8,128)(2,1)S(1)}) custom-call(bf16[512,1024]{1,0:T(8,128)(2,1)S(1)} %get-tuple-element.33.queries_ref, bf16[512,1024]{1,0:T(8,128)(2,1)S(1)} %get-tuple-element.34.others_ref, ...), custom_call_target="tpu_custom_call" | custom-call | flops 1610612736 | bytes 8388608 | tf_op jit(solution)/shard_map/rest_half/pallas_call | solution.py:463
  73.9 2.5 %collective-permute-start.4 = (f32[8,512]{1,0:T(8,128)S(1)}, f32[8,512]{1,0:T(8,128)S(1)}, u32[]{:S(2)}, u32[]{:S(2)}) collective-permute-start(f32[8,512]{1,0:T(8,128)S(1)} %get-tuple-element.39.stats_ref.here_ref), channel_id=1, source_target_pairs={{0,6},{2,4},{4,2},{6,0},{1,7},{3,5},{5,3},{7,1},{8,14},{10,12},{12... | collective-permute-start | bytes 49160 | tf_op jit(solution)/shard_map/ppermute | solution.py:821
  76.5 2.4 %early_grads.1 = (f32[512,1024]{1,0:T(8,128)S(1)}, f32[512,1024]{1,0:T(8,128)S(1)}) custom-call(f32[8,512]{1,0:T(8,128)S(1)} %get-tuple-element.39.stats_ref.here_ref, s32[8,512]{1,0:T(8,128)S(1)} %get-tuple-element.40.near_target_ref.target_ref, s32[8,512]{1,0:T(8,128)S(1)} %get-tuple-element.38.far_target_ref.target_ref, f32[512,512]{1,0:T(8,128)S(1)} %copy-done.11, ...), custom_call_target="tpu_custom_call" | custom-call | flops 137438953472 | bytes 4194304 | tf_op jit(solution)/shard_map/early_grads/pallas_call | solution.py:583
  79.5 3.0 %far_grads.1 = (bf16[8,128,1024]{2,1,0:T(8,128)(2,1)}, bf16[512,512]{1,0:T(8,128)(2,1)}, f32[8,512]{1,0:T(8,128)S(1)}, f32[1,512]{1,0:T(1,128)}) custom-call(bf16[512,1024]{1,0:T(8,128)(2,1)S(1)} %get-tuple-element.33.queries_ref, bf16[512,1024]{1,0:T(8,128)(2,1)S(1)} %copy-done.1, f32[2,512,512]{2,1,0:T(8,128)S(1)} %get-tuple-element.37.far_logits_ref.logits_ref, ...), custom_call_target="tpu_custom_call" | custom-call | flops 1073741824 | bytes 4194304 | tf_op jit(solution)/shard_map/far_grads/pallas_call | solution.py:659
  82.5 4.5 %all-to-all-start.2 = ((bf16[8,128,1024]{2,1,0:T(8,128)(2,1)}), bf16[8,128,1024]{2,1,0:T(8,128)(2,1)}, u32[]{:S(2)}, u32[]{:S(2)}) async-start(bf16[8,128,1024]{2,1,0:T(8,128)(2,1)} %get-tuple-element.52), calls=%async_computation.2 | async-start | bytes 4194304 | tf_op jit(solution)/shard_map/all_to_all | solution.py:789
  90.1 2.5 %collective-permute-start.5 = (bf16[512,1024]{1,0:T(8,128)(2,1)}, bf16[512,1024]{1,0:T(8,128)(2,1)}, u32[]{:S(2)}, u32[]{:S(2)}) collective-permute-start(bf16[512,1024]{1,0:T(8,128)(2,1)} %other_grads.1), channel_id=1, source_target_pairs={{0,6},{2,4},{4,2},{6,0},{1,7},{3,5},{5,3},{7,1},{8,14},{10,12},{12... | collective-permute-start | bytes 3145736 | tf_op jit(solution)/shard_map/ppermute | solution.py:834
  92.6 7.2 %near_grads.1 = (bf16[4,128,1024]{2,1,0:T(8,128)(2,1)}, bf16[128,1024]{1,0:T(8,128)(2,1)}, bf16[128,1024]{1,0:T(8,128)(2,1)}, bf16[128,1024]{1,0:T(8,128)(2,1)},...) custom-call(bf16[512,1024]{1,0:T(8,128)(2,1)S(1)} %get-tuple-element.33.queries_ref, bf16[512,1024]{1,0:T(8,128)(2,1)S(1)} %copy-done.2, ...), custom_call_target="tpu_custom_call" | custom-call | flops 2147483648 | bytes 8388608 | tf_op jit(solution)/shard_map/near_grads/pallas_call | solution.py:725
  104.0 1.6 %join_cores.1 = (bf16[256,1024]{1,0:T(8,128)(2,1)}, bf16[256,1024]{1,0:T(8,128)(2,1)}, bf16[256,1024]{1,0:T(8,128)(2,1)}, bf16[256,1024]{1,0:T(8,128)(2,1)}) custom-call(bf16[4,128,1024]{2,1,0:T(8,128)(2,1)S(1)} %copy-done.7, bf16[128,1024]{1,0:T(8,128)(2,1)S(1)} %collective-permute-done.6.refs_0_, bf16[128,1024]{1,0:T(8,128)(2,1)S(1)} %collective-permute-done.7.refs_1_, ...), custom_call_target="tpu_custom_call" | custom-call | flops 1048576 | bytes 4194304 | tf_op jit(solution)/shard_map/join_cores/pallas_call | solution.py:171
  105.6 1.8 %collective-permute-start.10 = (bf16[256,1024]{1,0:T(8,128)(2,1)}, bf16[256,1024]{1,0:T(8,128)(2,1)S(1)}, u32[]{:S(2)}, u32[]{:S(2)}) collective-permute-start(bf16[256,1024]{1,0:T(8,128)(2,1)} %get-tuple-element.59), channel_id=1, source_target_pairs={{0,8},{1,9},{8,0},{9,1},{16,24},{17,25},{24,16},{25,17},{2,10},{3,... | collective-permute-start | bytes 1572872 | tf_op jit(solution)/shard_map/ppermute | solution.py:838
  109.2 4.9 %all-to-all-done.2 = bf16[8,128,1024]{2,1,0:T(8,128)(2,1)} async-done(((bf16[8,128,1024]{2,1,0:T(8,128)(2,1)}), bf16[8,128,1024]{2,1,0:T(8,128)(2,1)}, u32[]{:S(2)}, u32[]{:S(2)}) %all-to-all-start.2) | async-done | bytes 2097184 | tf_op jit(solution)/shard_map/all_to_all | solution.py:789
  114.0 3.5 %segment_rows.2.refs_0_ = bf16[512,1024]{1,0:T(8,128)(2,1)} custom-call(bf16[512,1024]{1,0:T(8,128)(2,1)S(1)} %copy-done.4, bf16[1024,1024]{1,0:T(8,128)(2,1)} %bitcast.11.refs_0_), custom_call_target="tpu_custom_call" | custom-call | flops 1073741824 | bytes 4194304 | tf_op jit(solution)/shard_map/segment_rows/pallas_call | solution.py:230
  117.7 2.7 %add_parts.2.refs_4_ = bf16[512,1024]{1,0:T(8,128)(2,1)} custom-call(f32[512,1024]{1,0:T(8,128)} %get-tuple-element.50.own_ref, bf16[512,1024]{1,0:T(8,128)(2,1)} %collective-permute-done.5.part_ref, bf16[512,1024]{1,0:T(8,128)(2,1)} %segment_rows.2.refs_0_), custom_call_target="tpu_custom_call" | custom-call | flops 137438953472 | bytes 4194304 | tf_op jit(solution)/shard_map/add_parts/pallas_call | solution.py:762
  120.5 3.7 %collective-permute-done.10.refs_1_ = bf16[256,1024]{1,0:T(8,128)(2,1)S(1)} collective-permute-done((bf16[256,1024]{1,0:T(8,128)(2,1)}, bf16[256,1024]{1,0:T(8,128)(2,1)S(1)}, u32[]{:S(2)}, u32[]{:S(2)}) %collective-permute-start.10) | collective-permute-done | bytes 524320 | tf_op jit(solution)/shard_map/ppermute | solution.py:838
  125.1 11.0 %collective-permute-done.12.refs_3_ = bf16[256,1024]{1,0:T(8,128)(2,1)} collective-permute-done((bf16[256,1024]{1,0:T(8,128)(2,1)}, bf16[256,1024]{1,0:T(8,128)(2,1)}, u32[]{:S(2)}, u32[]{:S(2)}) %collective-permute-start.12) | collective-permute-done | bytes 524320 | tf_op jit(solution)/shard_map/ppermute | solution.py:838
  136.0 2.5 %segment_rows.3.own_ref = f32[512,1024]{1,0:T(8,128)S(1)} custom-call(bf16[512,1024]{1,0:T(8,128)(2,1)S(1)} %fusion.1.spread_ref, bf16[256,1024]{1,0:T(8,128)(2,1)S(1)} %copy-done.9, bf16[256,1024]{1,0:T(8,128)(2,1)S(1)} %collective-permute-done.10.refs_1_, bf16[256,1024]{1,0:T(8,128)(2,1)S(1)} %collective-permute-done.11.refs_2_, ...), custom_call_target="tpu_custom_call" | custom-call | flops 137438953472 | bytes 4194304 | tf_op jit(solution)/shard_map/segment_rows/pallas_call | solution.py:230
  140.1 2.1 %add_parts.3 = bf16[512,1024]{1,0:T(8,128)(2,1)} custom-call(f32[512,1024]{1,0:T(8,128)S(1)} %segment_rows.3.own_ref, bf16[512,1024]{1,0:T(8,128)(2,1)} %collective-permute-done.13.part_ref), custom_call_target="tpu_custom_call" | custom-call | flops 1048576 | bytes 4194304 | tf_op jit(solution)/shard_map/add_parts/pallas_call | solution.py:762
  (67 shorter events, 17.3 us)
Async XLA Ops:
  0.6 4.9 %copy-start.8 = (s32[32,4]{0,1:T(4,128)S(1)}, s32[32,4]{0,1:T(4,128)}, u32[]{:S(2)}) copy-start(s32[32,4]{0,1:T(4,128)} %param.8) | copy-start | bytes 1540
  0.6 26.5 %collective-permute-start.1 = (bf16[512,1024]{1,0:T(8,128)(2,1)}, bf16[512,1024]{1,0:T(8,128)(2,1)S(1)}, u32[]{:S(2)}, u32[]{:S(2)}) collective-permute-start(bf16[512,1024]{1,0:T(8,128)(2,1)} %bitcast.21), channel_id=1, source_target_pairs={{0,2},{2,0},{4,6},{6,4},{1,3},{3,1},{5,7},{7,5},{8,10},{10,8},{12,... | collective-permute-start | bytes 3145736 | tf_op jit(solution)/shard_map/ppermute | solution.py:794
  7.6 31.0 %all-to-all-start = ((bf16[8,128,1024]{2,1,0:T(8,128)(2,1)}), bf16[8,128,1024]{2,1,0:T(8,128)(2,1)}, u32[]{:S(2)}, u32[]{:S(2)}) async-start(bf16[8,128,1024]{2,1,0:T(8,128)(2,1)} %gather_rows.1), calls=%async_computation | async-start | bytes 4194304 | tf_op jit(solution)/shard_map/all_to_all | solution.py:789
  12.0 35.1 %collective-permute-start.3 = (s32[512]{0:T(512)}, s32[512]{0:T(512)}, u32[]{:S(2)}, u32[]{:S(2)}) collective-permute-start(s32[512]{0:T(512)} %param.9), channel_id=1, source_target_pairs={{0,6},{2,4},{4,2},{6,0},{1,7},{3,5},{5,3},{7,1},{8,14},{10,12},{12... | collective-permute-start | bytes 6152 | tf_op jit(solution)/shard_map/ppermute | solution.py:798
  14.6 32.6 %collective-permute-start = (bf16[512,1024]{1,0:T(8,128)(2,1)}, bf16[512,1024]{1,0:T(8,128)(2,1)}, u32[]{:S(2)}, u32[]{:S(2)}) collective-permute-start(bf16[512,1024]{1,0:T(8,128)(2,1)} %source_ref.1), channel_id=1, source_target_pairs={{2,4},{4,2},{3,5},{5,3},{10,12},{12,10},{11,13},{13,11},{18,20},{2... | collective-permute-start | bytes 3145736 | tf_op jit(solution)/shard_map/ppermute | solution.py:797
  29.4 1.0 copy-start.3
  30.4 28.4 %collective-permute-start.2 = (bf16[512,1024]{1,0:T(8,128)(2,1)}, bf16[512,1024]{1,0:T(8,128)(2,1)S(1)}, u32[]{:S(2)}, u32[]{:S(2)}) collective-permute-start(bf16[512,1024]{1,0:T(8,128)(2,1)} %after.1), channel_id=1, source_target_pairs={{0,6},{6,0},{1,7},{7,1},{8,14},{14,8},{9,15},{15,9},{16,22},{22,16... | collective-permute-start | bytes 3145736 | tf_op jit(solution)/shard_map/ppermute | solution.py:808
  38.7 31.0 %all-to-all-start.1 = ((bf16[8,128,1024]{2,1,0:T(8,128)(2,1)}), bf16[8,128,1024]{2,1,0:T(8,128)(2,1)}, u32[]{:S(2)}, u32[]{:S(2)}) async-start(bf16[8,128,1024]{2,1,0:T(8,128)(2,1)} %select_rows.1.refs_1_), calls=%async_computation.1 | async-start | bytes 4194304 | tf_op jit(solution)/shard_map/all_to_all | solution.py:789
  62.7 1.0 copy-start.10
  63.7 1.0 copy-start.12
  64.7 9.2 %copy-start = (bf16[512,1024]{1,0:T(8,128)(2,1)}, bf16[512,1024]{1,0:T(8,128)(2,1)S(1)}, u32[]{:S(2)}) copy-start(bf16[512,1024]{1,0:T(8,128)(2,1)S(1)} %get-tuple-element.34.others_ref) | copy-start | bytes 3145732
  69.7 6.8 %copy-start.11 = (f32[512,512]{1,0:T(8,128)S(1)}, f32[512,512]{1,0:T(8,128)}, u32[]{:S(2)}) copy-start(f32[512,512]{1,0:T(8,128)} %copy-done.10) | copy-start | bytes 3145732
  69.7 6.8 %copy-start.13 = (bf16[8,64,1024]{2,1,0:T(8,128)(2,1)S(1)}, bf16[8,64,1024]{2,1,0:T(8,128)(2,1)}, u32[]{:S(2)}) copy-start(bf16[8,64,1024]{2,1,0:T(8,128)(2,1)} %copy-done.12) | copy-start | bytes 3145732
  73.9 5.6 %collective-permute-start.4 = (f32[8,512]{1,0:T(8,128)S(1)}, f32[8,512]{1,0:T(8,128)S(1)}, u32[]{:S(2)}, u32[]{:S(2)}) collective-permute-start(f32[8,512]{1,0:T(8,128)S(1)} %get-tuple-element.39.stats_ref.here_ref), channel_id=1, source_target_pairs={{0,6},{2,4},{4,2},{6,0},{1,7},{3,5},{5,3},{7,1},{8,14},{10,12},{12... | collective-permute-start | bytes 49160 | tf_op jit(solution)/shard_map/ppermute | solution.py:821
  76.5 3.1 %copy-start.1 = (bf16[512,1024]{1,0:T(8,128)(2,1)S(1)}, bf16[512,1024]{1,0:T(8,128)(2,1)}, u32[]{:S(2)}) copy-start(bf16[512,1024]{1,0:T(8,128)(2,1)} %copy-done) | copy-start | bytes 3145732
  78.8 3.6 %copy-start.5 = (f32[512,1024]{1,0:T(8,128)}, f32[512,1024]{1,0:T(8,128)S(1)}, u32[]{:S(2)}) copy-start(f32[512,1024]{1,0:T(8,128)S(1)} %get-tuple-element.51.sums_ref) | copy-start | bytes 6291460
  82.5 31.5 %all-to-all-start.2 = ((bf16[8,128,1024]{2,1,0:T(8,128)(2,1)}), bf16[8,128,1024]{2,1,0:T(8,128)(2,1)}, u32[]{:S(2)}, u32[]{:S(2)}) async-start(bf16[8,128,1024]{2,1,0:T(8,128)(2,1)} %get-tuple-element.52), calls=%async_computation.2 | async-start | bytes 4194304 | tf_op jit(solution)/shard_map/all_to_all | solution.py:789
  87.0 1.6 %copy-start.6 = (f32[512,1024]{1,0:T(8,128)S(1)}, f32[512,1024]{1,0:T(8,128)}, u32[]{:S(2)}) copy-start(f32[512,1024]{1,0:T(8,128)} %copy-done.5) | copy-start | bytes 6291460
  88.6 4.0 %copy-start.2 = (bf16[512,1024]{1,0:T(8,128)(2,1)S(1)}, bf16[512,1024]{1,0:T(8,128)(2,1)}, u32[]{:S(2)}) copy-start(bf16[512,1024]{1,0:T(8,128)(2,1)} %copy-done) | copy-start | bytes 3145732
  90.1 27.6 %collective-permute-start.5 = (bf16[512,1024]{1,0:T(8,128)(2,1)}, bf16[512,1024]{1,0:T(8,128)(2,1)}, u32[]{:S(2)}, u32[]{:S(2)}) collective-permute-start(bf16[512,1024]{1,0:T(8,128)(2,1)} %other_grads.1), channel_id=1, source_target_pairs={{0,6},{2,4},{4,2},{6,0},{1,7},{3,5},{5,3},{7,1},{8,14},{10,12},{12... | collective-permute-start | bytes 3145736 | tf_op jit(solution)/shard_map/ppermute | solution.py:834
  92.6 8.3 %copy-start.14 = (s32[64,16]{1,0:T(8,128)S(1)}, s32[64,16]{1,0:T(8,128)}, u32[]{:S(2)}) copy-start(s32[64,16]{1,0:T(8,128)} %get-tuple-element.75) | copy-start | bytes 12292
  99.8 14.2 %copy-start.4 = (bf16[512,1024]{1,0:T(8,128)(2,1)S(1)}, bf16[512,1024]{1,0:T(8,128)(2,1)}, u32[]{:S(2)}) copy-start(bf16[512,1024]{1,0:T(8,128)(2,1)} %copy-done.3) | copy-start | bytes 3145732
  99.8 1.8 %collective-permute-start.6 = (bf16[128,1024]{1,0:T(8,128)(2,1)}, bf16[128,1024]{1,0:T(8,128)(2,1)S(1)}, u32[]{:S(2)}, u32[]{:S(2)}) collective-permute-start(bf16[128,1024]{1,0:T(8,128)(2,1)} %get-tuple-element.54), channel_id=1, source_target_pairs={{0,1},{1,0},{8,9},{9,8},{16,17},{17,16},{24,25},{25,24},{2,3},{3,2... | collective-permute-start | bytes 786440 | tf_op jit(solution)/shard_map/ppermute | solution.py:833
  99.9 2.1 %collective-permute-start.7 = (bf16[128,1024]{1,0:T(8,128)(2,1)}, bf16[128,1024]{1,0:T(8,128)(2,1)S(1)}, u32[]{:S(2)}, u32[]{:S(2)}) collective-permute-start(bf16[128,1024]{1,0:T(8,128)(2,1)} %get-tuple-element.55), channel_id=1, source_target_pairs={{0,1},{1,0},{8,9},{9,8},{16,17},{17,16},{24,25},{25,24},{2,3},{3,2... | collective-permute-start | bytes 786440 | tf_op jit(solution)/shard_map/ppermute | solution.py:833
  100.4 2.0 %collective-permute-start.8 = (bf16[128,1024]{1,0:T(8,128)(2,1)}, bf16[128,1024]{1,0:T(8,128)(2,1)S(1)}, u32[]{:S(2)}, u32[]{:S(2)}) collective-permute-start(bf16[128,1024]{1,0:T(8,128)(2,1)} %get-tuple-element.56), channel_id=1, source_target_pairs={{0,1},{1,0},{8,9},{9,8},{16,17},{17,16},{24,25},{25,24},{2,3},{3,2... | collective-permute-start | bytes 786440 | tf_op jit(solution)/shard_map/ppermute | solution.py:833
  100.5 2.3 %collective-permute-start.9 = (bf16[128,1024]{1,0:T(8,128)(2,1)}, bf16[128,1024]{1,0:T(8,128)(2,1)S(1)}, u32[]{:S(2)}, u32[]{:S(2)}) collective-permute-start(bf16[128,1024]{1,0:T(8,128)(2,1)} %get-tuple-element.57), channel_id=1, source_target_pairs={{0,1},{1,0},{8,9},{9,8},{16,17},{17,16},{24,25},{25,24},{2,3},{3,2... | collective-permute-start | bytes 786440 | tf_op jit(solution)/shard_map/ppermute | solution.py:833
  102.8 1.2 copy-start.7
  105.6 18.6 %collective-permute-start.10 = (bf16[256,1024]{1,0:T(8,128)(2,1)}, bf16[256,1024]{1,0:T(8,128)(2,1)S(1)}, u32[]{:S(2)}, u32[]{:S(2)}) collective-permute-start(bf16[256,1024]{1,0:T(8,128)(2,1)} %get-tuple-element.59), channel_id=1, source_target_pairs={{0,8},{1,9},{8,0},{9,1},{16,24},{17,25},{24,16},{25,17},{2,10},{3,... | collective-permute-start | bytes 1572872 | tf_op jit(solution)/shard_map/ppermute | solution.py:838
  107.4 17.7 %collective-permute-start.11 = (bf16[256,1024]{1,0:T(8,128)(2,1)}, bf16[256,1024]{1,0:T(8,128)(2,1)S(1)}, u32[]{:S(2)}, u32[]{:S(2)}) collective-permute-start(bf16[256,1024]{1,0:T(8,128)(2,1)} %get-tuple-element.60), channel_id=1, source_target_pairs={{0,16},{1,17},{8,24},{9,25},{16,0},{17,1},{24,8},{25,9},{2,18},{3,... | collective-permute-start | bytes 1572872 | tf_op jit(solution)/shard_map/ppermute | solution.py:838
  108.9 27.1 %collective-permute-start.12 = (bf16[256,1024]{1,0:T(8,128)(2,1)}, bf16[256,1024]{1,0:T(8,128)(2,1)}, u32[]{:S(2)}, u32[]{:S(2)}) collective-permute-start(bf16[256,1024]{1,0:T(8,128)(2,1)} %get-tuple-element.61), channel_id=1, source_target_pairs={{0,24},{1,25},{8,16},{9,17},{16,8},{17,9},{24,0},{25,1},{2,26},{3,... | collective-permute-start | bytes 1572872 | tf_op jit(solution)/shard_map/ppermute | solution.py:838
  117.5 22.6 %collective-permute-start.13 = (bf16[512,1024]{1,0:T(8,128)(2,1)}, bf16[512,1024]{1,0:T(8,128)(2,1)}, u32[]{:S(2)}, u32[]{:S(2)}) collective-permute-start(bf16[512,1024]{1,0:T(8,128)(2,1)} %segment_rows.2.refs_0_), channel_id=1, source_target_pairs={{0,2},{2,0},{4,6},{6,4},{1,3},{3,1},{5,7},{7,5},{8,10},{10,8},{12,... | collective-permute-start | bytes 3145736 | tf_op jit(solution)/shard_map/ppermute | solution.py:836
  117.7 18.3 %copy-start.9 = (bf16[256,1024]{1,0:T(8,128)(2,1)S(1)}, bf16[256,1024]{1,0:T(8,128)(2,1)}, u32[]{:S(2)}) copy-start(bf16[256,1024]{1,0:T(8,128)(2,1)} %get-tuple-element.58.refs_0_) | copy-start | bytes 1572868

commit v10 on v9

--- a/solution.py
+++ b/solution.py
@@ -222,7 +222,7 @@
 
 
 def segment_rows(spread, arrays, wait=None):
-    stripes = 2
+    stripes = 1
     rows, depth = spread.shape
     width = arrays[0].shape[-1]
     tile = width // stripes

time: 144 us -> 144 us (level)
  transfers between devices with their start and end apart: 17 -> 17, of which waited for: 15 -> 14; matrix products, arithmetic and copies ran while one was open for 3% -> 3% of each run, Pallas kernels for 25% -> 25%
where the time goes in v10:
time: 144 us; the launch traced here: 142 us
  waiting for transfers between devices  50 us (35%)
  Pallas kernels  45.1 us (31%)
  starting transfers between devices  36 us (25%)
  local copies, waits for them, and re-layouts  8.68 us (6%)
    ppermute x3, waiting for transfers between devices, on_device(): lax.ppermute(array, PLANE, [(i, i ^ 2 * g) for i in range(slabs)])  15.3 us
    all_to_all x3, starting transfers between devices, exchange(): lax.all_to_all(slab_array, PLANE, split_axis=0, concat_axis=0, tiled=True)  13.3 us
    all_to_all x3, waiting for transfers between devices, exchange(): lax.all_to_all(slab_array, PLANE, split_axis=0, concat_axis=0, tiled=True)  12.5 us
    ppermute x1, waiting for transfers between devices, on_device(): lax.ppermute(after(copy_rows(in_hbm(queries)), in_hbm(far_sent), where=HB...  11.7 us
    unnamed x32, local copies, waits for them, and re-layouts  7.72 us
    pallas_call x1, Pallas kernels, near_grads(): pl.pallas_call(functools.partial(near_kernel, ranks), in_specs=[VMEM] * 4...  7.16 us
    ppermute x1, waiting for transfers between devices, on_device(): lax.ppermute(passages.reshape(height * blocks, width), 'z', to_pair)  6.81 us
    pallas_call x2, Pallas kernels, segment_rows(): pl.pallas_call(functools.partial(segment_kernel, stripes, len(arrays)), i...  6.27 us
  transfers between devices with their start and end apart: 17, of which 14 were waited for; matrix products, arithmetic and copies ran while one was open for 3% of the time, Pallas kernels for 25%

profile of v10, /device:TPU:0, one launch (start us, length us, event | category | flops | bytes accessed | tf_op | source)
XLA Modules:
  0.0 142.3 jit_solution(151716659339045161)
XLA Ops:
  0.6 3.1 %collective-permute-start.1 = (bf16[512,1024]{1,0:T(8,128)(2,1)}, bf16[512,1024]{1,0:T(8,128)(2,1)S(1)}, u32[]{:S(2)}, u32[]{:S(2)}) collective-permute-start(bf16[512,1024]{1,0:T(8,128)(2,1)} %bitcast.21), channel_id=1, source_target_pairs={{0,2},{2,0},{4,6},{6,4},{1,3},{3,1},{5,7},{7,5},{8,10},{10,8},{12,... | collective-permute-start | bytes 3145736 | tf_op jit(solution)/shard_map/ppermute | solution.py:794
  3.7 1.8 %copy.17 = bf16[16,32,1024]{2,0,1:T(8,128)(2,1)S(1)} copy(bf16[16,32,1024]{2,1,0:T(8,128)(2,1)} %param.7) | data formatting | bytes 2097152 | tf_op args[1]
  5.6 2.1 %gather_rows.1 = bf16[8,128,1024]{2,1,0:T(8,128)(2,1)} custom-call(s32[4,32]{1,0:T(4,128)S(1)} %bitcast.20, bf16[32,16,1024]{2,1,0:T(8,128)(2,1)S(1)} %bitcast.19), custom_call_target="tpu_custom_call" | custom-call | bytes 4194304 | tf_op jit(solution)/shard_map/gather_rows/pallas_call | solution.py:107
  7.6 4.4 %all-to-all-start = ((bf16[8,128,1024]{2,1,0:T(8,128)(2,1)}), bf16[8,128,1024]{2,1,0:T(8,128)(2,1)}, u32[]{:S(2)}, u32[]{:S(2)}) async-start(bf16[8,128,1024]{2,1,0:T(8,128)(2,1)} %gather_rows.1), calls=%async_computation | async-start | bytes 4194304 | tf_op jit(solution)/shard_map/all_to_all | solution.py:789
  12.0 2.5 %collective-permute-start.3 = (s32[512]{0:T(512)}, s32[512]{0:T(512)}, u32[]{:S(2)}, u32[]{:S(2)}) collective-permute-start(s32[512]{0:T(512)} %param.9), channel_id=1, source_target_pairs={{0,6},{2,4},{4,2},{6,0},{1,7},{3,5},{5,3},{7,1},{8,14},{10,12},{12... | collective-permute-start | bytes 6152 | tf_op jit(solution)/shard_map/ppermute | solution.py:798
  14.6 1.6 %collective-permute-start = (bf16[512,1024]{1,0:T(8,128)(2,1)}, bf16[512,1024]{1,0:T(8,128)(2,1)}, u32[]{:S(2)}, u32[]{:S(2)}) collective-permute-start(bf16[512,1024]{1,0:T(8,128)(2,1)} %source_ref.1), channel_id=1, source_target_pairs={{2,4},{4,2},{3,5},{5,3},{10,12},{12,10},{11,13},{13,11},{18,20},{2... | collective-permute-start | bytes 3145736 | tf_op jit(solution)/shard_map/ppermute | solution.py:797
  16.5 2.0 %copy_rows.1.refs_0_ = bf16[512,1024]{1,0:T(8,128)(2,1)} custom-call(bf16[512,1024]{1,0:T(8,128)(2,1)} %source_ref.1), custom_call_target="tpu_custom_call" | custom-call | bytes 2097152 | tf_op jit(solution)/shard_map/copy_rows/pallas_call | solution.py:67
  20.3 6.8 %collective-permute-done.1.rows_ref = bf16[512,1024]{1,0:T(8,128)(2,1)S(1)} collective-permute-done((bf16[512,1024]{1,0:T(8,128)(2,1)}, bf16[512,1024]{1,0:T(8,128)(2,1)S(1)}, u32[]{:S(2)}, u32[]{:S(2)}) %collective-permute-start.1) | collective-permute-done | bytes 1048608 | tf_op jit(solution)/shard_map/ppermute | solution.py:794
  27.1 2.3 %select_rows.1.refs_1_ = bf16[8,128,1024]{2,1,0:T(8,128)(2,1)} custom-call(bf16[512,1024]{1,0:T(8,128)(2,1)S(1)} %fusion.spread_ref, bf16[512,1024]{1,0:T(8,128)(2,1)S(1)} %collective-permute-done.1.rows_ref), custom_call_target="tpu_custom_call" | custom-call | flops 137438953472 | bytes 4194304 | tf_op jit(solution)/shard_map/select_rows/pallas_call | solution.py:138
  30.4 5.7 %collective-permute-start.2 = (bf16[512,1024]{1,0:T(8,128)(2,1)}, bf16[512,1024]{1,0:T(8,128)(2,1)S(1)}, u32[]{:S(2)}, u32[]{:S(2)}) collective-permute-start(bf16[512,1024]{1,0:T(8,128)(2,1)} %after.1), channel_id=1, source_target_pairs={{0,6},{6,0},{1,7},{7,1},{8,14},{14,8},{9,15},{15,9},{16,22},{22,16... | collective-permute-start | bytes 3145736 | tf_op jit(solution)/shard_map/ppermute | solution.py:808
  36.1 2.6 %all-to-all-done.slabs_ref.near_ref = bf16[8,128,1024]{2,1,0:T(8,128)(2,1)} async-done(((bf16[8,128,1024]{2,1,0:T(8,128)(2,1)}), bf16[8,128,1024]{2,1,0:T(8,128)(2,1)}, u32[]{:S(2)}, u32[]{:S(2)}) %all-to-all-start) | async-done | bytes 2097184 | tf_op jit(solution)/shard_map/all_to_all | solution.py:789
  38.7 4.3 %all-to-all-start.1 = ((bf16[8,128,1024]{2,1,0:T(8,128)(2,1)}), bf16[8,128,1024]{2,1,0:T(8,128)(2,1)}, u32[]{:S(2)}, u32[]{:S(2)}) async-start(bf16[8,128,1024]{2,1,0:T(8,128)(2,1)} %select_rows.1.refs_1_), calls=%async_computation.1 | async-start | bytes 4194304 | tf_op jit(solution)/shard_map/all_to_all | solution.py:789
  43.0 4.1 %own_half.1 = (f32[512,512]{1,0:T(8,128)}, f32[8,512]{1,0:T(8,128)S(1)}, bf16[512,1024]{1,0:T(8,128)(2,1)S(1)}) custom-call(bf16[512,1024]{1,0:T(8,128)(2,1)} %source_ref.1, bf16[8,128,1024]{2,1,0:T(8,128)(2,1)} %all-to-all-done.slabs_ref.near_ref, s32[1,512]{1,0:T(1,128)} %bitcast.2.chosen_ref), custom_call_target="tpu_custom_call" | custom-call | flops 137438953472 | bytes 4194304 | tf_op jit(solution)/shard_map/own_half/pallas_call | solution.py:355
  47.2 11.7 %collective-permute-done.2.outer_ref = bf16[512,1024]{1,0:T(8,128)(2,1)S(1)} collective-permute-done((bf16[512,1024]{1,0:T(8,128)(2,1)}, bf16[512,1024]{1,0:T(8,128)(2,1)S(1)}, u32[]{:S(2)}, u32[]{:S(2)}) %collective-permute-start.2) | collective-permute-done | bytes 1048608 | tf_op jit(solution)/shard_map/ppermute | solution.py:808
  58.8 3.8 %other_half.1 = (f32[512,512]{1,0:T(8,128)S(1)}, f32[512,512]{1,0:T(8,128)}, f32[8,512]{1,0:T(8,128)S(1)}, bf16[512,1024]{1,0:T(8,128)(2,1)S(1)}, bf16[8,64,1024]{2,1,0:T(8,128)(2,1)S(1)}) custom-call(bf16[512,1024]{1,0:T(8,128)(2,1)} %collective-permute-done.inner_ref, bf16[512,1024]{1,0:T(8,128)(2,1)S(1)} %collective-permute-done.2.outer_ref, ...), custom_call_target="tpu_custom_call" | custom-call | flops 137438953472 | bytes 8388608 | tf_op jit(solution)/shard_map/other_half/pallas_call | solution.py:411
  64.7 5.0 %all-to-all-done.1.far_ref = bf16[8,128,1024]{2,1,0:T(8,128)(2,1)} async-done(((bf16[8,128,1024]{2,1,0:T(8,128)(2,1)}), bf16[8,128,1024]{2,1,0:T(8,128)(2,1)}, u32[]{:S(2)}, u32[]{:S(2)}) %all-to-all-start.1) | async-done | bytes 2097184 | tf_op jit(solution)/shard_map/all_to_all | solution.py:789
  69.7 4.2 %rest_half.1 = (f32[2,512,512]{2,1,0:T(8,128)S(1)}, f32[8,512]{1,0:T(8,128)S(1)}, s32[8,512]{1,0:T(8,128)S(1)}, s32[8,512]{1,0:T(8,128)S(1)}, bf16[8,64,1024]{2,1,0:T(8,128)(2,1)S(1)}) custom-call(bf16[512,1024]{1,0:T(8,128)(2,1)S(1)} %get-tuple-element.33.queries_ref, bf16[512,1024]{1,0:T(8,128)(2,1)S(1)} %get-tuple-element.34.others_ref, ...), custom_call_target="tpu_custom_call" | custom-call | flops 1610612736 | bytes 8388608 | tf_op jit(solution)/shard_map/rest_half/pallas_call | solution.py:463
  73.9 2.5 %collective-permute-start.4 = (f32[8,512]{1,0:T(8,128)S(1)}, f32[8,512]{1,0:T(8,128)S(1)}, u32[]{:S(2)}, u32[]{:S(2)}) collective-permute-start(f32[8,512]{1,0:T(8,128)S(1)} %get-tuple-element.39.stats_ref.here_ref), channel_id=1, source_target_pairs={{0,6},{2,4},{4,2},{6,0},{1,7},{3,5},{5,3},{7,1},{8,14},{10,12},{12... | collective-permute-start | bytes 49160 | tf_op jit(solution)/shard_map/ppermute | solution.py:821
  76.5 2.4 %early_grads.1 = (f32[512,1024]{1,0:T(8,128)S(1)}, f32[512,1024]{1,0:T(8,128)S(1)}) custom-call(f32[8,512]{1,0:T(8,128)S(1)} %get-tuple-element.39.stats_ref.here_ref, s32[8,512]{1,0:T(8,128)S(1)} %get-tuple-element.40.near_target_ref.target_ref, s32[8,512]{1,0:T(8,128)S(1)} %get-tuple-element.38.far_target_ref.target_ref, f32[512,512]{1,0:T(8,128)S(1)} %copy-done.11, ...), custom_call_target="tpu_custom_call" | custom-call | flops 137438953472 | bytes 4194304 | tf_op jit(solution)/shard_map/early_grads/pallas_call | solution.py:583
  79.5 3.0 %far_grads.1 = (bf16[8,128,1024]{2,1,0:T(8,128)(2,1)}, bf16[512,512]{1,0:T(8,128)(2,1)}, f32[8,512]{1,0:T(8,128)S(1)}, f32[1,512]{1,0:T(1,128)}) custom-call(bf16[512,1024]{1,0:T(8,128)(2,1)S(1)} %get-tuple-element.33.queries_ref, bf16[512,1024]{1,0:T(8,128)(2,1)S(1)} %copy-done.1, f32[2,512,512]{2,1,0:T(8,128)S(1)} %get-tuple-element.37.far_logits_ref.logits_ref, ...), custom_call_target="tpu_custom_call" | custom-call | flops 1073741824 | bytes 4194304 | tf_op jit(solution)/shard_map/far_grads/pallas_call | solution.py:659
  82.5 4.5 %all-to-all-start.2 = ((bf16[8,128,1024]{2,1,0:T(8,128)(2,1)}), bf16[8,128,1024]{2,1,0:T(8,128)(2,1)}, u32[]{:S(2)}, u32[]{:S(2)}) async-start(bf16[8,128,1024]{2,1,0:T(8,128)(2,1)} %get-tuple-element.52), calls=%async_computation.2 | async-start | bytes 4194304 | tf_op jit(solution)/shard_map/all_to_all | solution.py:789
  90.1 2.5 %collective-permute-start.5 = (bf16[512,1024]{1,0:T(8,128)(2,1)}, bf16[512,1024]{1,0:T(8,128)(2,1)}, u32[]{:S(2)}, u32[]{:S(2)}) collective-permute-start(bf16[512,1024]{1,0:T(8,128)(2,1)} %other_grads.1), channel_id=1, source_target_pairs={{0,6},{2,4},{4,2},{6,0},{1,7},{3,5},{5,3},{7,1},{8,14},{10,12},{12... | collective-permute-start | bytes 3145736 | tf_op jit(solution)/shard_map/ppermute | solution.py:834
  92.6 7.2 %near_grads.1 = (bf16[4,128,1024]{2,1,0:T(8,128)(2,1)}, bf16[128,1024]{1,0:T(8,128)(2,1)}, bf16[128,1024]{1,0:T(8,128)(2,1)}, bf16[128,1024]{1,0:T(8,128)(2,1)},...) custom-call(bf16[512,1024]{1,0:T(8,128)(2,1)S(1)} %get-tuple-element.33.queries_ref, bf16[512,1024]{1,0:T(8,128)(2,1)S(1)} %copy-done.2, ...), custom_call_target="tpu_custom_call" | custom-call | flops 2147483648 | bytes 8388608 | tf_op jit(solution)/shard_map/near_grads/pallas_call | solution.py:725
  105.6 1.8 %collective-permute-start.10 = (bf16[256,1024]{1,0:T(8,128)(2,1)}, bf16[256,1024]{1,0:T(8,128)(2,1)S(1)}, u32[]{:S(2)}, u32[]{:S(2)}) collective-permute-start(bf16[256,1024]{1,0:T(8,128)(2,1)} %get-tuple-element.59), channel_id=1, source_target_pairs={{0,8},{1,9},{8,0},{9,1},{16,24},{17,25},{24,16},{25,17},{2,10},{3,... | collective-permute-start | bytes 1572872 | tf_op jit(solution)/shard_map/ppermute | solution.py:838
  109.2 4.9 %all-to-all-done.2 = bf16[8,128,1024]{2,1,0:T(8,128)(2,1)} async-done(((bf16[8,128,1024]{2,1,0:T(8,128)(2,1)}), bf16[8,128,1024]{2,1,0:T(8,128)(2,1)}, u32[]{:S(2)}, u32[]{:S(2)}) %all-to-all-start.2) | async-done | bytes 2097184 | tf_op jit(solution)/shard_map/all_to_all | solution.py:789
  114.0 3.8 %segment_rows.2.refs_0_ = bf16[512,1024]{1,0:T(8,128)(2,1)} custom-call(bf16[512,1024]{1,0:T(8,128)(2,1)S(1)} %copy-done.4, bf16[1024,1024]{1,0:T(8,128)(2,1)} %bitcast.11.refs_0_), custom_call_target="tpu_custom_call" | custom-call | flops 1073741824 | bytes 4194304 | tf_op jit(solution)/shard_map/segment_rows/pallas_call | solution.py:230
  118.0 2.7 %add_parts.2.refs_4_ = bf16[512,1024]{1,0:T(8,128)(2,1)} custom-call(f32[512,1024]{1,0:T(8,128)} %get-tuple-element.50.own_ref, bf16[512,1024]{1,0:T(8,128)(2,1)} %collective-permute-done.5.part_ref, bf16[512,1024]{1,0:T(8,128)(2,1)} %segment_rows.2.refs_0_), custom_call_target="tpu_custom_call" | custom-call | flops 137438953472 | bytes 4194304 | tf_op jit(solution)/shard_map/add_parts/pallas_call | solution.py:762
  120.7 3.5 %collective-permute-done.10.refs_1_ = bf16[256,1024]{1,0:T(8,128)(2,1)S(1)} collective-permute-done((bf16[256,1024]{1,0:T(8,128)(2,1)}, bf16[256,1024]{1,0:T(8,128)(2,1)S(1)}, u32[]{:S(2)}, u32[]{:S(2)}) %collective-permute-start.10) | collective-permute-done | bytes 524320 | tf_op jit(solution)/shard_map/ppermute | solution.py:838
  125.1 11.0 %collective-permute-done.12.refs_3_ = bf16[256,1024]{1,0:T(8,128)(2,1)} collective-permute-done((bf16[256,1024]{1,0:T(8,128)(2,1)}, bf16[256,1024]{1,0:T(8,128)(2,1)}, u32[]{:S(2)}, u32[]{:S(2)}) %collective-permute-start.12) | collective-permute-done | bytes 524320 | tf_op jit(solution)/shard_map/ppermute | solution.py:838
  136.0 2.4 %segment_rows.3.own_ref = f32[512,1024]{1,0:T(8,128)S(1)} custom-call(bf16[512,1024]{1,0:T(8,128)(2,1)S(1)} %fusion.1.spread_ref, bf16[256,1024]{1,0:T(8,128)(2,1)S(1)} %copy-done.9, bf16[256,1024]{1,0:T(8,128)(2,1)S(1)} %collective-permute-done.10.refs_1_, bf16[256,1024]{1,0:T(8,128)(2,1)S(1)} %collective-permute-done.11.refs_2_, ...), custom_call_target="tpu_custom_call" | custom-call | flops 137438953472 | bytes 4194304 | tf_op jit(solution)/shard_map/segment_rows/pallas_call | solution.py:230
  138.5 1.6 %collective-permute-done.13.part_ref = bf16[512,1024]{1,0:T(8,128)(2,1)} collective-permute-done((bf16[512,1024]{1,0:T(8,128)(2,1)}, bf16[512,1024]{1,0:T(8,128)(2,1)}, u32[]{:S(2)}, u32[]{:S(2)}) %collective-permute-start.13) | collective-permute-done | bytes 1048608 | tf_op jit(solution)/shard_map/ppermute | solution.py:836
  140.1 2.1 %add_parts.3 = bf16[512,1024]{1,0:T(8,128)(2,1)} custom-call(f32[512,1024]{1,0:T(8,128)S(1)} %segment_rows.3.own_ref, bf16[512,1024]{1,0:T(8,128)(2,1)} %collective-permute-done.13.part_ref), custom_call_target="tpu_custom_call" | custom-call | flops 1048576 | bytes 4194304 | tf_op jit(solution)/shard_map/add_parts/pallas_call | solution.py:762
  (67 shorter events, 17.2 us)
Async XLA Ops:
  0.6 4.9 %copy-start.8 = (s32[32,4]{0,1:T(4,128)S(1)}, s32[32,4]{0,1:T(4,128)}, u32[]{:S(2)}) copy-start(s32[32,4]{0,1:T(4,128)} %param.8) | copy-start | bytes 1540
  0.6 26.5 %collective-permute-start.1 = (bf16[512,1024]{1,0:T(8,128)(2,1)}, bf16[512,1024]{1,0:T(8,128)(2,1)S(1)}, u32[]{:S(2)}, u32[]{:S(2)}) collective-permute-start(bf16[512,1024]{1,0:T(8,128)(2,1)} %bitcast.21), channel_id=1, source_target_pairs={{0,2},{2,0},{4,6},{6,4},{1,3},{3,1},{5,7},{7,5},{8,10},{10,8},{12,... | collective-permute-start | bytes 3145736 | tf_op jit(solution)/shard_map/ppermute | solution.py:794
  7.6 31.0 %all-to-all-start = ((bf16[8,128,1024]{2,1,0:T(8,128)(2,1)}), bf16[8,128,1024]{2,1,0:T(8,128)(2,1)}, u32[]{:S(2)}, u32[]{:S(2)}) async-start(bf16[8,128,1024]{2,1,0:T(8,128)(2,1)} %gather_rows.1), calls=%async_computation | async-start | bytes 4194304 | tf_op jit(solution)/shard_map/all_to_all | solution.py:789
  12.0 35.1 %collective-permute-start.3 = (s32[512]{0:T(512)}, s32[512]{0:T(512)}, u32[]{:S(2)}, u32[]{:S(2)}) collective-permute-start(s32[512]{0:T(512)} %param.9), channel_id=1, source_target_pairs={{0,6},{2,4},{4,2},{6,0},{1,7},{3,5},{5,3},{7,1},{8,14},{10,12},{12... | collective-permute-start | bytes 6152 | tf_op jit(solution)/shard_map/ppermute | solution.py:798
  14.6 32.6 %collective-permute-start = (bf16[512,1024]{1,0:T(8,128)(2,1)}, bf16[512,1024]{1,0:T(8,128)(2,1)}, u32[]{:S(2)}, u32[]{:S(2)}) collective-permute-start(bf16[512,1024]{1,0:T(8,128)(2,1)} %source_ref.1), channel_id=1, source_target_pairs={{2,4},{4,2},{3,5},{5,3},{10,12},{12,10},{11,13},{13,11},{18,20},{2... | collective-permute-start | bytes 3145736 | tf_op jit(solution)/shard_map/ppermute | solution.py:797
  29.4 1.0 copy-start.3
  30.4 28.4 %collective-permute-start.2 = (bf16[512,1024]{1,0:T(8,128)(2,1)}, bf16[512,1024]{1,0:T(8,128)(2,1)S(1)}, u32[]{:S(2)}, u32[]{:S(2)}) collective-permute-start(bf16[512,1024]{1,0:T(8,128)(2,1)} %after.1), channel_id=1, source_target_pairs={{0,6},{6,0},{1,7},{7,1},{8,14},{14,8},{9,15},{15,9},{16,22},{22,16... | collective-permute-start | bytes 3145736 | tf_op jit(solution)/shard_map/ppermute | solution.py:808
  38.7 31.0 %all-to-all-start.1 = ((bf16[8,128,1024]{2,1,0:T(8,128)(2,1)}), bf16[8,128,1024]{2,1,0:T(8,128)(2,1)}, u32[]{:S(2)}, u32[]{:S(2)}) async-start(bf16[8,128,1024]{2,1,0:T(8,128)(2,1)} %select_rows.1.refs_1_), calls=%async_computation.1 | async-start | bytes 4194304 | tf_op jit(solution)/shard_map/all_to_all | solution.py:789
  62.7 1.0 copy-start.10
  63.7 1.0 copy-start.12
  64.7 9.2 %copy-start = (bf16[512,1024]{1,0:T(8,128)(2,1)}, bf16[512,1024]{1,0:T(8,128)(2,1)S(1)}, u32[]{:S(2)}) copy-start(bf16[512,1024]{1,0:T(8,128)(2,1)S(1)} %get-tuple-element.34.others_ref) | copy-start | bytes 3145732
  69.7 6.8 %copy-start.11 = (f32[512,512]{1,0:T(8,128)S(1)}, f32[512,512]{1,0:T(8,128)}, u32[]{:S(2)}) copy-start(f32[512,512]{1,0:T(8,128)} %copy-done.10) | copy-start | bytes 3145732
  69.7 6.8 %copy-start.13 = (bf16[8,64,1024]{2,1,0:T(8,128)(2,1)S(1)}, bf16[8,64,1024]{2,1,0:T(8,128)(2,1)}, u32[]{:S(2)}) copy-start(bf16[8,64,1024]{2,1,0:T(8,128)(2,1)} %copy-done.12) | copy-start | bytes 3145732
  73.9 5.6 %collective-permute-start.4 = (f32[8,512]{1,0:T(8,128)S(1)}, f32[8,512]{1,0:T(8,128)S(1)}, u32[]{:S(2)}, u32[]{:S(2)}) collective-permute-start(f32[8,512]{1,0:T(8,128)S(1)} %get-tuple-element.39.stats_ref.here_ref), channel_id=1, source_target_pairs={{0,6},{2,4},{4,2},{6,0},{1,7},{3,5},{5,3},{7,1},{8,14},{10,12},{12... | collective-permute-start | bytes 49160 | tf_op jit(solution)/shard_map/ppermute | solution.py:821
  76.5 3.1 %copy-start.1 = (bf16[512,1024]{1,0:T(8,128)(2,1)S(1)}, bf16[512,1024]{1,0:T(8,128)(2,1)}, u32[]{:S(2)}) copy-start(bf16[512,1024]{1,0:T(8,128)(2,1)} %copy-done) | copy-start | bytes 3145732
  78.8 3.6 %copy-start.5 = (f32[512,1024]{1,0:T(8,128)}, f32[512,1024]{1,0:T(8,128)S(1)}, u32[]{:S(2)}) copy-start(f32[512,1024]{1,0:T(8,128)S(1)} %get-tuple-element.51.sums_ref) | copy-start | bytes 6291460
  82.5 31.5 %all-to-all-start.2 = ((bf16[8,128,1024]{2,1,0:T(8,128)(2,1)}), bf16[8,128,1024]{2,1,0:T(8,128)(2,1)}, u32[]{:S(2)}, u32[]{:S(2)}) async-start(bf16[8,128,1024]{2,1,0:T(8,128)(2,1)} %get-tuple-element.52), calls=%async_computation.2 | async-start | bytes 4194304 | tf_op jit(solution)/shard_map/all_to_all | solution.py:789
  87.0 1.6 %copy-start.6 = (f32[512,1024]{1,0:T(8,128)S(1)}, f32[512,1024]{1,0:T(8,128)}, u32[]{:S(2)}) copy-start(f32[512,1024]{1,0:T(8,128)} %copy-done.5) | copy-start | bytes 6291460
  88.6 4.0 %copy-start.2 = (bf16[512,1024]{1,0:T(8,128)(2,1)S(1)}, bf16[512,1024]{1,0:T(8,128)(2,1)}, u32[]{:S(2)}) copy-start(bf16[512,1024]{1,0:T(8,128)(2,1)} %copy-done) | copy-start | bytes 3145732
  90.1 27.9 %collective-permute-start.5 = (bf16[512,1024]{1,0:T(8,128)(2,1)}, bf16[512,1024]{1,0:T(8,128)(2,1)}, u32[]{:S(2)}, u32[]{:S(2)}) collective-permute-start(bf16[512,1024]{1,0:T(8,128)(2,1)} %other_grads.1), channel_id=1, source_target_pairs={{0,6},{2,4},{4,2},{6,0},{1,7},{3,5},{5,3},{7,1},{8,14},{10,12},{12... | collective-permute-start | bytes 3145736 | tf_op jit(solution)/shard_map/ppermute | solution.py:834
  92.6 8.3 %copy-start.14 = (s32[64,16]{1,0:T(8,128)S(1)}, s32[64,16]{1,0:T(8,128)}, u32[]{:S(2)}) copy-start(s32[64,16]{1,0:T(8,128)} %get-tuple-element.75) | copy-start | bytes 12292
  99.8 14.2 %copy-start.4 = (bf16[512,1024]{1,0:T(8,128)(2,1)S(1)}, bf16[512,1024]{1,0:T(8,128)(2,1)}, u32[]{:S(2)}) copy-start(bf16[512,1024]{1,0:T(8,128)(2,1)} %copy-done.3) | copy-start | bytes 3145732
  99.8 1.8 %collective-permute-start.6 = (bf16[128,1024]{1,0:T(8,128)(2,1)}, bf16[128,1024]{1,0:T(8,128)(2,1)S(1)}, u32[]{:S(2)}, u32[]{:S(2)}) collective-permute-start(bf16[128,1024]{1,0:T(8,128)(2,1)} %get-tuple-element.54), channel_id=1, source_target_pairs={{0,1},{1,0},{8,9},{9,8},{16,17},{17,16},{24,25},{25,24},{2,3},{3,2... | collective-permute-start | bytes 786440 | tf_op jit(solution)/shard_map/ppermute | solution.py:833
  99.9 2.1 %collective-permute-start.7 = (bf16[128,1024]{1,0:T(8,128)(2,1)}, bf16[128,1024]{1,0:T(8,128)(2,1)S(1)}, u32[]{:S(2)}, u32[]{:S(2)}) collective-permute-start(bf16[128,1024]{1,0:T(8,128)(2,1)} %get-tuple-element.55), channel_id=1, source_target_pairs={{0,1},{1,0},{8,9},{9,8},{16,17},{17,16},{24,25},{25,24},{2,3},{3,2... | collective-permute-start | bytes 786440 | tf_op jit(solution)/shard_map/ppermute | solution.py:833
  100.4 2.0 %collective-permute-start.8 = (bf16[128,1024]{1,0:T(8,128)(2,1)}, bf16[128,1024]{1,0:T(8,128)(2,1)S(1)}, u32[]{:S(2)}, u32[]{:S(2)}) collective-permute-start(bf16[128,1024]{1,0:T(8,128)(2,1)} %get-tuple-element.56), channel_id=1, source_target_pairs={{0,1},{1,0},{8,9},{9,8},{16,17},{17,16},{24,25},{25,24},{2,3},{3,2... | collective-permute-start | bytes 786440 | tf_op jit(solution)/shard_map/ppermute | solution.py:833
  100.5 2.3 %collective-permute-start.9 = (bf16[128,1024]{1,0:T(8,128)(2,1)}, bf16[128,1024]{1,0:T(8,128)(2,1)S(1)}, u32[]{:S(2)}, u32[]{:S(2)}) collective-permute-start(bf16[128,1024]{1,0:T(8,128)(2,1)} %get-tuple-element.57), channel_id=1, source_target_pairs={{0,1},{1,0},{8,9},{9,8},{16,17},{17,16},{24,25},{25,24},{2,3},{3,2... | collective-permute-start | bytes 786440 | tf_op jit(solution)/shard_map/ppermute | solution.py:833
  102.8 1.2 copy-start.7
  105.6 18.6 %collective-permute-start.10 = (bf16[256,1024]{1,0:T(8,128)(2,1)}, bf16[256,1024]{1,0:T(8,128)(2,1)S(1)}, u32[]{:S(2)}, u32[]{:S(2)}) collective-permute-start(bf16[256,1024]{1,0:T(8,128)(2,1)} %get-tuple-element.59), channel_id=1, source_target_pairs={{0,8},{1,9},{8,0},{9,1},{16,24},{17,25},{24,16},{25,17},{2,10},{3,... | collective-permute-start | bytes 1572872 | tf_op jit(solution)/shard_map/ppermute | solution.py:838
  107.4 17.7 %collective-permute-start.11 = (bf16[256,1024]{1,0:T(8,128)(2,1)}, bf16[256,1024]{1,0:T(8,128)(2,1)S(1)}, u32[]{:S(2)}, u32[]{:S(2)}) collective-permute-start(bf16[256,1024]{1,0:T(8,128)(2,1)} %get-tuple-element.60), channel_id=1, source_target_pairs={{0,16},{1,17},{8,24},{9,25},{16,0},{17,1},{24,8},{25,9},{2,18},{3,... | collective-permute-start | bytes 1572872 | tf_op jit(solution)/shard_map/ppermute | solution.py:838
  108.9 27.1 %collective-permute-start.12 = (bf16[256,1024]{1,0:T(8,128)(2,1)}, bf16[256,1024]{1,0:T(8,128)(2,1)}, u32[]{:S(2)}, u32[]{:S(2)}) collective-permute-start(bf16[256,1024]{1,0:T(8,128)(2,1)} %get-tuple-element.61), channel_id=1, source_target_pairs={{0,24},{1,25},{8,16},{9,17},{16,8},{17,9},{24,0},{25,1},{2,26},{3,... | collective-permute-start | bytes 1572872 | tf_op jit(solution)/shard_map/ppermute | solution.py:838
  117.9 22.2 %collective-permute-start.13 = (bf16[512,1024]{1,0:T(8,128)(2,1)}, bf16[512,1024]{1,0:T(8,128)(2,1)}, u32[]{:S(2)}, u32[]{:S(2)}) collective-permute-start(bf16[512,1024]{1,0:T(8,128)(2,1)} %segment_rows.2.refs_0_), channel_id=1, source_target_pairs={{0,2},{2,0},{4,6},{6,4},{1,3},{3,1},{5,7},{7,5},{8,10},{10,8},{12,... | collective-permute-start | bytes 3145736 | tf_op jit(solution)/shard_map/ppermute | solution.py:836
  118.0 18.0 %copy-start.9 = (bf16[256,1024]{1,0:T(8,128)(2,1)S(1)}, bf16[256,1024]{1,0:T(8,128)(2,1)}, u32[]{:S(2)}) copy-start(bf16[256,1024]{1,0:T(8,128)(2,1)} %get-tuple-element.58.refs_0_) | copy-start | bytes 1572868
